TPU v7x, 768 devices: a whole 4x8x12 slice. The times are simulated.
768 devices in a mesh: walk: 24 (over z, x_lo), par: 32 (over x_hi, y, core).
Axes of the slice: x: 4 (x_hi: 2, x_lo: 2; x = x_hi * 2 + x_lo), y: 8, z: 12, core: 2. Of those that a mesh axis runs over, the one named last changes fastest.
Arguments:
- jacobian: float32 [3072, 16384], P('walk', 'par'), may hold values from -0.046875 to 0.046875
- coeffs: float32 [3072], P('walk'), may hold values from -0.109375 to 0.109375
Outputs:
- gram: float32 [3072, 3072], P('walk', 'par')
- update: float32 [16384], P('par')
All inputs are finite; a program needn't handle non-finite values.
Results may differ from a plain program's by a relative error of at most 0.000084.
Values sent between devices are 32-bit elements; how exact they have to be, the bound alone decides.
No kernel may reach another device: no remote copies, remote signals or barrier semaphores. Data moves between devices by JAX's collectives and lax.ppermute only.
A program may use at most 32 MiB of HBM per device.

v0:
```python
import jax
import jax.numpy as jnp
from jax import lax
from jax.sharding import PartitionSpec as P


def tile_product(left, right):
    return jnp.dot(
        left, right.T, precision=lax.Precision.HIGHEST, preferred_element_type=jnp.float32
    )


def shards(jacobian, coeffs):
    partial_gram = tile_product(jacobian, lax.all_gather(jacobian, "walk", axis=0, tiled=True))
    gram = lax.psum_scatter(partial_gram, "par", scatter_dimension=1, tiled=True)
    local_term = jnp.dot(
        coeffs, jacobian, precision=lax.Precision.HIGHEST, preferred_element_type=jnp.float32
    )
    update = lax.psum(local_term, "walk")
    return (gram, update)


def solution(mesh):
    in_specs = (P("walk", "par"), P("walk"))
    out_specs = (P("walk", "par"), P("par"))
    return jax.shard_map(shards, mesh=mesh, in_specs=in_specs, out_specs=out_specs, check_vma=False)
```

profile of v0, /device:TPU:16, one launch (start us, length us, event | category | flops | bytes accessed | tf_op | source)
XLA Modules:
  0.0 316.4 jit_solution(5478498947985287660)
XLA Ops:
  7.2 0.0 copy-start
  7.2 0.0 copy-start.1
  7.2 0.0 all-gather.2.cloned.1.call-start
  7.2 0.7 all-gather.2.cloned.1.call-update
  7.9 0.0 reduce-scatter.2.cloned.1.call-start
  8.0 161.3 %all-gather.2.cloned.1.call-done = f32[3072,512]{1,0:T(8,128)} async-done(((f32[128,512]{1,0:T(8,128)}), f32[3072,512]{1,0:T(8,128)}) %all-gather.2.cloned.1.call-update) | async-done | bytes 6291472 | tf_op jit(solution)/shard_map/all_gather | solution.py:14
  169.3 8.1 %fusion.2 = f32[128,3072]{0,1:T(8,128)} fusion(f32[128,512]{1,0:T(8,128)} %param.2, f32[3072,512]{1,0:T(8,128)} %all-gather.2.cloned.1.call-done), kind=kOutput, calls=%fused_computation.2 | convolution fusion | flops 2415919104 | bytes 8126464 | tf_op jit(solution)/shard_map/dot_general | solution.py:8
  177.4 0.0 reduce-scatter.2.cloned.1.call-update
  177.4 0.0 copy-done
  177.4 0.0 copy-done.1
  177.4 0.2 fusion
  177.6 47.4 %psum.7 = f32[512]{0:T(512)} all-reduce(f32[512]{0:T(512)S(1)} %bitcast.7), channel_id=1, replica_groups=mesh['walk'=24,'par'=32] {'walk'}, use_global_device_ids=true, to_apply=%region_1.0 | all-reduce | flops 512 | bytes 4096 | tf_op jit(solution)/shard_map/psum | solution.py:19
  225.0 84.5 %reduce-scatter.2.cloned.1.call-done = f32[128,96]{0,1:T(8,128)} async-done(((f32[128,3072]{0,1:T(8,128)}), f32[128,96]{0,1:T(8,128)}) %reduce-scatter.2.cloned.1.call-update) | async-done | bytes 49168 | tf_op jit(solution)/shard_map/reduce_scatter | solution.py:15
Async XLA Ops:
  7.2 170.2 %copy-start = (f32[128]{0:T(128)S(1)}, f32[128]{0:T(128)}, u32[]{:S(2)}) copy-start(f32[128]{0:T(128)} %param.3) | copy-start | bytes 1540
  7.2 170.2 %copy-start.1 = (f32[128,512]{1,0:T(8,128)S(1)}, f32[128,512]{1,0:T(8,128)}, u32[]{:S(2)}) copy-start(f32[128,512]{1,0:T(8,128)} %param.2) | copy-start | bytes 786436
  7.2 162.1 %all-gather.2.cloned.1.call-start = ((), (), s32[]{:S(2)}) async-start(), calls=%async_computation.1 | async-start | bytes 6553600 | tf_op jit(solution)/shard_map/all_gather | solution.py:14
  7.9 301.6 %reduce-scatter.2.cloned.1.call-start = ((), (), s32[]{:S(2)}) async-start(), calls=%async_computation.2 | async-start | bytes 1622016 | tf_op jit(solution)/shard_map/reduce_scatter | solution.py:15
Sparse Core Ops, SparseCore 0:
  10.4 158.8 all-gather.1
  177.5 131.9 reduce-scatter.1
where the time goes:
time: 316 us
  waiting for transfers between devices  246 us (78%)
  blocking collectives  47.4 us (15%)
  between operations  14.1 us (4%)
  matrix products  8.31 us (3%)
    all_gather x1, waiting for transfers between devices, shards(): lax.all_gather(jacobian, 'walk', axis=0, tiled=True)  161 us
    reduce_scatter x1, waiting for transfers between devices, shards(): lax.psum_scatter(partial_gram, 'par', scatter_dimension=1, tiled=True)  84.5 us
    psum x1, blocking collectives, shards(): update = lax.psum(local_term, 'walk')  47.4 us
    dot_general x1, matrix products, tile_product(): jnp.dot(left, right.T, precision=lax.Precision.HIGHEST, preferred_element...  8.06 us
  transfers between devices with their start and end apart: 2, of which 2 were waited for; matrix products, arithmetic and copies ran while one was open for 0% of the time, Pallas kernels for 0%

commit v1 on v0

v1 whole, which is shorter than its diff:
```python
import numpy as np
import jax
import jax.numpy as jnp
from jax import lax
from jax.experimental import pallas as pl
from jax.experimental.pallas import tpu as pltpu
from jax.sharding import PartitionSpec as P

NZ = 12
NQ = 16
SLICE = 32
OTHER = 7

COL_OFFSET = (
    {0: 0, 1: 1, 2: 1, 3: 1, 4: 1, 5: 3, 6: 3, -1: 0, -2: 0, -3: 0, -4: -2, -5: -2},
    {0: 0, 1: 2, 2: 2, 3: 2, 4: 2, 5: 2, 6: 3, -1: 0, -2: 0, -3: 0, -4: -1, -5: -3},
)


def units_of(xl):
    units = [(c - d + 3, c + 3) for d, c in COL_OFFSET[xl].items()]
    for d in (range(-3, 3) if xl == 0 else range(-2, 4)):
        units += [(d + 3, OTHER), (OTHER, d + 3)]
    halves, counts = ([], []), [0, 0, 0]
    for unit in units:
        cls = class_of(unit[1], xl)
        halves[0 if counts[cls] < 4 else 1].append(unit)
        counts[cls] += 1
    assert len(halves[0]) == len(halves[1]) == 12
    return halves


def offset_of(block, xl):
    return (3, 1 - xl) if block == OTHER else (block - 3, xl)


def class_of(block, xl):
    d, x = offset_of(block, xl)
    return (2 * d + x) % 3


def plan():
    tables = np.zeros((3, 2, 2, 2, 12, 6), np.int32)
    pairs = [[], [], []]
    seen = set()
    for z in range(NZ):
        for xl in range(2):
            halves = units_of(xl)
            for core in range(2):
                rank = [0, 0, 0]
                for n, (row, col) in enumerate(halves[core]):
                    rd, rx = offset_of(row, xl)
                    cd, cx = offset_of(col, xl)
                    rz, cz = (z + rd) % NZ, (z + cd) % NZ
                    entry = [row, col]
                    for k in range(4):
                        index = 4 * (2 * cz + cx) + k
                        slot = index % 3
                        q = rank[slot]
                        rank[slot] += 1
                        entry.append(q * 3 + slot)
                        source = (z * 2 + xl) * 2 * NQ + q * 2 + core
                        target = (rz * 2 + rx) * 2 * NQ + index // 3
                        pairs[slot].append((source, target))
                        seen.add((target, slot))
                    for mine in range(2):
                        tables[z % 3, xl, mine, int(core != mine), n] = entry
                assert rank == [NQ, NQ, NQ]
    assert len(seen) == NZ * 2 * 2 * NQ * 3
    return tables.reshape(12, 2 * 12 * 6), pairs


def gram_kernel(table, *refs):
    blocks, keep, send, parts = refs[:8], refs[8], refs[9], refs[10]
    depth = blocks[0].shape[1]
    for b, ref in enumerate(blocks):
        value = ref[...]
        high = value.astype(jnp.bfloat16)
        parts[b, :, :depth] = high
        parts[b, :, depth:] = (value - high.astype(jnp.float32)).astype(jnp.bfloat16)
    dims = (((1,), (1,)), ((), ()))

    def dot(left, right):
        return lax.dot_general(left, right, dims, preferred_element_type=jnp.float32)

    for half, out in ((1, send), (0, keep)):
        for n in range(12):
            at = (half * 12 + n) * 6
            row, col = table[at], table[at + 1]
            row_high, row_low = parts[row, :, :depth], parts[row, :, depth:]
            col_high, col_low = parts[col, :, :depth], parts[col, :, depth:]
            tile = dot(col_high, row_high) + (dot(col_high, row_low) + dot(col_low, row_high))
            for k in range(4):
                out[table[at + 2 + k]] = tile[k * SLICE:(k + 1) * SLICE]


def gram_parts(table, blocks):
    rows, depth = blocks[0].shape
    out = jax.ShapeDtypeStruct((NQ * 3, SLICE, rows), jnp.float32)
    vmem = pl.BlockSpec(memory_space=pltpu.VMEM)
    return pl.pallas_call(
        gram_kernel,
        out_shape=(out, out),
        in_specs=[pl.BlockSpec(memory_space=pltpu.SMEM)] + [vmem] * len(blocks),
        out_specs=(vmem, vmem),
        scratch_shapes=[pltpu.VMEM((len(blocks), rows, 2 * depth), jnp.bfloat16)],
        compiler_params=pltpu.CompilerParams(vmem_limit_bytes=32 * 2**20),
    )(table, *blocks)


def walk_perm(dz, flip):
    return [
        (((z + dz) % NZ) * 2 + (x ^ flip), z * 2 + x) for z in range(NZ) for x in range(2)
    ]


def solution(mesh):
    tables, last_pairs = plan()

    def shards(jacobian, coeffs):
        walk, par = lax.axis_index("walk"), lax.axis_index("par")
        z, xl, core = walk // 2, walk % 2, par % 2
        table = lax.dynamic_index_in_dim(
            jnp.asarray(tables), ((z % 3) * 2 + xl) * 2 + core, 0, keepdims=False
        )

        def walk_get(value, dz, flip=0):
            return lax.ppermute(value, "walk", walk_perm(dz, flip))

        up1, down1 = walk_get(jacobian, 1), walk_get(jacobian, -1)
        up2, down2 = walk_get(up1, 1), walk_get(down1, -1)
        up3, down3 = walk_get(up2, 1), walk_get(down2, -1)
        other = walk_get(up2, 1, 1)

        term = jnp.sum(coeffs[:, None] * jacobian, axis=0)
        term = term + walk_get(term, 0, 1)
        term = term + walk_get(term, 6)
        term = term + walk_get(term, 3)
        after, before = walk_get(term, 1), walk_get(term, -1)
        place = z % 3
        first = jnp.where(place == 0, term, jnp.where(place == 1, before, after))
        second = jnp.where(place == 0, after, jnp.where(place == 1, term, before))
        third = jnp.where(place == 0, before, jnp.where(place == 1, after, term))
        update = (first + second) + third

        keep, send = gram_parts(
            table, (down3, down2, down1, jacobian, up1, up2, up3, other)
        )
        swap = [(p, p ^ 1) for p in range(2 * NQ)]
        mine = keep + lax.ppermute(send, "par", swap)
        groups = [[q * 2 + c for q in range(NQ)] for c in range(2)]
        mine = mine.reshape(NQ, 3, SLICE, -1)
        mine = lax.all_to_all(mine, "par", 0, 0, axis_index_groups=groups, tiled=True)
        mine = jnp.sum(mine, axis=0)
        slices = [
            lax.ppermute(mine[slot], ("walk", "par"), last_pairs[slot]) for slot in range(3)
        ]
        return jnp.concatenate(slices, axis=0).T, update

    in_specs = (P("walk", "par"), P("walk"))
    out_specs = (P("walk", "par"), P("par"))
    return jax.shard_map(shards, mesh=mesh, in_specs=in_specs, out_specs=out_specs, check_vma=False)
```

time: 316 us -> 127 us (0.40)
  the two profiles are of different devices: /device:TPU:16 before, /device:TPU:89 now
where the time goes in v1:
time: 127 us; the launch traced here: 126 us
  starting transfers between devices  82 us (65%)
  waiting for transfers between devices  35.3 us (28%)
  Pallas kernels  3.61 us (3%)
  other arithmetic  2.41 us (2%)
  local copies, waits for them, and re-layouts  1.67 us (1%)
    ppermute x12, starting transfers between devices, walk_get(): return lax.ppermute(value, 'walk', walk_perm(dz, flip))  45.9 us
    ppermute x12, waiting for transfers between devices, walk_get(): return lax.ppermute(value, 'walk', walk_perm(dz, flip))  24.5 us
    ppermute x3, starting transfers between devices, shards(): lax.ppermute(mine[slot], ('walk', 'par'), last_pairs[slot])  20.9 us
    all_to_all x1, starting transfers between devices, shards(): lax.all_to_all(mine, 'par', 0, 0, axis_index_groups=groups, tiled=True)  9.07 us
    ppermute x3, waiting for transfers between devices, shards(): lax.ppermute(mine[slot], ('walk', 'par'), last_pairs[slot])  8.86 us
    ppermute x1, starting transfers between devices, shards(): mine = keep + lax.ppermute(send, 'par', swap)  6.09 us
    pallas_call x1, Pallas kernels, gram_parts(): pl.pallas_call(gram_kernel, out_shape=(out, out), in_specs=[pl.BlockSpec(...  3.61 us
  transfers between devices with their start and end apart: 17, of which 10 were waited for; matrix products, arithmetic and copies ran while one was open for 1% of the time, Pallas kernels for 0%

profile of v1, /device:TPU:89, one launch (start us, length us, event | category | flops | bytes accessed | tf_op | source)
XLA Modules:
  0.0 125.9 jit_solution(11117896239072798391)
XLA Ops:
  0.6 1.9 %collective-permute-start.3 = (f32[128,512]{1,0:T(8,128)}, f32[128,512]{1,0:T(8,128)S(1)}, u32[]{:S(2)}, u32[]{:S(2)}) collective-permute-start(f32[128,512]{1,0:T(8,128)} %refs_3_.1), channel_id=1, source_target_pairs={{64,0},{96,32},{128,64},{160,96},{192,128},{224,160},{256,192},{28... | collective-permute-start | bytes 786440 | tf_op jit(solution)/shard_map/ppermute | solution.py:128
  2.6 4.0 %collective-permute-start = (f32[128,512]{1,0:T(8,128)}, f32[128,512]{1,0:T(8,128)S(1)}, u32[]{:S(2)}, u32[]{:S(2)}) collective-permute-start(f32[128,512]{1,0:T(8,128)} %refs_3_.1), channel_id=1, source_target_pairs={{704,0},{736,32},{0,64},{32,96},{64,128},{96,160},{128,192},{160,2... | collective-permute-start | bytes 786440 | tf_op jit(solution)/shard_map/ppermute | solution.py:128
  6.6 4.3 %collective-permute-done.3.refs_4_ = f32[128,512]{1,0:T(8,128)S(1)} collective-permute-done((f32[128,512]{1,0:T(8,128)}, f32[128,512]{1,0:T(8,128)S(1)}, u32[]{:S(2)}, u32[]{:S(2)}) %collective-permute-start.3) | collective-permute-done | bytes 262176 | tf_op jit(solution)/shard_map/ppermute | solution.py:128
  10.9 10.6 %collective-permute-start.4 = (f32[128,512]{1,0:T(8,128)S(1)}, f32[128,512]{1,0:T(8,128)S(1)}, u32[]{:S(2)}, u32[]{:S(2)}) collective-permute-start(f32[128,512]{1,0:T(8,128)S(1)} %collective-permute-done.3.refs_4_), channel_id=1, source_target_pairs={{64,0},{96,32},{128,64},{160,96},{192,128},{224,160},{256,192},{28... | collective-permute-start | bytes 786440 | tf_op jit(solution)/shard_map/ppermute | solution.py:128
  21.5 0.7 collective-permute-done.refs_2_
  22.1 1.9 %collective-permute-start.1 = (f32[128,512]{1,0:T(8,128)S(1)}, f32[128,512]{1,0:T(8,128)S(1)}, u32[]{:S(2)}, u32[]{:S(2)}) collective-permute-start(f32[128,512]{1,0:T(8,128)S(1)} %collective-permute-done.refs_2_), channel_id=1, source_target_pairs={{704,0},{736,32},{0,64},{32,96},{64,128},{96,160},{128,192},{160,2... | collective-permute-start | bytes 786440 | tf_op jit(solution)/shard_map/ppermute | solution.py:128
  24.1 1.5 %collective-permute-done.4.refs_5_ = f32[128,512]{1,0:T(8,128)S(1)} collective-permute-done((f32[128,512]{1,0:T(8,128)S(1)}, f32[128,512]{1,0:T(8,128)S(1)}, u32[]{:S(2)}, u32[]{:S(2)}) %collective-permute-start.4) | collective-permute-done | bytes 262176 | tf_op jit(solution)/shard_map/ppermute | solution.py:128
  25.5 5.2 %collective-permute-start.5 = (f32[128,512]{1,0:T(8,128)S(1)}, f32[128,512]{1,0:T(8,128)S(1)}, u32[]{:S(2)}, u32[]{:S(2)}) collective-permute-start(f32[128,512]{1,0:T(8,128)S(1)} %collective-permute-done.4.refs_5_), channel_id=1, source_target_pairs={{64,0},{96,32},{128,64},{160,96},{192,128},{224,160},{256,192},{28... | collective-permute-start | bytes 786440 | tf_op jit(solution)/shard_map/ppermute | solution.py:128
  30.7 6.2 %collective-permute-start.6 = (f32[128,512]{1,0:T(8,128)S(1)}, f32[128,512]{1,0:T(8,128)S(1)}, u32[]{:S(2)}, u32[]{:S(2)}) collective-permute-start(f32[128,512]{1,0:T(8,128)S(1)} %collective-permute-done.4.refs_5_), channel_id=1, source_target_pairs={{96,0},{64,32},{160,64},{128,96},{224,128},{192,160},{288,192},{25... | collective-permute-start | bytes 786440 | tf_op jit(solution)/shard_map/ppermute | solution.py:128
  37.0 0.0 collective-permute-done.1.refs_1_
  37.0 1.9 %collective-permute-start.2 = (f32[128,512]{1,0:T(8,128)S(1)}, f32[128,512]{1,0:T(8,128)S(1)}, u32[]{:S(2)}, u32[]{:S(2)}) collective-permute-start(f32[128,512]{1,0:T(8,128)S(1)} %collective-permute-done.1.refs_1_), channel_id=1, source_target_pairs={{704,0},{736,32},{0,64},{32,96},{64,128},{96,160},{128,192},{160,2... | collective-permute-start | bytes 786440 | tf_op jit(solution)/shard_map/ppermute | solution.py:128
  39.0 0.7 constant_dynamic-slice_fusion
  39.7 0.0 collective-permute-done.5.refs_6_
  39.7 0.6 collective-permute-done.6.refs_7_
  40.3 3.8 %collective-permute-done.2.refs_0_ = f32[128,512]{1,0:T(8,128)S(1)} collective-permute-done((f32[128,512]{1,0:T(8,128)S(1)}, f32[128,512]{1,0:T(8,128)S(1)}, u32[]{:S(2)}, u32[]{:S(2)}) %collective-permute-start.2) | collective-permute-done | bytes 262176 | tf_op jit(solution)/shard_map/ppermute | solution.py:128
  44.1 0.0 copy-start
  44.1 0.9 copy-done
  45.1 3.6 %shard_map.50 = (f32[48,32,128]{2,1,0:T(8,128)S(1)}, f32[48,32,128]{2,1,0:T(8,128)S(1)}) custom-call(s32[144]{0:T(256)S(1)} %bitcast.10, f32[128,512]{1,0:T(8,128)S(1)} %collective-permute-done.2.refs_0_, f32[128,512]{1,0:T(8,128)S(1)} %collective-permute-done.1.refs_1_, f32[128,512]{1,0:T(8,128)S(1)} %collective-permute-done.refs_2_, ...), custom_call_target="tpu_custom_call" | custom-call | tf_op jit(solution)/shard_map/pallas_call | solution.py:101
  48.7 6.1 %collective-permute-start.7 = (f32[48,32,128]{2,1,0:T(8,128)S(1)}, f32[48,32,128]{2,1,0:T(8,128)S(1)}, u32[]{:S(2)}, u32[]{:S(2)}) collective-permute-start(f32[48,32,128]{2,1,0:T(8,128)S(1)} %get-tuple-element.5), channel_id=1, source_target_pairs={{0,1},{1,0},{2,3},{3,2},{4,5},{5,4},{6,7},{7,6},{8,9},{9,8},{10,11... | collective-permute-start | bytes 2359304 | tf_op jit(solution)/shard_map/ppermute | solution.py:150
  54.8 1.9 %collective-permute-done.7 = f32[48,32,128]{2,1,0:T(8,128)S(1)} collective-permute-done((f32[48,32,128]{2,1,0:T(8,128)S(1)}, f32[48,32,128]{2,1,0:T(8,128)S(1)}, u32[]{:S(2)}, u32[]{:S(2)}) %collective-permute-start.7) | collective-permute-done | bytes 786464 | tf_op jit(solution)/shard_map/ppermute | solution.py:150
  56.7 1.0 add.46
  57.7 0.0 copy-start.1
  57.7 0.0 copy-start.2
  57.7 9.1 %all-to-all-start = ((f32[16,3,32,128]{3,2,1,0:T(8,128)}), f32[16,3,32,128]{3,2,1,0:T(8,128)S(1)}, u32[]{:S(2)}, u32[]{:S(2)}) async-start(f32[16,3,32,128]{3,2,1,0:T(8,128)} %bitcast.1), calls=%async_computation | async-start | bytes 1572864 | tf_op jit(solution)/shard_map/all_to_all | solution.py:153
  66.8 0.0 copy-done.1
  66.8 0.0 copy-done.2
  66.8 0.1 multiply_reduce_fusion
  66.9 1.9 %collective-permute-start.11 = (f32[512]{0:T(512)S(1)}, f32[512]{0:T(512)S(1)}, u32[]{:S(2)}, u32[]{:S(2)}) collective-permute-start(f32[512]{0:T(512)S(1)} %multiply_reduce_fusion), channel_id=1, source_target_pairs={{32,0},{0,32},{96,64},{64,96},{160,128},{128,160},{224,192},{192,2... | collective-permute-start | bytes 6152 | tf_op jit(solution)/shard_map/ppermute | solution.py:128
  68.8 2.7 %collective-permute-done.11 = f32[512]{0:T(512)S(1)} collective-permute-done((f32[512]{0:T(512)S(1)}, f32[512]{0:T(512)S(1)}, u32[]{:S(2)}, u32[]{:S(2)}) %collective-permute-start.11) | collective-permute-done | bytes 2080 | tf_op jit(solution)/shard_map/ppermute | solution.py:128
  71.5 4.5 %collective-permute-start.12 = (f32[512]{0:T(512)S(1)}, f32[512]{0:T(512)S(1)}, u32[]{:S(2)}, u32[]{:S(2)}) collective-permute-start(f32[512]{0:T(512)S(1)} %add.47), channel_id=1, source_target_pairs={{384,0},{416,32},{448,64},{480,96},{512,128},{544,160},{576,192},{... | collective-permute-start | bytes 6152 | tf_op jit(solution)/shard_map/ppermute | solution.py:128
  76.0 6.1 %collective-permute-done.12 = f32[512]{0:T(512)S(1)} collective-permute-done((f32[512]{0:T(512)S(1)}, f32[512]{0:T(512)S(1)}, u32[]{:S(2)}, u32[]{:S(2)}) %collective-permute-start.12) | collective-permute-done | bytes 2080 | tf_op jit(solution)/shard_map/ppermute | solution.py:128
  82.2 2.4 %collective-permute-start.13 = (f32[512]{0:T(512)S(1)}, f32[512]{0:T(512)S(1)}, u32[]{:S(2)}, u32[]{:S(2)}) collective-permute-start(f32[512]{0:T(512)S(1)} %add.48), channel_id=1, source_target_pairs={{192,0},{224,32},{256,64},{288,96},{320,128},{352,160},{384,192},{... | collective-permute-start | bytes 6152 | tf_op jit(solution)/shard_map/ppermute | solution.py:128
  84.6 4.9 %collective-permute-done.13 = f32[512]{0:T(512)S(1)} collective-permute-done((f32[512]{0:T(512)S(1)}, f32[512]{0:T(512)S(1)}, u32[]{:S(2)}, u32[]{:S(2)}) %collective-permute-start.13) | collective-permute-done | bytes 2080 | tf_op jit(solution)/shard_map/ppermute | solution.py:128
  89.5 1.9 %collective-permute-start.14 = (f32[512]{0:T(512)S(1)}, f32[512]{0:T(512)S(1)}, u32[]{:S(2)}, u32[]{:S(2)}) collective-permute-start(f32[512]{0:T(512)S(1)} %add.49), channel_id=1, source_target_pairs={{704,0},{736,32},{0,64},{32,96},{64,128},{96,160},{128,192},{160,2... | collective-permute-start | bytes 6152 | tf_op jit(solution)/shard_map/ppermute | solution.py:128
  91.4 3.4 %collective-permute-start.15 = (f32[512]{0:T(512)S(1)}, f32[512]{0:T(512)S(1)}, u32[]{:S(2)}, u32[]{:S(2)}) collective-permute-start(f32[512]{0:T(512)S(1)} %add.49), channel_id=1, source_target_pairs={{64,0},{96,32},{128,64},{160,96},{192,128},{224,160},{256,192},{28... | collective-permute-start | bytes 6152 | tf_op jit(solution)/shard_map/ppermute | solution.py:128
  94.8 0.0 all-to-all-done
  94.8 0.1 reduce_sum.18
  94.9 2.9 %collective-permute-start.10 = (f32[32,128]{1,0:T(8,128)S(1)}, f32[32,128]{1,0:T(8,128)S(1)}, u32[]{:S(2)}, u32[]{:S(2)}) collective-permute-start(f32[32,128]{1,0:T(8,128)S(1)} %get-tuple-element.7), channel_id=1, source_target_pairs={{0,0},{2,2},{4,3},{6,706},{8,707},{10,642},{12,643},{14,578},{16,5... | collective-permute-start | bytes 49160 | tf_op jit(solution)/shard_map/ppermute | solution.py:156
  97.8 14.6 %collective-permute-start.8 = (f32[32,128]{1,0:T(8,128)S(1)}, f32[32,128]{1,0:T(8,128)S(1)}, u32[]{:S(2)}, u32[]{:S(2)}) collective-permute-start(f32[32,128]{1,0:T(8,128)S(1)} %get-tuple-element.6), channel_id=1, source_target_pairs={{0,0},{2,1},{4,3},{6,707},{8,643},{10,579},{12,648},{14,649},{16,5... | collective-permute-start | bytes 49160 | tf_op jit(solution)/shard_map/ppermute | solution.py:156
  112.4 3.4 %collective-permute-start.9 = (f32[32,128]{1,0:T(8,128)S(1)}, f32[32,128]{1,0:T(8,128)S(1)}, u32[]{:S(2)}, u32[]{:S(2)}) collective-permute-start(f32[32,128]{1,0:T(8,128)S(1)} %get-tuple-element.8), channel_id=1, source_target_pairs={{0,0},{2,3},{4,707},{6,643},{8,579},{10,648},{12,584},{14,64},{16,... | collective-permute-start | bytes 49160 | tf_op jit(solution)/shard_map/ppermute | solution.py:156
  115.8 0.0 collective-permute-done.14
  115.8 0.0 collective-permute-done.15
  115.8 0.6 select_add_fusion
  116.4 0.0 collective-permute-done.10
  116.4 0.0 collective-permute-done.8
  116.4 8.9 %collective-permute-done.9 = f32[32,128]{1,0:T(8,128)S(1)} collective-permute-done((f32[32,128]{1,0:T(8,128)S(1)}, f32[32,128]{1,0:T(8,128)S(1)}, u32[]{:S(2)}, u32[]{:S(2)}) %collective-permute-start.9) | collective-permute-done | bytes 16416 | tf_op jit(solution)/shard_map/ppermute | solution.py:156
  125.3 0.6 maximum_bitcast_fusion
  (4 shorter events, 0.0 us)
Async XLA Ops:
  0.6 10.2 %collective-permute-start.3 = (f32[128,512]{1,0:T(8,128)}, f32[128,512]{1,0:T(8,128)S(1)}, u32[]{:S(2)}, u32[]{:S(2)}) collective-permute-start(f32[128,512]{1,0:T(8,128)} %refs_3_.1), channel_id=1, source_target_pairs={{64,0},{96,32},{128,64},{160,96},{192,128},{224,160},{256,192},{28... | collective-permute-start | bytes 786440 | tf_op jit(solution)/shard_map/ppermute | solution.py:128
  2.6 19.6 %collective-permute-start = (f32[128,512]{1,0:T(8,128)}, f32[128,512]{1,0:T(8,128)S(1)}, u32[]{:S(2)}, u32[]{:S(2)}) collective-permute-start(f32[128,512]{1,0:T(8,128)} %refs_3_.1), channel_id=1, source_target_pairs={{704,0},{736,32},{0,64},{32,96},{64,128},{96,160},{128,192},{160,2... | collective-permute-start | bytes 786440 | tf_op jit(solution)/shard_map/ppermute | solution.py:128
  10.9 14.7 %collective-permute-start.4 = (f32[128,512]{1,0:T(8,128)S(1)}, f32[128,512]{1,0:T(8,128)S(1)}, u32[]{:S(2)}, u32[]{:S(2)}) collective-permute-start(f32[128,512]{1,0:T(8,128)S(1)} %collective-permute-done.3.refs_4_), channel_id=1, source_target_pairs={{64,0},{96,32},{128,64},{160,96},{192,128},{224,160},{256,192},{28... | collective-permute-start | bytes 786440 | tf_op jit(solution)/shard_map/ppermute | solution.py:128
  22.1 14.8 %collective-permute-start.1 = (f32[128,512]{1,0:T(8,128)S(1)}, f32[128,512]{1,0:T(8,128)S(1)}, u32[]{:S(2)}, u32[]{:S(2)}) collective-permute-start(f32[128,512]{1,0:T(8,128)S(1)} %collective-permute-done.refs_2_), channel_id=1, source_target_pairs={{704,0},{736,32},{0,64},{32,96},{64,128},{96,160},{128,192},{160,2... | collective-permute-start | bytes 786440 | tf_op jit(solution)/shard_map/ppermute | solution.py:128
  25.5 14.2 %collective-permute-start.5 = (f32[128,512]{1,0:T(8,128)S(1)}, f32[128,512]{1,0:T(8,128)S(1)}, u32[]{:S(2)}, u32[]{:S(2)}) collective-permute-start(f32[128,512]{1,0:T(8,128)S(1)} %collective-permute-done.4.refs_5_), channel_id=1, source_target_pairs={{64,0},{96,32},{128,64},{160,96},{192,128},{224,160},{256,192},{28... | collective-permute-start | bytes 786440 | tf_op jit(solution)/shard_map/ppermute | solution.py:128
  30.7 9.5 %collective-permute-start.6 = (f32[128,512]{1,0:T(8,128)S(1)}, f32[128,512]{1,0:T(8,128)S(1)}, u32[]{:S(2)}, u32[]{:S(2)}) collective-permute-start(f32[128,512]{1,0:T(8,128)S(1)} %collective-permute-done.4.refs_5_), channel_id=1, source_target_pairs={{96,0},{64,32},{160,64},{128,96},{224,128},{192,160},{288,192},{25... | collective-permute-start | bytes 786440 | tf_op jit(solution)/shard_map/ppermute | solution.py:128
  37.0 7.1 %collective-permute-start.2 = (f32[128,512]{1,0:T(8,128)S(1)}, f32[128,512]{1,0:T(8,128)S(1)}, u32[]{:S(2)}, u32[]{:S(2)}) collective-permute-start(f32[128,512]{1,0:T(8,128)S(1)} %collective-permute-done.1.refs_1_), channel_id=1, source_target_pairs={{704,0},{736,32},{0,64},{32,96},{64,128},{96,160},{128,192},{160,2... | collective-permute-start | bytes 786440 | tf_op jit(solution)/shard_map/ppermute | solution.py:128
  44.1 1.0 copy-start
  48.7 8.0 %collective-permute-start.7 = (f32[48,32,128]{2,1,0:T(8,128)S(1)}, f32[48,32,128]{2,1,0:T(8,128)S(1)}, u32[]{:S(2)}, u32[]{:S(2)}) collective-permute-start(f32[48,32,128]{2,1,0:T(8,128)S(1)} %get-tuple-element.5), channel_id=1, source_target_pairs={{0,1},{1,0},{2,3},{3,2},{4,5},{5,4},{6,7},{7,6},{8,9},{9,8},{10,11... | collective-permute-start | bytes 2359304 | tf_op jit(solution)/shard_map/ppermute | solution.py:150
  57.7 9.1 %copy-start.1 = (f32[128,512]{1,0:T(8,128)S(1)}, f32[128,512]{1,0:T(8,128)}, u32[]{:S(2)}) copy-start(f32[128,512]{1,0:T(8,128)} %refs_3_.1) | copy-start | bytes 786436
  57.7 9.1 %copy-start.2 = (f32[128]{0:T(128)S(1)}, f32[128]{0:T(128)}, u32[]{:S(2)}) copy-start(f32[128]{0:T(128)} %param.4) | copy-start | bytes 1540
  57.7 37.1 %all-to-all-start = ((f32[16,3,32,128]{3,2,1,0:T(8,128)}), f32[16,3,32,128]{3,2,1,0:T(8,128)S(1)}, u32[]{:S(2)}, u32[]{:S(2)}) async-start(f32[16,3,32,128]{3,2,1,0:T(8,128)} %bitcast.1), calls=%async_computation | async-start | bytes 1572864 | tf_op jit(solution)/shard_map/all_to_all | solution.py:153
  66.9 4.6 %collective-permute-start.11 = (f32[512]{0:T(512)S(1)}, f32[512]{0:T(512)S(1)}, u32[]{:S(2)}, u32[]{:S(2)}) collective-permute-start(f32[512]{0:T(512)S(1)} %multiply_reduce_fusion), channel_id=1, source_target_pairs={{32,0},{0,32},{96,64},{64,96},{160,128},{128,160},{224,192},{192,2... | collective-permute-start | bytes 6152 | tf_op jit(solution)/shard_map/ppermute | solution.py:128
  71.5 10.6 %collective-permute-start.12 = (f32[512]{0:T(512)S(1)}, f32[512]{0:T(512)S(1)}, u32[]{:S(2)}, u32[]{:S(2)}) collective-permute-start(f32[512]{0:T(512)S(1)} %add.47), channel_id=1, source_target_pairs={{384,0},{416,32},{448,64},{480,96},{512,128},{544,160},{576,192},{... | collective-permute-start | bytes 6152 | tf_op jit(solution)/shard_map/ppermute | solution.py:128
  82.2 7.3 %collective-permute-start.13 = (f32[512]{0:T(512)S(1)}, f32[512]{0:T(512)S(1)}, u32[]{:S(2)}, u32[]{:S(2)}) collective-permute-start(f32[512]{0:T(512)S(1)} %add.48), channel_id=1, source_target_pairs={{192,0},{224,32},{256,64},{288,96},{320,128},{352,160},{384,192},{... | collective-permute-start | bytes 6152 | tf_op jit(solution)/shard_map/ppermute | solution.py:128
  89.5 26.3 %collective-permute-start.14 = (f32[512]{0:T(512)S(1)}, f32[512]{0:T(512)S(1)}, u32[]{:S(2)}, u32[]{:S(2)}) collective-permute-start(f32[512]{0:T(512)S(1)} %add.49), channel_id=1, source_target_pairs={{704,0},{736,32},{0,64},{32,96},{64,128},{96,160},{128,192},{160,2... | collective-permute-start | bytes 6152 | tf_op jit(solution)/shard_map/ppermute | solution.py:128
  91.4 24.4 %collective-permute-start.15 = (f32[512]{0:T(512)S(1)}, f32[512]{0:T(512)S(1)}, u32[]{:S(2)}, u32[]{:S(2)}) collective-permute-start(f32[512]{0:T(512)S(1)} %add.49), channel_id=1, source_target_pairs={{64,0},{96,32},{128,64},{160,96},{192,128},{224,160},{256,192},{28... | collective-permute-start | bytes 6152 | tf_op jit(solution)/shard_map/ppermute | solution.py:128
  94.9 21.5 %collective-permute-start.10 = (f32[32,128]{1,0:T(8,128)S(1)}, f32[32,128]{1,0:T(8,128)S(1)}, u32[]{:S(2)}, u32[]{:S(2)}) collective-permute-start(f32[32,128]{1,0:T(8,128)S(1)} %get-tuple-element.7), channel_id=1, source_target_pairs={{0,0},{2,2},{4,3},{6,706},{8,707},{10,642},{12,643},{14,578},{16,5... | collective-permute-start | bytes 49160 | tf_op jit(solution)/shard_map/ppermute | solution.py:156
  97.8 18.7 %collective-permute-start.8 = (f32[32,128]{1,0:T(8,128)S(1)}, f32[32,128]{1,0:T(8,128)S(1)}, u32[]{:S(2)}, u32[]{:S(2)}) collective-permute-start(f32[32,128]{1,0:T(8,128)S(1)} %get-tuple-element.6), channel_id=1, source_target_pairs={{0,0},{2,1},{4,3},{6,707},{8,643},{10,579},{12,648},{14,649},{16,5... | collective-permute-start | bytes 49160 | tf_op jit(solution)/shard_map/ppermute | solution.py:156
  112.4 12.9 %collective-permute-start.9 = (f32[32,128]{1,0:T(8,128)S(1)}, f32[32,128]{1,0:T(8,128)S(1)}, u32[]{:S(2)}, u32[]{:S(2)}) collective-permute-start(f32[32,128]{1,0:T(8,128)S(1)} %get-tuple-element.8), channel_id=1, source_target_pairs={{0,0},{2,3},{4,707},{6,643},{8,579},{10,648},{12,584},{14,64},{16,... | collective-permute-start | bytes 49160 | tf_op jit(solution)/shard_map/ppermute | solution.py:156

commit v2 on v1

--- a/solution.py
+++ b/solution.py
@@ -39,6 +39,11 @@
     return (2 * d + x) % 3
 
 
+def place_of(index):
+    par, slot = divmod(index, 3)
+    return (slot + 2) % 3 if par % 4 == 1 else slot
+
+
 def plan():
     tables = np.zeros((3, 2, 2, 2, 12, 6), np.int32)
     pairs = [[], [], []]
@@ -55,7 +60,7 @@
                     entry = [row, col]
                     for k in range(4):
                         index = 4 * (2 * cz + cx) + k
-                        slot = index % 3
+                        slot = place_of(index)
                         q = rank[slot]
                         rank[slot] += 1
                         entry.append(q * 3 + slot)
@@ -67,6 +72,7 @@
                         tables[z % 3, xl, mine, int(core != mine), n] = entry
                 assert rank == [NQ, NQ, NQ]
     assert len(seen) == NZ * 2 * 2 * NQ * 3
+    assert sorted(pairs[0]) == sorted(pairs[1])
     return tables.reshape(12, 2 * 12 * 6), pairs
 
 
@@ -115,7 +121,7 @@
 
 
 def solution(mesh):
-    tables, last_pairs = plan()
+    tables, (pair_perm, _, single_perm) = plan()
 
     def shards(jacobian, coeffs):
         walk, par = lax.axis_index("walk"), lax.axis_index("par")
@@ -127,35 +133,43 @@
         def walk_get(value, dz, flip=0):
             return lax.ppermute(value, "walk", walk_perm(dz, flip))
 
+        tie = lax.optimization_barrier
+
         up1, down1 = walk_get(jacobian, 1), walk_get(jacobian, -1)
+        term = jnp.sum(coeffs[:, None] * jacobian, axis=0)
+        up1, term = tie((up1, term + walk_get(term, 0, 1)))
         up2, down2 = walk_get(up1, 1), walk_get(down1, -1)
+        up2, term = tie((up2, term + walk_get(term, 6)))
         up3, down3 = walk_get(up2, 1), walk_get(down2, -1)
         other = walk_get(up2, 1, 1)
-
-        term = jnp.sum(coeffs[:, None] * jacobian, axis=0)
-        term = term + walk_get(term, 0, 1)
-        term = term + walk_get(term, 6)
-        term = term + walk_get(term, 3)
-        after, before = walk_get(term, 1), walk_get(term, -1)
-        place = z % 3
-        first = jnp.where(place == 0, term, jnp.where(place == 1, before, after))
-        second = jnp.where(place == 0, after, jnp.where(place == 1, term, before))
-        third = jnp.where(place == 0, before, jnp.where(place == 1, after, term))
-        update = (first + second) + third
+        other, term = tie((other, term + walk_get(term, 3)))
 
         keep, send = gram_parts(
             table, (down3, down2, down1, jacobian, up1, up2, up3, other)
         )
         swap = [(p, p ^ 1) for p in range(2 * NQ)]
         mine = keep + lax.ppermute(send, "par", swap)
+        mine, term = tie((mine, term))
         groups = [[q * 2 + c for q in range(NQ)] for c in range(2)]
         mine = mine.reshape(NQ, 3, SLICE, -1)
         mine = lax.all_to_all(mine, "par", 0, 0, axis_index_groups=groups, tiled=True)
-        mine = jnp.sum(mine, axis=0)
-        slices = [
-            lax.ppermute(mine[slot], ("walk", "par"), last_pairs[slot]) for slot in range(3)
-        ]
-        return jnp.concatenate(slices, axis=0).T, update
+
+        after, before = walk_get(term, 1), walk_get(term, -1)
+        place = z % 3
+        first = jnp.where(place == 0, term, jnp.where(place == 1, before, after))
+        second = jnp.where(place == 0, after, jnp.where(place == 1, term, before))
+        third = jnp.where(place == 0, before, jnp.where(place == 1, after, term))
+        mine, update = tie((mine, (first + second) + third))
+
+        mine = jnp.sum(mine, axis=0).reshape(3 * SLICE, -1)
+        pair = lax.ppermute(mine[:2 * SLICE], ("walk", "par"), pair_perm)
+        single = lax.ppermute(mine[2 * SLICE:], ("walk", "par"), single_perm)
+        gram = jnp.where(
+            par % 4 == 1,
+            jnp.concatenate((single, pair), axis=0),
+            jnp.concatenate((pair, single), axis=0),
+        )
+        return gram.T, update
 
     in_specs = (P("walk", "par"), P("walk"))
     out_specs = (P("walk", "par"), P("par"))

time: 127 us -> 123 us (0.969)
  the two profiles are of different devices: /device:TPU:89 before, /device:TPU:12 now
where the time goes in v2:
time: 123 us; the launch traced here: 122 us
  starting transfers between devices  75.3 us (61%)
  waiting for transfers between devices  38.5 us (31%)
  Pallas kernels  3.61 us (3%)
  other arithmetic  3.37 us (3%)
    ppermute x12, starting transfers between devices, walk_get(): return lax.ppermute(value, 'walk', walk_perm(dz, flip))  51.4 us
    ppermute x12, waiting for transfers between devices, walk_get(): return lax.ppermute(value, 'walk', walk_perm(dz, flip))  18.8 us
    all_to_all x1, starting transfers between devices, shards(): lax.all_to_all(mine, 'par', 0, 0, axis_index_groups=groups, tiled=True)  9.97 us
    all_to_all x1, waiting for transfers between devices, shards(): lax.all_to_all(mine, 'par', 0, 0, axis_index_groups=groups, tiled=True)  9.31 us
    ppermute x1, waiting for transfers between devices, shards(): single = lax.ppermute(mine[2 * SLICE:], ('walk', 'par'), single_perm)  8.06 us
    ppermute x1, starting transfers between devices, shards(): single = lax.ppermute(mine[2 * SLICE:], ('walk', 'par'), single_perm)  6.3 us
    ppermute x1, starting transfers between devices, shards(): pair = lax.ppermute(mine[:2 * SLICE], ('walk', 'par'), pair_perm)  5.71 us
    pallas_call x1, Pallas kernels, gram_parts(): pl.pallas_call(gram_kernel, out_shape=(out, out), in_specs=[pl.BlockSpec(...  3.61 us
  transfers between devices with their start and end apart: 16, of which 7 were waited for; matrix products, arithmetic and copies ran while one was open for 2% of the time, Pallas kernels for 0%

profile of v2, /device:TPU:12, one launch (start us, length us, event | category | flops | bytes accessed | tf_op | source)
XLA Modules:
  0.0 122.3 jit_solution(5843641386537505622)
XLA Ops:
  0.6 0.0 copy-start
  0.6 14.7 %collective-permute-start.3 = (f32[128,512]{1,0:T(8,128)}, f32[128,512]{1,0:T(8,128)S(1)}, u32[]{:S(2)}, u32[]{:S(2)}) collective-permute-start(f32[128,512]{1,0:T(8,128)} %refs_3_.1), channel_id=1, source_target_pairs={{64,0},{96,32},{128,64},{160,96},{192,128},{224,160},{256,192},{28... | collective-permute-start | bytes 786440 | tf_op jit(solution)/shard_map/ppermute | solution.py:134
  15.4 1.9 %collective-permute-start = (f32[128,512]{1,0:T(8,128)}, f32[128,512]{1,0:T(8,128)S(1)}, u32[]{:S(2)}, u32[]{:S(2)}) collective-permute-start(f32[128,512]{1,0:T(8,128)} %refs_3_.1), channel_id=1, source_target_pairs={{704,0},{736,32},{0,64},{32,96},{64,128},{96,160},{128,192},{160,2... | collective-permute-start | bytes 786440 | tf_op jit(solution)/shard_map/ppermute | solution.py:134
  17.3 1.1 multiply_reduce_fusion
  18.4 3.1 %collective-permute-start.4 = (f32[512]{0:T(512)S(1)}, f32[512]{0:T(512)S(1)}, u32[]{:S(2)}, u32[]{:S(2)}) collective-permute-start(f32[512]{0:T(512)S(1)} %multiply_reduce_fusion), channel_id=1, source_target_pairs={{32,0},{0,32},{96,64},{64,96},{160,128},{128,160},{224,192},{192,2... | collective-permute-start | bytes 6152 | tf_op jit(solution)/shard_map/ppermute | solution.py:134
  21.5 2.4 %collective-permute-done.4 = f32[512]{0:T(512)S(1)} collective-permute-done((f32[512]{0:T(512)S(1)}, f32[512]{0:T(512)S(1)}, u32[]{:S(2)}, u32[]{:S(2)}) %collective-permute-start.4) | collective-permute-done | bytes 2080 | tf_op jit(solution)/shard_map/ppermute | solution.py:134
  23.8 0.0 collective-permute-done.3.refs_4_
  23.8 5.1 %collective-permute-start.5 = (f32[128,512]{1,0:T(8,128)S(1)}, f32[128,512]{1,0:T(8,128)S(1)}, u32[]{:S(2)}, u32[]{:S(2)}) collective-permute-start(f32[128,512]{1,0:T(8,128)S(1)} %collective-permute-done.3.refs_4_), channel_id=1, source_target_pairs={{64,0},{96,32},{128,64},{160,96},{192,128},{224,160},{256,192},{28... | collective-permute-start | bytes 786440 | tf_op jit(solution)/shard_map/ppermute | solution.py:134
  29.0 0.0 collective-permute-done.refs_2_
  29.0 1.9 %collective-permute-start.1 = (f32[128,512]{1,0:T(8,128)S(1)}, f32[128,512]{1,0:T(8,128)S(1)}, u32[]{:S(2)}, u32[]{:S(2)}) collective-permute-start(f32[128,512]{1,0:T(8,128)S(1)} %collective-permute-done.refs_2_), channel_id=1, source_target_pairs={{704,0},{736,32},{0,64},{32,96},{64,128},{96,160},{128,192},{160,2... | collective-permute-start | bytes 786440 | tf_op jit(solution)/shard_map/ppermute | solution.py:134
  30.9 4.5 %collective-permute-start.6 = (f32[512]{0:T(512)S(1)}, f32[512]{0:T(512)S(1)}, u32[]{:S(2)}, u32[]{:S(2)}) collective-permute-start(f32[512]{0:T(512)S(1)} %add.50), channel_id=1, source_target_pairs={{384,0},{416,32},{448,64},{480,96},{512,128},{544,160},{576,192},{... | collective-permute-start | bytes 6152 | tf_op jit(solution)/shard_map/ppermute | solution.py:134
  35.5 7.2 %collective-permute-done.6 = f32[512]{0:T(512)S(1)} collective-permute-done((f32[512]{0:T(512)S(1)}, f32[512]{0:T(512)S(1)}, u32[]{:S(2)}, u32[]{:S(2)}) %collective-permute-start.6) | collective-permute-done | bytes 2080 | tf_op jit(solution)/shard_map/ppermute | solution.py:134
  42.7 0.0 collective-permute-done.5.refs_5_
  42.7 5.9 %collective-permute-start.8 = (f32[128,512]{1,0:T(8,128)S(1)}, f32[128,512]{1,0:T(8,128)S(1)}, u32[]{:S(2)}, u32[]{:S(2)}) collective-permute-start(f32[128,512]{1,0:T(8,128)S(1)} %collective-permute-done.5.refs_5_), channel_id=1, source_target_pairs={{96,0},{64,32},{160,64},{128,96},{224,128},{192,160},{288,192},{25... | collective-permute-start | bytes 786440 | tf_op jit(solution)/shard_map/ppermute | solution.py:134
  48.6 1.9 %collective-permute-start.7 = (f32[128,512]{1,0:T(8,128)S(1)}, f32[128,512]{1,0:T(8,128)S(1)}, u32[]{:S(2)}, u32[]{:S(2)}) collective-permute-start(f32[128,512]{1,0:T(8,128)S(1)} %collective-permute-done.5.refs_5_), channel_id=1, source_target_pairs={{64,0},{96,32},{128,64},{160,96},{192,128},{224,160},{256,192},{28... | collective-permute-start | bytes 786440 | tf_op jit(solution)/shard_map/ppermute | solution.py:134
  50.5 0.0 collective-permute-done.1.refs_1_
  50.5 3.9 %collective-permute-start.2 = (f32[128,512]{1,0:T(8,128)S(1)}, f32[128,512]{1,0:T(8,128)S(1)}, u32[]{:S(2)}, u32[]{:S(2)}) collective-permute-start(f32[128,512]{1,0:T(8,128)S(1)} %collective-permute-done.1.refs_1_), channel_id=1, source_target_pairs={{704,0},{736,32},{0,64},{32,96},{64,128},{96,160},{128,192},{160,2... | collective-permute-start | bytes 786440 | tf_op jit(solution)/shard_map/ppermute | solution.py:134
  54.5 2.1 %collective-permute-start.9 = (f32[512]{0:T(512)S(1)}, f32[512]{0:T(512)S(1)}, u32[]{:S(2)}, u32[]{:S(2)}) collective-permute-start(f32[512]{0:T(512)S(1)} %add.51), channel_id=1, source_target_pairs={{192,0},{224,32},{256,64},{288,96},{320,128},{352,160},{384,192},{... | collective-permute-start | bytes 6152 | tf_op jit(solution)/shard_map/ppermute | solution.py:134
  56.6 0.7 constant_dynamic-slice_fusion
  57.3 4.5 %collective-permute-done.9 = f32[512]{0:T(512)S(1)} collective-permute-done((f32[512]{0:T(512)S(1)}, f32[512]{0:T(512)S(1)}, u32[]{:S(2)}, u32[]{:S(2)}) %collective-permute-start.9) | collective-permute-done | bytes 2080 | tf_op jit(solution)/shard_map/ppermute | solution.py:134
  61.8 0.0 collective-permute-done.8.refs_7_
  61.8 0.0 collective-permute-done.7.refs_6_
  61.8 0.0 collective-permute-done.2.refs_0_
  61.8 0.0 copy-done
  61.8 3.6 %shard_map.50 = (f32[48,32,128]{2,1,0:T(8,128)S(1)}, f32[48,32,128]{2,1,0:T(8,128)S(1)}) custom-call(s32[144]{0:T(256)S(1)} %bitcast.7, f32[128,512]{1,0:T(8,128)S(1)} %collective-permute-done.2.refs_0_, f32[128,512]{1,0:T(8,128)S(1)} %collective-permute-done.1.refs_1_, f32[128,512]{1,0:T(8,128)S(1)} %collective-permute-done.refs_2_, ...), custom_call_target="tpu_custom_call" | custom-call | tf_op jit(solution)/shard_map/pallas_call | solution.py:107
  65.4 1.9 %collective-permute-start.10 = (f32[48,32,128]{2,1,0:T(8,128)S(1)}, f32[48,32,128]{2,1,0:T(8,128)S(1)}, u32[]{:S(2)}, u32[]{:S(2)}) collective-permute-start(f32[48,32,128]{2,1,0:T(8,128)S(1)} %get-tuple-element.20), channel_id=1, source_target_pairs={{0,1},{1,0},{2,3},{3,2},{4,5},{5,4},{6,7},{7,6},{8,9},{9,8},{10,11... | collective-permute-start | bytes 2359304 | tf_op jit(solution)/shard_map/ppermute | solution.py:151
  67.4 2.3 %collective-permute-done.10 = f32[48,32,128]{2,1,0:T(8,128)S(1)} collective-permute-done((f32[48,32,128]{2,1,0:T(8,128)S(1)}, f32[48,32,128]{2,1,0:T(8,128)S(1)}, u32[]{:S(2)}, u32[]{:S(2)}) %collective-permute-start.10) | collective-permute-done | bytes 786464 | tf_op jit(solution)/shard_map/ppermute | solution.py:151
  69.6 1.0 add.53
  70.6 10.0 %all-to-all-start = ((f32[16,3,32,128]{3,2,1,0:T(8,128)}), f32[16,3,32,128]{3,2,1,0:T(8,128)S(1)}, u32[]{:S(2)}, u32[]{:S(2)}) async-start(f32[16,3,32,128]{3,2,1,0:T(8,128)} %bitcast.1), calls=%async_computation | async-start | bytes 1572864 | tf_op jit(solution)/shard_map/all_to_all | solution.py:155
  80.6 4.3 %collective-permute-start.12 = (f32[512]{0:T(512)S(1)}, f32[512]{0:T(512)S(1)}, u32[]{:S(2)}, u32[]{:S(2)}) collective-permute-start(f32[512]{0:T(512)S(1)} %add.52), channel_id=1, source_target_pairs={{64,0},{96,32},{128,64},{160,96},{192,128},{224,160},{256,192},{28... | collective-permute-start | bytes 6152 | tf_op jit(solution)/shard_map/ppermute | solution.py:134
  84.9 1.9 %collective-permute-start.11 = (f32[512]{0:T(512)S(1)}, f32[512]{0:T(512)S(1)}, u32[]{:S(2)}, u32[]{:S(2)}) collective-permute-start(f32[512]{0:T(512)S(1)} %add.52), channel_id=1, source_target_pairs={{704,0},{736,32},{0,64},{32,96},{64,128},{96,160},{128,192},{160,2... | collective-permute-start | bytes 6152 | tf_op jit(solution)/shard_map/ppermute | solution.py:134
  86.9 0.0 collective-permute-done.12
  86.9 4.7 %collective-permute-done.11 = f32[512]{0:T(512)S(1)} collective-permute-done((f32[512]{0:T(512)S(1)}, f32[512]{0:T(512)S(1)}, u32[]{:S(2)}, u32[]{:S(2)}) %collective-permute-start.11) | collective-permute-done | bytes 2080 | tf_op jit(solution)/shard_map/ppermute | solution.py:134
  91.6 0.6 select_add_fusion
  92.2 9.3 %all-to-all-done = f32[16,3,32,128]{3,2,1,0:T(8,128)S(1)} async-done(((f32[16,3,32,128]{3,2,1,0:T(8,128)}), f32[16,3,32,128]{3,2,1,0:T(8,128)S(1)}, u32[]{:S(2)}, u32[]{:S(2)}) %all-to-all-start) | async-done | bytes 786464 | tf_op jit(solution)/shard_map/all_to_all | solution.py:155
  101.5 0.1 reduce_sum.19
  101.6 5.7 %collective-permute-start.14 = (f32[64,128]{1,0:T(8,128)S(1)}, f32[64,128]{1,0:T(8,128)S(1)}, u32[]{:S(2)}, u32[]{:S(2)}) collective-permute-start(f32[64,128]{1,0:T(8,128)S(1)} %bitcast.8), channel_id=1, source_target_pairs={{0,0},{2,3},{4,707},{6,643},{8,579},{10,648},{12,584},{14,64},{16,... | collective-permute-start | bytes 98312 | tf_op jit(solution)/shard_map/ppermute | solution.py:165
  107.3 6.3 %collective-permute-start.13 = (f32[32,128]{1,0:T(8,128)S(1)}, f32[32,128]{1,0:T(8,128)S(1)}, u32[]{:S(2)}, u32[]{:S(2)}) collective-permute-start(f32[32,128]{1,0:T(8,128)S(1)} %slice_bitcast_fusion), channel_id=1, source_target_pairs={{0,0},{2,1},{4,2},{6,3},{8,706},{10,707},{12,642},{14,643},{16,578... | collective-permute-start | bytes 49160 | tf_op jit(solution)/shard_map/ppermute | solution.py:166
  113.6 8.1 %collective-permute-done.13 = f32[32,128]{1,0:T(8,128)S(1)} collective-permute-done((f32[32,128]{1,0:T(8,128)S(1)}, f32[32,128]{1,0:T(8,128)S(1)}, u32[]{:S(2)}, u32[]{:S(2)}) %collective-permute-start.13) | collective-permute-done | bytes 16416 | tf_op jit(solution)/shard_map/ppermute | solution.py:166
  121.7 0.0 collective-permute-done.14
  121.7 0.6 fusion
  (5 shorter events, 0.0 us)
Async XLA Ops:
  0.6 61.2 %copy-start = (f32[128,512]{1,0:T(8,128)S(1)}, f32[128,512]{1,0:T(8,128)}, u32[]{:S(2)}) copy-start(f32[128,512]{1,0:T(8,128)} %refs_3_.1) | copy-start | bytes 786436
  0.6 23.2 %collective-permute-start.3 = (f32[128,512]{1,0:T(8,128)}, f32[128,512]{1,0:T(8,128)S(1)}, u32[]{:S(2)}, u32[]{:S(2)}) collective-permute-start(f32[128,512]{1,0:T(8,128)} %refs_3_.1), channel_id=1, source_target_pairs={{64,0},{96,32},{128,64},{160,96},{192,128},{224,160},{256,192},{28... | collective-permute-start | bytes 786440 | tf_op jit(solution)/shard_map/ppermute | solution.py:134
  15.4 13.6 %collective-permute-start = (f32[128,512]{1,0:T(8,128)}, f32[128,512]{1,0:T(8,128)S(1)}, u32[]{:S(2)}, u32[]{:S(2)}) collective-permute-start(f32[128,512]{1,0:T(8,128)} %refs_3_.1), channel_id=1, source_target_pairs={{704,0},{736,32},{0,64},{32,96},{64,128},{96,160},{128,192},{160,2... | collective-permute-start | bytes 786440 | tf_op jit(solution)/shard_map/ppermute | solution.py:134
  18.4 5.5 %collective-permute-start.4 = (f32[512]{0:T(512)S(1)}, f32[512]{0:T(512)S(1)}, u32[]{:S(2)}, u32[]{:S(2)}) collective-permute-start(f32[512]{0:T(512)S(1)} %multiply_reduce_fusion), channel_id=1, source_target_pairs={{32,0},{0,32},{96,64},{64,96},{160,128},{128,160},{224,192},{192,2... | collective-permute-start | bytes 6152 | tf_op jit(solution)/shard_map/ppermute | solution.py:134
  23.8 18.9 %collective-permute-start.5 = (f32[128,512]{1,0:T(8,128)S(1)}, f32[128,512]{1,0:T(8,128)S(1)}, u32[]{:S(2)}, u32[]{:S(2)}) collective-permute-start(f32[128,512]{1,0:T(8,128)S(1)} %collective-permute-done.3.refs_4_), channel_id=1, source_target_pairs={{64,0},{96,32},{128,64},{160,96},{192,128},{224,160},{256,192},{28... | collective-permute-start | bytes 786440 | tf_op jit(solution)/shard_map/ppermute | solution.py:134
  29.0 21.5 %collective-permute-start.1 = (f32[128,512]{1,0:T(8,128)S(1)}, f32[128,512]{1,0:T(8,128)S(1)}, u32[]{:S(2)}, u32[]{:S(2)}) collective-permute-start(f32[128,512]{1,0:T(8,128)S(1)} %collective-permute-done.refs_2_), channel_id=1, source_target_pairs={{704,0},{736,32},{0,64},{32,96},{64,128},{96,160},{128,192},{160,2... | collective-permute-start | bytes 786440 | tf_op jit(solution)/shard_map/ppermute | solution.py:134
  30.9 11.8 %collective-permute-start.6 = (f32[512]{0:T(512)S(1)}, f32[512]{0:T(512)S(1)}, u32[]{:S(2)}, u32[]{:S(2)}) collective-permute-start(f32[512]{0:T(512)S(1)} %add.50), channel_id=1, source_target_pairs={{384,0},{416,32},{448,64},{480,96},{512,128},{544,160},{576,192},{... | collective-permute-start | bytes 6152 | tf_op jit(solution)/shard_map/ppermute | solution.py:134
  42.7 19.1 %collective-permute-start.8 = (f32[128,512]{1,0:T(8,128)S(1)}, f32[128,512]{1,0:T(8,128)S(1)}, u32[]{:S(2)}, u32[]{:S(2)}) collective-permute-start(f32[128,512]{1,0:T(8,128)S(1)} %collective-permute-done.5.refs_5_), channel_id=1, source_target_pairs={{96,0},{64,32},{160,64},{128,96},{224,128},{192,160},{288,192},{25... | collective-permute-start | bytes 786440 | tf_op jit(solution)/shard_map/ppermute | solution.py:134
  48.6 13.2 %collective-permute-start.7 = (f32[128,512]{1,0:T(8,128)S(1)}, f32[128,512]{1,0:T(8,128)S(1)}, u32[]{:S(2)}, u32[]{:S(2)}) collective-permute-start(f32[128,512]{1,0:T(8,128)S(1)} %collective-permute-done.5.refs_5_), channel_id=1, source_target_pairs={{64,0},{96,32},{128,64},{160,96},{192,128},{224,160},{256,192},{28... | collective-permute-start | bytes 786440 | tf_op jit(solution)/shard_map/ppermute | solution.py:134
  50.5 11.3 %collective-permute-start.2 = (f32[128,512]{1,0:T(8,128)S(1)}, f32[128,512]{1,0:T(8,128)S(1)}, u32[]{:S(2)}, u32[]{:S(2)}) collective-permute-start(f32[128,512]{1,0:T(8,128)S(1)} %collective-permute-done.1.refs_1_), channel_id=1, source_target_pairs={{704,0},{736,32},{0,64},{32,96},{64,128},{96,160},{128,192},{160,2... | collective-permute-start | bytes 786440 | tf_op jit(solution)/shard_map/ppermute | solution.py:134
  54.5 7.3 %collective-permute-start.9 = (f32[512]{0:T(512)S(1)}, f32[512]{0:T(512)S(1)}, u32[]{:S(2)}, u32[]{:S(2)}) collective-permute-start(f32[512]{0:T(512)S(1)} %add.51), channel_id=1, source_target_pairs={{192,0},{224,32},{256,64},{288,96},{320,128},{352,160},{384,192},{... | collective-permute-start | bytes 6152 | tf_op jit(solution)/shard_map/ppermute | solution.py:134
  65.4 4.2 %collective-permute-start.10 = (f32[48,32,128]{2,1,0:T(8,128)S(1)}, f32[48,32,128]{2,1,0:T(8,128)S(1)}, u32[]{:S(2)}, u32[]{:S(2)}) collective-permute-start(f32[48,32,128]{2,1,0:T(8,128)S(1)} %get-tuple-element.20), channel_id=1, source_target_pairs={{0,1},{1,0},{2,3},{3,2},{4,5},{5,4},{6,7},{7,6},{8,9},{9,8},{10,11... | collective-permute-start | bytes 2359304 | tf_op jit(solution)/shard_map/ppermute | solution.py:151
  70.6 30.9 %all-to-all-start = ((f32[16,3,32,128]{3,2,1,0:T(8,128)}), f32[16,3,32,128]{3,2,1,0:T(8,128)S(1)}, u32[]{:S(2)}, u32[]{:S(2)}) async-start(f32[16,3,32,128]{3,2,1,0:T(8,128)} %bitcast.1), calls=%async_computation | async-start | bytes 1572864 | tf_op jit(solution)/shard_map/all_to_all | solution.py:155
  80.6 6.3 %collective-permute-start.12 = (f32[512]{0:T(512)S(1)}, f32[512]{0:T(512)S(1)}, u32[]{:S(2)}, u32[]{:S(2)}) collective-permute-start(f32[512]{0:T(512)S(1)} %add.52), channel_id=1, source_target_pairs={{64,0},{96,32},{128,64},{160,96},{192,128},{224,160},{256,192},{28... | collective-permute-start | bytes 6152 | tf_op jit(solution)/shard_map/ppermute | solution.py:134
  84.9 6.7 %collective-permute-start.11 = (f32[512]{0:T(512)S(1)}, f32[512]{0:T(512)S(1)}, u32[]{:S(2)}, u32[]{:S(2)}) collective-permute-start(f32[512]{0:T(512)S(1)} %add.52), channel_id=1, source_target_pairs={{704,0},{736,32},{0,64},{32,96},{64,128},{96,160},{128,192},{160,2... | collective-permute-start | bytes 6152 | tf_op jit(solution)/shard_map/ppermute | solution.py:134
  101.6 20.1 %collective-permute-start.14 = (f32[64,128]{1,0:T(8,128)S(1)}, f32[64,128]{1,0:T(8,128)S(1)}, u32[]{:S(2)}, u32[]{:S(2)}) collective-permute-start(f32[64,128]{1,0:T(8,128)S(1)} %bitcast.8), channel_id=1, source_target_pairs={{0,0},{2,3},{4,707},{6,643},{8,579},{10,648},{12,584},{14,64},{16,... | collective-permute-start | bytes 98312 | tf_op jit(solution)/shard_map/ppermute | solution.py:165
  107.3 14.4 %collective-permute-start.13 = (f32[32,128]{1,0:T(8,128)S(1)}, f32[32,128]{1,0:T(8,128)S(1)}, u32[]{:S(2)}, u32[]{:S(2)}) collective-permute-start(f32[32,128]{1,0:T(8,128)S(1)} %slice_bitcast_fusion), channel_id=1, source_target_pairs={{0,0},{2,1},{4,2},{6,3},{8,706},{10,707},{12,642},{14,643},{16,578... | collective-permute-start | bytes 49160 | tf_op jit(solution)/shard_map/ppermute | solution.py:166

commit v3 on v2

v3 whole, which is shorter than its diff:
```python
import numpy as np
import jax
import jax.numpy as jnp
from jax import lax
from jax.experimental import pallas as pl
from jax.experimental.pallas import tpu as pltpu
from jax.sharding import PartitionSpec as P

NZ = 12
NQ = 16
SLICE = 32
OTHER = 7

COL_OFFSET = (
    {0: 0, 1: 1, 2: 1, 3: 1, 4: 1, 5: 3, 6: 3, -1: 0, -2: 0, -3: 0, -4: -2, -5: -2},
    {0: 0, 1: 2, 2: 2, 3: 2, 4: 2, 5: 2, 6: 3, -1: 0, -2: 0, -3: 0, -4: -1, -5: -3},
)


def offset_of(block, xl):
    return (3, 1 - xl) if block == OTHER else (block - 3, xl)


def units_of(xl):
    units = [(c - d + 3, c + 3) for d, c in COL_OFFSET[xl].items()]
    for d in (range(-3, 3) if xl == 0 else range(-2, 4)):
        units += [(d + 3, OTHER), (OTHER, d + 3)]
    halves, counts = ([], []), [0, 0, 0]
    for unit in units:
        d, x = offset_of(unit[1], xl)
        cls = (2 * d + x) % 3
        halves[0 if counts[cls] < 4 else 1].append(unit)
        counts[cls] += 1
    assert len(halves[0]) == len(halves[1]) == 12
    return halves


def place_of(index):
    par, slot = divmod(index, 3)
    return (slot + 2) % 3 if par % 4 == 1 else slot


PLACES = tuple(tuple(place_of(4 * cls + k) for k in range(4)) for cls in range(3))


def ring_distance(a, b, n):
    return min((a - b) % n, (b - a) % n)


def distance(source, target):
    (w0, p0), (w1, p1) = source, target
    x0, x1 = (p0 // 16) * 2 + w0 % 2, (p1 // 16) * 2 + w1 % 2
    return (
        ring_distance(w0 // 2, w1 // 2, NZ)
        + ring_distance(x0, x1, 4)
        + ring_distance(p0 // 2 % 8, p1 // 2 % 8, 8)
    )


def assign(walk, core, targets):
    cost = [[distance((walk, q * 2 + core), t) ** 2 for q in range(NQ)] for t in targets]
    pick = []
    for row in cost:
        pick.append(min((q for q in range(NQ) if q not in pick), key=lambda q: row[q]))
    better = True
    while better:
        better = False
        for a in range(NQ):
            for b in range(a):
                now = cost[a][pick[a]] + cost[b][pick[b]]
                if cost[a][pick[b]] + cost[b][pick[a]] < now:
                    pick[a], pick[b] = pick[b], pick[a]
                    better = True
    return pick


def plan():
    tables = np.zeros((2 * NZ, 2, 2, 12, 6), np.int32)
    pairs = [[], [], []]
    seen = set()
    for walk in range(2 * NZ):
        z, xl = divmod(walk, 2)
        for core, half in enumerate(units_of(xl)):
            entries = []
            for row, col in half:
                rd, rx = offset_of(row, xl)
                cd, cx = offset_of(col, xl)
                entries.append(
                    (2 * ((z + cd) % NZ) + cx, 2 * ((z + rd) % NZ) + rx, row, col)
                )
            entries.sort(key=lambda e: (e[0] % 3, e[0], e[1]))
            assert [e[0] % 3 for e in entries] == [0] * 4 + [1] * 4 + [2] * 4
            slices = [
                (n, k, PLACES[e[0] % 3][k], (e[1], (4 * e[0] + k) // 3))
                for n, e in enumerate(entries)
                for k in range(4)
            ]
            table = np.zeros((12, 6), np.int32)
            for n, e in enumerate(entries):
                table[n, :2] = e[2:]
            for slot in range(3):
                chosen = [s for s in slices if s[2] == slot]
                if slot != 1:
                    picks = assign(walk, core, [s[3] for s in chosen])
                for (n, k, _, target), q in zip(chosen, picks, strict=True):
                    table[n, 2 + k] = q if slot == 2 else q * 2 + slot
                    source = walk * 2 * NQ + q * 2 + core
                    pairs[slot].append((source, target[0] * 2 * NQ + target[1]))
                    seen.add((target, slot))
            tables[walk, core, 0] = table
            tables[walk, 1 - core, 1] = table
    assert len(seen) == NZ * 2 * 2 * NQ * 3
    assert sorted(pairs[0]) == sorted(pairs[1])
    return tables.reshape(4 * NZ, 2 * 12 * 6), pairs[0], pairs[2]


def gram_kernel(table, *refs):
    blocks, outs, parts = refs[:8], refs[8:12], refs[12]
    depth = blocks[0].shape[1]
    for b, ref in enumerate(blocks):
        value = ref[...]
        high = value.astype(jnp.bfloat16)
        parts[b, :, :depth] = high
        parts[b, :, depth:] = (value - high.astype(jnp.float32)).astype(jnp.bfloat16)
    dims = (((1,), (1,)), ((), ()))

    def dot(left, right):
        return lax.dot_general(left, right, dims, preferred_element_type=jnp.float32)

    for half in (1, 0):
        for n in range(12):
            at = (half * 12 + n) * 6
            row, col = table[at], table[at + 1]
            row_high, row_low = parts[row, :, :depth], parts[row, :, depth:]
            col_high, col_low = parts[col, :, :depth], parts[col, :, depth:]
            tile = dot(col_high, row_high) + (dot(col_high, row_low) + dot(col_low, row_high))
            for k in range(4):
                out = outs[2 * half + int(PLACES[n // 4][k] == 2)]
                out[table[at + 2 + k]] = tile[k * SLICE:(k + 1) * SLICE]


def gram_parts(table, blocks):
    rows, depth = blocks[0].shape
    pairs = jax.ShapeDtypeStruct((NQ * 2, SLICE, rows), jnp.float32)
    singles = jax.ShapeDtypeStruct((NQ, SLICE, rows), jnp.float32)
    vmem = pl.BlockSpec(memory_space=pltpu.VMEM)
    return pl.pallas_call(
        gram_kernel,
        out_shape=(pairs, singles, pairs, singles),
        in_specs=[pl.BlockSpec(memory_space=pltpu.SMEM)] + [vmem] * len(blocks),
        out_specs=(vmem,) * 4,
        scratch_shapes=[pltpu.VMEM((len(blocks), rows, 2 * depth), jnp.bfloat16)],
        compiler_params=pltpu.CompilerParams(vmem_limit_bytes=32 * 2**20),
    )(table, *blocks)


def walk_perm(dz, flip):
    return [
        (((z + dz) % NZ) * 2 + (x ^ flip), z * 2 + x) for z in range(NZ) for x in range(2)
    ]


def solution(mesh):
    tables, pair_perm, single_perm = plan()
    swap = [(p, p ^ 1) for p in range(2 * NQ)]
    groups = [[q * 2 + c for q in range(NQ)] for c in range(2)]

    def shards(jacobian, coeffs):
        walk, par = lax.axis_index("walk"), lax.axis_index("par")
        table = lax.dynamic_index_in_dim(
            jnp.asarray(tables), walk * 2 + par % 2, 0, keepdims=False
        )
        tie = lax.optimization_barrier

        def walk_get(value, dz, flip=0):
            return lax.ppermute(value, "walk", walk_perm(dz, flip))

        up1, down1 = walk_get(jacobian, 1), walk_get(jacobian, -1)
        term = jnp.sum(coeffs[:, None] * jacobian, axis=0)
        up1, term = tie((up1, term + walk_get(term, 0, 1)))
        up2, down2 = walk_get(up1, 1), walk_get(down1, -1)
        up3, down3 = walk_get(up2, 1), walk_get(down2, -1)
        other = walk_get(up2, 1, 1)

        keep_pair, keep_single, send_pair, send_single = gram_parts(
            table, (down3, down2, down1, jacobian, up1, up2, up3, other)
        )
        pair = keep_pair + lax.ppermute(send_pair, "par", swap)
        single = keep_single + lax.ppermute(send_single, "par", swap)

        def across(value):
            return lax.all_to_all(value, "par", 0, 0, axis_index_groups=groups, tiled=True)

        pair, term = tie((pair, term))
        pair = across(pair.reshape(NQ, 2 * SLICE, -1))
        single = across(single)
        pair, term = tie((pair, term + walk_get(term, 6)))
        pair = lax.ppermute(jnp.sum(pair, axis=0), ("walk", "par"), pair_perm)
        single, pair, term = tie((single, pair, term + walk_get(term, 3)))
        after, before = walk_get(term, 1), walk_get(term, -1)
        place = walk // 2 % 3
        first = jnp.where(place == 0, term, jnp.where(place == 1, before, after))
        second = jnp.where(place == 0, after, jnp.where(place == 1, term, before))
        third = jnp.where(place == 0, before, jnp.where(place == 1, after, term))
        update = (first + second) + third

        single = lax.ppermute(jnp.sum(single, axis=0), ("walk", "par"), single_perm)
        gram = jnp.where(
            par % 4 == 1,
            jnp.concatenate((single, pair), axis=0),
            jnp.concatenate((pair, single), axis=0),
        )
        return gram.T, update

    in_specs = (P("walk", "par"), P("walk"))
    out_specs = (P("walk", "par"), P("par"))
    return jax.shard_map(shards, mesh=mesh, in_specs=in_specs, out_specs=out_specs, check_vma=False)
```

time: 123 us -> 136 us (1.11)
  the two profiles are of different devices: /device:TPU:12 before, /device:TPU:6 now
where the time goes in v3:
time: 136 us; the launch traced here: 135 us
  starting transfers between devices  78.3 us (58%)
  waiting for transfers between devices  47.7 us (35%)
  other arithmetic  3.95 us (3%)
  Pallas kernels  3.61 us (3%)
    ppermute x12, starting transfers between devices, walk_get(): return lax.ppermute(value, 'walk', walk_perm(dz, flip))  53.4 us
    ppermute x12, waiting for transfers between devices, walk_get(): return lax.ppermute(value, 'walk', walk_perm(dz, flip))  22.9 us
    all_to_all x2, starting transfers between devices, across(): lax.all_to_all(value, 'par', 0, 0, axis_index_groups=groups, tiled=True)  17.2 us
    all_to_all x2, waiting for transfers between devices, across(): lax.all_to_all(value, 'par', 0, 0, axis_index_groups=groups, tiled=True)  10.8 us
    ppermute x1, waiting for transfers between devices, shards(): single = lax.ppermute(jnp.sum(single, axis=0), ('walk', 'par'), single_perm)  9.15 us
    pallas_call x1, Pallas kernels, gram_parts(): pl.pallas_call(gram_kernel, out_shape=(pairs, singles, pairs, singles), i...  3.61 us
  transfers between devices with their start and end apart: 18, of which 12 were waited for; matrix products, arithmetic and copies ran while one was open for 2% of the time, Pallas kernels for 0%

profile of v3, /device:TPU:6, one launch (start us, length us, event | category | flops | bytes accessed | tf_op | source)
XLA Modules:
  0.0 135.1 jit_solution(5914629712614316878)
XLA Ops:
  0.6 0.0 copy-start
  0.6 14.7 %collective-permute-start.3 = (f32[128,512]{1,0:T(8,128)}, f32[128,512]{1,0:T(8,128)S(1)}, u32[]{:S(2)}, u32[]{:S(2)}) collective-permute-start(f32[128,512]{1,0:T(8,128)} %refs_3_.1), channel_id=1, source_target_pairs={{64,0},{96,32},{128,64},{160,96},{192,128},{224,160},{256,192},{28... | collective-permute-start | bytes 786440 | tf_op jit(solution)/shard_map/ppermute | solution.py:176
  15.4 1.9 %collective-permute-start = (f32[128,512]{1,0:T(8,128)}, f32[128,512]{1,0:T(8,128)S(1)}, u32[]{:S(2)}, u32[]{:S(2)}) collective-permute-start(f32[128,512]{1,0:T(8,128)} %refs_3_.1), channel_id=1, source_target_pairs={{704,0},{736,32},{0,64},{32,96},{64,128},{96,160},{128,192},{160,2... | collective-permute-start | bytes 786440 | tf_op jit(solution)/shard_map/ppermute | solution.py:176
  17.3 1.1 multiply_reduce_fusion
  18.4 2.7 %collective-permute-start.4 = (f32[512]{0:T(512)S(1)}, f32[512]{0:T(512)S(1)}, u32[]{:S(2)}, u32[]{:S(2)}) collective-permute-start(f32[512]{0:T(512)S(1)} %multiply_reduce_fusion), channel_id=1, source_target_pairs={{32,0},{0,32},{96,64},{64,96},{160,128},{128,160},{224,192},{192,2... | collective-permute-start | bytes 6152 | tf_op jit(solution)/shard_map/ppermute | solution.py:176
  21.1 2.7 %collective-permute-done.4 = f32[512]{0:T(512)S(1)} collective-permute-done((f32[512]{0:T(512)S(1)}, f32[512]{0:T(512)S(1)}, u32[]{:S(2)}, u32[]{:S(2)}) %collective-permute-start.4) | collective-permute-done | bytes 2080 | tf_op jit(solution)/shard_map/ppermute | solution.py:176
  23.8 0.0 collective-permute-done.3.refs_4_
  23.8 5.1 %collective-permute-start.5 = (f32[128,512]{1,0:T(8,128)S(1)}, f32[128,512]{1,0:T(8,128)S(1)}, u32[]{:S(2)}, u32[]{:S(2)}) collective-permute-start(f32[128,512]{1,0:T(8,128)S(1)} %collective-permute-done.3.refs_4_), channel_id=1, source_target_pairs={{64,0},{96,32},{128,64},{160,96},{192,128},{224,160},{256,192},{28... | collective-permute-start | bytes 786440 | tf_op jit(solution)/shard_map/ppermute | solution.py:176
  29.0 0.0 collective-permute-done.refs_2_
  29.0 1.9 %collective-permute-start.1 = (f32[128,512]{1,0:T(8,128)S(1)}, f32[128,512]{1,0:T(8,128)S(1)}, u32[]{:S(2)}, u32[]{:S(2)}) collective-permute-start(f32[128,512]{1,0:T(8,128)S(1)} %collective-permute-done.refs_2_), channel_id=1, source_target_pairs={{704,0},{736,32},{0,64},{32,96},{64,128},{96,160},{128,192},{160,2... | collective-permute-start | bytes 786440 | tf_op jit(solution)/shard_map/ppermute | solution.py:176
  30.9 2.2 %collective-permute-done.5.refs_5_ = f32[128,512]{1,0:T(8,128)S(1)} collective-permute-done((f32[128,512]{1,0:T(8,128)S(1)}, f32[128,512]{1,0:T(8,128)S(1)}, u32[]{:S(2)}, u32[]{:S(2)}) %collective-permute-start.5) | collective-permute-done | bytes 262176 | tf_op jit(solution)/shard_map/ppermute | solution.py:176
  33.1 5.9 %collective-permute-start.7 = (f32[128,512]{1,0:T(8,128)S(1)}, f32[128,512]{1,0:T(8,128)S(1)}, u32[]{:S(2)}, u32[]{:S(2)}) collective-permute-start(f32[128,512]{1,0:T(8,128)S(1)} %collective-permute-done.5.refs_5_), channel_id=1, source_target_pairs={{96,0},{64,32},{160,64},{128,96},{224,128},{192,160},{288,192},{25... | collective-permute-start | bytes 786440 | tf_op jit(solution)/shard_map/ppermute | solution.py:176
  39.0 1.9 %collective-permute-start.6 = (f32[128,512]{1,0:T(8,128)S(1)}, f32[128,512]{1,0:T(8,128)S(1)}, u32[]{:S(2)}, u32[]{:S(2)}) collective-permute-start(f32[128,512]{1,0:T(8,128)S(1)} %collective-permute-done.5.refs_5_), channel_id=1, source_target_pairs={{64,0},{96,32},{128,64},{160,96},{192,128},{224,160},{256,192},{28... | collective-permute-start | bytes 786440 | tf_op jit(solution)/shard_map/ppermute | solution.py:176
  40.9 0.0 collective-permute-done.1.refs_1_
  40.9 3.9 %collective-permute-start.2 = (f32[128,512]{1,0:T(8,128)S(1)}, f32[128,512]{1,0:T(8,128)S(1)}, u32[]{:S(2)}, u32[]{:S(2)}) collective-permute-start(f32[128,512]{1,0:T(8,128)S(1)} %collective-permute-done.1.refs_1_), channel_id=1, source_target_pairs={{704,0},{736,32},{0,64},{32,96},{64,128},{96,160},{128,192},{160,2... | collective-permute-start | bytes 786440 | tf_op jit(solution)/shard_map/ppermute | solution.py:176
  44.8 0.7 constant_dynamic-slice_fusion
  45.6 0.0 collective-permute-done.7.refs_7_
  45.6 2.2 %collective-permute-done.6.refs_6_ = f32[128,512]{1,0:T(8,128)S(1)} collective-permute-done((f32[128,512]{1,0:T(8,128)S(1)}, f32[128,512]{1,0:T(8,128)S(1)}, u32[]{:S(2)}, u32[]{:S(2)}) %collective-permute-start.6) | collective-permute-done | bytes 262176 | tf_op jit(solution)/shard_map/ppermute | solution.py:176
  47.8 2.6 %collective-permute-done.2.refs_0_ = f32[128,512]{1,0:T(8,128)S(1)} collective-permute-done((f32[128,512]{1,0:T(8,128)S(1)}, f32[128,512]{1,0:T(8,128)S(1)}, u32[]{:S(2)}, u32[]{:S(2)}) %collective-permute-start.2) | collective-permute-done | bytes 262176 | tf_op jit(solution)/shard_map/ppermute | solution.py:176
  50.4 0.0 copy-done
  50.4 3.6 %shard_map.50 = (f32[32,32,128]{2,1,0:T(8,128)S(1)}, f32[16,32,128]{2,1,0:T(8,128)S(1)}, f32[32,32,128]{2,1,0:T(8,128)S(1)}, f32[16,32,128]{2,1,0:T(8,128)S(1)}) custom-call(s32[144]{0:T(256)S(1)} %bitcast.4, f32[128,512]{1,0:T(8,128)S(1)} %collective-permute-done.2.refs_0_, f32[128,512]{1,0:T(8,128)S(1)} %collective-permute-done.1.refs_1_, ...), custom_call_target="tpu_custom_call" | custom-call | tf_op jit(solution)/shard_map/pallas_call | solution.py:147
  54.0 1.9 %collective-permute-start.9 = (f32[32,32,128]{2,1,0:T(8,128)S(1)}, f32[32,32,128]{2,1,0:T(8,128)S(1)}, u32[]{:S(2)}, u32[]{:S(2)}) collective-permute-start(f32[32,32,128]{2,1,0:T(8,128)S(1)} %get-tuple-element.19), channel_id=1, source_target_pairs={{0,1},{1,0},{2,3},{3,2},{4,5},{5,4},{6,7},{7,6},{8,9},{9,8},{10,11... | collective-permute-start | bytes 1572872 | tf_op jit(solution)/shard_map/ppermute | solution.py:188
  55.9 1.9 %collective-permute-done.9 = f32[32,32,128]{2,1,0:T(8,128)S(1)} collective-permute-done((f32[32,32,128]{2,1,0:T(8,128)S(1)}, f32[32,32,128]{2,1,0:T(8,128)S(1)}, u32[]{:S(2)}, u32[]{:S(2)}) %collective-permute-start.9) | collective-permute-done | bytes 524320 | tf_op jit(solution)/shard_map/ppermute | solution.py:188
  57.8 0.9 add.45
  58.7 10.1 %all-to-all-start.1 = ((f32[16,64,128]{2,1,0:T(8,128)}), f32[16,64,128]{2,1,0:T(8,128)S(1)}, u32[]{:S(2)}, u32[]{:S(2)}) async-start(f32[16,64,128]{2,1,0:T(8,128)} %bitcast.1), calls=%async_computation.1 | async-start | bytes 1048576 | tf_op jit(solution)/shard_map/all_to_all | solution.py:192
  68.8 1.9 %collective-permute-start.8 = (f32[16,32,128]{2,1,0:T(8,128)S(1)}, f32[16,32,128]{2,1,0:T(8,128)S(1)}, u32[]{:S(2)}, u32[]{:S(2)}) collective-permute-start(f32[16,32,128]{2,1,0:T(8,128)S(1)} %get-tuple-element.17), channel_id=1, source_target_pairs={{0,1},{1,0},{2,3},{3,2},{4,5},{5,4},{6,7},{7,6},{8,9},{9,8},{10,11... | collective-permute-start | bytes 786440 | tf_op jit(solution)/shard_map/ppermute | solution.py:189
  70.7 1.5 %collective-permute-done.8 = f32[16,32,128]{2,1,0:T(8,128)S(1)} collective-permute-done((f32[16,32,128]{2,1,0:T(8,128)S(1)}, f32[16,32,128]{2,1,0:T(8,128)S(1)}, u32[]{:S(2)}, u32[]{:S(2)}) %collective-permute-start.8) | collective-permute-done | bytes 262176 | tf_op jit(solution)/shard_map/ppermute | solution.py:189
  72.2 0.7 add.44
  72.9 10.7 %all-to-all-done.1 = f32[16,64,128]{2,1,0:T(8,128)S(1)} async-done(((f32[16,64,128]{2,1,0:T(8,128)}), f32[16,64,128]{2,1,0:T(8,128)S(1)}, u32[]{:S(2)}, u32[]{:S(2)}) %all-to-all-start.1) | async-done | bytes 524320 | tf_op jit(solution)/shard_map/all_to_all | solution.py:192
  83.7 7.2 %all-to-all-start = ((f32[16,32,128]{2,1,0:T(8,128)}), f32[16,32,128]{2,1,0:T(8,128)S(1)}, u32[]{:S(2)}, u32[]{:S(2)}) async-start(f32[16,32,128]{2,1,0:T(8,128)} %add.44), calls=%async_computation | async-start | bytes 524288 | tf_op jit(solution)/shard_map/all_to_all | solution.py:192
  90.8 2.4 %collective-permute-start.10 = (f32[512]{0:T(512)S(1)}, f32[512]{0:T(512)S(1)}, u32[]{:S(2)}, u32[]{:S(2)}) collective-permute-start(f32[512]{0:T(512)S(1)} %add.43), channel_id=1, source_target_pairs={{384,0},{416,32},{448,64},{480,96},{512,128},{544,160},{576,192},{... | collective-permute-start | bytes 6152 | tf_op jit(solution)/shard_map/ppermute | solution.py:176
  93.2 9.3 %collective-permute-done.10 = f32[512]{0:T(512)S(1)} collective-permute-done((f32[512]{0:T(512)S(1)}, f32[512]{0:T(512)S(1)}, u32[]{:S(2)}, u32[]{:S(2)}) %collective-permute-start.10) | collective-permute-done | bytes 2080 | tf_op jit(solution)/shard_map/ppermute | solution.py:176
  102.6 1.9 %collective-permute-start.11 = (f32[64,128]{1,0:T(8,128)S(1)}, f32[64,128]{1,0:T(8,128)S(1)}, u32[]{:S(2)}, u32[]{:S(2)}) collective-permute-start(f32[64,128]{1,0:T(8,128)S(1)} %reduce_sum.28), channel_id=1, source_target_pairs={{16,0},{0,64},{8,584},{6,648},{10,585},{12,586},{24,649},{14,650},... | collective-permute-start | bytes 98312 | tf_op jit(solution)/shard_map/ppermute | solution.py:198
  104.6 4.1 %collective-permute-start.12 = (f32[512]{0:T(512)S(1)}, f32[512]{0:T(512)S(1)}, u32[]{:S(2)}, u32[]{:S(2)}) collective-permute-start(f32[512]{0:T(512)S(1)} %add.46), channel_id=1, source_target_pairs={{192,0},{224,32},{256,64},{288,96},{320,128},{352,160},{384,192},{... | collective-permute-start | bytes 6152 | tf_op jit(solution)/shard_map/ppermute | solution.py:176
  108.7 3.2 %collective-permute-done.12 = f32[512]{0:T(512)S(1)} collective-permute-done((f32[512]{0:T(512)S(1)}, f32[512]{0:T(512)S(1)}, u32[]{:S(2)}, u32[]{:S(2)}) %collective-permute-start.12) | collective-permute-done | bytes 2080 | tf_op jit(solution)/shard_map/ppermute | solution.py:176
  111.8 0.0 all-to-all-done
  111.8 1.5 %collective-permute-done.11 = f32[64,128]{1,0:T(8,128)S(1)} collective-permute-done((f32[64,128]{1,0:T(8,128)S(1)}, f32[64,128]{1,0:T(8,128)S(1)}, u32[]{:S(2)}, u32[]{:S(2)}) %collective-permute-start.11) | collective-permute-done | bytes 32800 | tf_op jit(solution)/shard_map/ppermute | solution.py:198
  113.4 4.7 %collective-permute-start.15 = (f32[512]{0:T(512)S(1)}, f32[512]{0:T(512)S(1)}, u32[]{:S(2)}, u32[]{:S(2)}) collective-permute-start(f32[512]{0:T(512)S(1)} %add.47), channel_id=1, source_target_pairs={{64,0},{96,32},{128,64},{160,96},{192,128},{224,160},{256,192},{28... | collective-permute-start | bytes 6152 | tf_op jit(solution)/shard_map/ppermute | solution.py:176
  118.1 4.1 %collective-permute-start.14 = (f32[512]{0:T(512)S(1)}, f32[512]{0:T(512)S(1)}, u32[]{:S(2)}, u32[]{:S(2)}) collective-permute-start(f32[512]{0:T(512)S(1)} %add.47), channel_id=1, source_target_pairs={{704,0},{736,32},{0,64},{32,96},{64,128},{96,160},{128,192},{160,2... | collective-permute-start | bytes 6152 | tf_op jit(solution)/shard_map/ppermute | solution.py:176
  122.2 1.9 %collective-permute-start.13 = (f32[32,128]{1,0:T(8,128)S(1)}, f32[32,128]{1,0:T(8,128)S(1)}, u32[]{:S(2)}, u32[]{:S(2)}) collective-permute-start(f32[32,128]{1,0:T(8,128)S(1)} %reduce_sum.29), channel_id=1, source_target_pairs={{30,0},{28,1},{12,64},{16,65},{10,584},{8,585},{24,648},{26,649},{... | collective-permute-start | bytes 49160 | tf_op jit(solution)/shard_map/ppermute | solution.py:207
  124.2 0.0 collective-permute-done.15
  124.2 0.6 collective-permute-done.14
  124.8 0.6 select_add_fusion
  125.4 9.1 %collective-permute-done.13 = f32[32,128]{1,0:T(8,128)S(1)} collective-permute-done((f32[32,128]{1,0:T(8,128)S(1)}, f32[32,128]{1,0:T(8,128)S(1)}, u32[]{:S(2)}, u32[]{:S(2)}) %collective-permute-start.13) | collective-permute-done | bytes 16416 | tf_op jit(solution)/shard_map/ppermute | solution.py:207
  134.5 0.6 fusion
  (5 shorter events, 0.1 us)
Async XLA Ops:
  0.6 49.7 %copy-start = (f32[128,512]{1,0:T(8,128)S(1)}, f32[128,512]{1,0:T(8,128)}, u32[]{:S(2)}) copy-start(f32[128,512]{1,0:T(8,128)} %refs_3_.1) | copy-start | bytes 786436
  0.6 23.2 %collective-permute-start.3 = (f32[128,512]{1,0:T(8,128)}, f32[128,512]{1,0:T(8,128)S(1)}, u32[]{:S(2)}, u32[]{:S(2)}) collective-permute-start(f32[128,512]{1,0:T(8,128)} %refs_3_.1), channel_id=1, source_target_pairs={{64,0},{96,32},{128,64},{160,96},{192,128},{224,160},{256,192},{28... | collective-permute-start | bytes 786440 | tf_op jit(solution)/shard_map/ppermute | solution.py:176
  15.4 13.6 %collective-permute-start = (f32[128,512]{1,0:T(8,128)}, f32[128,512]{1,0:T(8,128)S(1)}, u32[]{:S(2)}, u32[]{:S(2)}) collective-permute-start(f32[128,512]{1,0:T(8,128)} %refs_3_.1), channel_id=1, source_target_pairs={{704,0},{736,32},{0,64},{32,96},{64,128},{96,160},{128,192},{160,2... | collective-permute-start | bytes 786440 | tf_op jit(solution)/shard_map/ppermute | solution.py:176
  18.4 5.5 %collective-permute-start.4 = (f32[512]{0:T(512)S(1)}, f32[512]{0:T(512)S(1)}, u32[]{:S(2)}, u32[]{:S(2)}) collective-permute-start(f32[512]{0:T(512)S(1)} %multiply_reduce_fusion), channel_id=1, source_target_pairs={{32,0},{0,32},{96,64},{64,96},{160,128},{128,160},{224,192},{192,2... | collective-permute-start | bytes 6152 | tf_op jit(solution)/shard_map/ppermute | solution.py:176
  23.8 9.3 %collective-permute-start.5 = (f32[128,512]{1,0:T(8,128)S(1)}, f32[128,512]{1,0:T(8,128)S(1)}, u32[]{:S(2)}, u32[]{:S(2)}) collective-permute-start(f32[128,512]{1,0:T(8,128)S(1)} %collective-permute-done.3.refs_4_), channel_id=1, source_target_pairs={{64,0},{96,32},{128,64},{160,96},{192,128},{224,160},{256,192},{28... | collective-permute-start | bytes 786440 | tf_op jit(solution)/shard_map/ppermute | solution.py:176
  29.0 11.9 %collective-permute-start.1 = (f32[128,512]{1,0:T(8,128)S(1)}, f32[128,512]{1,0:T(8,128)S(1)}, u32[]{:S(2)}, u32[]{:S(2)}) collective-permute-start(f32[128,512]{1,0:T(8,128)S(1)} %collective-permute-done.refs_2_), channel_id=1, source_target_pairs={{704,0},{736,32},{0,64},{32,96},{64,128},{96,160},{128,192},{160,2... | collective-permute-start | bytes 786440 | tf_op jit(solution)/shard_map/ppermute | solution.py:176
  33.1 12.5 %collective-permute-start.7 = (f32[128,512]{1,0:T(8,128)S(1)}, f32[128,512]{1,0:T(8,128)S(1)}, u32[]{:S(2)}, u32[]{:S(2)}) collective-permute-start(f32[128,512]{1,0:T(8,128)S(1)} %collective-permute-done.5.refs_5_), channel_id=1, source_target_pairs={{96,0},{64,32},{160,64},{128,96},{224,128},{192,160},{288,192},{25... | collective-permute-start | bytes 786440 | tf_op jit(solution)/shard_map/ppermute | solution.py:176
  39.0 8.8 %collective-permute-start.6 = (f32[128,512]{1,0:T(8,128)S(1)}, f32[128,512]{1,0:T(8,128)S(1)}, u32[]{:S(2)}, u32[]{:S(2)}) collective-permute-start(f32[128,512]{1,0:T(8,128)S(1)} %collective-permute-done.5.refs_5_), channel_id=1, source_target_pairs={{64,0},{96,32},{128,64},{160,96},{192,128},{224,160},{256,192},{28... | collective-permute-start | bytes 786440 | tf_op jit(solution)/shard_map/ppermute | solution.py:176
  40.9 9.5 %collective-permute-start.2 = (f32[128,512]{1,0:T(8,128)S(1)}, f32[128,512]{1,0:T(8,128)S(1)}, u32[]{:S(2)}, u32[]{:S(2)}) collective-permute-start(f32[128,512]{1,0:T(8,128)S(1)} %collective-permute-done.1.refs_1_), channel_id=1, source_target_pairs={{704,0},{736,32},{0,64},{32,96},{64,128},{96,160},{128,192},{160,2... | collective-permute-start | bytes 786440 | tf_op jit(solution)/shard_map/ppermute | solution.py:176
  54.0 3.8 %collective-permute-start.9 = (f32[32,32,128]{2,1,0:T(8,128)S(1)}, f32[32,32,128]{2,1,0:T(8,128)S(1)}, u32[]{:S(2)}, u32[]{:S(2)}) collective-permute-start(f32[32,32,128]{2,1,0:T(8,128)S(1)} %get-tuple-element.19), channel_id=1, source_target_pairs={{0,1},{1,0},{2,3},{3,2},{4,5},{5,4},{6,7},{7,6},{8,9},{9,8},{10,11... | collective-permute-start | bytes 1572872 | tf_op jit(solution)/shard_map/ppermute | solution.py:188
  58.7 25.0 %all-to-all-start.1 = ((f32[16,64,128]{2,1,0:T(8,128)}), f32[16,64,128]{2,1,0:T(8,128)S(1)}, u32[]{:S(2)}, u32[]{:S(2)}) async-start(f32[16,64,128]{2,1,0:T(8,128)} %bitcast.1), calls=%async_computation.1 | async-start | bytes 1048576 | tf_op jit(solution)/shard_map/all_to_all | solution.py:192
  68.8 3.4 %collective-permute-start.8 = (f32[16,32,128]{2,1,0:T(8,128)S(1)}, f32[16,32,128]{2,1,0:T(8,128)S(1)}, u32[]{:S(2)}, u32[]{:S(2)}) collective-permute-start(f32[16,32,128]{2,1,0:T(8,128)S(1)} %get-tuple-element.17), channel_id=1, source_target_pairs={{0,1},{1,0},{2,3},{3,2},{4,5},{5,4},{6,7},{7,6},{8,9},{9,8},{10,11... | collective-permute-start | bytes 786440 | tf_op jit(solution)/shard_map/ppermute | solution.py:189
  83.7 28.2 %all-to-all-start = ((f32[16,32,128]{2,1,0:T(8,128)}), f32[16,32,128]{2,1,0:T(8,128)S(1)}, u32[]{:S(2)}, u32[]{:S(2)}) async-start(f32[16,32,128]{2,1,0:T(8,128)} %add.44), calls=%async_computation | async-start | bytes 524288 | tf_op jit(solution)/shard_map/all_to_all | solution.py:192
  90.8 11.8 %collective-permute-start.10 = (f32[512]{0:T(512)S(1)}, f32[512]{0:T(512)S(1)}, u32[]{:S(2)}, u32[]{:S(2)}) collective-permute-start(f32[512]{0:T(512)S(1)} %add.43), channel_id=1, source_target_pairs={{384,0},{416,32},{448,64},{480,96},{512,128},{544,160},{576,192},{... | collective-permute-start | bytes 6152 | tf_op jit(solution)/shard_map/ppermute | solution.py:176
  102.6 10.7 %collective-permute-start.11 = (f32[64,128]{1,0:T(8,128)S(1)}, f32[64,128]{1,0:T(8,128)S(1)}, u32[]{:S(2)}, u32[]{:S(2)}) collective-permute-start(f32[64,128]{1,0:T(8,128)S(1)} %reduce_sum.28), channel_id=1, source_target_pairs={{16,0},{0,64},{8,584},{6,648},{10,585},{12,586},{24,649},{14,650},... | collective-permute-start | bytes 98312 | tf_op jit(solution)/shard_map/ppermute | solution.py:198
  104.6 7.3 %collective-permute-start.12 = (f32[512]{0:T(512)S(1)}, f32[512]{0:T(512)S(1)}, u32[]{:S(2)}, u32[]{:S(2)}) collective-permute-start(f32[512]{0:T(512)S(1)} %add.46), channel_id=1, source_target_pairs={{192,0},{224,32},{256,64},{288,96},{320,128},{352,160},{384,192},{... | collective-permute-start | bytes 6152 | tf_op jit(solution)/shard_map/ppermute | solution.py:176
  113.4 10.8 %collective-permute-start.15 = (f32[512]{0:T(512)S(1)}, f32[512]{0:T(512)S(1)}, u32[]{:S(2)}, u32[]{:S(2)}) collective-permute-start(f32[512]{0:T(512)S(1)} %add.47), channel_id=1, source_target_pairs={{64,0},{96,32},{128,64},{160,96},{192,128},{224,160},{256,192},{28... | collective-permute-start | bytes 6152 | tf_op jit(solution)/shard_map/ppermute | solution.py:176
  118.1 6.7 %collective-permute-start.14 = (f32[512]{0:T(512)S(1)}, f32[512]{0:T(512)S(1)}, u32[]{:S(2)}, u32[]{:S(2)}) collective-permute-start(f32[512]{0:T(512)S(1)} %add.47), channel_id=1, source_target_pairs={{704,0},{736,32},{0,64},{32,96},{64,128},{96,160},{128,192},{160,2... | collective-permute-start | bytes 6152 | tf_op jit(solution)/shard_map/ppermute | solution.py:176
  122.2 12.3 %collective-permute-start.13 = (f32[32,128]{1,0:T(8,128)S(1)}, f32[32,128]{1,0:T(8,128)S(1)}, u32[]{:S(2)}, u32[]{:S(2)}) collective-permute-start(f32[32,128]{1,0:T(8,128)S(1)} %reduce_sum.29), channel_id=1, source_target_pairs={{30,0},{28,1},{12,64},{16,65},{10,584},{8,585},{24,648},{26,649},{... | collective-permute-start | bytes 49160 | tf_op jit(solution)/shard_map/ppermute | solution.py:207

commit v4 on v3

--- a/solution.py
+++ b/solution.py
@@ -38,9 +38,6 @@
 def place_of(index):
     par, slot = divmod(index, 3)
     return (slot + 2) % 3 if par % 4 == 1 else slot
-
-
-PLACES = tuple(tuple(place_of(4 * cls + k) for k in range(4)) for cls in range(3))
 
 
 def ring_distance(a, b, n):
@@ -88,10 +85,8 @@
                 entries.append(
                     (2 * ((z + cd) % NZ) + cx, 2 * ((z + rd) % NZ) + rx, row, col)
                 )
-            entries.sort(key=lambda e: (e[0] % 3, e[0], e[1]))
-            assert [e[0] % 3 for e in entries] == [0] * 4 + [1] * 4 + [2] * 4
             slices = [
-                (n, k, PLACES[e[0] % 3][k], (e[1], (4 * e[0] + k) // 3))
+                (n, k, place_of(4 * e[0] + k), (e[1], (4 * e[0] + k) // 3))
                 for n, e in enumerate(entries)
                 for k in range(4)
             ]
@@ -103,7 +98,7 @@
                 if slot != 1:
                     picks = assign(walk, core, [s[3] for s in chosen])
                 for (n, k, _, target), q in zip(chosen, picks, strict=True):
-                    table[n, 2 + k] = q if slot == 2 else q * 2 + slot
+                    table[n, 2 + k] = q * 3 + slot
                     source = walk * 2 * NQ + q * 2 + core
                     pairs[slot].append((source, target[0] * 2 * NQ + target[1]))
                     seen.add((target, slot))
@@ -115,7 +110,7 @@
 
 
 def gram_kernel(table, *refs):
-    blocks, outs, parts = refs[:8], refs[8:12], refs[12]
+    blocks, keep, send, parts = refs[:8], refs[8], refs[9], refs[10]
     depth = blocks[0].shape[1]
     for b, ref in enumerate(blocks):
         value = ref[...]
@@ -127,7 +122,7 @@
     def dot(left, right):
         return lax.dot_general(left, right, dims, preferred_element_type=jnp.float32)
 
-    for half in (1, 0):
+    for half, out in ((1, send), (0, keep)):
         for n in range(12):
             at = (half * 12 + n) * 6
             row, col = table[at], table[at + 1]
@@ -135,20 +130,18 @@
             col_high, col_low = parts[col, :, :depth], parts[col, :, depth:]
             tile = dot(col_high, row_high) + (dot(col_high, row_low) + dot(col_low, row_high))
             for k in range(4):
-                out = outs[2 * half + int(PLACES[n // 4][k] == 2)]
                 out[table[at + 2 + k]] = tile[k * SLICE:(k + 1) * SLICE]
 
 
 def gram_parts(table, blocks):
     rows, depth = blocks[0].shape
-    pairs = jax.ShapeDtypeStruct((NQ * 2, SLICE, rows), jnp.float32)
-    singles = jax.ShapeDtypeStruct((NQ, SLICE, rows), jnp.float32)
+    out = jax.ShapeDtypeStruct((NQ * 3, SLICE, rows), jnp.float32)
     vmem = pl.BlockSpec(memory_space=pltpu.VMEM)
     return pl.pallas_call(
         gram_kernel,
-        out_shape=(pairs, singles, pairs, singles),
+        out_shape=(out, out),
         in_specs=[pl.BlockSpec(memory_space=pltpu.SMEM)] + [vmem] * len(blocks),
-        out_specs=(vmem,) * 4,
+        out_specs=(vmem, vmem),
         scratch_shapes=[pltpu.VMEM((len(blocks), rows, 2 * depth), jnp.bfloat16)],
         compiler_params=pltpu.CompilerParams(vmem_limit_bytes=32 * 2**20),
     )(table, *blocks)
@@ -182,29 +175,24 @@
         up3, down3 = walk_get(up2, 1), walk_get(down2, -1)
         other = walk_get(up2, 1, 1)
 
-        keep_pair, keep_single, send_pair, send_single = gram_parts(
+        keep, send = gram_parts(
             table, (down3, down2, down1, jacobian, up1, up2, up3, other)
         )
-        pair = keep_pair + lax.ppermute(send_pair, "par", swap)
-        single = keep_single + lax.ppermute(send_single, "par", swap)
-
-        def across(value):
-            return lax.all_to_all(value, "par", 0, 0, axis_index_groups=groups, tiled=True)
-
-        pair, term = tie((pair, term))
-        pair = across(pair.reshape(NQ, 2 * SLICE, -1))
-        single = across(single)
-        pair, term = tie((pair, term + walk_get(term, 6)))
-        pair = lax.ppermute(jnp.sum(pair, axis=0), ("walk", "par"), pair_perm)
-        single, pair, term = tie((single, pair, term + walk_get(term, 3)))
-        after, before = walk_get(term, 1), walk_get(term, -1)
-        place = walk // 2 % 3
+        mine = keep + lax.ppermute(send, "par", swap)
+        mine, term = tie((mine.reshape(NQ, 3 * SLICE, -1), term))
+        mine = lax.all_to_all(mine, "par", 0, 0, axis_index_groups=groups, tiled=True)
+
+        after, before = walk_get(term, 4), walk_get(term, -4)
+        place = walk // 2 // 4
         first = jnp.where(place == 0, term, jnp.where(place == 1, before, after))
         second = jnp.where(place == 0, after, jnp.where(place == 1, term, before))
         third = jnp.where(place == 0, before, jnp.where(place == 1, after, term))
-        update = (first + second) + third
-
-        single = lax.ppermute(jnp.sum(single, axis=0), ("walk", "par"), single_perm)
+        term = (first + second) + third
+        update = (term + walk_get(term, 2)) + (walk_get(term, 1) + walk_get(term, -1))
+
+        mine = jnp.sum(mine, axis=0)
+        pair = lax.ppermute(mine[:2 * SLICE], ("walk", "par"), pair_perm)
+        single = lax.ppermute(mine[2 * SLICE:], ("walk", "par"), single_perm)
         gram = jnp.where(
             par % 4 == 1,
             jnp.concatenate((single, pair), axis=0),

time: 136 us -> 109 us (0.80)
  the two profiles are of different devices: /device:TPU:6 before, /device:TPU:29 now
where the time goes in v4:
time: 109 us; the launch traced here: 108 us
  starting transfers between devices  81.6 us (75%)
  waiting for transfers between devices  17.7 us (16%)
  Pallas kernels  3.61 us (3%)
  other arithmetic  3.37 us (3%)
    ppermute x13, starting transfers between devices, walk_get(): return lax.ppermute(value, 'walk', walk_perm(dz, flip))  54.7 us
    ppermute x13, waiting for transfers between devices, walk_get(): return lax.ppermute(value, 'walk', walk_perm(dz, flip))  9.75 us
    ppermute x1, starting transfers between devices, shards(): single = lax.ppermute(mine[2 * SLICE:], ('walk', 'par'), single_perm)  9.46 us
    all_to_all x1, starting transfers between devices, shards(): lax.all_to_all(mine, 'par', 0, 0, axis_index_groups=groups, tiled=True)  9.18 us
    ppermute x1, starting transfers between devices, shards(): mine = keep + lax.ppermute(send, 'par', swap)  6.35 us
    ppermute x1, waiting for transfers between devices, shards(): pair = lax.ppermute(mine[:2 * SLICE], ('walk', 'par'), pair_perm)  6.02 us
    pallas_call x1, Pallas kernels, gram_parts(): pl.pallas_call(gram_kernel, out_shape=(out, out), in_specs=[pl.BlockSpec(...  3.61 us
  transfers between devices with their start and end apart: 17, of which 7 were waited for; matrix products, arithmetic and copies ran while one was open for 2% of the time, Pallas kernels for 0%

profile of v4, /device:TPU:29, one launch (start us, length us, event | category | flops | bytes accessed | tf_op | source)
XLA Modules:
  0.0 107.9 jit_solution(3618020722716187790)
XLA Ops:
  0.6 0.0 copy-start
  0.6 14.4 %collective-permute-start.3 = (f32[128,512]{1,0:T(8,128)}, f32[128,512]{1,0:T(8,128)S(1)}, u32[]{:S(2)}, u32[]{:S(2)}) collective-permute-start(f32[128,512]{1,0:T(8,128)} %refs_3_.1), channel_id=1, source_target_pairs={{64,0},{96,32},{128,64},{160,96},{192,128},{224,160},{256,192},{28... | collective-permute-start | bytes 786440 | tf_op jit(solution)/shard_map/ppermute | solution.py:169
  15.1 1.9 %collective-permute-start = (f32[128,512]{1,0:T(8,128)}, f32[128,512]{1,0:T(8,128)S(1)}, u32[]{:S(2)}, u32[]{:S(2)}) collective-permute-start(f32[128,512]{1,0:T(8,128)} %refs_3_.1), channel_id=1, source_target_pairs={{704,0},{736,32},{0,64},{32,96},{64,128},{96,160},{128,192},{160,2... | collective-permute-start | bytes 786440 | tf_op jit(solution)/shard_map/ppermute | solution.py:169
  17.0 1.1 multiply_reduce_fusion
  18.1 2.8 %collective-permute-start.4 = (f32[512]{0:T(512)S(1)}, f32[512]{0:T(512)S(1)}, u32[]{:S(2)}, u32[]{:S(2)}) collective-permute-start(f32[512]{0:T(512)S(1)} %multiply_reduce_fusion), channel_id=1, source_target_pairs={{32,0},{0,32},{96,64},{64,96},{160,128},{128,160},{224,192},{192,2... | collective-permute-start | bytes 6152 | tf_op jit(solution)/shard_map/ppermute | solution.py:169
  20.9 1.8 %collective-permute-done.4 = f32[512]{0:T(512)S(1)} collective-permute-done((f32[512]{0:T(512)S(1)}, f32[512]{0:T(512)S(1)}, u32[]{:S(2)}, u32[]{:S(2)}) %collective-permute-start.4) | collective-permute-done | bytes 2080 | tf_op jit(solution)/shard_map/ppermute | solution.py:169
  22.7 0.0 collective-permute-done.3.refs_4_
  22.7 4.6 %collective-permute-start.5 = (f32[128,512]{1,0:T(8,128)S(1)}, f32[128,512]{1,0:T(8,128)S(1)}, u32[]{:S(2)}, u32[]{:S(2)}) collective-permute-start(f32[128,512]{1,0:T(8,128)S(1)} %collective-permute-done.3.refs_4_), channel_id=1, source_target_pairs={{64,0},{96,32},{128,64},{160,96},{192,128},{224,160},{256,192},{28... | collective-permute-start | bytes 786440 | tf_op jit(solution)/shard_map/ppermute | solution.py:169
  27.3 0.0 collective-permute-done.refs_2_
  27.3 1.9 %collective-permute-start.1 = (f32[128,512]{1,0:T(8,128)S(1)}, f32[128,512]{1,0:T(8,128)S(1)}, u32[]{:S(2)}, u32[]{:S(2)}) collective-permute-start(f32[128,512]{1,0:T(8,128)S(1)} %collective-permute-done.refs_2_), channel_id=1, source_target_pairs={{704,0},{736,32},{0,64},{32,96},{64,128},{96,160},{128,192},{160,2... | collective-permute-start | bytes 786440 | tf_op jit(solution)/shard_map/ppermute | solution.py:169
  29.2 1.4 %collective-permute-done.5.refs_5_ = f32[128,512]{1,0:T(8,128)S(1)} collective-permute-done((f32[128,512]{1,0:T(8,128)S(1)}, f32[128,512]{1,0:T(8,128)S(1)}, u32[]{:S(2)}, u32[]{:S(2)}) %collective-permute-start.5) | collective-permute-done | bytes 262176 | tf_op jit(solution)/shard_map/ppermute | solution.py:169
  30.6 6.1 %collective-permute-start.7 = (f32[128,512]{1,0:T(8,128)S(1)}, f32[128,512]{1,0:T(8,128)S(1)}, u32[]{:S(2)}, u32[]{:S(2)}) collective-permute-start(f32[128,512]{1,0:T(8,128)S(1)} %collective-permute-done.5.refs_5_), channel_id=1, source_target_pairs={{96,0},{64,32},{160,64},{128,96},{224,128},{192,160},{288,192},{25... | collective-permute-start | bytes 786440 | tf_op jit(solution)/shard_map/ppermute | solution.py:169
  36.7 1.9 %collective-permute-start.6 = (f32[128,512]{1,0:T(8,128)S(1)}, f32[128,512]{1,0:T(8,128)S(1)}, u32[]{:S(2)}, u32[]{:S(2)}) collective-permute-start(f32[128,512]{1,0:T(8,128)S(1)} %collective-permute-done.5.refs_5_), channel_id=1, source_target_pairs={{64,0},{96,32},{128,64},{160,96},{192,128},{224,160},{256,192},{28... | collective-permute-start | bytes 786440 | tf_op jit(solution)/shard_map/ppermute | solution.py:169
  38.6 0.0 collective-permute-done.1.refs_1_
  38.6 3.4 %collective-permute-start.2 = (f32[128,512]{1,0:T(8,128)S(1)}, f32[128,512]{1,0:T(8,128)S(1)}, u32[]{:S(2)}, u32[]{:S(2)}) collective-permute-start(f32[128,512]{1,0:T(8,128)S(1)} %collective-permute-done.1.refs_1_), channel_id=1, source_target_pairs={{704,0},{736,32},{0,64},{32,96},{64,128},{96,160},{128,192},{160,2... | collective-permute-start | bytes 786440 | tf_op jit(solution)/shard_map/ppermute | solution.py:169
  42.0 0.7 constant_dynamic-slice_fusion
  42.7 0.0 collective-permute-done.7.refs_7_
  42.8 2.1 %collective-permute-done.6.refs_6_ = f32[128,512]{1,0:T(8,128)S(1)} collective-permute-done((f32[128,512]{1,0:T(8,128)S(1)}, f32[128,512]{1,0:T(8,128)S(1)}, u32[]{:S(2)}, u32[]{:S(2)}) %collective-permute-start.6) | collective-permute-done | bytes 262176 | tf_op jit(solution)/shard_map/ppermute | solution.py:169
  44.9 2.1 %collective-permute-done.2.refs_0_ = f32[128,512]{1,0:T(8,128)S(1)} collective-permute-done((f32[128,512]{1,0:T(8,128)S(1)}, f32[128,512]{1,0:T(8,128)S(1)}, u32[]{:S(2)}, u32[]{:S(2)}) %collective-permute-start.2) | collective-permute-done | bytes 262176 | tf_op jit(solution)/shard_map/ppermute | solution.py:169
  47.0 0.0 copy-done
  47.0 3.6 %shard_map.50 = (f32[48,32,128]{2,1,0:T(8,128)S(1)}, f32[48,32,128]{2,1,0:T(8,128)S(1)}) custom-call(s32[144]{0:T(256)S(1)} %bitcast.4, f32[128,512]{1,0:T(8,128)S(1)} %collective-permute-done.2.refs_0_, f32[128,512]{1,0:T(8,128)S(1)} %collective-permute-done.1.refs_1_, f32[128,512]{1,0:T(8,128)S(1)} %collective-permute-done.refs_2_, ...), custom_call_target="tpu_custom_call" | custom-call | tf_op jit(solution)/shard_map/pallas_call | solution.py:140
  50.6 6.3 %collective-permute-start.8 = (f32[48,32,128]{2,1,0:T(8,128)S(1)}, f32[48,32,128]{2,1,0:T(8,128)S(1)}, u32[]{:S(2)}, u32[]{:S(2)}) collective-permute-start(f32[48,32,128]{2,1,0:T(8,128)S(1)} %get-tuple-element.10), channel_id=1, source_target_pairs={{0,1},{1,0},{2,3},{3,2},{4,5},{5,4},{6,7},{7,6},{8,9},{9,8},{10,11... | collective-permute-start | bytes 2359304 | tf_op jit(solution)/shard_map/ppermute | solution.py:181
  57.0 1.9 %collective-permute-done.8 = f32[48,32,128]{2,1,0:T(8,128)S(1)} collective-permute-done((f32[48,32,128]{2,1,0:T(8,128)S(1)}, f32[48,32,128]{2,1,0:T(8,128)S(1)}, u32[]{:S(2)}, u32[]{:S(2)}) %collective-permute-start.8) | collective-permute-done | bytes 786464 | tf_op jit(solution)/shard_map/ppermute | solution.py:181
  58.8 1.1 add.42
  59.9 9.2 %all-to-all-start = ((f32[16,96,128]{2,1,0:T(8,128)}), f32[16,96,128]{2,1,0:T(8,128)S(1)}, u32[]{:S(2)}, u32[]{:S(2)}) async-start(f32[16,96,128]{2,1,0:T(8,128)} %bitcast.1), calls=%async_computation | async-start | bytes 1572864 | tf_op jit(solution)/shard_map/all_to_all | solution.py:183
  69.1 3.3 %collective-permute-start.12 = (f32[512]{0:T(512)S(1)}, f32[512]{0:T(512)S(1)}, u32[]{:S(2)}, u32[]{:S(2)}) collective-permute-start(f32[512]{0:T(512)S(1)} %add.41), channel_id=1, source_target_pairs={{256,0},{288,32},{320,64},{352,96},{384,128},{416,160},{448,192},{... | collective-permute-start | bytes 6152 | tf_op jit(solution)/shard_map/ppermute | solution.py:169
  72.4 5.8 %collective-permute-start.11 = (f32[512]{0:T(512)S(1)}, f32[512]{0:T(512)S(1)}, u32[]{:S(2)}, u32[]{:S(2)}) collective-permute-start(f32[512]{0:T(512)S(1)} %add.41), channel_id=1, source_target_pairs={{512,0},{544,32},{576,64},{608,96},{640,128},{672,160},{704,192},{... | collective-permute-start | bytes 6152 | tf_op jit(solution)/shard_map/ppermute | solution.py:169
  78.3 0.0 collective-permute-done.12
  78.3 2.4 %collective-permute-done.11 = f32[512]{0:T(512)S(1)} collective-permute-done((f32[512]{0:T(512)S(1)}, f32[512]{0:T(512)S(1)}, u32[]{:S(2)}, u32[]{:S(2)}) %collective-permute-start.11) | collective-permute-done | bytes 2080 | tf_op jit(solution)/shard_map/ppermute | solution.py:169
  80.7 2.4 %collective-permute-start.15 = (f32[512]{0:T(512)S(1)}, f32[512]{0:T(512)S(1)}, u32[]{:S(2)}, u32[]{:S(2)}) collective-permute-start(f32[512]{0:T(512)S(1)} %select_add_fusion), channel_id=1, source_target_pairs={{704,0},{736,32},{0,64},{32,96},{64,128},{96,160},{128,192},{160,2... | collective-permute-start | bytes 6152 | tf_op jit(solution)/shard_map/ppermute | solution.py:169
  83.1 4.1 %collective-permute-start.14 = (f32[512]{0:T(512)S(1)}, f32[512]{0:T(512)S(1)}, u32[]{:S(2)}, u32[]{:S(2)}) collective-permute-start(f32[512]{0:T(512)S(1)} %select_add_fusion), channel_id=1, source_target_pairs={{64,0},{96,32},{128,64},{160,96},{192,128},{224,160},{256,192},{28... | collective-permute-start | bytes 6152 | tf_op jit(solution)/shard_map/ppermute | solution.py:169
  87.2 1.9 %collective-permute-start.13 = (f32[512]{0:T(512)S(1)}, f32[512]{0:T(512)S(1)}, u32[]{:S(2)}, u32[]{:S(2)}) collective-permute-start(f32[512]{0:T(512)S(1)} %select_add_fusion), channel_id=1, source_target_pairs={{128,0},{160,32},{192,64},{224,96},{256,128},{288,160},{320,192},{... | collective-permute-start | bytes 6152 | tf_op jit(solution)/shard_map/ppermute | solution.py:169
  89.1 0.0 all-to-all-done
  89.2 9.5 %collective-permute-start.9 = (f32[32,128]{1,0:T(8,128)S(1)}, f32[32,128]{1,0:T(8,128)S(1)}, u32[]{:S(2)}, u32[]{:S(2)}) collective-permute-start(f32[32,128]{1,0:T(8,128)S(1)} %slice.8), channel_id=1, source_target_pairs={{28,0},{30,1},{22,2},{20,3},{18,706},{14,707},{6,642},{0,643},{2,5... | collective-permute-start | bytes 49160 | tf_op jit(solution)/shard_map/ppermute | solution.py:195
  98.7 1.9 %collective-permute-start.10 = (f32[64,128]{1,0:T(8,128)S(1)}, f32[64,128]{1,0:T(8,128)S(1)}, u32[]{:S(2)}, u32[]{:S(2)}) collective-permute-start(f32[64,128]{1,0:T(8,128)S(1)} %slice.9), channel_id=1, source_target_pairs={{16,0},{20,3},{18,707},{4,643},{2,579},{24,648},{8,584},{0,64},{10... | collective-permute-start | bytes 98312 | tf_op jit(solution)/shard_map/ppermute | solution.py:194
  100.6 0.0 collective-permute-done.15
  100.6 0.0 collective-permute-done.14
  100.6 0.0 collective-permute-done.13
  100.6 0.6 add_add_fusion
  101.2 0.0 collective-permute-done.9
  101.2 6.0 %collective-permute-done.10 = f32[64,128]{1,0:T(8,128)S(1)} collective-permute-done((f32[64,128]{1,0:T(8,128)S(1)}, f32[64,128]{1,0:T(8,128)S(1)}, u32[]{:S(2)}, u32[]{:S(2)}) %collective-permute-start.10) | collective-permute-done | bytes 32800 | tf_op jit(solution)/shard_map/ppermute | solution.py:194
  107.2 0.6 fusion
  (5 shorter events, 0.1 us)
Async XLA Ops:
  0.6 46.3 %copy-start = (f32[128,512]{1,0:T(8,128)S(1)}, f32[128,512]{1,0:T(8,128)}, u32[]{:S(2)}) copy-start(f32[128,512]{1,0:T(8,128)} %refs_3_.1) | copy-start | bytes 786436
  0.6 22.1 %collective-permute-start.3 = (f32[128,512]{1,0:T(8,128)}, f32[128,512]{1,0:T(8,128)S(1)}, u32[]{:S(2)}, u32[]{:S(2)}) collective-permute-start(f32[128,512]{1,0:T(8,128)} %refs_3_.1), channel_id=1, source_target_pairs={{64,0},{96,32},{128,64},{160,96},{192,128},{224,160},{256,192},{28... | collective-permute-start | bytes 786440 | tf_op jit(solution)/shard_map/ppermute | solution.py:169
  15.1 12.2 %collective-permute-start = (f32[128,512]{1,0:T(8,128)}, f32[128,512]{1,0:T(8,128)S(1)}, u32[]{:S(2)}, u32[]{:S(2)}) collective-permute-start(f32[128,512]{1,0:T(8,128)} %refs_3_.1), channel_id=1, source_target_pairs={{704,0},{736,32},{0,64},{32,96},{64,128},{96,160},{128,192},{160,2... | collective-permute-start | bytes 786440 | tf_op jit(solution)/shard_map/ppermute | solution.py:169
  18.1 4.6 %collective-permute-start.4 = (f32[512]{0:T(512)S(1)}, f32[512]{0:T(512)S(1)}, u32[]{:S(2)}, u32[]{:S(2)}) collective-permute-start(f32[512]{0:T(512)S(1)} %multiply_reduce_fusion), channel_id=1, source_target_pairs={{32,0},{0,32},{96,64},{64,96},{160,128},{128,160},{224,192},{192,2... | collective-permute-start | bytes 6152 | tf_op jit(solution)/shard_map/ppermute | solution.py:169
  22.7 7.9 %collective-permute-start.5 = (f32[128,512]{1,0:T(8,128)S(1)}, f32[128,512]{1,0:T(8,128)S(1)}, u32[]{:S(2)}, u32[]{:S(2)}) collective-permute-start(f32[128,512]{1,0:T(8,128)S(1)} %collective-permute-done.3.refs_4_), channel_id=1, source_target_pairs={{64,0},{96,32},{128,64},{160,96},{192,128},{224,160},{256,192},{28... | collective-permute-start | bytes 786440 | tf_op jit(solution)/shard_map/ppermute | solution.py:169
  27.3 11.4 %collective-permute-start.1 = (f32[128,512]{1,0:T(8,128)S(1)}, f32[128,512]{1,0:T(8,128)S(1)}, u32[]{:S(2)}, u32[]{:S(2)}) collective-permute-start(f32[128,512]{1,0:T(8,128)S(1)} %collective-permute-done.refs_2_), channel_id=1, source_target_pairs={{704,0},{736,32},{0,64},{32,96},{64,128},{96,160},{128,192},{160,2... | collective-permute-start | bytes 786440 | tf_op jit(solution)/shard_map/ppermute | solution.py:169
  30.6 12.2 %collective-permute-start.7 = (f32[128,512]{1,0:T(8,128)S(1)}, f32[128,512]{1,0:T(8,128)S(1)}, u32[]{:S(2)}, u32[]{:S(2)}) collective-permute-start(f32[128,512]{1,0:T(8,128)S(1)} %collective-permute-done.5.refs_5_), channel_id=1, source_target_pairs={{96,0},{64,32},{160,64},{128,96},{224,128},{192,160},{288,192},{25... | collective-permute-start | bytes 786440 | tf_op jit(solution)/shard_map/ppermute | solution.py:169
  36.7 8.2 %collective-permute-start.6 = (f32[128,512]{1,0:T(8,128)S(1)}, f32[128,512]{1,0:T(8,128)S(1)}, u32[]{:S(2)}, u32[]{:S(2)}) collective-permute-start(f32[128,512]{1,0:T(8,128)S(1)} %collective-permute-done.5.refs_5_), channel_id=1, source_target_pairs={{64,0},{96,32},{128,64},{160,96},{192,128},{224,160},{256,192},{28... | collective-permute-start | bytes 786440 | tf_op jit(solution)/shard_map/ppermute | solution.py:169
  38.6 8.3 %collective-permute-start.2 = (f32[128,512]{1,0:T(8,128)S(1)}, f32[128,512]{1,0:T(8,128)S(1)}, u32[]{:S(2)}, u32[]{:S(2)}) collective-permute-start(f32[128,512]{1,0:T(8,128)S(1)} %collective-permute-done.1.refs_1_), channel_id=1, source_target_pairs={{704,0},{736,32},{0,64},{32,96},{64,128},{96,160},{128,192},{160,2... | collective-permute-start | bytes 786440 | tf_op jit(solution)/shard_map/ppermute | solution.py:169
  50.6 8.2 %collective-permute-start.8 = (f32[48,32,128]{2,1,0:T(8,128)S(1)}, f32[48,32,128]{2,1,0:T(8,128)S(1)}, u32[]{:S(2)}, u32[]{:S(2)}) collective-permute-start(f32[48,32,128]{2,1,0:T(8,128)S(1)} %get-tuple-element.10), channel_id=1, source_target_pairs={{0,1},{1,0},{2,3},{3,2},{4,5},{5,4},{6,7},{7,6},{8,9},{9,8},{10,11... | collective-permute-start | bytes 2359304 | tf_op jit(solution)/shard_map/ppermute | solution.py:181
  59.9 29.2 %all-to-all-start = ((f32[16,96,128]{2,1,0:T(8,128)}), f32[16,96,128]{2,1,0:T(8,128)S(1)}, u32[]{:S(2)}, u32[]{:S(2)}) async-start(f32[16,96,128]{2,1,0:T(8,128)} %bitcast.1), calls=%async_computation | async-start | bytes 1572864 | tf_op jit(solution)/shard_map/all_to_all | solution.py:183
  69.1 9.2 %collective-permute-start.12 = (f32[512]{0:T(512)S(1)}, f32[512]{0:T(512)S(1)}, u32[]{:S(2)}, u32[]{:S(2)}) collective-permute-start(f32[512]{0:T(512)S(1)} %add.41), channel_id=1, source_target_pairs={{256,0},{288,32},{320,64},{352,96},{384,128},{416,160},{448,192},{... | collective-permute-start | bytes 6152 | tf_op jit(solution)/shard_map/ppermute | solution.py:169
  72.4 8.2 %collective-permute-start.11 = (f32[512]{0:T(512)S(1)}, f32[512]{0:T(512)S(1)}, u32[]{:S(2)}, u32[]{:S(2)}) collective-permute-start(f32[512]{0:T(512)S(1)} %add.41), channel_id=1, source_target_pairs={{512,0},{544,32},{576,64},{608,96},{640,128},{672,160},{704,192},{... | collective-permute-start | bytes 6152 | tf_op jit(solution)/shard_map/ppermute | solution.py:169
  80.7 19.9 %collective-permute-start.15 = (f32[512]{0:T(512)S(1)}, f32[512]{0:T(512)S(1)}, u32[]{:S(2)}, u32[]{:S(2)}) collective-permute-start(f32[512]{0:T(512)S(1)} %select_add_fusion), channel_id=1, source_target_pairs={{704,0},{736,32},{0,64},{32,96},{64,128},{96,160},{128,192},{160,2... | collective-permute-start | bytes 6152 | tf_op jit(solution)/shard_map/ppermute | solution.py:169
  83.1 17.5 %collective-permute-start.14 = (f32[512]{0:T(512)S(1)}, f32[512]{0:T(512)S(1)}, u32[]{:S(2)}, u32[]{:S(2)}) collective-permute-start(f32[512]{0:T(512)S(1)} %select_add_fusion), channel_id=1, source_target_pairs={{64,0},{96,32},{128,64},{160,96},{192,128},{224,160},{256,192},{28... | collective-permute-start | bytes 6152 | tf_op jit(solution)/shard_map/ppermute | solution.py:169
  87.2 13.4 %collective-permute-start.13 = (f32[512]{0:T(512)S(1)}, f32[512]{0:T(512)S(1)}, u32[]{:S(2)}, u32[]{:S(2)}) collective-permute-start(f32[512]{0:T(512)S(1)} %select_add_fusion), channel_id=1, source_target_pairs={{128,0},{160,32},{192,64},{224,96},{256,128},{288,160},{320,192},{... | collective-permute-start | bytes 6152 | tf_op jit(solution)/shard_map/ppermute | solution.py:169
  89.2 12.0 %collective-permute-start.9 = (f32[32,128]{1,0:T(8,128)S(1)}, f32[32,128]{1,0:T(8,128)S(1)}, u32[]{:S(2)}, u32[]{:S(2)}) collective-permute-start(f32[32,128]{1,0:T(8,128)S(1)} %slice.8), channel_id=1, source_target_pairs={{28,0},{30,1},{22,2},{20,3},{18,706},{14,707},{6,642},{0,643},{2,5... | collective-permute-start | bytes 49160 | tf_op jit(solution)/shard_map/ppermute | solution.py:195
  98.7 8.6 %collective-permute-start.10 = (f32[64,128]{1,0:T(8,128)S(1)}, f32[64,128]{1,0:T(8,128)S(1)}, u32[]{:S(2)}, u32[]{:S(2)}) collective-permute-start(f32[64,128]{1,0:T(8,128)S(1)} %slice.9), channel_id=1, source_target_pairs={{16,0},{20,3},{18,707},{4,643},{2,579},{24,648},{8,584},{0,64},{10... | collective-permute-start | bytes 98312 | tf_op jit(solution)/shard_map/ppermute | solution.py:194

commit v5 on v4

--- a/solution.py
+++ b/solution.py
@@ -9,30 +9,27 @@
 NZ = 12
 NQ = 16
 SLICE = 32
-OTHER = 7
 
-COL_OFFSET = (
-    {0: 0, 1: 1, 2: 1, 3: 1, 4: 1, 5: 3, 6: 3, -1: 0, -2: 0, -3: 0, -4: -2, -5: -2},
-    {0: 0, 1: 2, 2: 2, 3: 2, 4: 2, 5: 2, 6: 3, -1: 0, -2: 0, -3: 0, -4: -1, -5: -3},
+BLOCKS = ((0, 0), (1, 0), (2, 0), (-3, 0), (0, 1), (1, 1), (3, 0), (-3, 1))
+EARLY = 6
+SHARE = 12
+
+
+SHARES = (
+    (
+        ((3, 0), (2, 3), (1, 3), (5, 3), (0, 2), (4, 2), (3, 4), (1, 1), (5, 1), (7, 2), (7, 1), (6, 1)),
+        ((0, 3), (4, 3), (2, 5), (3, 2), (2, 4), (0, 1), (4, 1), (3, 1), (2, 1), (3, 6), (6, 7), (2, 7)),
+    ),
+    (
+        ((1, 1), (5, 1), (3, 4), (3, 1), (3, 0), (2, 3), (1, 3), (1, 2), (5, 2), (3, 6), (7, 2), (6, 2)),
+        ((2, 4), (5, 3), (0, 3), (4, 3), (2, 0), (0, 2), (4, 2), (3, 2), (2, 5), (7, 1), (6, 7), (2, 7)),
+    ),
 )
 
 
-def offset_of(block, xl):
-    return (3, 1 - xl) if block == OTHER else (block - 3, xl)
-
-
-def units_of(xl):
-    units = [(c - d + 3, c + 3) for d, c in COL_OFFSET[xl].items()]
-    for d in (range(-3, 3) if xl == 0 else range(-2, 4)):
-        units += [(d + 3, OTHER), (OTHER, d + 3)]
-    halves, counts = ([], []), [0, 0, 0]
-    for unit in units:
-        d, x = offset_of(unit[1], xl)
-        cls = (2 * d + x) % 3
-        halves[0 if counts[cls] < 4 else 1].append(unit)
-        counts[cls] += 1
-    assert len(halves[0]) == len(halves[1]) == 12
-    return halves
+def walker_block(walk, block):
+    d, e = BLOCKS[block]
+    return 2 * ((walk // 2 + d) % NZ) + (walk % 2 ^ e)
 
 
 def place_of(index):
@@ -72,25 +69,20 @@
 
 
 def plan():
-    tables = np.zeros((2 * NZ, 2, 2, 12, 6), np.int32)
+    tables = np.zeros((2 * NZ, 2, 2, SHARE, 6), np.int32)
     pairs = [[], [], []]
     seen = set()
     for walk in range(2 * NZ):
-        z, xl = divmod(walk, 2)
-        for core, half in enumerate(units_of(xl)):
-            entries = []
-            for row, col in half:
-                rd, rx = offset_of(row, xl)
-                cd, cx = offset_of(col, xl)
-                entries.append(
-                    (2 * ((z + cd) % NZ) + cx, 2 * ((z + rd) % NZ) + rx, row, col)
-                )
+        for core, share in enumerate(SHARES[walk % 2]):
+            entries = [
+                (walker_block(walk, col), walker_block(walk, row), row, col) for row, col in share
+            ]
             slices = [
                 (n, k, place_of(4 * e[0] + k), (e[1], (4 * e[0] + k) // 3))
                 for n, e in enumerate(entries)
                 for k in range(4)
             ]
-            table = np.zeros((12, 6), np.int32)
+            table = np.zeros((SHARE, 6), np.int32)
             for n, e in enumerate(entries):
                 table[n, :2] = e[2:]
             for slot in range(3):
@@ -106,11 +98,11 @@
             tables[walk, 1 - core, 1] = table
     assert len(seen) == NZ * 2 * 2 * NQ * 3
     assert sorted(pairs[0]) == sorted(pairs[1])
-    return tables.reshape(4 * NZ, 2 * 12 * 6), pairs[0], pairs[2]
+    return tables.reshape(4 * NZ, 2 * SHARE * 6), pairs[0], pairs[2]
 
 
 def gram_kernel(table, *refs):
-    blocks, keep, send, parts = refs[:8], refs[8], refs[9], refs[10]
+    *blocks, keep, send, parts = refs
     depth = blocks[0].shape[1]
     for b, ref in enumerate(blocks):
         value = ref[...]
@@ -123,8 +115,8 @@
         return lax.dot_general(left, right, dims, preferred_element_type=jnp.float32)
 
     for half, out in ((1, send), (0, keep)):
-        for n in range(12):
-            at = (half * 12 + n) * 6
+        for n in range(SHARE):
+            at = (half * SHARE + n) * 6
             row, col = table[at], table[at + 1]
             row_high, row_low = parts[row, :, :depth], parts[row, :, depth:]
             col_high, col_low = parts[col, :, :depth], parts[col, :, depth:]
@@ -168,16 +160,16 @@
         def walk_get(value, dz, flip=0):
             return lax.ppermute(value, "walk", walk_perm(dz, flip))
 
-        up1, down1 = walk_get(jacobian, 1), walk_get(jacobian, -1)
+        down3, up2, up1 = (walk_get(jacobian, dz) for dz in (-3, 2, 1))
+        pair0 = walk_get(jacobian, 0, 1)
+        pair1 = walk_get(up1, 0, 1)
+        up2, pair0 = tie((up2, pair0))
+        down3, pair1 = tie((down3, pair1))
+        pair3, up3 = walk_get(down3, 0, 1), walk_get(up2, 1)
         term = jnp.sum(coeffs[:, None] * jacobian, axis=0)
-        up1, term = tie((up1, term + walk_get(term, 0, 1)))
-        up2, down2 = walk_get(up1, 1), walk_get(down1, -1)
-        up3, down3 = walk_get(up2, 1), walk_get(down2, -1)
-        other = walk_get(up2, 1, 1)
+        up3, term = tie((up3, term + walk_get(term, 0, 1)))
 
-        keep, send = gram_parts(
-            table, (down3, down2, down1, jacobian, up1, up2, up3, other)
-        )
+        keep, send = gram_parts(table, (jacobian, up1, up2, down3, pair0, pair1, up3, pair3))
         mine = keep + lax.ppermute(send, "par", swap)
         mine, term = tie((mine.reshape(NQ, 3 * SLICE, -1), term))
         mine = lax.all_to_all(mine, "par", 0, 0, axis_index_groups=groups, tiled=True)

time: 109 us -> 113 us (1.037)
  the two profiles are of different devices: /device:TPU:29 before, /device:TPU:30 now
where the time goes in v5:
time: 113 us
  starting transfers between devices  78.3 us (69%)
  waiting for transfers between devices  25.8 us (23%)
  Pallas kernels  3.61 us (3%)
  other arithmetic  3.37 us (3%)
    ppermute x13, starting transfers between devices, walk_get(): return lax.ppermute(value, 'walk', walk_perm(dz, flip))  58.6 us
    ppermute x13, waiting for transfers between devices, walk_get(): return lax.ppermute(value, 'walk', walk_perm(dz, flip))  14.9 us
    all_to_all x1, starting transfers between devices, shards(): lax.all_to_all(mine, 'par', 0, 0, axis_index_groups=groups, tiled=True)  9.75 us
    ppermute x1, waiting for transfers between devices, shards(): pair = lax.ppermute(mine[:2 * SLICE], ('walk', 'par'), pair_perm)  7.51 us
    ppermute x1, starting transfers between devices, shards(): single = lax.ppermute(mine[2 * SLICE:], ('walk', 'par'), single_perm)  6.12 us
    pallas_call x1, Pallas kernels, gram_parts(): pl.pallas_call(gram_kernel, out_shape=(out, out), in_specs=[pl.BlockSpec(...  3.61 us
  transfers between devices with their start and end apart: 17, of which 8 were waited for; matrix products, arithmetic and copies ran while one was open for 2% of the time, Pallas kernels for 0%

profile of v5, /device:TPU:30, one launch (start us, length us, event | category | flops | bytes accessed | tf_op | source)
XLA Modules:
  0.0 112.8 jit_solution(1170437364358411818)
XLA Ops:
  0.6 0.0 copy-start
  0.6 14.7 %collective-permute-start = (f32[128,512]{1,0:T(8,128)}, f32[128,512]{1,0:T(8,128)S(1)}, u32[]{:S(2)}, u32[]{:S(2)}) collective-permute-start(f32[128,512]{1,0:T(8,128)} %refs_0_.1), channel_id=1, source_target_pairs={{64,0},{96,32},{128,64},{160,96},{192,128},{224,160},{256,192},{28... | collective-permute-start | bytes 786440 | tf_op jit(solution)/shard_map/ppermute | solution.py:161
  15.4 2.7 %collective-permute-start.2 = (f32[128,512]{1,0:T(8,128)}, f32[128,512]{1,0:T(8,128)S(1)}, u32[]{:S(2)}, u32[]{:S(2)}) collective-permute-start(f32[128,512]{1,0:T(8,128)} %refs_0_.1), channel_id=1, source_target_pairs={{32,0},{0,32},{96,64},{64,96},{160,128},{128,160},{224,192},{192,2... | collective-permute-start | bytes 786440 | tf_op jit(solution)/shard_map/ppermute | solution.py:161
  18.1 2.5 %collective-permute-start.1 = (f32[128,512]{1,0:T(8,128)}, f32[128,512]{1,0:T(8,128)S(1)}, u32[]{:S(2)}, u32[]{:S(2)}) collective-permute-start(f32[128,512]{1,0:T(8,128)} %refs_0_.1), channel_id=1, source_target_pairs={{128,0},{160,32},{192,64},{224,96},{256,128},{288,160},{320,192},{... | collective-permute-start | bytes 786440 | tf_op jit(solution)/shard_map/ppermute | solution.py:161
  20.6 1.9 %collective-permute-start.3 = (f32[128,512]{1,0:T(8,128)}, f32[128,512]{1,0:T(8,128)S(1)}, u32[]{:S(2)}, u32[]{:S(2)}) collective-permute-start(f32[128,512]{1,0:T(8,128)} %refs_0_.1), channel_id=1, source_target_pairs={{576,0},{608,32},{640,64},{672,96},{704,128},{736,160},{0,192},{32... | collective-permute-start | bytes 786440 | tf_op jit(solution)/shard_map/ppermute | solution.py:161
  22.5 1.0 collective-permute-done.refs_1_
  23.5 2.1 %collective-permute-start.4 = (f32[128,512]{1,0:T(8,128)S(1)}, f32[128,512]{1,0:T(8,128)S(1)}, u32[]{:S(2)}, u32[]{:S(2)}) collective-permute-start(f32[128,512]{1,0:T(8,128)S(1)} %collective-permute-done.refs_1_), channel_id=1, source_target_pairs={{32,0},{0,32},{96,64},{64,96},{160,128},{128,160},{224,192},{192,2... | collective-permute-start | bytes 786440 | tf_op jit(solution)/shard_map/ppermute | solution.py:161
  25.6 0.0 collective-permute-done.2.refs_4_
  25.6 3.6 %collective-permute-done.1.refs_2_ = f32[128,512]{1,0:T(8,128)S(1)} collective-permute-done((f32[128,512]{1,0:T(8,128)}, f32[128,512]{1,0:T(8,128)S(1)}, u32[]{:S(2)}, u32[]{:S(2)}) %collective-permute-start.1) | collective-permute-done | bytes 262176 | tf_op jit(solution)/shard_map/ppermute | solution.py:161
  29.2 8.7 %collective-permute-start.5 = (f32[128,512]{1,0:T(8,128)S(1)}, f32[128,512]{1,0:T(8,128)S(1)}, u32[]{:S(2)}, u32[]{:S(2)}) collective-permute-start(f32[128,512]{1,0:T(8,128)S(1)} %collective-permute-done.1.refs_2_), channel_id=1, source_target_pairs={{64,0},{96,32},{128,64},{160,96},{192,128},{224,160},{256,192},{28... | collective-permute-start | bytes 786440 | tf_op jit(solution)/shard_map/ppermute | solution.py:161
  38.0 4.5 %collective-permute-done.3.refs_3_ = f32[128,512]{1,0:T(8,128)S(1)} collective-permute-done((f32[128,512]{1,0:T(8,128)}, f32[128,512]{1,0:T(8,128)S(1)}, u32[]{:S(2)}, u32[]{:S(2)}) %collective-permute-start.3) | collective-permute-done | bytes 262176 | tf_op jit(solution)/shard_map/ppermute | solution.py:161
  42.4 0.0 collective-permute-done.4.refs_5_
  42.4 3.1 %collective-permute-start.7 = (f32[128,512]{1,0:T(8,128)S(1)}, f32[128,512]{1,0:T(8,128)S(1)}, u32[]{:S(2)}, u32[]{:S(2)}) collective-permute-start(f32[128,512]{1,0:T(8,128)S(1)} %collective-permute-done.3.refs_3_), channel_id=1, source_target_pairs={{32,0},{0,32},{96,64},{64,96},{160,128},{128,160},{224,192},{192,2... | collective-permute-start | bytes 786440 | tf_op jit(solution)/shard_map/ppermute | solution.py:161
  45.6 1.1 multiply_reduce_fusion
  46.6 2.7 %collective-permute-start.6 = (f32[512]{0:T(512)S(1)}, f32[512]{0:T(512)S(1)}, u32[]{:S(2)}, u32[]{:S(2)}) collective-permute-start(f32[512]{0:T(512)S(1)} %multiply_reduce_fusion), channel_id=1, source_target_pairs={{32,0},{0,32},{96,64},{64,96},{160,128},{128,160},{224,192},{192,2... | collective-permute-start | bytes 6152 | tf_op jit(solution)/shard_map/ppermute | solution.py:161
  49.4 0.7 constant_dynamic-slice_fusion
  50.1 2.0 %collective-permute-done.6 = f32[512]{0:T(512)S(1)} collective-permute-done((f32[512]{0:T(512)S(1)}, f32[512]{0:T(512)S(1)}, u32[]{:S(2)}, u32[]{:S(2)}) %collective-permute-start.6) | collective-permute-done | bytes 2080 | tf_op jit(solution)/shard_map/ppermute | solution.py:161
  52.1 0.0 collective-permute-done.5.refs_6_
  52.1 0.0 collective-permute-done.7.refs_7_
  52.1 0.0 copy-done
  52.1 3.6 %shard_map.50 = (f32[48,32,128]{2,1,0:T(8,128)S(1)}, f32[48,32,128]{2,1,0:T(8,128)S(1)}) custom-call(s32[144]{0:T(256)S(1)} %bitcast.4, f32[128,512]{1,0:T(8,128)S(1)} %copy-done, f32[128,512]{1,0:T(8,128)S(1)} %collective-permute-done.refs_1_, f32[128,512]{1,0:T(8,128)S(1)} %collective-permute-done.1.refs_2_, ...), custom_call_target="tpu_custom_call" | custom-call | tf_op jit(solution)/shard_map/pallas_call | solution.py:132
  55.7 1.9 %collective-permute-start.8 = (f32[48,32,128]{2,1,0:T(8,128)S(1)}, f32[48,32,128]{2,1,0:T(8,128)S(1)}, u32[]{:S(2)}, u32[]{:S(2)}) collective-permute-start(f32[48,32,128]{2,1,0:T(8,128)S(1)} %get-tuple-element.18), channel_id=1, source_target_pairs={{0,1},{1,0},{2,3},{3,2},{4,5},{5,4},{6,7},{7,6},{8,9},{9,8},{10,11... | collective-permute-start | bytes 2359304 | tf_op jit(solution)/shard_map/ppermute | solution.py:173
  57.6 2.3 %collective-permute-done.8 = f32[48,32,128]{2,1,0:T(8,128)S(1)} collective-permute-done((f32[48,32,128]{2,1,0:T(8,128)S(1)}, f32[48,32,128]{2,1,0:T(8,128)S(1)}, u32[]{:S(2)}, u32[]{:S(2)}) %collective-permute-start.8) | collective-permute-done | bytes 786464 | tf_op jit(solution)/shard_map/ppermute | solution.py:173
  59.9 1.1 add.42
  61.0 9.7 %all-to-all-start = ((f32[16,96,128]{2,1,0:T(8,128)}), f32[16,96,128]{2,1,0:T(8,128)S(1)}, u32[]{:S(2)}, u32[]{:S(2)}) async-start(f32[16,96,128]{2,1,0:T(8,128)} %bitcast.1), calls=%async_computation | async-start | bytes 1572864 | tf_op jit(solution)/shard_map/all_to_all | solution.py:175
  70.7 4.1 %collective-permute-start.12 = (f32[512]{0:T(512)S(1)}, f32[512]{0:T(512)S(1)}, u32[]{:S(2)}, u32[]{:S(2)}) collective-permute-start(f32[512]{0:T(512)S(1)} %add.41), channel_id=1, source_target_pairs={{256,0},{288,32},{320,64},{352,96},{384,128},{416,160},{448,192},{... | collective-permute-start | bytes 6152 | tf_op jit(solution)/shard_map/ppermute | solution.py:161
  74.8 5.6 %collective-permute-start.11 = (f32[512]{0:T(512)S(1)}, f32[512]{0:T(512)S(1)}, u32[]{:S(2)}, u32[]{:S(2)}) collective-permute-start(f32[512]{0:T(512)S(1)} %add.41), channel_id=1, source_target_pairs={{512,0},{544,32},{576,64},{608,96},{640,128},{672,160},{704,192},{... | collective-permute-start | bytes 6152 | tf_op jit(solution)/shard_map/ppermute | solution.py:161
  80.5 0.0 collective-permute-done.12
  80.5 3.7 %collective-permute-done.11 = f32[512]{0:T(512)S(1)} collective-permute-done((f32[512]{0:T(512)S(1)}, f32[512]{0:T(512)S(1)}, u32[]{:S(2)}, u32[]{:S(2)}) %collective-permute-start.11) | collective-permute-done | bytes 2080 | tf_op jit(solution)/shard_map/ppermute | solution.py:161
  84.2 3.6 %collective-permute-start.15 = (f32[512]{0:T(512)S(1)}, f32[512]{0:T(512)S(1)}, u32[]{:S(2)}, u32[]{:S(2)}) collective-permute-start(f32[512]{0:T(512)S(1)} %select_add_fusion), channel_id=1, source_target_pairs={{704,0},{736,32},{0,64},{32,96},{64,128},{96,160},{128,192},{160,2... | collective-permute-start | bytes 6152 | tf_op jit(solution)/shard_map/ppermute | solution.py:161
  87.9 3.4 %collective-permute-start.14 = (f32[512]{0:T(512)S(1)}, f32[512]{0:T(512)S(1)}, u32[]{:S(2)}, u32[]{:S(2)}) collective-permute-start(f32[512]{0:T(512)S(1)} %select_add_fusion), channel_id=1, source_target_pairs={{64,0},{96,32},{128,64},{160,96},{192,128},{224,160},{256,192},{28... | collective-permute-start | bytes 6152 | tf_op jit(solution)/shard_map/ppermute | solution.py:161
  91.3 3.4 %collective-permute-start.13 = (f32[512]{0:T(512)S(1)}, f32[512]{0:T(512)S(1)}, u32[]{:S(2)}, u32[]{:S(2)}) collective-permute-start(f32[512]{0:T(512)S(1)} %select_add_fusion), channel_id=1, source_target_pairs={{128,0},{160,32},{192,64},{224,96},{256,128},{288,160},{320,192},{... | collective-permute-start | bytes 6152 | tf_op jit(solution)/shard_map/ppermute | solution.py:161
  94.7 0.0 all-to-all-done
  94.8 6.1 %collective-permute-start.9 = (f32[32,128]{1,0:T(8,128)S(1)}, f32[32,128]{1,0:T(8,128)S(1)}, u32[]{:S(2)}, u32[]{:S(2)}) collective-permute-start(f32[32,128]{1,0:T(8,128)S(1)} %slice.8), channel_id=1, source_target_pairs={{0,576},{14,577},{24,152},{22,153},{28,88},{26,89},{8,120},{10,121... | collective-permute-start | bytes 49160 | tf_op jit(solution)/shard_map/ppermute | solution.py:187
  100.9 1.9 %collective-permute-start.10 = (f32[64,128]{1,0:T(8,128)S(1)}, f32[64,128]{1,0:T(8,128)S(1)}, u32[]{:S(2)}, u32[]{:S(2)}) collective-permute-start(f32[64,128]{1,0:T(8,128)S(1)} %slice.9), channel_id=1, source_target_pairs={{16,576},{24,152},{28,88},{26,120},{10,5},{12,6},{6,37},{8,38},{14... | collective-permute-start | bytes 98312 | tf_op jit(solution)/shard_map/ppermute | solution.py:186
  102.8 0.0 collective-permute-done.15
  102.8 0.0 collective-permute-done.14
  102.8 0.0 collective-permute-done.13
  102.8 0.6 add_add_fusion
  103.4 1.2 %collective-permute-done.9 = f32[32,128]{1,0:T(8,128)S(1)} collective-permute-done((f32[32,128]{1,0:T(8,128)S(1)}, f32[32,128]{1,0:T(8,128)S(1)}, u32[]{:S(2)}, u32[]{:S(2)}) %collective-permute-start.9) | collective-permute-done | bytes 16416 | tf_op jit(solution)/shard_map/ppermute | solution.py:187
  104.6 7.5 %collective-permute-done.10 = f32[64,128]{1,0:T(8,128)S(1)} collective-permute-done((f32[64,128]{1,0:T(8,128)S(1)}, f32[64,128]{1,0:T(8,128)S(1)}, u32[]{:S(2)}, u32[]{:S(2)}) %collective-permute-start.10) | collective-permute-done | bytes 32800 | tf_op jit(solution)/shard_map/ppermute | solution.py:186
  112.1 0.6 fusion
  (5 shorter events, 0.1 us)
Async XLA Ops:
  0.6 51.5 %copy-start = (f32[128,512]{1,0:T(8,128)S(1)}, f32[128,512]{1,0:T(8,128)}, u32[]{:S(2)}) copy-start(f32[128,512]{1,0:T(8,128)} %refs_0_.1) | copy-start | bytes 786436
  0.6 22.9 %collective-permute-start = (f32[128,512]{1,0:T(8,128)}, f32[128,512]{1,0:T(8,128)S(1)}, u32[]{:S(2)}, u32[]{:S(2)}) collective-permute-start(f32[128,512]{1,0:T(8,128)} %refs_0_.1), channel_id=1, source_target_pairs={{64,0},{96,32},{128,64},{160,96},{192,128},{224,160},{256,192},{28... | collective-permute-start | bytes 786440 | tf_op jit(solution)/shard_map/ppermute | solution.py:161
  15.4 10.3 %collective-permute-start.2 = (f32[128,512]{1,0:T(8,128)}, f32[128,512]{1,0:T(8,128)S(1)}, u32[]{:S(2)}, u32[]{:S(2)}) collective-permute-start(f32[128,512]{1,0:T(8,128)} %refs_0_.1), channel_id=1, source_target_pairs={{32,0},{0,32},{96,64},{64,96},{160,128},{128,160},{224,192},{192,2... | collective-permute-start | bytes 786440 | tf_op jit(solution)/shard_map/ppermute | solution.py:161
  18.1 11.1 %collective-permute-start.1 = (f32[128,512]{1,0:T(8,128)}, f32[128,512]{1,0:T(8,128)S(1)}, u32[]{:S(2)}, u32[]{:S(2)}) collective-permute-start(f32[128,512]{1,0:T(8,128)} %refs_0_.1), channel_id=1, source_target_pairs={{128,0},{160,32},{192,64},{224,96},{256,128},{288,160},{320,192},{... | collective-permute-start | bytes 786440 | tf_op jit(solution)/shard_map/ppermute | solution.py:161
  20.6 21.9 %collective-permute-start.3 = (f32[128,512]{1,0:T(8,128)}, f32[128,512]{1,0:T(8,128)S(1)}, u32[]{:S(2)}, u32[]{:S(2)}) collective-permute-start(f32[128,512]{1,0:T(8,128)} %refs_0_.1), channel_id=1, source_target_pairs={{576,0},{608,32},{640,64},{672,96},{704,128},{736,160},{0,192},{32... | collective-permute-start | bytes 786440 | tf_op jit(solution)/shard_map/ppermute | solution.py:161
  23.5 18.9 %collective-permute-start.4 = (f32[128,512]{1,0:T(8,128)S(1)}, f32[128,512]{1,0:T(8,128)S(1)}, u32[]{:S(2)}, u32[]{:S(2)}) collective-permute-start(f32[128,512]{1,0:T(8,128)S(1)} %collective-permute-done.refs_1_), channel_id=1, source_target_pairs={{32,0},{0,32},{96,64},{64,96},{160,128},{128,160},{224,192},{192,2... | collective-permute-start | bytes 786440 | tf_op jit(solution)/shard_map/ppermute | solution.py:161
  29.2 22.8 %collective-permute-start.5 = (f32[128,512]{1,0:T(8,128)S(1)}, f32[128,512]{1,0:T(8,128)S(1)}, u32[]{:S(2)}, u32[]{:S(2)}) collective-permute-start(f32[128,512]{1,0:T(8,128)S(1)} %collective-permute-done.1.refs_2_), channel_id=1, source_target_pairs={{64,0},{96,32},{128,64},{160,96},{192,128},{224,160},{256,192},{28... | collective-permute-start | bytes 786440 | tf_op jit(solution)/shard_map/ppermute | solution.py:161
  42.4 9.6 %collective-permute-start.7 = (f32[128,512]{1,0:T(8,128)S(1)}, f32[128,512]{1,0:T(8,128)S(1)}, u32[]{:S(2)}, u32[]{:S(2)}) collective-permute-start(f32[128,512]{1,0:T(8,128)S(1)} %collective-permute-done.3.refs_3_), channel_id=1, source_target_pairs={{32,0},{0,32},{96,64},{64,96},{160,128},{128,160},{224,192},{192,2... | collective-permute-start | bytes 786440 | tf_op jit(solution)/shard_map/ppermute | solution.py:161
  46.6 5.5 %collective-permute-start.6 = (f32[512]{0:T(512)S(1)}, f32[512]{0:T(512)S(1)}, u32[]{:S(2)}, u32[]{:S(2)}) collective-permute-start(f32[512]{0:T(512)S(1)} %multiply_reduce_fusion), channel_id=1, source_target_pairs={{32,0},{0,32},{96,64},{64,96},{160,128},{128,160},{224,192},{192,2... | collective-permute-start | bytes 6152 | tf_op jit(solution)/shard_map/ppermute | solution.py:161
  55.7 4.2 %collective-permute-start.8 = (f32[48,32,128]{2,1,0:T(8,128)S(1)}, f32[48,32,128]{2,1,0:T(8,128)S(1)}, u32[]{:S(2)}, u32[]{:S(2)}) collective-permute-start(f32[48,32,128]{2,1,0:T(8,128)S(1)} %get-tuple-element.18), channel_id=1, source_target_pairs={{0,1},{1,0},{2,3},{3,2},{4,5},{5,4},{6,7},{7,6},{8,9},{9,8},{10,11... | collective-permute-start | bytes 2359304 | tf_op jit(solution)/shard_map/ppermute | solution.py:173
  61.0 33.7 %all-to-all-start = ((f32[16,96,128]{2,1,0:T(8,128)}), f32[16,96,128]{2,1,0:T(8,128)S(1)}, u32[]{:S(2)}, u32[]{:S(2)}) async-start(f32[16,96,128]{2,1,0:T(8,128)} %bitcast.1), calls=%async_computation | async-start | bytes 1572864 | tf_op jit(solution)/shard_map/all_to_all | solution.py:175
  70.7 9.8 %collective-permute-start.12 = (f32[512]{0:T(512)S(1)}, f32[512]{0:T(512)S(1)}, u32[]{:S(2)}, u32[]{:S(2)}) collective-permute-start(f32[512]{0:T(512)S(1)} %add.41), channel_id=1, source_target_pairs={{256,0},{288,32},{320,64},{352,96},{384,128},{416,160},{448,192},{... | collective-permute-start | bytes 6152 | tf_op jit(solution)/shard_map/ppermute | solution.py:161
  74.8 9.4 %collective-permute-start.11 = (f32[512]{0:T(512)S(1)}, f32[512]{0:T(512)S(1)}, u32[]{:S(2)}, u32[]{:S(2)}) collective-permute-start(f32[512]{0:T(512)S(1)} %add.41), channel_id=1, source_target_pairs={{512,0},{544,32},{576,64},{608,96},{640,128},{672,160},{704,192},{... | collective-permute-start | bytes 6152 | tf_op jit(solution)/shard_map/ppermute | solution.py:161
  84.2 18.6 %collective-permute-start.15 = (f32[512]{0:T(512)S(1)}, f32[512]{0:T(512)S(1)}, u32[]{:S(2)}, u32[]{:S(2)}) collective-permute-start(f32[512]{0:T(512)S(1)} %select_add_fusion), channel_id=1, source_target_pairs={{704,0},{736,32},{0,64},{32,96},{64,128},{96,160},{128,192},{160,2... | collective-permute-start | bytes 6152 | tf_op jit(solution)/shard_map/ppermute | solution.py:161
  87.9 15.0 %collective-permute-start.14 = (f32[512]{0:T(512)S(1)}, f32[512]{0:T(512)S(1)}, u32[]{:S(2)}, u32[]{:S(2)}) collective-permute-start(f32[512]{0:T(512)S(1)} %select_add_fusion), channel_id=1, source_target_pairs={{64,0},{96,32},{128,64},{160,96},{192,128},{224,160},{256,192},{28... | collective-permute-start | bytes 6152 | tf_op jit(solution)/shard_map/ppermute | solution.py:161
  91.3 11.5 %collective-permute-start.13 = (f32[512]{0:T(512)S(1)}, f32[512]{0:T(512)S(1)}, u32[]{:S(2)}, u32[]{:S(2)}) collective-permute-start(f32[512]{0:T(512)S(1)} %select_add_fusion), channel_id=1, source_target_pairs={{128,0},{160,32},{192,64},{224,96},{256,128},{288,160},{320,192},{... | collective-permute-start | bytes 6152 | tf_op jit(solution)/shard_map/ppermute | solution.py:161
  94.8 9.9 %collective-permute-start.9 = (f32[32,128]{1,0:T(8,128)S(1)}, f32[32,128]{1,0:T(8,128)S(1)}, u32[]{:S(2)}, u32[]{:S(2)}) collective-permute-start(f32[32,128]{1,0:T(8,128)S(1)} %slice.8), channel_id=1, source_target_pairs={{0,576},{14,577},{24,152},{22,153},{28,88},{26,89},{8,120},{10,121... | collective-permute-start | bytes 49160 | tf_op jit(solution)/shard_map/ppermute | solution.py:187
  100.9 11.2 %collective-permute-start.10 = (f32[64,128]{1,0:T(8,128)S(1)}, f32[64,128]{1,0:T(8,128)S(1)}, u32[]{:S(2)}, u32[]{:S(2)}) collective-permute-start(f32[64,128]{1,0:T(8,128)S(1)} %slice.9), channel_id=1, source_target_pairs={{16,576},{24,152},{28,88},{26,120},{10,5},{12,6},{6,37},{8,38},{14... | collective-permute-start | bytes 98312 | tf_op jit(solution)/shard_map/ppermute | solution.py:186

commit v6 on v5

--- a/solution.py
+++ b/solution.py
@@ -162,25 +162,18 @@
 
         down3, up2, up1 = (walk_get(jacobian, dz) for dz in (-3, 2, 1))
         pair0 = walk_get(jacobian, 0, 1)
+        term = jnp.sum(coeffs[:, None] * jacobian, axis=0).reshape(1, 4, -1)
+        terms = lax.all_to_all(jnp.broadcast_to(term, (2 * NZ,) + term.shape[1:]), "walk", 0, 0, tiled=True)
         pair1 = walk_get(up1, 0, 1)
         up2, pair0 = tie((up2, pair0))
-        down3, pair1 = tie((down3, pair1))
+        down3, pair1, terms = tie((down3, pair1, terms))
         pair3, up3 = walk_get(down3, 0, 1), walk_get(up2, 1)
-        term = jnp.sum(coeffs[:, None] * jacobian, axis=0)
-        up3, term = tie((up3, term + walk_get(term, 0, 1)))
+        update = jnp.sum(terms, axis=0).reshape(-1)
 
         keep, send = gram_parts(table, (jacobian, up1, up2, down3, pair0, pair1, up3, pair3))
         mine = keep + lax.ppermute(send, "par", swap)
-        mine, term = tie((mine.reshape(NQ, 3 * SLICE, -1), term))
+        mine = mine.reshape(NQ, 3 * SLICE, -1)
         mine = lax.all_to_all(mine, "par", 0, 0, axis_index_groups=groups, tiled=True)
-
-        after, before = walk_get(term, 4), walk_get(term, -4)
-        place = walk // 2 // 4
-        first = jnp.where(place == 0, term, jnp.where(place == 1, before, after))
-        second = jnp.where(place == 0, after, jnp.where(place == 1, term, before))
-        third = jnp.where(place == 0, before, jnp.where(place == 1, after, term))
-        term = (first + second) + third
-        update = (term + walk_get(term, 2)) + (walk_get(term, 1) + walk_get(term, -1))
 
         mine = jnp.sum(mine, axis=0)
         pair = lax.ppermute(mine[:2 * SLICE], ("walk", "par"), pair_perm)

time: 113 us -> 112 us (level)
  the two profiles are of different devices: /device:TPU:30 before, /device:TPU:57 now
where the time goes in v6:
time: 112 us; the launch traced here: 111 us
  starting transfers between devices  54.7 us (49%)
  blocking collectives  29.7 us (27%)
  waiting for transfers between devices  18.6 us (17%)
  Pallas kernels  3.61 us (3%)
  other arithmetic  2.48 us (2%)
  local copies, waits for them, and re-layouts  1.35 us (1%)
    ppermute x7, starting transfers between devices, walk_get(): return lax.ppermute(value, 'walk', walk_perm(dz, flip))  31.6 us
    all_to_all x1, blocking collectives, shards(): lax.all_to_all(mine, 'par', 0, 0, axis_index_groups=groups, tiled=True)  29.7 us
    ppermute x1, waiting for transfers between devices, shards(): single = lax.ppermute(mine[2 * SLICE:], ('walk', 'par'), single_perm)  8.52 us
    all_to_all x1, starting transfers between devices, shards(): lax.all_to_all(jnp.broadcast_to(term, (2 * NZ,) + term.shape[1:]), 'walk'...  8.1 us
    ppermute x1, starting transfers between devices, shards(): pair = lax.ppermute(mine[:2 * SLICE], ('walk', 'par'), pair_perm)  6.56 us
    ppermute x1, starting transfers between devices, shards(): mine = keep + lax.ppermute(send, 'par', swap)  6.56 us
    all_to_all x1, waiting for transfers between devices, shards(): lax.all_to_all(jnp.broadcast_to(term, (2 * NZ,) + term.shape[1:]), 'walk'...  4.4 us
    ppermute x7, waiting for transfers between devices, walk_get(): return lax.ppermute(value, 'walk', walk_perm(dz, flip))  3.83 us
  transfers between devices with their start and end apart: 11, of which 4 were waited for; matrix products, arithmetic and copies ran while one was open for 3% of the time, Pallas kernels for 0%

profile of v6, /device:TPU:57, one launch (start us, length us, event | category | flops | bytes accessed | tf_op | source)
XLA Modules:
  0.0 111.4 jit_solution(17326622353104195995)
XLA Ops:
  0.6 0.0 copy-start
  0.6 14.4 %collective-permute-start = (f32[128,512]{1,0:T(8,128)}, f32[128,512]{1,0:T(8,128)S(1)}, u32[]{:S(2)}, u32[]{:S(2)}) collective-permute-start(f32[128,512]{1,0:T(8,128)} %refs_0_.1), channel_id=1, source_target_pairs={{64,0},{96,32},{128,64},{160,96},{192,128},{224,160},{256,192},{28... | collective-permute-start | bytes 786440 | tf_op jit(solution)/shard_map/ppermute | solution.py:161
  15.1 1.9 %collective-permute-start.3 = (f32[128,512]{1,0:T(8,128)}, f32[128,512]{1,0:T(8,128)S(1)}, u32[]{:S(2)}, u32[]{:S(2)}) collective-permute-start(f32[128,512]{1,0:T(8,128)} %refs_0_.1), channel_id=1, source_target_pairs={{576,0},{608,32},{640,64},{672,96},{704,128},{736,160},{0,192},{32... | collective-permute-start | bytes 786440 | tf_op jit(solution)/shard_map/ppermute | solution.py:161
  17.0 3.1 %collective-permute-start.2 = (f32[128,512]{1,0:T(8,128)}, f32[128,512]{1,0:T(8,128)S(1)}, u32[]{:S(2)}, u32[]{:S(2)}) collective-permute-start(f32[128,512]{1,0:T(8,128)} %refs_0_.1), channel_id=1, source_target_pairs={{32,0},{0,32},{96,64},{64,96},{160,128},{128,160},{224,192},{192,2... | collective-permute-start | bytes 786440 | tf_op jit(solution)/shard_map/ppermute | solution.py:161
  20.1 2.2 %collective-permute-start.1 = (f32[128,512]{1,0:T(8,128)}, f32[128,512]{1,0:T(8,128)S(1)}, u32[]{:S(2)}, u32[]{:S(2)}) collective-permute-start(f32[128,512]{1,0:T(8,128)} %refs_0_.1), channel_id=1, source_target_pairs={{128,0},{160,32},{192,64},{224,96},{256,128},{288,160},{320,192},{... | collective-permute-start | bytes 786440 | tf_op jit(solution)/shard_map/ppermute | solution.py:161
  22.3 0.0 collective-permute-done.refs_1_
  22.3 2.2 %collective-permute-start.4 = (f32[128,512]{1,0:T(8,128)S(1)}, f32[128,512]{1,0:T(8,128)S(1)}, u32[]{:S(2)}, u32[]{:S(2)}) collective-permute-start(f32[128,512]{1,0:T(8,128)S(1)} %collective-permute-done.refs_1_), channel_id=1, source_target_pairs={{32,0},{0,32},{96,64},{64,96},{160,128},{128,160},{224,192},{192,2... | collective-permute-start | bytes 786440 | tf_op jit(solution)/shard_map/ppermute | solution.py:161
  24.5 1.1 multiply_reduce_fusion
  25.5 0.6 broadcast_in_dim.9
  26.2 8.1 %all-to-all-start = ((f32[24,4,128]{2,1,0:T(4,128)}), f32[24,4,128]{2,1,0:T(4,128)S(1)}, u32[]{:S(2)}, u32[]{:S(2)}) async-start(f32[24,4,128]{2,1,0:T(4,128)} %broadcast_in_dim.9), calls=%async_computation | async-start | bytes 98304 | tf_op jit(solution)/shard_map/all_to_all | solution.py:166
  34.3 0.0 collective-permute-done.2.refs_4_
  34.3 0.0 collective-permute-done.1.refs_2_
  34.3 5.2 %collective-permute-start.5 = (f32[128,512]{1,0:T(8,128)S(1)}, f32[128,512]{1,0:T(8,128)S(1)}, u32[]{:S(2)}, u32[]{:S(2)}) collective-permute-start(f32[128,512]{1,0:T(8,128)S(1)} %collective-permute-done.1.refs_2_), channel_id=1, source_target_pairs={{64,0},{96,32},{128,64},{160,96},{192,128},{224,160},{256,192},{28... | collective-permute-start | bytes 786440 | tf_op jit(solution)/shard_map/ppermute | solution.py:161
  39.6 4.4 %all-to-all-done = f32[24,4,128]{2,1,0:T(4,128)S(1)} async-done(((f32[24,4,128]{2,1,0:T(4,128)}), f32[24,4,128]{2,1,0:T(4,128)S(1)}, u32[]{:S(2)}, u32[]{:S(2)}) %all-to-all-start) | async-done | bytes 49184 | tf_op jit(solution)/shard_map/all_to_all | solution.py:166
  44.0 0.0 collective-permute-done.3.refs_3_
  44.0 0.0 collective-permute-done.4.refs_5_
  44.0 2.5 %collective-permute-start.6 = (f32[128,512]{1,0:T(8,128)S(1)}, f32[128,512]{1,0:T(8,128)S(1)}, u32[]{:S(2)}, u32[]{:S(2)}) collective-permute-start(f32[128,512]{1,0:T(8,128)S(1)} %collective-permute-done.3.refs_3_), channel_id=1, source_target_pairs={{32,0},{0,32},{96,64},{64,96},{160,128},{128,160},{224,192},{192,2... | collective-permute-start | bytes 786440 | tf_op jit(solution)/shard_map/ppermute | solution.py:161
  46.5 0.7 constant_dynamic-slice_fusion
  47.3 0.0 collective-permute-done.5.refs_6_
  47.3 3.8 %collective-permute-done.6.refs_7_ = f32[128,512]{1,0:T(8,128)S(1)} collective-permute-done((f32[128,512]{1,0:T(8,128)S(1)}, f32[128,512]{1,0:T(8,128)S(1)}, u32[]{:S(2)}, u32[]{:S(2)}) %collective-permute-start.6) | collective-permute-done | bytes 262176 | tf_op jit(solution)/shard_map/ppermute | solution.py:161
  51.1 0.0 copy-done
  51.1 3.6 %shard_map.50 = (f32[48,32,128]{2,1,0:T(8,128)S(1)}, f32[48,32,128]{2,1,0:T(8,128)S(1)}) custom-call(s32[144]{0:T(256)S(1)} %bitcast.6, f32[128,512]{1,0:T(8,128)S(1)} %copy-done, f32[128,512]{1,0:T(8,128)S(1)} %collective-permute-done.refs_1_, f32[128,512]{1,0:T(8,128)S(1)} %collective-permute-done.1.refs_2_, ...), custom_call_target="tpu_custom_call" | custom-call | tf_op jit(solution)/shard_map/pallas_call | solution.py:132
  54.7 6.6 %collective-permute-start.7 = (f32[48,32,128]{2,1,0:T(8,128)S(1)}, f32[48,32,128]{2,1,0:T(8,128)S(1)}, u32[]{:S(2)}, u32[]{:S(2)}) collective-permute-start(f32[48,32,128]{2,1,0:T(8,128)S(1)} %get-tuple-element.14), channel_id=1, source_target_pairs={{0,1},{1,0},{2,3},{3,2},{4,5},{5,4},{6,7},{7,6},{8,9},{9,8},{10,11... | collective-permute-start | bytes 2359304 | tf_op jit(solution)/shard_map/ppermute | solution.py:174
  61.3 1.9 %collective-permute-done.7 = f32[48,32,128]{2,1,0:T(8,128)S(1)} collective-permute-done((f32[48,32,128]{2,1,0:T(8,128)S(1)}, f32[48,32,128]{2,1,0:T(8,128)S(1)}, u32[]{:S(2)}, u32[]{:S(2)}) %collective-permute-start.7) | collective-permute-done | bytes 786464 | tf_op jit(solution)/shard_map/ppermute | solution.py:174
  63.1 0.1 add.21
  63.3 29.7 %all_to_all.10 = f32[16,96,128]{2,1,0:T(8,128)S(1)} all-to-all(f32[16,96,128]{2,1,0:T(8,128)S(1)} %bitcast.7), channel_id=1, replica_groups={{0,2,4,6,8,10,12,14,16,18,20,22,24,26,28,30},{1,3,5,7,9,11,13,15,17,19,..., dimensions={0} | all-to-all | bytes 1572864 | tf_op jit(solution)/shard_map/all_to_all | solution.py:176
  93.1 6.6 %collective-permute-start.9 = (f32[64,128]{1,0:T(8,128)S(1)}, f32[64,128]{1,0:T(8,128)S(1)}, u32[]{:S(2)}, u32[]{:S(2)}) collective-permute-start(f32[64,128]{1,0:T(8,128)S(1)} %slice.9), channel_id=1, source_target_pairs={{16,576},{24,152},{28,88},{26,120},{10,5},{12,6},{6,37},{8,38},{14... | collective-permute-start | bytes 98312 | tf_op jit(solution)/shard_map/ppermute | solution.py:179
  99.7 1.9 %collective-permute-start.8 = (f32[32,128]{1,0:T(8,128)S(1)}, f32[32,128]{1,0:T(8,128)S(1)}, u32[]{:S(2)}, u32[]{:S(2)}) collective-permute-start(f32[32,128]{1,0:T(8,128)S(1)} %slice.8), channel_id=1, source_target_pairs={{0,576},{14,577},{24,152},{22,153},{28,88},{26,89},{8,120},{10,121... | collective-permute-start | bytes 49160 | tf_op jit(solution)/shard_map/ppermute | solution.py:180
  101.6 0.6 reduce_sum.29
  102.2 8.5 %collective-permute-done.8 = f32[32,128]{1,0:T(8,128)S(1)} collective-permute-done((f32[32,128]{1,0:T(8,128)S(1)}, f32[32,128]{1,0:T(8,128)S(1)}, u32[]{:S(2)}, u32[]{:S(2)}) %collective-permute-start.8) | collective-permute-done | bytes 16416 | tf_op jit(solution)/shard_map/ppermute | solution.py:180
  110.7 0.0 collective-permute-done.9
  110.7 0.6 fusion
  (3 shorter events, 0.1 us)
Async XLA Ops:
  0.6 50.4 %copy-start = (f32[128,512]{1,0:T(8,128)S(1)}, f32[128,512]{1,0:T(8,128)}, u32[]{:S(2)}) copy-start(f32[128,512]{1,0:T(8,128)} %refs_0_.1) | copy-start | bytes 786436
  0.6 21.7 %collective-permute-start = (f32[128,512]{1,0:T(8,128)}, f32[128,512]{1,0:T(8,128)S(1)}, u32[]{:S(2)}, u32[]{:S(2)}) collective-permute-start(f32[128,512]{1,0:T(8,128)} %refs_0_.1), channel_id=1, source_target_pairs={{64,0},{96,32},{128,64},{160,96},{192,128},{224,160},{256,192},{28... | collective-permute-start | bytes 786440 | tf_op jit(solution)/shard_map/ppermute | solution.py:161
  15.1 28.9 %collective-permute-start.3 = (f32[128,512]{1,0:T(8,128)}, f32[128,512]{1,0:T(8,128)S(1)}, u32[]{:S(2)}, u32[]{:S(2)}) collective-permute-start(f32[128,512]{1,0:T(8,128)} %refs_0_.1), channel_id=1, source_target_pairs={{576,0},{608,32},{640,64},{672,96},{704,128},{736,160},{0,192},{32... | collective-permute-start | bytes 786440 | tf_op jit(solution)/shard_map/ppermute | solution.py:161
  17.0 17.3 %collective-permute-start.2 = (f32[128,512]{1,0:T(8,128)}, f32[128,512]{1,0:T(8,128)S(1)}, u32[]{:S(2)}, u32[]{:S(2)}) collective-permute-start(f32[128,512]{1,0:T(8,128)} %refs_0_.1), channel_id=1, source_target_pairs={{32,0},{0,32},{96,64},{64,96},{160,128},{128,160},{224,192},{192,2... | collective-permute-start | bytes 786440 | tf_op jit(solution)/shard_map/ppermute | solution.py:161
  20.1 14.2 %collective-permute-start.1 = (f32[128,512]{1,0:T(8,128)}, f32[128,512]{1,0:T(8,128)S(1)}, u32[]{:S(2)}, u32[]{:S(2)}) collective-permute-start(f32[128,512]{1,0:T(8,128)} %refs_0_.1), channel_id=1, source_target_pairs={{128,0},{160,32},{192,64},{224,96},{256,128},{288,160},{320,192},{... | collective-permute-start | bytes 786440 | tf_op jit(solution)/shard_map/ppermute | solution.py:161
  22.3 21.6 %collective-permute-start.4 = (f32[128,512]{1,0:T(8,128)S(1)}, f32[128,512]{1,0:T(8,128)S(1)}, u32[]{:S(2)}, u32[]{:S(2)}) collective-permute-start(f32[128,512]{1,0:T(8,128)S(1)} %collective-permute-done.refs_1_), channel_id=1, source_target_pairs={{32,0},{0,32},{96,64},{64,96},{160,128},{128,160},{224,192},{192,2... | collective-permute-start | bytes 786440 | tf_op jit(solution)/shard_map/ppermute | solution.py:161
  26.2 17.8 %all-to-all-start = ((f32[24,4,128]{2,1,0:T(4,128)}), f32[24,4,128]{2,1,0:T(4,128)S(1)}, u32[]{:S(2)}, u32[]{:S(2)}) async-start(f32[24,4,128]{2,1,0:T(4,128)} %broadcast_in_dim.9), calls=%async_computation | async-start | bytes 98304 | tf_op jit(solution)/shard_map/all_to_all | solution.py:166
  34.3 12.9 %collective-permute-start.5 = (f32[128,512]{1,0:T(8,128)S(1)}, f32[128,512]{1,0:T(8,128)S(1)}, u32[]{:S(2)}, u32[]{:S(2)}) collective-permute-start(f32[128,512]{1,0:T(8,128)S(1)} %collective-permute-done.1.refs_2_), channel_id=1, source_target_pairs={{64,0},{96,32},{128,64},{160,96},{192,128},{224,160},{256,192},{28... | collective-permute-start | bytes 786440 | tf_op jit(solution)/shard_map/ppermute | solution.py:161
  44.0 7.1 %collective-permute-start.6 = (f32[128,512]{1,0:T(8,128)S(1)}, f32[128,512]{1,0:T(8,128)S(1)}, u32[]{:S(2)}, u32[]{:S(2)}) collective-permute-start(f32[128,512]{1,0:T(8,128)S(1)} %collective-permute-done.3.refs_3_), channel_id=1, source_target_pairs={{32,0},{0,32},{96,64},{64,96},{160,128},{128,160},{224,192},{192,2... | collective-permute-start | bytes 786440 | tf_op jit(solution)/shard_map/ppermute | solution.py:161
  54.7 8.5 %collective-permute-start.7 = (f32[48,32,128]{2,1,0:T(8,128)S(1)}, f32[48,32,128]{2,1,0:T(8,128)S(1)}, u32[]{:S(2)}, u32[]{:S(2)}) collective-permute-start(f32[48,32,128]{2,1,0:T(8,128)S(1)} %get-tuple-element.14), channel_id=1, source_target_pairs={{0,1},{1,0},{2,3},{3,2},{4,5},{5,4},{6,7},{7,6},{8,9},{9,8},{10,11... | collective-permute-start | bytes 2359304 | tf_op jit(solution)/shard_map/ppermute | solution.py:174
  93.1 17.7 %collective-permute-start.9 = (f32[64,128]{1,0:T(8,128)S(1)}, f32[64,128]{1,0:T(8,128)S(1)}, u32[]{:S(2)}, u32[]{:S(2)}) collective-permute-start(f32[64,128]{1,0:T(8,128)S(1)} %slice.9), channel_id=1, source_target_pairs={{16,576},{24,152},{28,88},{26,120},{10,5},{12,6},{6,37},{8,38},{14... | collective-permute-start | bytes 98312 | tf_op jit(solution)/shard_map/ppermute | solution.py:179
  99.7 11.1 %collective-permute-start.8 = (f32[32,128]{1,0:T(8,128)S(1)}, f32[32,128]{1,0:T(8,128)S(1)}, u32[]{:S(2)}, u32[]{:S(2)}) collective-permute-start(f32[32,128]{1,0:T(8,128)S(1)} %slice.8), channel_id=1, source_target_pairs={{0,576},{14,577},{24,152},{22,153},{28,88},{26,89},{8,120},{10,121... | collective-permute-start | bytes 49160 | tf_op jit(solution)/shard_map/ppermute | solution.py:180

commit v7 on v6

v7 whole, which is shorter than its diff:
```python
import functools

import numpy as np
import jax
import jax.numpy as jnp
from jax import lax
from jax.experimental import pallas as pl
from jax.experimental.pallas import tpu as pltpu
from jax.sharding import PartitionSpec as P

NZ = 12
NY = 8
NQ = 16
SLICE = 32

BLOCKS = ((0, 0), (1, 0), (2, 0), (-3, 0), (0, 1), (1, 1), (3, 0), (-3, 1))
EARLY = (0, 1, 2, 3, 4, 5)
LATE = (1, 2, 3, 6, 7)
NEARLY, NLATE = 9, 3

SHARES = (
    (
        ((3, 0), (2, 3), (1, 3), (5, 3), (0, 2), (4, 2), (3, 4), (1, 1), (5, 1), (7, 2), (7, 1), (6, 1)),
        ((0, 3), (4, 3), (2, 5), (3, 2), (2, 4), (0, 1), (4, 1), (3, 1), (2, 1), (3, 6), (6, 7), (2, 7)),
    ),
    (
        ((1, 1), (5, 1), (3, 4), (3, 1), (3, 0), (2, 3), (1, 3), (1, 2), (5, 2), (3, 6), (7, 2), (6, 2)),
        ((2, 4), (5, 3), (0, 3), (4, 3), (2, 0), (0, 2), (4, 2), (3, 2), (2, 5), (7, 1), (6, 7), (2, 7)),
    ),
)


def walker_block(walk, block):
    d, e = BLOCKS[block]
    return 2 * ((walk // 2 + d) % NZ) + (walk % 2 ^ e)


def place_of(index):
    par, slot = divmod(index, 3)
    return (slot + 2) % 3 if par % 4 == 1 else slot


def ring_distance(a, b, n):
    return min((a - b) % n, (b - a) % n)


def distance(source, target):
    (w0, p0), (w1, p1) = source, target
    x0, x1 = (p0 // 16) * 2 + w0 % 2, (p1 // 16) * 2 + w1 % 2
    return (
        ring_distance(w0 // 2, w1 // 2, NZ)
        + ring_distance(x0, x1, 4)
        + ring_distance(p0 // 2 % 8, p1 // 2 % 8, 8)
    )


def assign(walk, core, targets, late, quota):
    cost = [[distance((walk, q * 2 + core), t) ** 2 for q in range(NQ)] for t in targets]
    order = sorted(range(NQ), key=lambda n: not late[n])
    lates = sum(late)
    first = order[:quota] + order[lates:lates + NY - quota]
    pick = [0] * NQ
    for q, n in enumerate(first + [n for n in order if n not in first]):
        pick[n] = q
    better = True
    while better:
        better = False
        for a in range(NQ):
            for b in range(a):
                if late[a] != late[b] and pick[a] // NY != pick[b] // NY:
                    continue
                now = cost[a][pick[a]] + cost[b][pick[b]]
                if cost[a][pick[b]] + cost[b][pick[a]] < now:
                    pick[a], pick[b] = pick[b], pick[a]
                    better = True
    return pick


def plan():
    early_table = np.zeros((2 * NZ, 2, 2, 2, NEARLY, 6), np.int32)
    late_table = np.zeros((2 * NZ, 2, 2, 2, NLATE, 6), np.int32)
    places = np.zeros((2 * NZ, 2, 2, 2 * (NEARLY + NLATE)), np.int32)
    pairs = [[], [], []]
    seen = set()
    for walk in range(2 * NZ):
        for core, share in enumerate(SHARES[walk % 2]):
            slices = []
            for n, (row, col) in enumerate(share):
                for k in range(4):
                    index = 4 * walker_block(walk, col) + k
                    target = (walker_block(walk, row), index // 3)
                    slices.append((n, k, place_of(index), target))
            picked = {}
            quota = None
            for slot in (0, 2):
                chosen = [s for s in slices if s[2] == slot]
                late = [s[0] >= NEARLY for s in chosen]
                quota = sum(late) // 2 if slot == 0 else 2 * NLATE - 2 * quota
                for s, q in zip(chosen, assign(walk, core, [s[3] for s in chosen], late, quota)):
                    picked[s[:2]] = q
                    if slot == 0:
                        picked[s[0], s[1] + 1] = q
            rank = np.zeros((2, 2), np.int32)
            dest = {}
            for n, k, slot, target in slices:
                q = picked[n, k]
                xh, y = divmod(q, NY)
                late = int(n >= NEARLY)
                own = int(rank[late, xh])
                rank[late, xh] += 1
                dest[n, k] = xh, own
                places[walk, xh, core, late * 2 * NEARLY + own] = y * 3 + slot
                source = walk * 2 * NQ + q * 2 + core
                pairs[slot].append((source, target[0] * 2 * NQ + target[1]))
                seen.add((target, slot))
            assert (rank == [[2 * NEARLY] * 2, [2 * NLATE] * 2]).all()
            for n, (row, col) in enumerate(share):
                for xh in range(2):
                    for mine in range(2):
                        if n < NEARLY:
                            table, at, names, half = early_table, n, EARLY, 2 * NEARLY
                        else:
                            table, at, names, half = late_table, n - NEARLY, LATE, 2 * NLATE
                        entry = [names.index(row), names.index(col)]
                        for k in range(4):
                            there, own = dest[n, k]
                            entry.append(int(there != xh) * half + own)
                        table[walk, xh, mine, int(core != mine), at] = entry
    assert len(seen) == NZ * 2 * 2 * NQ * 3
    assert sorted(pairs[0]) == sorted(pairs[1])
    tables = [t.reshape(8 * NZ, -1) for t in (early_table, late_table, places)]
    return tables, pairs[0], pairs[2]


def product_kernel(count, table, *refs):
    *blocks, keep, send, parts = refs
    depth = blocks[0].shape[1]
    for b, ref in enumerate(blocks):
        value = ref[...]
        high = value.astype(jnp.bfloat16)
        parts[b, :, :depth] = high
        parts[b, :, depth:] = (value - high.astype(jnp.float32)).astype(jnp.bfloat16)
    dims = (((1,), (1,)), ((), ()))

    def dot(left, right):
        return lax.dot_general(left, right, dims, preferred_element_type=jnp.float32)

    for half, out in ((1, send), (0, keep)):
        for n in range(count):
            at = (half * count + n) * 6
            row, col = table[at], table[at + 1]
            row_high, row_low = parts[row, :, :depth], parts[row, :, depth:]
            col_high, col_low = parts[col, :, :depth], parts[col, :, depth:]
            tile = dot(col_high, row_high) + (dot(col_high, row_low) + dot(col_low, row_high))
            for k in range(4):
                out[table[at + 2 + k]] = tile[k * SLICE:(k + 1) * SLICE]


VMEM = pl.BlockSpec(memory_space=pltpu.VMEM)
SMEM = pl.BlockSpec(memory_space=pltpu.SMEM)


def products(table, count, blocks, cost):
    rows, depth = blocks[0].shape
    out = jax.ShapeDtypeStruct((4 * count, SLICE, rows), jnp.float32)
    return pl.pallas_call(
        functools.partial(product_kernel, count),
        out_shape=(out, out),
        in_specs=[SMEM] + [VMEM] * len(blocks),
        out_specs=(VMEM, VMEM),
        scratch_shapes=[pltpu.VMEM((len(blocks), rows, 2 * depth), jnp.bfloat16)],
        compiler_params=pltpu.CompilerParams(vmem_limit_bytes=32 * 2**20),
        cost_estimate=pl.CostEstimate(flops=cost, bytes_accessed=2**20, transcendentals=0),
    )(table, *blocks)


def join_kernel(places, *refs):
    *terms, out = refs
    at = 0
    for group in (terms[:3], terms[3:]):
        for n in range(group[2].shape[0]):
            out[places[at]] = group[0][n] + group[1][n] + group[2][n]
            at += 1


def join(places, early, late):
    return pl.pallas_call(
        join_kernel,
        out_shape=jax.ShapeDtypeStruct((3 * NY, SLICE, early[0].shape[2]), jnp.float32),
        in_specs=[SMEM] + [VMEM] * 6,
        out_specs=VMEM,
        compiler_params=pltpu.CompilerParams(vmem_limit_bytes=32 * 2**20),
    )(places, *early, *late)


def walk_perm(dz, flip):
    return [
        (((z + dz) % NZ) * 2 + (x ^ flip), z * 2 + x) for z in range(NZ) for x in range(2)
    ]


def solution(mesh):
    tables, pair_perm, single_perm = plan()
    core_swap = [(p, p ^ 1) for p in range(2 * NQ)]
    xh_swap = [(p, p ^ NQ) for p in range(2 * NQ)]
    along_y = [[h * NQ + y * 2 + c for y in range(NY)] for h in range(2) for c in range(2)]

    def shards(jacobian, coeffs):
        walk, par = lax.axis_index("walk"), lax.axis_index("par")
        variant = walk * 4 + par // NQ * 2 + par % 2
        early_table, late_table, places = (
            lax.dynamic_index_in_dim(jnp.asarray(t), variant, 0, keepdims=False) for t in tables
        )
        tie = lax.optimization_barrier

        def walk_get(value, dz, flip=0):
            return lax.ppermute(value, "walk", walk_perm(dz, flip))

        down3, up2, up1 = (walk_get(jacobian, dz) for dz in (-3, 2, 1))
        pair0 = walk_get(jacobian, 0, 1)
        term = jnp.sum(coeffs[:, None] * jacobian, axis=0).reshape(1, 4, -1)
        terms = lax.all_to_all(jnp.broadcast_to(term, (2 * NZ,) + term.shape[1:]), "walk", 0, 0, tiled=True)
        pair1 = walk_get(up1, 0, 1)
        up2, pair0 = tie((up2, pair0))
        down3, pair1, terms = tie((down3, pair1, terms))
        update = jnp.sum(terms, axis=0).reshape(-1)
        pair3, up3 = walk_get(down3, 0, 1), walk_get(up2, 1)

        def between(keep, send, half):
            got = lax.ppermute(send, "par", core_swap)
            away = keep[half:] + got[half:]
            return keep, got, away

        keep, send = products(early_table, NEARLY, (jacobian, up1, up2, down3, pair0, pair1), 2**28)
        keep, got, away = between(keep, send, 2 * NEARLY)
        early = (keep, got, lax.ppermute(away, "par", xh_swap))
        keep, send = products(late_table, NLATE, (up1, up2, down3, up3, pair3), 2**35)
        keep, got, away = between(keep, send, 2 * NLATE)
        late = (keep, got, lax.ppermute(away, "par", xh_swap))

        mine = join(places, early, late).reshape(NY, 3 * SLICE, -1)
        mine = lax.all_to_all(mine, "par", 0, 0, axis_index_groups=along_y, tiled=True)

        mine = jnp.sum(mine, axis=0)
        pair = lax.ppermute(mine[:2 * SLICE], ("walk", "par"), pair_perm)
        single = lax.ppermute(mine[2 * SLICE:], ("walk", "par"), single_perm)
        gram = jnp.where(
            par % 4 == 1,
            jnp.concatenate((single, pair), axis=0),
            jnp.concatenate((pair, single), axis=0),
        )
        return gram.T, update

    in_specs = (P("walk", "par"), P("walk"))
    out_specs = (P("walk", "par"), P("par"))
    return jax.shard_map(shards, mesh=mesh, in_specs=in_specs, out_specs=out_specs, check_vma=False)
```

time: 112 us -> 110 us (0.982)
  the two profiles are of different devices: /device:TPU:57 before, /device:TPU:71 now
where the time goes in v7:
time: 110 us; the launch traced here: 109 us
  starting transfers between devices  57.2 us (52%)
  waiting for transfers between devices  21.8 us (20%)
  blocking collectives  19.2 us (17%)
  Pallas kernels  5.07 us (5%)
  local copies, waits for them, and re-layouts  2.73 us (2%)
  other arithmetic  2.37 us (2%)
    ppermute x7, starting transfers between devices, walk_get(): return lax.ppermute(value, 'walk', walk_perm(dz, flip))  27.8 us
    all_to_all x1, blocking collectives, shards(): lax.all_to_all(mine, 'par', 0, 0, axis_index_groups=along_y, tiled=True)  19.2 us
    ppermute x1, waiting for transfers between devices, shards(): single = lax.ppermute(mine[2 * SLICE:], ('walk', 'par'), single_perm)  9.73 us
    all_to_all x1, starting transfers between devices, shards(): lax.all_to_all(jnp.broadcast_to(term, (2 * NZ,) + term.shape[1:]), 'walk'...  8.17 us
    ppermute x2, starting transfers between devices, between(): got = lax.ppermute(send, 'par', core_swap)  7.72 us
    ppermute x1, waiting for transfers between devices, shards(): late = (keep, got, lax.ppermute(away, 'par', xh_swap))  6.04 us
    all_to_all x1, waiting for transfers between devices, shards(): lax.all_to_all(jnp.broadcast_to(term, (2 * NZ,) + term.shape[1:]), 'walk'...  5.98 us
    ppermute x1, starting transfers between devices, shards(): pair = lax.ppermute(mine[:2 * SLICE], ('walk', 'par'), pair_perm)  4.85 us
  transfers between devices with their start and end apart: 14, of which 3 were waited for; matrix products, arithmetic and copies ran while one was open for 4% of the time, Pallas kernels for 4%

profile of v7, /device:TPU:71, one launch (start us, length us, event | category | flops | bytes accessed | tf_op | source)
XLA Modules:
  0.0 109.3 jit_solution(8482928762436090484)
XLA Ops:
  0.6 0.0 copy-start
  0.6 2.1 %collective-permute-start = (f32[128,512]{1,0:T(8,128)}, f32[128,512]{1,0:T(8,128)S(1)}, u32[]{:S(2)}, u32[]{:S(2)}) collective-permute-start(f32[128,512]{1,0:T(8,128)} %refs_0_.1), channel_id=1, source_target_pairs={{64,0},{96,32},{128,64},{160,96},{192,128},{224,160},{256,192},{28... | collective-permute-start | bytes 786440 | tf_op jit(solution)/shard_map/ppermute | solution.py:217
  2.7 8.8 %collective-permute-start.3 = (f32[128,512]{1,0:T(8,128)}, f32[128,512]{1,0:T(8,128)S(1)}, u32[]{:S(2)}, u32[]{:S(2)}) collective-permute-start(f32[128,512]{1,0:T(8,128)} %refs_0_.1), channel_id=1, source_target_pairs={{576,0},{608,32},{640,64},{672,96},{704,128},{736,160},{0,192},{32... | collective-permute-start | bytes 786440 | tf_op jit(solution)/shard_map/ppermute | solution.py:217
  11.5 2.5 %collective-permute-start.2 = (f32[128,512]{1,0:T(8,128)}, f32[128,512]{1,0:T(8,128)S(1)}, u32[]{:S(2)}, u32[]{:S(2)}) collective-permute-start(f32[128,512]{1,0:T(8,128)} %refs_0_.1), channel_id=1, source_target_pairs={{32,0},{0,32},{96,64},{64,96},{160,128},{128,160},{224,192},{192,2... | collective-permute-start | bytes 786440 | tf_op jit(solution)/shard_map/ppermute | solution.py:217
  14.0 6.7 %collective-permute-start.1 = (f32[128,512]{1,0:T(8,128)}, f32[128,512]{1,0:T(8,128)S(1)}, u32[]{:S(2)}, u32[]{:S(2)}) collective-permute-start(f32[128,512]{1,0:T(8,128)} %refs_0_.1), channel_id=1, source_target_pairs={{128,0},{160,32},{192,64},{224,96},{256,128},{288,160},{320,192},{... | collective-permute-start | bytes 786440 | tf_op jit(solution)/shard_map/ppermute | solution.py:217
  20.8 0.0 collective-permute-done.refs_1_.refs_0_
  20.8 2.8 %collective-permute-start.4 = (f32[128,512]{1,0:T(8,128)S(1)}, f32[128,512]{1,0:T(8,128)S(1)}, u32[]{:S(2)}, u32[]{:S(2)}) collective-permute-start(f32[128,512]{1,0:T(8,128)S(1)} %collective-permute-done.refs_1_.refs_0_), channel_id=1, source_target_pairs={{32,0},{0,32},{96,64},{64,96},{160,128},{128,160},{224,192},{192,2... | collective-permute-start | bytes 786440 | tf_op jit(solution)/shard_map/ppermute | solution.py:217
  23.6 1.1 multiply_reduce_fusion
  24.6 0.6 broadcast_in_dim.9
  25.3 8.2 %all-to-all-start = ((f32[24,4,128]{2,1,0:T(4,128)}), f32[24,4,128]{2,1,0:T(4,128)S(1)}, u32[]{:S(2)}, u32[]{:S(2)}) async-start(f32[24,4,128]{2,1,0:T(4,128)} %broadcast_in_dim.9), calls=%async_computation | async-start | bytes 98304 | tf_op jit(solution)/shard_map/all_to_all | solution.py:222
  33.5 0.0 collective-permute-done.2.refs_4_
  33.5 0.0 collective-permute-done.1.refs_2_.refs_1_
  33.5 2.2 %collective-permute-start.7 = (f32[128,512]{1,0:T(8,128)S(1)}, f32[128,512]{1,0:T(8,128)S(1)}, u32[]{:S(2)}, u32[]{:S(2)}) collective-permute-start(f32[128,512]{1,0:T(8,128)S(1)} %collective-permute-done.1.refs_2_.refs_1_), channel_id=1, source_target_pairs={{64,0},{96,32},{128,64},{160,96},{192,128},{224,160},{256,192},{28... | collective-permute-start | bytes 786440 | tf_op jit(solution)/shard_map/ppermute | solution.py:217
  35.7 6.0 %all-to-all-done = f32[24,4,128]{2,1,0:T(4,128)S(1)} async-done(((f32[24,4,128]{2,1,0:T(4,128)}), f32[24,4,128]{2,1,0:T(4,128)S(1)}, u32[]{:S(2)}, u32[]{:S(2)}) %all-to-all-start) | async-done | bytes 49184 | tf_op jit(solution)/shard_map/all_to_all | solution.py:222
  41.7 0.0 collective-permute-done.3.refs_3_.refs_2_
  41.7 0.0 collective-permute-done.4.refs_5_
  41.7 2.7 %collective-permute-start.8 = (f32[128,512]{1,0:T(8,128)S(1)}, f32[128,512]{1,0:T(8,128)S(1)}, u32[]{:S(2)}, u32[]{:S(2)}) collective-permute-start(f32[128,512]{1,0:T(8,128)S(1)} %collective-permute-done.3.refs_3_.refs_2_), channel_id=1, source_target_pairs={{32,0},{0,32},{96,64},{64,96},{160,128},{128,160},{224,192},{192,2... | collective-permute-start | bytes 786440 | tf_op jit(solution)/shard_map/ppermute | solution.py:217
  44.4 0.7 fusion.2.table
  45.1 0.7 fusion.3.table
  45.8 0.0 copy-done
  45.8 2.9 %shard_map.68 = (f32[36,32,128]{2,1,0:T(8,128)S(1)}, f32[36,32,128]{2,1,0:T(8,128)S(1)}) custom-call(s32[108]{0:T(128)S(1)} %fusion.2.table, f32[128,512]{1,0:T(8,128)S(1)} %copy-done, f32[128,512]{1,0:T(8,128)S(1)} %collective-permute-done.refs_1_.refs_0_, f32[128,512]{1,0:T(8,128)S(1)} %collective-permute-done.1.refs_2_.refs_1_, ...), custom_call_target="tpu_custom_call" | custom-call | flops 268435456 | bytes 1048576 | tf_op jit(solution)/shard_map/pallas_call | solution.py:166
  48.6 5.8 %collective-permute-start.5 = (f32[36,32,128]{2,1,0:T(8,128)S(1)}, f32[36,32,128]{2,1,0:T(8,128)S(1)}, u32[]{:S(2)}, u32[]{:S(2)}) collective-permute-start(f32[36,32,128]{2,1,0:T(8,128)S(1)} %get-tuple-element.16), channel_id=1, source_target_pairs={{0,1},{1,0},{2,3},{3,2},{4,5},{5,4},{6,7},{7,6},{8,9},{9,8},{10,11... | collective-permute-start | bytes 1769480 | tf_op jit(solution)/shard_map/ppermute | solution.py:230
  54.4 0.0 collective-permute-done.7.refs_3_
  54.5 0.0 collective-permute-done.8.refs_4_
  54.5 1.6 %shard_map.69 = (f32[12,32,128]{2,1,0:T(8,128)S(1)}, f32[12,32,128]{2,1,0:T(8,128)S(1)}) custom-call(s32[36]{0:T(128)S(1)} %fusion.3.table, f32[128,512]{1,0:T(8,128)S(1)} %collective-permute-done.refs_1_.refs_0_, f32[128,512]{1,0:T(8,128)S(1)} %collective-permute-done.1.refs_2_.refs_1_, f32[128,512]{1,0:T(8,128)S(1)} %collective-permute-done.3.refs_3_.refs_2_, ...), custom_call_target="tpu_custom_call" | custom-call | flops 34359738368 | bytes 1048576 | tf_op jit(solution)/shard_map/pallas_call | solution.py:166
  56.1 1.9 %collective-permute-start.9 = (f32[12,32,128]{2,1,0:T(8,128)S(1)}, f32[12,32,128]{2,1,0:T(8,128)S(1)}, u32[]{:S(2)}, u32[]{:S(2)}) collective-permute-start(f32[12,32,128]{2,1,0:T(8,128)S(1)} %get-tuple-element.18), channel_id=1, source_target_pairs={{0,1},{1,0},{2,3},{3,2},{4,5},{5,4},{6,7},{7,6},{8,9},{9,8},{10,11... | collective-permute-start | bytes 589832 | tf_op jit(solution)/shard_map/ppermute | solution.py:230
  58.0 0.0 collective-permute-done.5.refs_1_
  58.1 3.0 %collective-permute-start.6 = (f32[18,32,128]{2,1,0:T(8,128)S(1)}, f32[18,32,128]{2,1,0:T(8,128)S(1)}, u32[]{:S(2)}, u32[]{:S(2)}) collective-permute-start(f32[18,32,128]{2,1,0:T(8,128)S(1)} %slice_add_fusion), channel_id=1, source_target_pairs={{0,16},{1,17},{2,18},{3,19},{4,20},{5,21},{6,22},{7,23},{8,24},{9,... | collective-permute-start | bytes 884744 | tf_op jit(solution)/shard_map/ppermute | solution.py:236
  61.1 0.0 collective-permute-done.9.refs_4_
  61.1 3.8 %collective-permute-start.10 = (f32[6,32,128]{2,1,0:T(8,128)S(1)}, f32[6,32,128]{2,1,0:T(8,128)S(1)}, u32[]{:S(2)}, u32[]{:S(2)}) collective-permute-start(f32[6,32,128]{2,1,0:T(8,128)S(1)} %slice_add_fusion.1), channel_id=1, source_target_pairs={{0,16},{1,17},{2,18},{3,19},{4,20},{5,21},{6,22},{7,23},{8,24},{9,... | collective-permute-start | bytes 294920 | tf_op jit(solution)/shard_map/ppermute | solution.py:239
  64.9 0.7 fusion.1.places
  65.6 6.0 %collective-permute-done.10.refs_5_ = f32[6,32,128]{2,1,0:T(8,128)S(1)} collective-permute-done((f32[6,32,128]{2,1,0:T(8,128)S(1)}, f32[6,32,128]{2,1,0:T(8,128)S(1)}, u32[]{:S(2)}, u32[]{:S(2)}) %collective-permute-start.10) | collective-permute-done | bytes 98336 | tf_op jit(solution)/shard_map/ppermute | solution.py:239
  71.6 0.0 collective-permute-done.6.refs_2_
  71.6 0.6 shard_map.70
  72.2 19.2 %all_to_all.10 = f32[8,96,128]{2,1,0:T(8,128)S(1)} all-to-all(f32[8,96,128]{2,1,0:T(8,128)S(1)} %bitcast.11), channel_id=1, replica_groups={{0,2,4,6,8,10,12,14},{1,3,5,7,9,11,13,15},{16,18,20,22,24,26,28,30},{17..., dimensions={0} | all-to-all | bytes 786432 | tf_op jit(solution)/shard_map/all_to_all | solution.py:242
  91.5 4.9 %collective-permute-start.12 = (f32[64,128]{1,0:T(8,128)S(1)}, f32[64,128]{1,0:T(8,128)S(1)}, u32[]{:S(2)}, u32[]{:S(2)}) collective-permute-start(f32[64,128]{1,0:T(8,128)S(1)} %slice.27), channel_id=1, source_target_pairs={{0,576},{24,152},{28,88},{26,120},{8,5},{10,6},{20,37},{22,38},{14... | collective-permute-start | bytes 98312 | tf_op jit(solution)/shard_map/ppermute | solution.py:245
  96.4 1.9 %collective-permute-start.11 = (f32[32,128]{1,0:T(8,128)S(1)}, f32[32,128]{1,0:T(8,128)S(1)}, u32[]{:S(2)}, u32[]{:S(2)}) collective-permute-start(f32[32,128]{1,0:T(8,128)S(1)} %slice.26), channel_id=1, source_target_pairs={{14,576},{12,577},{26,152},{24,153},{28,88},{8,89},{10,120},{6,121... | collective-permute-start | bytes 49160 | tf_op jit(solution)/shard_map/ppermute | solution.py:246
  98.3 0.6 reduce_sum.29
  98.9 9.7 %collective-permute-done.11 = f32[32,128]{1,0:T(8,128)S(1)} collective-permute-done((f32[32,128]{1,0:T(8,128)S(1)}, f32[32,128]{1,0:T(8,128)S(1)}, u32[]{:S(2)}, u32[]{:S(2)}) %collective-permute-start.11) | collective-permute-done | bytes 16416 | tf_op jit(solution)/shard_map/ppermute | solution.py:246
  108.7 0.0 collective-permute-done.12
  108.7 0.6 fusion
  (5 shorter events, 0.1 us)
Async XLA Ops:
  0.6 45.1 %copy-start = (f32[128,512]{1,0:T(8,128)S(1)}, f32[128,512]{1,0:T(8,128)}, u32[]{:S(2)}) copy-start(f32[128,512]{1,0:T(8,128)} %refs_0_.1) | copy-start | bytes 786436
  0.6 20.1 %collective-permute-start = (f32[128,512]{1,0:T(8,128)}, f32[128,512]{1,0:T(8,128)S(1)}, u32[]{:S(2)}, u32[]{:S(2)}) collective-permute-start(f32[128,512]{1,0:T(8,128)} %refs_0_.1), channel_id=1, source_target_pairs={{64,0},{96,32},{128,64},{160,96},{192,128},{224,160},{256,192},{28... | collective-permute-start | bytes 786440 | tf_op jit(solution)/shard_map/ppermute | solution.py:217
  2.7 39.0 %collective-permute-start.3 = (f32[128,512]{1,0:T(8,128)}, f32[128,512]{1,0:T(8,128)S(1)}, u32[]{:S(2)}, u32[]{:S(2)}) collective-permute-start(f32[128,512]{1,0:T(8,128)} %refs_0_.1), channel_id=1, source_target_pairs={{576,0},{608,32},{640,64},{672,96},{704,128},{736,160},{0,192},{32... | collective-permute-start | bytes 786440 | tf_op jit(solution)/shard_map/ppermute | solution.py:217
  11.5 21.9 %collective-permute-start.2 = (f32[128,512]{1,0:T(8,128)}, f32[128,512]{1,0:T(8,128)S(1)}, u32[]{:S(2)}, u32[]{:S(2)}) collective-permute-start(f32[128,512]{1,0:T(8,128)} %refs_0_.1), channel_id=1, source_target_pairs={{32,0},{0,32},{96,64},{64,96},{160,128},{128,160},{224,192},{192,2... | collective-permute-start | bytes 786440 | tf_op jit(solution)/shard_map/ppermute | solution.py:217
  14.0 19.5 %collective-permute-start.1 = (f32[128,512]{1,0:T(8,128)}, f32[128,512]{1,0:T(8,128)S(1)}, u32[]{:S(2)}, u32[]{:S(2)}) collective-permute-start(f32[128,512]{1,0:T(8,128)} %refs_0_.1), channel_id=1, source_target_pairs={{128,0},{160,32},{192,64},{224,96},{256,128},{288,160},{320,192},{... | collective-permute-start | bytes 786440 | tf_op jit(solution)/shard_map/ppermute | solution.py:217
  20.8 20.9 %collective-permute-start.4 = (f32[128,512]{1,0:T(8,128)S(1)}, f32[128,512]{1,0:T(8,128)S(1)}, u32[]{:S(2)}, u32[]{:S(2)}) collective-permute-start(f32[128,512]{1,0:T(8,128)S(1)} %collective-permute-done.refs_1_.refs_0_), channel_id=1, source_target_pairs={{32,0},{0,32},{96,64},{64,96},{160,128},{128,160},{224,192},{192,2... | collective-permute-start | bytes 786440 | tf_op jit(solution)/shard_map/ppermute | solution.py:217
  25.3 16.4 %all-to-all-start = ((f32[24,4,128]{2,1,0:T(4,128)}), f32[24,4,128]{2,1,0:T(4,128)S(1)}, u32[]{:S(2)}, u32[]{:S(2)}) async-start(f32[24,4,128]{2,1,0:T(4,128)} %broadcast_in_dim.9), calls=%async_computation | async-start | bytes 98304 | tf_op jit(solution)/shard_map/all_to_all | solution.py:222
  33.5 21.0 %collective-permute-start.7 = (f32[128,512]{1,0:T(8,128)S(1)}, f32[128,512]{1,0:T(8,128)S(1)}, u32[]{:S(2)}, u32[]{:S(2)}) collective-permute-start(f32[128,512]{1,0:T(8,128)S(1)} %collective-permute-done.1.refs_2_.refs_1_), channel_id=1, source_target_pairs={{64,0},{96,32},{128,64},{160,96},{192,128},{224,160},{256,192},{28... | collective-permute-start | bytes 786440 | tf_op jit(solution)/shard_map/ppermute | solution.py:217
  41.7 12.8 %collective-permute-start.8 = (f32[128,512]{1,0:T(8,128)S(1)}, f32[128,512]{1,0:T(8,128)S(1)}, u32[]{:S(2)}, u32[]{:S(2)}) collective-permute-start(f32[128,512]{1,0:T(8,128)S(1)} %collective-permute-done.3.refs_3_.refs_2_), channel_id=1, source_target_pairs={{32,0},{0,32},{96,64},{64,96},{160,128},{128,160},{224,192},{192,2... | collective-permute-start | bytes 786440 | tf_op jit(solution)/shard_map/ppermute | solution.py:217
  48.6 9.4 %collective-permute-start.5 = (f32[36,32,128]{2,1,0:T(8,128)S(1)}, f32[36,32,128]{2,1,0:T(8,128)S(1)}, u32[]{:S(2)}, u32[]{:S(2)}) collective-permute-start(f32[36,32,128]{2,1,0:T(8,128)S(1)} %get-tuple-element.16), channel_id=1, source_target_pairs={{0,1},{1,0},{2,3},{3,2},{4,5},{5,4},{6,7},{7,6},{8,9},{9,8},{10,11... | collective-permute-start | bytes 1769480 | tf_op jit(solution)/shard_map/ppermute | solution.py:230
  56.1 5.0 %collective-permute-start.9 = (f32[12,32,128]{2,1,0:T(8,128)S(1)}, f32[12,32,128]{2,1,0:T(8,128)S(1)}, u32[]{:S(2)}, u32[]{:S(2)}) collective-permute-start(f32[12,32,128]{2,1,0:T(8,128)S(1)} %get-tuple-element.18), channel_id=1, source_target_pairs={{0,1},{1,0},{2,3},{3,2},{4,5},{5,4},{6,7},{7,6},{8,9},{9,8},{10,11... | collective-permute-start | bytes 589832 | tf_op jit(solution)/shard_map/ppermute | solution.py:230
  58.1 13.6 %collective-permute-start.6 = (f32[18,32,128]{2,1,0:T(8,128)S(1)}, f32[18,32,128]{2,1,0:T(8,128)S(1)}, u32[]{:S(2)}, u32[]{:S(2)}) collective-permute-start(f32[18,32,128]{2,1,0:T(8,128)S(1)} %slice_add_fusion), channel_id=1, source_target_pairs={{0,16},{1,17},{2,18},{3,19},{4,20},{5,21},{6,22},{7,23},{8,24},{9,... | collective-permute-start | bytes 884744 | tf_op jit(solution)/shard_map/ppermute | solution.py:236
  61.1 10.5 %collective-permute-start.10 = (f32[6,32,128]{2,1,0:T(8,128)S(1)}, f32[6,32,128]{2,1,0:T(8,128)S(1)}, u32[]{:S(2)}, u32[]{:S(2)}) collective-permute-start(f32[6,32,128]{2,1,0:T(8,128)S(1)} %slice_add_fusion.1), channel_id=1, source_target_pairs={{0,16},{1,17},{2,18},{3,19},{4,20},{5,21},{6,22},{7,23},{8,24},{9,... | collective-permute-start | bytes 294920 | tf_op jit(solution)/shard_map/ppermute | solution.py:239
  91.5 17.2 %collective-permute-start.12 = (f32[64,128]{1,0:T(8,128)S(1)}, f32[64,128]{1,0:T(8,128)S(1)}, u32[]{:S(2)}, u32[]{:S(2)}) collective-permute-start(f32[64,128]{1,0:T(8,128)S(1)} %slice.27), channel_id=1, source_target_pairs={{0,576},{24,152},{28,88},{26,120},{8,5},{10,6},{20,37},{22,38},{14... | collective-permute-start | bytes 98312 | tf_op jit(solution)/shard_map/ppermute | solution.py:245
  96.4 12.3 %collective-permute-start.11 = (f32[32,128]{1,0:T(8,128)S(1)}, f32[32,128]{1,0:T(8,128)S(1)}, u32[]{:S(2)}, u32[]{:S(2)}) collective-permute-start(f32[32,128]{1,0:T(8,128)S(1)} %slice.26), channel_id=1, source_target_pairs={{14,576},{12,577},{26,152},{24,153},{28,88},{8,89},{10,120},{6,121... | collective-permute-start | bytes 49160 | tf_op jit(solution)/shard_map/ppermute | solution.py:246

commit v8 on v5

--- a/solution.py
+++ b/solution.py
@@ -1,3 +1,5 @@
+import functools
+
 import numpy as np
 import jax
 import jax.numpy as jnp
@@ -11,9 +13,9 @@
 SLICE = 32
 
 BLOCKS = ((0, 0), (1, 0), (2, 0), (-3, 0), (0, 1), (1, 1), (3, 0), (-3, 1))
-EARLY = 6
-SHARE = 12
-
+EARLY = (0, 1, 2, 3, 4, 5)
+LATE = (1, 2, 3, 6, 7)
+NEARLY, NLATE, SHARE = 9, 3, 12
 
 SHARES = (
     (
@@ -68,40 +70,47 @@
     return pick
 
 
+def held(block, core):
+    return block ^ 1 if core and block in (2, 3, 6, 7) else block
+
+
 def plan():
-    tables = np.zeros((2 * NZ, 2, 2, SHARE, 6), np.int32)
+    early_table = np.zeros((2 * NZ, 2, 2, NEARLY, 2), np.int32)
+    late_table = np.zeros((2 * NZ, 2, 2, NLATE, 2), np.int32)
+    places = np.zeros((2 * NZ, 2, SHARE, 4), np.int32)
     pairs = [[], [], []]
     seen = set()
     for walk in range(2 * NZ):
         for core, share in enumerate(SHARES[walk % 2]):
-            entries = [
-                (walker_block(walk, col), walker_block(walk, row), row, col) for row, col in share
-            ]
-            slices = [
-                (n, k, place_of(4 * e[0] + k), (e[1], (4 * e[0] + k) // 3))
-                for n, e in enumerate(entries)
-                for k in range(4)
-            ]
-            table = np.zeros((SHARE, 6), np.int32)
-            for n, e in enumerate(entries):
-                table[n, :2] = e[2:]
+            slices = []
+            for n, (row, col) in enumerate(share):
+                for k in range(4):
+                    index = 4 * walker_block(walk, col) + k
+                    target = (walker_block(walk, row), index // 3)
+                    slices.append((n, k, place_of(index), target))
             for slot in range(3):
                 chosen = [s for s in slices if s[2] == slot]
                 if slot != 1:
                     picks = assign(walk, core, [s[3] for s in chosen])
                 for (n, k, _, target), q in zip(chosen, picks, strict=True):
-                    table[n, 2 + k] = q * 3 + slot
+                    places[walk, core, n, k] = q * 3 + slot
                     source = walk * 2 * NQ + q * 2 + core
                     pairs[slot].append((source, target[0] * 2 * NQ + target[1]))
                     seen.add((target, slot))
-            tables[walk, core, 0] = table
-            tables[walk, 1 - core, 1] = table
+            for n, (row, col) in enumerate(share):
+                for mine in range(2):
+                    at = [held(row, mine), held(col, mine)]
+                    if n < NEARLY:
+                        early_table[walk, mine, int(core != mine), n] = [EARLY.index(b) for b in at]
+                    else:
+                        late_table[walk, mine, int(core != mine), n - NEARLY] = [LATE.index(b) for b in at]
     assert len(seen) == NZ * 2 * 2 * NQ * 3
     assert sorted(pairs[0]) == sorted(pairs[1])
-    return tables.reshape(4 * NZ, 2 * SHARE * 6), pairs[0], pairs[2]
-
-
-def gram_kernel(table, *refs):
+    tables = [t.reshape(4 * NZ, -1) for t in (early_table, late_table, places)]
+    return np.concatenate(tables, axis=1), pairs[0], pairs[2]
+
+
+def product_kernel(base, count, table, *refs):
     *blocks, keep, send, parts = refs
     depth = blocks[0].shape[1]
     for b, ref in enumerate(blocks):
@@ -115,28 +124,51 @@
         return lax.dot_general(left, right, dims, preferred_element_type=jnp.float32)
 
     for half, out in ((1, send), (0, keep)):
-        for n in range(SHARE):
-            at = (half * SHARE + n) * 6
+        for n in range(count):
+            at = base + (half * count + n) * 2
             row, col = table[at], table[at + 1]
             row_high, row_low = parts[row, :, :depth], parts[row, :, depth:]
             col_high, col_low = parts[col, :, :depth], parts[col, :, depth:]
-            tile = dot(col_high, row_high) + (dot(col_high, row_low) + dot(col_low, row_high))
-            for k in range(4):
-                out[table[at + 2 + k]] = tile[k * SLICE:(k + 1) * SLICE]
-
-
-def gram_parts(table, blocks):
+            out[n] = dot(col_high, row_high) + (dot(col_high, row_low) + dot(col_low, row_high))
+
+
+VMEM = pl.BlockSpec(memory_space=pltpu.VMEM)
+SMEM = pl.BlockSpec(memory_space=pltpu.SMEM)
+
+
+def products(table, base, count, blocks, cost):
     rows, depth = blocks[0].shape
-    out = jax.ShapeDtypeStruct((NQ * 3, SLICE, rows), jnp.float32)
-    vmem = pl.BlockSpec(memory_space=pltpu.VMEM)
+    out = jax.ShapeDtypeStruct((count, rows, rows), jnp.float32)
     return pl.pallas_call(
-        gram_kernel,
+        functools.partial(product_kernel, base, count),
         out_shape=(out, out),
-        in_specs=[pl.BlockSpec(memory_space=pltpu.SMEM)] + [vmem] * len(blocks),
-        out_specs=(vmem, vmem),
+        in_specs=[SMEM] + [VMEM] * len(blocks),
+        out_specs=(VMEM, VMEM),
         scratch_shapes=[pltpu.VMEM((len(blocks), rows, 2 * depth), jnp.bfloat16)],
         compiler_params=pltpu.CompilerParams(vmem_limit_bytes=32 * 2**20),
+        cost_estimate=pl.CostEstimate(flops=cost, bytes_accessed=2**20, transcendentals=0),
     )(table, *blocks)
+
+
+def join_kernel(table, *refs):
+    *terms, out = refs
+    at = 4 * SHARE
+    for kept, got in (terms[:2], terms[2:]):
+        for n in range(kept.shape[0]):
+            tile = kept[n] + got[n]
+            for k in range(4):
+                out[table[at]] = tile[k * SLICE:(k + 1) * SLICE]
+                at += 1
+
+
+def join(table, *terms):
+    return pl.pallas_call(
+        join_kernel,
+        out_shape=jax.ShapeDtypeStruct((3 * NQ, SLICE, terms[0].shape[2]), jnp.float32),
+        in_specs=[SMEM] + [VMEM] * len(terms),
+        out_specs=VMEM,
+        compiler_params=pltpu.CompilerParams(vmem_limit_bytes=32 * 2**20),
+    )(table, *terms)
 
 
 def walk_perm(dz, flip):
@@ -145,9 +177,17 @@
     ]
 
 
+def mixed_perm(moves):
+    return [
+        (source * 2 * NQ + p, target * 2 * NQ + p)
+        for p in range(2 * NQ)
+        for source, target in walk_perm(*moves[p % 2])
+    ]
+
+
 def solution(mesh):
     tables, pair_perm, single_perm = plan()
-    swap = [(p, p ^ 1) for p in range(2 * NQ)]
+    core_swap = [(p, p ^ 1) for p in range(2 * NQ)]
     groups = [[q * 2 + c for q in range(NQ)] for c in range(2)]
 
     def shards(jacobian, coeffs):
@@ -160,18 +200,28 @@
         def walk_get(value, dz, flip=0):
             return lax.ppermute(value, "walk", walk_perm(dz, flip))
 
-        down3, up2, up1 = (walk_get(jacobian, dz) for dz in (-3, 2, 1))
+        def mixed_get(value, *moves):
+            return lax.ppermute(value, ("walk", "par"), mixed_perm(moves))
+
+        far_a = mixed_get(jacobian, (2, 0), (-3, 0))
+        far_b = mixed_get(jacobian, (-3, 0), (2, 0))
+        up1 = walk_get(jacobian, 1)
         pair0 = walk_get(jacobian, 0, 1)
         pair1 = walk_get(up1, 0, 1)
-        up2, pair0 = tie((up2, pair0))
-        down3, pair1 = tie((down3, pair1))
-        pair3, up3 = walk_get(down3, 0, 1), walk_get(up2, 1)
+        far_a, pair0 = tie((far_a, pair0))
+        far_b, pair1 = tie((far_b, pair1))
+        late_a = mixed_get(far_a, (1, 0), (0, 1))
+        late_b = mixed_get(far_b, (0, 1), (1, 0))
         term = jnp.sum(coeffs[:, None] * jacobian, axis=0)
-        up3, term = tie((up3, term + walk_get(term, 0, 1)))
-
-        keep, send = gram_parts(table, (jacobian, up1, up2, down3, pair0, pair1, up3, pair3))
-        mine = keep + lax.ppermute(send, "par", swap)
-        mine, term = tie((mine.reshape(NQ, 3 * SLICE, -1), term))
+        near, term = tie((up1, term + walk_get(term, 0, 1)))
+
+        keep, send = products(table, 0, NEARLY, (jacobian, near, far_a, far_b, pair0, pair1), 2**28)
+        early = (keep, lax.ppermute(send, "par", core_swap))
+        keep, send = products(table, 4 * NEARLY, NLATE, (up1, far_a, far_b, late_a, late_b), 2**35)
+        late = (keep, lax.ppermute(send, "par", core_swap))
+
+        mine = join(table, *early, *late).reshape(NQ, 3 * SLICE, -1)
+        mine, term = tie((mine, term))
         mine = lax.all_to_all(mine, "par", 0, 0, axis_index_groups=groups, tiled=True)
 
         after, before = walk_get(term, 4), walk_get(term, -4)

time: 113 us -> 112 us (level)
  waiting for transfers between devices: 25.8 us -> 20 us
  starting transfers between devices: 78.3 us -> 81.6 us
  Pallas kernels: 3.61 us -> 5.98 us
    ppermute x1 -> x6, starting transfers between devices: 1.92 us -> 19.8 us  [the longest x4 15.5 us: mixed_get(): return lax.ppermute(value, ('walk', 'par'), mixed_perm(moves))]
    ppermute x13 -> x9, starting transfers between devices: 58.6 us -> 43.1 us  [walk_get(): return lax.ppermute(value, 'walk', walk_perm(dz, flip))]
    ppermute x13 -> x9, waiting for transfers between devices: 14.9 us -> 5.16 us  [walk_get(): return lax.ppermute(value, 'walk', walk_perm(dz, flip))]
    ppermute x1 -> x6, waiting for transfers between devices: 2.25 us -> 6.78 us  [the longest x4 5.73 us: mixed_get(): return lax.ppermute(value, ('walk', 'par'), mixed_perm(moves))]
    pallas_call x1 -> x3, Pallas kernels: 3.61 us -> 5.98 us  [the longest x2 4.46 us: products(): pl.pallas_call(functools.partial(product_kernel, base, count), out_shape=...]
  transfers between devices with their start and end apart: 17 -> 18, of which waited for: 8 -> 6; matrix products, arithmetic and copies ran while one was open for 2% -> 2% of each run, Pallas kernels for 0% -> 4%
where the time goes in v8:
time: 112 us
  starting transfers between devices  81.6 us (73%)
  waiting for transfers between devices  20 us (18%)
  Pallas kernels  5.98 us (5%)
  other arithmetic  2.32 us (2%)
    ppermute x9, starting transfers between devices, walk_get(): return lax.ppermute(value, 'walk', walk_perm(dz, flip))  43.1 us
    ppermute x4, starting transfers between devices, mixed_get(): return lax.ppermute(value, ('walk', 'par'), mixed_perm(moves))  15.5 us
    all_to_all x1, starting transfers between devices, shards(): lax.all_to_all(mine, 'par', 0, 0, axis_index_groups=groups, tiled=True)  9.76 us
    ppermute x1, waiting for transfers between devices, shards(): pair = lax.ppermute(mine[:2 * SLICE], ('walk', 'par'), pair_perm)  7.74 us
    ppermute x1, starting transfers between devices, shards(): single = lax.ppermute(mine[2 * SLICE:], ('walk', 'par'), single_perm)  6.34 us
    ppermute x4, waiting for transfers between devices, mixed_get(): return lax.ppermute(value, ('walk', 'par'), mixed_perm(moves))  5.73 us
    ppermute x9, waiting for transfers between devices, walk_get(): return lax.ppermute(value, 'walk', walk_perm(dz, flip))  5.16 us
    pallas_call x2, Pallas kernels, products(): pl.pallas_call(functools.partial(product_kernel, base, count), out_shape=...  4.46 us
  transfers between devices with their start and end apart: 18, of which 6 were waited for; matrix products, arithmetic and copies ran while one was open for 2% of the time, Pallas kernels for 4%

profile of v8, /device:TPU:30, one launch (start us, length us, event | category | flops | bytes accessed | tf_op | source)
XLA Modules:
  0.0 111.5 jit_solution(14807400065030485287)
XLA Ops:
  0.6 0.0 copy-start
  0.6 14.7 %collective-permute-start = (f32[128,512]{1,0:T(8,128)}, f32[128,512]{1,0:T(8,128)S(1)}, u32[]{:S(2)}, u32[]{:S(2)}) collective-permute-start(f32[128,512]{1,0:T(8,128)} %refs_0_.1), channel_id=1, source_target_pairs={{64,0},{96,32},{128,64},{160,96},{192,128},{224,160},{256,192},{28... | collective-permute-start | bytes 786440 | tf_op jit(solution)/shard_map/ppermute | solution.py:201
  15.4 2.7 %collective-permute-start.3 = (f32[128,512]{1,0:T(8,128)}, f32[128,512]{1,0:T(8,128)S(1)}, u32[]{:S(2)}, u32[]{:S(2)}) collective-permute-start(f32[128,512]{1,0:T(8,128)} %refs_0_.1), channel_id=1, source_target_pairs={{32,0},{0,32},{96,64},{64,96},{160,128},{128,160},{224,192},{192,2... | collective-permute-start | bytes 786440 | tf_op jit(solution)/shard_map/ppermute | solution.py:201
  18.1 2.5 %collective-permute-start.2 = (f32[128,512]{1,0:T(8,128)}, f32[128,512]{1,0:T(8,128)S(1)}, u32[]{:S(2)}, u32[]{:S(2)}) collective-permute-start(f32[128,512]{1,0:T(8,128)} %refs_0_.1), channel_id=1, source_target_pairs={{128,0},{160,32},{192,64},{224,96},{256,128},{288,160},{320,192},{... | collective-permute-start | bytes 786440 | tf_op jit(solution)/shard_map/ppermute | solution.py:204
  20.6 1.9 %collective-permute-start.4 = (f32[128,512]{1,0:T(8,128)}, f32[128,512]{1,0:T(8,128)S(1)}, u32[]{:S(2)}, u32[]{:S(2)}) collective-permute-start(f32[128,512]{1,0:T(8,128)} %refs_0_.1), channel_id=1, source_target_pairs={{576,0},{608,32},{640,64},{672,96},{704,128},{736,160},{0,192},{32... | collective-permute-start | bytes 786440 | tf_op jit(solution)/shard_map/ppermute | solution.py:204
  22.5 0.0 collective-permute-done.refs_1_.refs_0_
  22.5 3.1 %collective-permute-start.5 = (f32[128,512]{1,0:T(8,128)S(1)}, f32[128,512]{1,0:T(8,128)S(1)}, u32[]{:S(2)}, u32[]{:S(2)}) collective-permute-start(f32[128,512]{1,0:T(8,128)S(1)} %collective-permute-done.refs_1_.refs_0_), channel_id=1, source_target_pairs={{32,0},{0,32},{96,64},{64,96},{160,128},{128,160},{224,192},{192,2... | collective-permute-start | bytes 786440 | tf_op jit(solution)/shard_map/ppermute | solution.py:201
  25.6 0.0 collective-permute-done.3.refs_4_
  25.6 5.7 %collective-permute-done.2.refs_2_.refs_1_ = f32[128,512]{1,0:T(8,128)S(1)} collective-permute-done((f32[128,512]{1,0:T(8,128)}, f32[128,512]{1,0:T(8,128)S(1)}, u32[]{:S(2)}, u32[]{:S(2)}) %collective-permute-start.2) | collective-permute-done | bytes 262176 | tf_op jit(solution)/shard_map/ppermute | solution.py:204
  31.4 8.0 %collective-permute-start.7 = (f32[128,512]{1,0:T(8,128)S(1)}, f32[128,512]{1,0:T(8,128)S(1)}, u32[]{:S(2)}, u32[]{:S(2)}) collective-permute-start(f32[128,512]{1,0:T(8,128)S(1)} %collective-permute-done.2.refs_2_.refs_1_), channel_id=1, source_target_pairs={{64,0},{96,32},{128,64},{160,96},{192,128},{224,160},{256,192},{28... | collective-permute-start | bytes 786440 | tf_op jit(solution)/shard_map/ppermute | solution.py:204
  39.4 0.0 collective-permute-done.4.refs_3_.refs_2_
  39.4 0.0 collective-permute-done.5.refs_5_
  39.4 3.1 %collective-permute-start.8 = (f32[128,512]{1,0:T(8,128)S(1)}, f32[128,512]{1,0:T(8,128)S(1)}, u32[]{:S(2)}, u32[]{:S(2)}) collective-permute-start(f32[128,512]{1,0:T(8,128)S(1)} %collective-permute-done.4.refs_3_.refs_2_), channel_id=1, source_target_pairs={{32,0},{0,32},{96,64},{64,96},{160,128},{128,160},{224,192},{192,2... | collective-permute-start | bytes 786440 | tf_op jit(solution)/shard_map/ppermute | solution.py:204
  42.5 1.1 multiply_reduce_fusion
  43.6 2.7 %collective-permute-start.1 = (f32[512]{0:T(512)S(1)}, f32[512]{0:T(512)S(1)}, u32[]{:S(2)}, u32[]{:S(2)}) collective-permute-start(f32[512]{0:T(512)S(1)} %multiply_reduce_fusion), channel_id=1, source_target_pairs={{32,0},{0,32},{96,64},{64,96},{160,128},{128,160},{224,192},{192,2... | collective-permute-start | bytes 6152 | tf_op jit(solution)/shard_map/ppermute | solution.py:201
  46.3 0.7 dynamic-slice_bitcast_fusion.table
  47.0 2.0 %collective-permute-done.1 = f32[512]{0:T(512)S(1)} collective-permute-done((f32[512]{0:T(512)S(1)}, f32[512]{0:T(512)S(1)}, u32[]{:S(2)}, u32[]{:S(2)}) %collective-permute-start.1) | collective-permute-done | bytes 2080 | tf_op jit(solution)/shard_map/ppermute | solution.py:201
  49.1 0.0 copy-done
  49.1 2.9 %shard_map.50 = (f32[9,128,128]{2,1,0:T(8,128)S(1)}, f32[9,128,128]{2,1,0:T(8,128)S(1)}) custom-call(s32[96]{0:T(128)S(1)} %dynamic-slice_bitcast_fusion.table, f32[128,512]{1,0:T(8,128)S(1)} %copy-done, f32[128,512]{1,0:T(8,128)S(1)} %collective-permute-done.refs_1_.refs_0_, f32[128,512]{1,0:T(8,128)S(1)} %collective-permute-done.2.refs_2_.refs_1_, ...), custom_call_target="tpu_custom_call" | custom-call | flops 268435456 | bytes 1048576 | tf_op jit(solution)/shard_map/pallas_call | solution.py:142
  51.9 1.9 %collective-permute-start.6 = (f32[9,128,128]{2,1,0:T(8,128)S(1)}, f32[9,128,128]{2,1,0:T(8,128)S(1)}, u32[]{:S(2)}, u32[]{:S(2)}) collective-permute-start(f32[9,128,128]{2,1,0:T(8,128)S(1)} %get-tuple-element.20), channel_id=1, source_target_pairs={{0,1},{1,0},{2,3},{3,2},{4,5},{5,4},{6,7},{7,6},{8,9},{9,8},{10,11... | collective-permute-start | bytes 1769480 | tf_op jit(solution)/shard_map/ppermute | solution.py:219
  53.9 0.0 collective-permute-done.7.refs_3_
  53.9 0.0 collective-permute-done.8.refs_4_
  53.9 1.6 %shard_map.51 = (f32[3,128,128]{2,1,0:T(8,128)S(1)}, f32[3,128,128]{2,1,0:T(8,128)S(1)}) custom-call(s32[96]{0:T(128)S(1)} %dynamic-slice_bitcast_fusion.table, f32[128,512]{1,0:T(8,128)S(1)} %collective-permute-done.refs_1_.refs_0_, f32[128,512]{1,0:T(8,128)S(1)} %collective-permute-done.2.refs_2_.refs_1_, ...), custom_call_target="tpu_custom_call" | custom-call | flops 34359738368 | bytes 1048576 | tf_op jit(solution)/shard_map/pallas_call | solution.py:142
  55.5 2.4 %collective-permute-start.9 = (f32[3,128,128]{2,1,0:T(8,128)S(1)}, f32[3,128,128]{2,1,0:T(8,128)S(1)}, u32[]{:S(2)}, u32[]{:S(2)}) collective-permute-start(f32[3,128,128]{2,1,0:T(8,128)S(1)} %get-tuple-element.22), channel_id=1, source_target_pairs={{0,1},{1,0},{2,3},{3,2},{4,5},{5,4},{6,7},{7,6},{8,9},{9,8},{10,11... | collective-permute-start | bytes 589832 | tf_op jit(solution)/shard_map/ppermute | solution.py:221
  57.9 1.0 collective-permute-done.9.refs_3_
  58.9 0.0 collective-permute-done.6.refs_1_
  58.9 1.5 %shard_map.52 = f32[48,32,128]{2,1,0:T(8,128)} custom-call(s32[96]{0:T(128)S(1)} %dynamic-slice_bitcast_fusion.table, f32[9,128,128]{2,1,0:T(8,128)S(1)} %get-tuple-element.19.refs_0_, f32[9,128,128]{2,1,0:T(8,128)S(1)} %collective-permute-done.6.refs_1_, f32[3,128,128]{2,1,0:T(8,128)S(1)} %get-tuple-element.21.refs_2_, ...), custom_call_target="tpu_custom_call" | custom-call | tf_op jit(solution)/shard_map/pallas_call | solution.py:165
  60.5 9.8 %all-to-all-start = ((f32[16,96,128]{2,1,0:T(8,128)}), f32[16,96,128]{2,1,0:T(8,128)S(1)}, u32[]{:S(2)}, u32[]{:S(2)}) async-start(f32[16,96,128]{2,1,0:T(8,128)} %bitcast.1), calls=%async_computation | async-start | bytes 1572864 | tf_op jit(solution)/shard_map/all_to_all | solution.py:225
  70.2 3.5 %collective-permute-start.13 = (f32[512]{0:T(512)S(1)}, f32[512]{0:T(512)S(1)}, u32[]{:S(2)}, u32[]{:S(2)}) collective-permute-start(f32[512]{0:T(512)S(1)} %add.38), channel_id=1, source_target_pairs={{256,0},{288,32},{320,64},{352,96},{384,128},{416,160},{448,192},{... | collective-permute-start | bytes 6152 | tf_op jit(solution)/shard_map/ppermute | solution.py:201
  73.8 6.2 %collective-permute-start.12 = (f32[512]{0:T(512)S(1)}, f32[512]{0:T(512)S(1)}, u32[]{:S(2)}, u32[]{:S(2)}) collective-permute-start(f32[512]{0:T(512)S(1)} %add.38), channel_id=1, source_target_pairs={{512,0},{544,32},{576,64},{608,96},{640,128},{672,160},{704,192},{... | collective-permute-start | bytes 6152 | tf_op jit(solution)/shard_map/ppermute | solution.py:201
  80.0 0.0 collective-permute-done.13
  80.0 3.1 %collective-permute-done.12 = f32[512]{0:T(512)S(1)} collective-permute-done((f32[512]{0:T(512)S(1)}, f32[512]{0:T(512)S(1)}, u32[]{:S(2)}, u32[]{:S(2)}) %collective-permute-start.12) | collective-permute-done | bytes 2080 | tf_op jit(solution)/shard_map/ppermute | solution.py:201
  83.2 1.9 %collective-permute-start.16 = (f32[512]{0:T(512)S(1)}, f32[512]{0:T(512)S(1)}, u32[]{:S(2)}, u32[]{:S(2)}) collective-permute-start(f32[512]{0:T(512)S(1)} %select_add_fusion), channel_id=1, source_target_pairs={{704,0},{736,32},{0,64},{32,96},{64,128},{96,160},{128,192},{160,2... | collective-permute-start | bytes 6152 | tf_op jit(solution)/shard_map/ppermute | solution.py:201
  85.1 5.1 %collective-permute-start.15 = (f32[512]{0:T(512)S(1)}, f32[512]{0:T(512)S(1)}, u32[]{:S(2)}, u32[]{:S(2)}) collective-permute-start(f32[512]{0:T(512)S(1)} %select_add_fusion), channel_id=1, source_target_pairs={{64,0},{96,32},{128,64},{160,96},{192,128},{224,160},{256,192},{28... | collective-permute-start | bytes 6152 | tf_op jit(solution)/shard_map/ppermute | solution.py:201
  90.2 3.0 %collective-permute-start.14 = (f32[512]{0:T(512)S(1)}, f32[512]{0:T(512)S(1)}, u32[]{:S(2)}, u32[]{:S(2)}) collective-permute-start(f32[512]{0:T(512)S(1)} %select_add_fusion), channel_id=1, source_target_pairs={{128,0},{160,32},{192,64},{224,96},{256,128},{288,160},{320,192},{... | collective-permute-start | bytes 6152 | tf_op jit(solution)/shard_map/ppermute | solution.py:201
  93.2 0.0 all-to-all-done
  93.3 6.3 %collective-permute-start.10 = (f32[32,128]{1,0:T(8,128)S(1)}, f32[32,128]{1,0:T(8,128)S(1)}, u32[]{:S(2)}, u32[]{:S(2)}) collective-permute-start(f32[32,128]{1,0:T(8,128)S(1)} %slice.8), channel_id=1, source_target_pairs={{0,576},{14,577},{24,152},{22,153},{28,88},{26,89},{8,120},{10,121... | collective-permute-start | bytes 49160 | tf_op jit(solution)/shard_map/ppermute | solution.py:237
  99.7 2.6 %collective-permute-start.11 = (f32[64,128]{1,0:T(8,128)S(1)}, f32[64,128]{1,0:T(8,128)S(1)}, u32[]{:S(2)}, u32[]{:S(2)}) collective-permute-start(f32[64,128]{1,0:T(8,128)S(1)} %slice.9), channel_id=1, source_target_pairs={{16,576},{24,152},{28,88},{26,120},{10,5},{12,6},{6,37},{8,38},{14... | collective-permute-start | bytes 98312 | tf_op jit(solution)/shard_map/ppermute | solution.py:236
  102.2 0.0 collective-permute-done.16
  102.2 0.0 collective-permute-done.15
  102.3 0.0 collective-permute-done.14
  102.3 0.6 add_add_fusion
  102.9 0.3 collective-permute-done.10
  103.2 7.7 %collective-permute-done.11 = f32[64,128]{1,0:T(8,128)S(1)} collective-permute-done((f32[64,128]{1,0:T(8,128)S(1)}, f32[64,128]{1,0:T(8,128)S(1)}, u32[]{:S(2)}, u32[]{:S(2)}) %collective-permute-start.11) | collective-permute-done | bytes 32800 | tf_op jit(solution)/shard_map/ppermute | solution.py:236
  110.9 0.6 fusion
  (5 shorter events, 0.1 us)
Async XLA Ops:
  0.6 48.4 %copy-start = (f32[128,512]{1,0:T(8,128)S(1)}, f32[128,512]{1,0:T(8,128)}, u32[]{:S(2)}) copy-start(f32[128,512]{1,0:T(8,128)} %refs_0_.1) | copy-start | bytes 786436
  0.6 21.9 %collective-permute-start = (f32[128,512]{1,0:T(8,128)}, f32[128,512]{1,0:T(8,128)S(1)}, u32[]{:S(2)}, u32[]{:S(2)}) collective-permute-start(f32[128,512]{1,0:T(8,128)} %refs_0_.1), channel_id=1, source_target_pairs={{64,0},{96,32},{128,64},{160,96},{192,128},{224,160},{256,192},{28... | collective-permute-start | bytes 786440 | tf_op jit(solution)/shard_map/ppermute | solution.py:201
  15.4 10.3 %collective-permute-start.3 = (f32[128,512]{1,0:T(8,128)}, f32[128,512]{1,0:T(8,128)S(1)}, u32[]{:S(2)}, u32[]{:S(2)}) collective-permute-start(f32[128,512]{1,0:T(8,128)} %refs_0_.1), channel_id=1, source_target_pairs={{32,0},{0,32},{96,64},{64,96},{160,128},{128,160},{224,192},{192,2... | collective-permute-start | bytes 786440 | tf_op jit(solution)/shard_map/ppermute | solution.py:201
  18.1 13.2 %collective-permute-start.2 = (f32[128,512]{1,0:T(8,128)}, f32[128,512]{1,0:T(8,128)S(1)}, u32[]{:S(2)}, u32[]{:S(2)}) collective-permute-start(f32[128,512]{1,0:T(8,128)} %refs_0_.1), channel_id=1, source_target_pairs={{128,0},{160,32},{192,64},{224,96},{256,128},{288,160},{320,192},{... | collective-permute-start | bytes 786440 | tf_op jit(solution)/shard_map/ppermute | solution.py:204
  20.6 18.8 %collective-permute-start.4 = (f32[128,512]{1,0:T(8,128)}, f32[128,512]{1,0:T(8,128)S(1)}, u32[]{:S(2)}, u32[]{:S(2)}) collective-permute-start(f32[128,512]{1,0:T(8,128)} %refs_0_.1), channel_id=1, source_target_pairs={{576,0},{608,32},{640,64},{672,96},{704,128},{736,160},{0,192},{32... | collective-permute-start | bytes 786440 | tf_op jit(solution)/shard_map/ppermute | solution.py:204
  22.5 16.9 %collective-permute-start.5 = (f32[128,512]{1,0:T(8,128)S(1)}, f32[128,512]{1,0:T(8,128)S(1)}, u32[]{:S(2)}, u32[]{:S(2)}) collective-permute-start(f32[128,512]{1,0:T(8,128)S(1)} %collective-permute-done.refs_1_.refs_0_), channel_id=1, source_target_pairs={{32,0},{0,32},{96,64},{64,96},{160,128},{128,160},{224,192},{192,2... | collective-permute-start | bytes 786440 | tf_op jit(solution)/shard_map/ppermute | solution.py:201
  31.4 22.5 %collective-permute-start.7 = (f32[128,512]{1,0:T(8,128)S(1)}, f32[128,512]{1,0:T(8,128)S(1)}, u32[]{:S(2)}, u32[]{:S(2)}) collective-permute-start(f32[128,512]{1,0:T(8,128)S(1)} %collective-permute-done.2.refs_2_.refs_1_), channel_id=1, source_target_pairs={{64,0},{96,32},{128,64},{160,96},{192,128},{224,160},{256,192},{28... | collective-permute-start | bytes 786440 | tf_op jit(solution)/shard_map/ppermute | solution.py:204
  39.4 14.5 %collective-permute-start.8 = (f32[128,512]{1,0:T(8,128)S(1)}, f32[128,512]{1,0:T(8,128)S(1)}, u32[]{:S(2)}, u32[]{:S(2)}) collective-permute-start(f32[128,512]{1,0:T(8,128)S(1)} %collective-permute-done.4.refs_3_.refs_2_), channel_id=1, source_target_pairs={{32,0},{0,32},{96,64},{64,96},{160,128},{128,160},{224,192},{192,2... | collective-permute-start | bytes 786440 | tf_op jit(solution)/shard_map/ppermute | solution.py:204
  43.6 5.5 %collective-permute-start.1 = (f32[512]{0:T(512)S(1)}, f32[512]{0:T(512)S(1)}, u32[]{:S(2)}, u32[]{:S(2)}) collective-permute-start(f32[512]{0:T(512)S(1)} %multiply_reduce_fusion), channel_id=1, source_target_pairs={{32,0},{0,32},{96,64},{64,96},{160,128},{128,160},{224,192},{192,2... | collective-permute-start | bytes 6152 | tf_op jit(solution)/shard_map/ppermute | solution.py:201
  51.9 7.0 %collective-permute-start.6 = (f32[9,128,128]{2,1,0:T(8,128)S(1)}, f32[9,128,128]{2,1,0:T(8,128)S(1)}, u32[]{:S(2)}, u32[]{:S(2)}) collective-permute-start(f32[9,128,128]{2,1,0:T(8,128)S(1)} %get-tuple-element.20), channel_id=1, source_target_pairs={{0,1},{1,0},{2,3},{3,2},{4,5},{5,4},{6,7},{7,6},{8,9},{9,8},{10,11... | collective-permute-start | bytes 1769480 | tf_op jit(solution)/shard_map/ppermute | solution.py:219
  55.5 3.5 %collective-permute-start.9 = (f32[3,128,128]{2,1,0:T(8,128)S(1)}, f32[3,128,128]{2,1,0:T(8,128)S(1)}, u32[]{:S(2)}, u32[]{:S(2)}) collective-permute-start(f32[3,128,128]{2,1,0:T(8,128)S(1)} %get-tuple-element.22), channel_id=1, source_target_pairs={{0,1},{1,0},{2,3},{3,2},{4,5},{5,4},{6,7},{7,6},{8,9},{9,8},{10,11... | collective-permute-start | bytes 589832 | tf_op jit(solution)/shard_map/ppermute | solution.py:221
  60.5 32.8 %all-to-all-start = ((f32[16,96,128]{2,1,0:T(8,128)}), f32[16,96,128]{2,1,0:T(8,128)S(1)}, u32[]{:S(2)}, u32[]{:S(2)}) async-start(f32[16,96,128]{2,1,0:T(8,128)} %bitcast.1), calls=%async_computation | async-start | bytes 1572864 | tf_op jit(solution)/shard_map/all_to_all | solution.py:225
  70.2 9.8 %collective-permute-start.13 = (f32[512]{0:T(512)S(1)}, f32[512]{0:T(512)S(1)}, u32[]{:S(2)}, u32[]{:S(2)}) collective-permute-start(f32[512]{0:T(512)S(1)} %add.38), channel_id=1, source_target_pairs={{256,0},{288,32},{320,64},{352,96},{384,128},{416,160},{448,192},{... | collective-permute-start | bytes 6152 | tf_op jit(solution)/shard_map/ppermute | solution.py:201
  73.8 9.4 %collective-permute-start.12 = (f32[512]{0:T(512)S(1)}, f32[512]{0:T(512)S(1)}, u32[]{:S(2)}, u32[]{:S(2)}) collective-permute-start(f32[512]{0:T(512)S(1)} %add.38), channel_id=1, source_target_pairs={{512,0},{544,32},{576,64},{608,96},{640,128},{672,160},{704,192},{... | collective-permute-start | bytes 6152 | tf_op jit(solution)/shard_map/ppermute | solution.py:201
  83.2 19.1 %collective-permute-start.16 = (f32[512]{0:T(512)S(1)}, f32[512]{0:T(512)S(1)}, u32[]{:S(2)}, u32[]{:S(2)}) collective-permute-start(f32[512]{0:T(512)S(1)} %select_add_fusion), channel_id=1, source_target_pairs={{704,0},{736,32},{0,64},{32,96},{64,128},{96,160},{128,192},{160,2... | collective-permute-start | bytes 6152 | tf_op jit(solution)/shard_map/ppermute | solution.py:201
  85.1 17.2 %collective-permute-start.15 = (f32[512]{0:T(512)S(1)}, f32[512]{0:T(512)S(1)}, u32[]{:S(2)}, u32[]{:S(2)}) collective-permute-start(f32[512]{0:T(512)S(1)} %select_add_fusion), channel_id=1, source_target_pairs={{64,0},{96,32},{128,64},{160,96},{192,128},{224,160},{256,192},{28... | collective-permute-start | bytes 6152 | tf_op jit(solution)/shard_map/ppermute | solution.py:201
  90.2 12.0 %collective-permute-start.14 = (f32[512]{0:T(512)S(1)}, f32[512]{0:T(512)S(1)}, u32[]{:S(2)}, u32[]{:S(2)}) collective-permute-start(f32[512]{0:T(512)S(1)} %select_add_fusion), channel_id=1, source_target_pairs={{128,0},{160,32},{192,64},{224,96},{256,128},{288,160},{320,192},{... | collective-permute-start | bytes 6152 | tf_op jit(solution)/shard_map/ppermute | solution.py:201
  93.3 9.9 %collective-permute-start.10 = (f32[32,128]{1,0:T(8,128)S(1)}, f32[32,128]{1,0:T(8,128)S(1)}, u32[]{:S(2)}, u32[]{:S(2)}) collective-permute-start(f32[32,128]{1,0:T(8,128)S(1)} %slice.8), channel_id=1, source_target_pairs={{0,576},{14,577},{24,152},{22,153},{28,88},{26,89},{8,120},{10,121... | collective-permute-start | bytes 49160 | tf_op jit(solution)/shard_map/ppermute | solution.py:237
  99.7 11.2 %collective-permute-start.11 = (f32[64,128]{1,0:T(8,128)S(1)}, f32[64,128]{1,0:T(8,128)S(1)}, u32[]{:S(2)}, u32[]{:S(2)}) collective-permute-start(f32[64,128]{1,0:T(8,128)S(1)} %slice.9), channel_id=1, source_target_pairs={{16,576},{24,152},{28,88},{26,120},{10,5},{12,6},{6,37},{8,38},{14... | collective-permute-start | bytes 98312 | tf_op jit(solution)/shard_map/ppermute | solution.py:236

commit v9 on v8

--- a/solution.py
+++ b/solution.py
@@ -19,12 +19,12 @@
 
 SHARES = (
     (
-        ((3, 0), (2, 3), (1, 3), (5, 3), (0, 2), (4, 2), (3, 4), (1, 1), (5, 1), (7, 2), (7, 1), (6, 1)),
-        ((0, 3), (4, 3), (2, 5), (3, 2), (2, 4), (0, 1), (4, 1), (3, 1), (2, 1), (3, 6), (6, 7), (2, 7)),
+        ((2, 5), (5, 3), (4, 3), (3, 0), (0, 2), (4, 2), (3, 4), (1, 1), (5, 1), (6, 7), (7, 1), (6, 1)),
+        ((2, 3), (1, 3), (0, 3), (3, 2), (2, 4), (2, 1), (0, 1), (4, 1), (3, 1), (3, 6), (7, 2), (2, 7)),
     ),
     (
-        ((1, 1), (5, 1), (3, 4), (3, 1), (3, 0), (2, 3), (1, 3), (1, 2), (5, 2), (3, 6), (7, 2), (6, 2)),
-        ((2, 4), (5, 3), (0, 3), (4, 3), (2, 0), (0, 2), (4, 2), (3, 2), (2, 5), (7, 1), (6, 7), (2, 7)),
+        ((5, 1), (4, 1), (3, 4), (3, 1), (2, 0), (5, 3), (4, 3), (2, 2), (1, 2), (3, 6), (6, 2), (7, 2)),
+        ((2, 4), (3, 0), (2, 3), (1, 3), (0, 3), (2, 5), (0, 2), (4, 2), (3, 2), (6, 7), (7, 1), (2, 7)),
     ),
 )
 
@@ -208,14 +208,13 @@
         up1 = walk_get(jacobian, 1)
         pair0 = walk_get(jacobian, 0, 1)
         pair1 = walk_get(up1, 0, 1)
-        far_a, pair0 = tie((far_a, pair0))
+        term = jnp.sum(coeffs[:, None] * jacobian, axis=0)
+        far_a, pair0, term = tie((far_a, pair0, term + walk_get(term, 0, 1)))
         far_b, pair1 = tie((far_b, pair1))
         late_a = mixed_get(far_a, (1, 0), (0, 1))
         late_b = mixed_get(far_b, (0, 1), (1, 0))
-        term = jnp.sum(coeffs[:, None] * jacobian, axis=0)
-        near, term = tie((up1, term + walk_get(term, 0, 1)))
-
-        keep, send = products(table, 0, NEARLY, (jacobian, near, far_a, far_b, pair0, pair1), 2**28)
+
+        keep, send = products(table, 0, NEARLY, (jacobian, up1, far_a, far_b, pair0, pair1), 2**28)
         early = (keep, lax.ppermute(send, "par", core_swap))
         keep, send = products(table, 4 * NEARLY, NLATE, (up1, far_a, far_b, late_a, late_b), 2**35)
         late = (keep, lax.ppermute(send, "par", core_swap))

time: 112 us -> 105 us (0.938)
  the two profiles are of different devices: /device:TPU:30 before, /device:TPU:21 now
where the time goes in v9:
time: 105 us; the launch traced here: 104 us
  starting transfers between devices  77.7 us (74%)
  waiting for transfers between devices  16.6 us (16%)
  Pallas kernels  5.98 us (6%)
  other arithmetic  2.32 us (2%)
    ppermute x9, starting transfers between devices, walk_get(): return lax.ppermute(value, 'walk', walk_perm(dz, flip))  40.8 us
    all_to_all x1, starting transfers between devices, shards(): lax.all_to_all(mine, 'par', 0, 0, axis_index_groups=groups, tiled=True)  9.3 us
    ppermute x4, starting transfers between devices, mixed_get(): return lax.ppermute(value, ('walk', 'par'), mixed_perm(moves))  8.46 us
    ppermute x1, starting transfers between devices, shards(): single = lax.ppermute(mine[2 * SLICE:], ('walk', 'par'), single_perm)  7.93 us
    ppermute x4, waiting for transfers between devices, mixed_get(): return lax.ppermute(value, ('walk', 'par'), mixed_perm(moves))  6.9 us
    ppermute x1, starting transfers between devices, shards(): pair = lax.ppermute(mine[:2 * SLICE], ('walk', 'par'), pair_perm)  5.66 us
    ppermute x9, waiting for transfers between devices, walk_get(): return lax.ppermute(value, 'walk', walk_perm(dz, flip))  4.78 us
    pallas_call x2, Pallas kernels, products(): pl.pallas_call(functools.partial(product_kernel, base, count), out_shape=...  4.45 us
  transfers between devices with their start and end apart: 18, of which 5 were waited for; matrix products, arithmetic and copies ran while one was open for 2% of the time, Pallas kernels for 4%

profile of v9, /device:TPU:21, one launch (start us, length us, event | category | flops | bytes accessed | tf_op | source)
XLA Modules:
  0.0 104.2 jit_solution(731522402681192828)
XLA Ops:
  0.6 0.0 copy-start
  0.6 14.4 %collective-permute-start = (f32[128,512]{1,0:T(8,128)}, f32[128,512]{1,0:T(8,128)S(1)}, u32[]{:S(2)}, u32[]{:S(2)}) collective-permute-start(f32[128,512]{1,0:T(8,128)} %refs_0_.1), channel_id=1, source_target_pairs={{64,0},{96,32},{128,64},{160,96},{192,128},{224,160},{256,192},{28... | collective-permute-start | bytes 786440 | tf_op jit(solution)/shard_map/ppermute | solution.py:201
  15.1 2.8 %collective-permute-start.2 = (f32[128,512]{1,0:T(8,128)}, f32[128,512]{1,0:T(8,128)S(1)}, u32[]{:S(2)}, u32[]{:S(2)}) collective-permute-start(f32[128,512]{1,0:T(8,128)} %refs_0_.1), channel_id=1, source_target_pairs={{32,0},{0,32},{96,64},{64,96},{160,128},{128,160},{224,192},{192,2... | collective-permute-start | bytes 786440 | tf_op jit(solution)/shard_map/ppermute | solution.py:201
  17.9 1.9 %collective-permute-start.1 = (f32[128,512]{1,0:T(8,128)}, f32[128,512]{1,0:T(8,128)S(1)}, u32[]{:S(2)}, u32[]{:S(2)}) collective-permute-start(f32[128,512]{1,0:T(8,128)} %refs_0_.1), channel_id=1, source_target_pairs={{128,0},{160,32},{192,64},{224,96},{256,128},{288,160},{320,192},{... | collective-permute-start | bytes 786440 | tf_op jit(solution)/shard_map/ppermute | solution.py:204
  19.8 2.2 %collective-permute-start.4 = (f32[128,512]{1,0:T(8,128)}, f32[128,512]{1,0:T(8,128)S(1)}, u32[]{:S(2)}, u32[]{:S(2)}) collective-permute-start(f32[128,512]{1,0:T(8,128)} %refs_0_.1), channel_id=1, source_target_pairs={{576,0},{608,32},{640,64},{672,96},{704,128},{736,160},{0,192},{32... | collective-permute-start | bytes 786440 | tf_op jit(solution)/shard_map/ppermute | solution.py:204
  22.0 0.0 collective-permute-done.refs_1_.refs_0_
  22.0 2.5 %collective-permute-start.5 = (f32[128,512]{1,0:T(8,128)S(1)}, f32[128,512]{1,0:T(8,128)S(1)}, u32[]{:S(2)}, u32[]{:S(2)}) collective-permute-start(f32[128,512]{1,0:T(8,128)S(1)} %collective-permute-done.refs_1_.refs_0_), channel_id=1, source_target_pairs={{32,0},{0,32},{96,64},{64,96},{160,128},{128,160},{224,192},{192,2... | collective-permute-start | bytes 786440 | tf_op jit(solution)/shard_map/ppermute | solution.py:201
  24.5 1.1 %multiply_reduce_fusion = f32[512]{0:T(512)S(1)} fusion(f32[128,512]{1,0:T(8,128)} %refs_0_.1, f32[128]{0:T(128)} %param.4), kind=kLoop, calls=%fused_computation | loop fusion | flops 130560 | bytes 264704 | tf_op jit(solution)/shard_map/reduce_sum | solution.py:211
  25.5 2.8 %collective-permute-start.3 = (f32[512]{0:T(512)S(1)}, f32[512]{0:T(512)S(1)}, u32[]{:S(2)}, u32[]{:S(2)}) collective-permute-start(f32[512]{0:T(512)S(1)} %multiply_reduce_fusion), channel_id=1, source_target_pairs={{32,0},{0,32},{96,64},{64,96},{160,128},{128,160},{224,192},{192,2... | collective-permute-start | bytes 6152 | tf_op jit(solution)/shard_map/ppermute | solution.py:201
  28.4 1.9 %collective-permute-done.3 = f32[512]{0:T(512)S(1)} collective-permute-done((f32[512]{0:T(512)S(1)}, f32[512]{0:T(512)S(1)}, u32[]{:S(2)}, u32[]{:S(2)}) %collective-permute-start.3) | collective-permute-done | bytes 2080 | tf_op jit(solution)/shard_map/ppermute | solution.py:201
  30.3 0.0 collective-permute-done.2.refs_4_
  30.3 6.9 %collective-permute-done.1.refs_2_.refs_1_ = f32[128,512]{1,0:T(8,128)S(1)} collective-permute-done((f32[128,512]{1,0:T(8,128)}, f32[128,512]{1,0:T(8,128)S(1)}, u32[]{:S(2)}, u32[]{:S(2)}) %collective-permute-start.1) | collective-permute-done | bytes 262176 | tf_op jit(solution)/shard_map/ppermute | solution.py:204
  37.2 2.4 %collective-permute-start.7 = (f32[128,512]{1,0:T(8,128)S(1)}, f32[128,512]{1,0:T(8,128)S(1)}, u32[]{:S(2)}, u32[]{:S(2)}) collective-permute-start(f32[128,512]{1,0:T(8,128)S(1)} %collective-permute-done.1.refs_2_.refs_1_), channel_id=1, source_target_pairs={{64,0},{96,32},{128,64},{160,96},{192,128},{224,160},{256,192},{28... | collective-permute-start | bytes 786440 | tf_op jit(solution)/shard_map/ppermute | solution.py:204
  39.6 0.0 collective-permute-done.4.refs_3_.refs_2_
  39.6 0.0 collective-permute-done.5.refs_5_
  39.6 1.9 %collective-permute-start.8 = (f32[128,512]{1,0:T(8,128)S(1)}, f32[128,512]{1,0:T(8,128)S(1)}, u32[]{:S(2)}, u32[]{:S(2)}) collective-permute-start(f32[128,512]{1,0:T(8,128)S(1)} %collective-permute-done.4.refs_3_.refs_2_), channel_id=1, source_target_pairs={{32,0},{0,32},{96,64},{64,96},{160,128},{128,160},{224,192},{192,2... | collective-permute-start | bytes 786440 | tf_op jit(solution)/shard_map/ppermute | solution.py:204
  41.6 0.7 dynamic-slice_bitcast_fusion.table
  42.3 0.0 copy-done
  42.3 2.9 %shard_map.50 = (f32[9,128,128]{2,1,0:T(8,128)S(1)}, f32[9,128,128]{2,1,0:T(8,128)S(1)}) custom-call(s32[96]{0:T(128)S(1)} %dynamic-slice_bitcast_fusion.table, f32[128,512]{1,0:T(8,128)S(1)} %copy-done, f32[128,512]{1,0:T(8,128)S(1)} %collective-permute-done.refs_1_.refs_0_, f32[128,512]{1,0:T(8,128)S(1)} %collective-permute-done.1.refs_2_.refs_1_, ...), custom_call_target="tpu_custom_call" | custom-call | flops 268435456 | bytes 1048576 | tf_op jit(solution)/shard_map/pallas_call | solution.py:142
  45.2 3.6 %collective-permute-start.6 = (f32[9,128,128]{2,1,0:T(8,128)S(1)}, f32[9,128,128]{2,1,0:T(8,128)S(1)}, u32[]{:S(2)}, u32[]{:S(2)}) collective-permute-start(f32[9,128,128]{2,1,0:T(8,128)S(1)} %get-tuple-element.18), channel_id=1, source_target_pairs={{0,1},{1,0},{2,3},{3,2},{4,5},{5,4},{6,7},{7,6},{8,9},{9,8},{10,11... | collective-permute-start | bytes 1769480 | tf_op jit(solution)/shard_map/ppermute | solution.py:218
  48.7 0.0 collective-permute-done.7.refs_3_
  48.7 0.0 collective-permute-done.8.refs_4_
  48.7 1.6 %shard_map.51 = (f32[3,128,128]{2,1,0:T(8,128)S(1)}, f32[3,128,128]{2,1,0:T(8,128)S(1)}) custom-call(s32[96]{0:T(128)S(1)} %dynamic-slice_bitcast_fusion.table, f32[128,512]{1,0:T(8,128)S(1)} %collective-permute-done.refs_1_.refs_0_, f32[128,512]{1,0:T(8,128)S(1)} %collective-permute-done.1.refs_2_.refs_1_, ...), custom_call_target="tpu_custom_call" | custom-call | flops 34359738368 | bytes 1048576 | tf_op jit(solution)/shard_map/pallas_call | solution.py:142
  50.3 1.9 %collective-permute-start.9 = (f32[3,128,128]{2,1,0:T(8,128)S(1)}, f32[3,128,128]{2,1,0:T(8,128)S(1)}, u32[]{:S(2)}, u32[]{:S(2)}) collective-permute-start(f32[3,128,128]{2,1,0:T(8,128)S(1)} %get-tuple-element.20), channel_id=1, source_target_pairs={{0,1},{1,0},{2,3},{3,2},{4,5},{5,4},{6,7},{7,6},{8,9},{9,8},{10,11... | collective-permute-start | bytes 589832 | tf_op jit(solution)/shard_map/ppermute | solution.py:220
  52.3 1.4 %collective-permute-done.9.refs_3_ = f32[3,128,128]{2,1,0:T(8,128)S(1)} collective-permute-done((f32[3,128,128]{2,1,0:T(8,128)S(1)}, f32[3,128,128]{2,1,0:T(8,128)S(1)}, u32[]{:S(2)}, u32[]{:S(2)}) %collective-permute-start.9) | collective-permute-done | bytes 196640 | tf_op jit(solution)/shard_map/ppermute | solution.py:220
  53.7 0.0 collective-permute-done.6.refs_1_
  53.7 1.5 %shard_map.52 = f32[48,32,128]{2,1,0:T(8,128)} custom-call(s32[96]{0:T(128)S(1)} %dynamic-slice_bitcast_fusion.table, f32[9,128,128]{2,1,0:T(8,128)S(1)} %get-tuple-element.17.refs_0_, f32[9,128,128]{2,1,0:T(8,128)S(1)} %collective-permute-done.6.refs_1_, f32[3,128,128]{2,1,0:T(8,128)S(1)} %get-tuple-element.19.refs_2_, ...), custom_call_target="tpu_custom_call" | custom-call | tf_op jit(solution)/shard_map/pallas_call | solution.py:165
  55.2 9.3 %all-to-all-start = ((f32[16,96,128]{2,1,0:T(8,128)}), f32[16,96,128]{2,1,0:T(8,128)S(1)}, u32[]{:S(2)}, u32[]{:S(2)}) async-start(f32[16,96,128]{2,1,0:T(8,128)} %bitcast.1), calls=%async_computation | async-start | bytes 1572864 | tf_op jit(solution)/shard_map/all_to_all | solution.py:224
  64.5 3.6 %collective-permute-start.13 = (f32[512]{0:T(512)S(1)}, f32[512]{0:T(512)S(1)}, u32[]{:S(2)}, u32[]{:S(2)}) collective-permute-start(f32[512]{0:T(512)S(1)} %add.38), channel_id=1, source_target_pairs={{256,0},{288,32},{320,64},{352,96},{384,128},{416,160},{448,192},{... | collective-permute-start | bytes 6152 | tf_op jit(solution)/shard_map/ppermute | solution.py:201
  68.1 5.6 %collective-permute-start.12 = (f32[512]{0:T(512)S(1)}, f32[512]{0:T(512)S(1)}, u32[]{:S(2)}, u32[]{:S(2)}) collective-permute-start(f32[512]{0:T(512)S(1)} %add.38), channel_id=1, source_target_pairs={{512,0},{544,32},{576,64},{608,96},{640,128},{672,160},{704,192},{... | collective-permute-start | bytes 6152 | tf_op jit(solution)/shard_map/ppermute | solution.py:201
  73.7 0.0 collective-permute-done.13
  73.7 2.9 %collective-permute-done.12 = f32[512]{0:T(512)S(1)} collective-permute-done((f32[512]{0:T(512)S(1)}, f32[512]{0:T(512)S(1)}, u32[]{:S(2)}, u32[]{:S(2)}) %collective-permute-start.12) | collective-permute-done | bytes 2080 | tf_op jit(solution)/shard_map/ppermute | solution.py:201
  76.6 2.5 %collective-permute-start.16 = (f32[512]{0:T(512)S(1)}, f32[512]{0:T(512)S(1)}, u32[]{:S(2)}, u32[]{:S(2)}) collective-permute-start(f32[512]{0:T(512)S(1)} %select_add_fusion), channel_id=1, source_target_pairs={{704,0},{736,32},{0,64},{32,96},{64,128},{96,160},{128,192},{160,2... | collective-permute-start | bytes 6152 | tf_op jit(solution)/shard_map/ppermute | solution.py:201
  79.1 4.0 %collective-permute-start.15 = (f32[512]{0:T(512)S(1)}, f32[512]{0:T(512)S(1)}, u32[]{:S(2)}, u32[]{:S(2)}) collective-permute-start(f32[512]{0:T(512)S(1)} %select_add_fusion), channel_id=1, source_target_pairs={{64,0},{96,32},{128,64},{160,96},{192,128},{224,160},{256,192},{28... | collective-permute-start | bytes 6152 | tf_op jit(solution)/shard_map/ppermute | solution.py:201
  83.1 2.6 %collective-permute-start.14 = (f32[512]{0:T(512)S(1)}, f32[512]{0:T(512)S(1)}, u32[]{:S(2)}, u32[]{:S(2)}) collective-permute-start(f32[512]{0:T(512)S(1)} %select_add_fusion), channel_id=1, source_target_pairs={{128,0},{160,32},{192,64},{224,96},{256,128},{288,160},{320,192},{... | collective-permute-start | bytes 6152 | tf_op jit(solution)/shard_map/ppermute | solution.py:201
  85.8 0.0 all-to-all-done
  85.9 7.9 %collective-permute-start.10 = (f32[32,128]{1,0:T(8,128)S(1)}, f32[32,128]{1,0:T(8,128)S(1)}, u32[]{:S(2)}, u32[]{:S(2)}) collective-permute-start(f32[32,128]{1,0:T(8,128)S(1)} %slice.8), channel_id=1, source_target_pairs={{8,132},{20,133},{24,120},{26,121},{28,56},{10,57},{0,576},{14,577... | collective-permute-start | bytes 49160 | tf_op jit(solution)/shard_map/ppermute | solution.py:236
  93.8 5.7 %collective-permute-start.11 = (f32[64,128]{1,0:T(8,128)S(1)}, f32[64,128]{1,0:T(8,128)S(1)}, u32[]{:S(2)}, u32[]{:S(2)}) collective-permute-start(f32[64,128]{1,0:T(8,128)S(1)} %slice.9), channel_id=1, source_target_pairs={{6,132},{8,120},{28,56},{0,576},{20,5},{10,6},{30,37},{22,38},{14,... | collective-permute-start | bytes 98312 | tf_op jit(solution)/shard_map/ppermute | solution.py:235
  99.5 0.0 collective-permute-done.16
  99.5 0.0 collective-permute-done.15
  99.5 0.0 collective-permute-done.14
  99.5 0.6 add_add_fusion
  100.1 0.0 collective-permute-done.10
  100.1 3.5 %collective-permute-done.11 = f32[64,128]{1,0:T(8,128)S(1)} collective-permute-done((f32[64,128]{1,0:T(8,128)S(1)}, f32[64,128]{1,0:T(8,128)S(1)}, u32[]{:S(2)}, u32[]{:S(2)}) %collective-permute-start.11) | collective-permute-done | bytes 32800 | tf_op jit(solution)/shard_map/ppermute | solution.py:235
  103.6 0.6 fusion
  (5 shorter events, 0.1 us)
Async XLA Ops:
  0.6 41.7 %copy-start = (f32[128,512]{1,0:T(8,128)S(1)}, f32[128,512]{1,0:T(8,128)}, u32[]{:S(2)}) copy-start(f32[128,512]{1,0:T(8,128)} %refs_0_.1) | copy-start | bytes 786436
  0.6 21.4 %collective-permute-start = (f32[128,512]{1,0:T(8,128)}, f32[128,512]{1,0:T(8,128)S(1)}, u32[]{:S(2)}, u32[]{:S(2)}) collective-permute-start(f32[128,512]{1,0:T(8,128)} %refs_0_.1), channel_id=1, source_target_pairs={{64,0},{96,32},{128,64},{160,96},{192,128},{224,160},{256,192},{28... | collective-permute-start | bytes 786440 | tf_op jit(solution)/shard_map/ppermute | solution.py:201
  15.1 15.2 %collective-permute-start.2 = (f32[128,512]{1,0:T(8,128)}, f32[128,512]{1,0:T(8,128)S(1)}, u32[]{:S(2)}, u32[]{:S(2)}) collective-permute-start(f32[128,512]{1,0:T(8,128)} %refs_0_.1), channel_id=1, source_target_pairs={{32,0},{0,32},{96,64},{64,96},{160,128},{128,160},{224,192},{192,2... | collective-permute-start | bytes 786440 | tf_op jit(solution)/shard_map/ppermute | solution.py:201
  17.9 19.2 %collective-permute-start.1 = (f32[128,512]{1,0:T(8,128)}, f32[128,512]{1,0:T(8,128)S(1)}, u32[]{:S(2)}, u32[]{:S(2)}) collective-permute-start(f32[128,512]{1,0:T(8,128)} %refs_0_.1), channel_id=1, source_target_pairs={{128,0},{160,32},{192,64},{224,96},{256,128},{288,160},{320,192},{... | collective-permute-start | bytes 786440 | tf_op jit(solution)/shard_map/ppermute | solution.py:204
  19.8 19.8 %collective-permute-start.4 = (f32[128,512]{1,0:T(8,128)}, f32[128,512]{1,0:T(8,128)S(1)}, u32[]{:S(2)}, u32[]{:S(2)}) collective-permute-start(f32[128,512]{1,0:T(8,128)} %refs_0_.1), channel_id=1, source_target_pairs={{576,0},{608,32},{640,64},{672,96},{704,128},{736,160},{0,192},{32... | collective-permute-start | bytes 786440 | tf_op jit(solution)/shard_map/ppermute | solution.py:204
  22.0 17.6 %collective-permute-start.5 = (f32[128,512]{1,0:T(8,128)S(1)}, f32[128,512]{1,0:T(8,128)S(1)}, u32[]{:S(2)}, u32[]{:S(2)}) collective-permute-start(f32[128,512]{1,0:T(8,128)S(1)} %collective-permute-done.refs_1_.refs_0_), channel_id=1, source_target_pairs={{32,0},{0,32},{96,64},{64,96},{160,128},{128,160},{224,192},{192,2... | collective-permute-start | bytes 786440 | tf_op jit(solution)/shard_map/ppermute | solution.py:201
  25.5 4.7 %collective-permute-start.3 = (f32[512]{0:T(512)S(1)}, f32[512]{0:T(512)S(1)}, u32[]{:S(2)}, u32[]{:S(2)}) collective-permute-start(f32[512]{0:T(512)S(1)} %multiply_reduce_fusion), channel_id=1, source_target_pairs={{32,0},{0,32},{96,64},{64,96},{160,128},{128,160},{224,192},{192,2... | collective-permute-start | bytes 6152 | tf_op jit(solution)/shard_map/ppermute | solution.py:201
  37.2 11.6 %collective-permute-start.7 = (f32[128,512]{1,0:T(8,128)S(1)}, f32[128,512]{1,0:T(8,128)S(1)}, u32[]{:S(2)}, u32[]{:S(2)}) collective-permute-start(f32[128,512]{1,0:T(8,128)S(1)} %collective-permute-done.1.refs_2_.refs_1_), channel_id=1, source_target_pairs={{64,0},{96,32},{128,64},{160,96},{192,128},{224,160},{256,192},{28... | collective-permute-start | bytes 786440 | tf_op jit(solution)/shard_map/ppermute | solution.py:204
  39.6 9.1 %collective-permute-start.8 = (f32[128,512]{1,0:T(8,128)S(1)}, f32[128,512]{1,0:T(8,128)S(1)}, u32[]{:S(2)}, u32[]{:S(2)}) collective-permute-start(f32[128,512]{1,0:T(8,128)S(1)} %collective-permute-done.4.refs_3_.refs_2_), channel_id=1, source_target_pairs={{32,0},{0,32},{96,64},{64,96},{160,128},{128,160},{224,192},{192,2... | collective-permute-start | bytes 786440 | tf_op jit(solution)/shard_map/ppermute | solution.py:204
  45.2 8.5 %collective-permute-start.6 = (f32[9,128,128]{2,1,0:T(8,128)S(1)}, f32[9,128,128]{2,1,0:T(8,128)S(1)}, u32[]{:S(2)}, u32[]{:S(2)}) collective-permute-start(f32[9,128,128]{2,1,0:T(8,128)S(1)} %get-tuple-element.18), channel_id=1, source_target_pairs={{0,1},{1,0},{2,3},{3,2},{4,5},{5,4},{6,7},{7,6},{8,9},{9,8},{10,11... | collective-permute-start | bytes 1769480 | tf_op jit(solution)/shard_map/ppermute | solution.py:218
  50.3 3.3 %collective-permute-start.9 = (f32[3,128,128]{2,1,0:T(8,128)S(1)}, f32[3,128,128]{2,1,0:T(8,128)S(1)}, u32[]{:S(2)}, u32[]{:S(2)}) collective-permute-start(f32[3,128,128]{2,1,0:T(8,128)S(1)} %get-tuple-element.20), channel_id=1, source_target_pairs={{0,1},{1,0},{2,3},{3,2},{4,5},{5,4},{6,7},{7,6},{8,9},{9,8},{10,11... | collective-permute-start | bytes 589832 | tf_op jit(solution)/shard_map/ppermute | solution.py:220
  55.2 30.6 %all-to-all-start = ((f32[16,96,128]{2,1,0:T(8,128)}), f32[16,96,128]{2,1,0:T(8,128)S(1)}, u32[]{:S(2)}, u32[]{:S(2)}) async-start(f32[16,96,128]{2,1,0:T(8,128)} %bitcast.1), calls=%async_computation | async-start | bytes 1572864 | tf_op jit(solution)/shard_map/all_to_all | solution.py:224
  64.5 9.2 %collective-permute-start.13 = (f32[512]{0:T(512)S(1)}, f32[512]{0:T(512)S(1)}, u32[]{:S(2)}, u32[]{:S(2)}) collective-permute-start(f32[512]{0:T(512)S(1)} %add.38), channel_id=1, source_target_pairs={{256,0},{288,32},{320,64},{352,96},{384,128},{416,160},{448,192},{... | collective-permute-start | bytes 6152 | tf_op jit(solution)/shard_map/ppermute | solution.py:201
  68.1 8.5 %collective-permute-start.12 = (f32[512]{0:T(512)S(1)}, f32[512]{0:T(512)S(1)}, u32[]{:S(2)}, u32[]{:S(2)}) collective-permute-start(f32[512]{0:T(512)S(1)} %add.38), channel_id=1, source_target_pairs={{512,0},{544,32},{576,64},{608,96},{640,128},{672,160},{704,192},{... | collective-permute-start | bytes 6152 | tf_op jit(solution)/shard_map/ppermute | solution.py:201
  76.6 22.9 %collective-permute-start.16 = (f32[512]{0:T(512)S(1)}, f32[512]{0:T(512)S(1)}, u32[]{:S(2)}, u32[]{:S(2)}) collective-permute-start(f32[512]{0:T(512)S(1)} %select_add_fusion), channel_id=1, source_target_pairs={{704,0},{736,32},{0,64},{32,96},{64,128},{96,160},{128,192},{160,2... | collective-permute-start | bytes 6152 | tf_op jit(solution)/shard_map/ppermute | solution.py:201
  79.1 20.4 %collective-permute-start.15 = (f32[512]{0:T(512)S(1)}, f32[512]{0:T(512)S(1)}, u32[]{:S(2)}, u32[]{:S(2)}) collective-permute-start(f32[512]{0:T(512)S(1)} %select_add_fusion), channel_id=1, source_target_pairs={{64,0},{96,32},{128,64},{160,96},{192,128},{224,160},{256,192},{28... | collective-permute-start | bytes 6152 | tf_op jit(solution)/shard_map/ppermute | solution.py:201
  83.1 16.4 %collective-permute-start.14 = (f32[512]{0:T(512)S(1)}, f32[512]{0:T(512)S(1)}, u32[]{:S(2)}, u32[]{:S(2)}) collective-permute-start(f32[512]{0:T(512)S(1)} %select_add_fusion), channel_id=1, source_target_pairs={{128,0},{160,32},{192,64},{224,96},{256,128},{288,160},{320,192},{... | collective-permute-start | bytes 6152 | tf_op jit(solution)/shard_map/ppermute | solution.py:201
  85.9 14.2 %collective-permute-start.10 = (f32[32,128]{1,0:T(8,128)S(1)}, f32[32,128]{1,0:T(8,128)S(1)}, u32[]{:S(2)}, u32[]{:S(2)}) collective-permute-start(f32[32,128]{1,0:T(8,128)S(1)} %slice.8), channel_id=1, source_target_pairs={{8,132},{20,133},{24,120},{26,121},{28,56},{10,57},{0,576},{14,577... | collective-permute-start | bytes 49160 | tf_op jit(solution)/shard_map/ppermute | solution.py:236
  93.8 9.8 %collective-permute-start.11 = (f32[64,128]{1,0:T(8,128)S(1)}, f32[64,128]{1,0:T(8,128)S(1)}, u32[]{:S(2)}, u32[]{:S(2)}) collective-permute-start(f32[64,128]{1,0:T(8,128)S(1)} %slice.9), channel_id=1, source_target_pairs={{6,132},{8,120},{28,56},{0,576},{20,5},{10,6},{30,37},{22,38},{14,... | collective-permute-start | bytes 98312 | tf_op jit(solution)/shard_map/ppermute | solution.py:235

commit v10 on v9

--- a/solution.py
+++ b/solution.py
@@ -209,7 +209,7 @@
         pair0 = walk_get(jacobian, 0, 1)
         pair1 = walk_get(up1, 0, 1)
         term = jnp.sum(coeffs[:, None] * jacobian, axis=0)
-        far_a, pair0, term = tie((far_a, pair0, term + walk_get(term, 0, 1)))
+        far_a, term = tie((far_a, term + walk_get(term, 0, 1)))
         far_b, pair1 = tie((far_b, pair1))
         late_a = mixed_get(far_a, (1, 0), (0, 1))
         late_b = mixed_get(far_b, (0, 1), (1, 0))

time: 105 us -> 107 us (1.019)
  starting transfers between devices: 77.7 us -> 80.1 us
    ppermute x1, starting transfers between devices: 3.55 us -> 8.69 us  [shards(): early = (keep, lax.ppermute(send, 'par', core_swap))]
    ppermute x4, waiting for transfers between devices: 6.9 us -> 2.84 us  [mixed_get(): return lax.ppermute(value, ('walk', 'par'), mixed_perm(moves))]
    ppermute x1, starting transfers between devices: 5.66 us -> 2.93 us  [shards(): pair = lax.ppermute(mine[:2 * SLICE], ('walk', 'par'), pair_perm)]
    ppermute x1, waiting for transfers between devices: 3.49 us -> 6.22 us  [shards(): pair = lax.ppermute(mine[:2 * SLICE], ('walk', 'par'), pair_perm)]
  transfers between devices with their start and end apart: 18 -> 18, of which waited for: 5 -> 7; matrix products, arithmetic and copies ran while one was open for 2% -> 2% of each run, Pallas kernels for 4% -> 4%
where the time goes in v10:
time: 107 us; the launch traced here: 106 us
  starting transfers between devices  80.1 us (75%)
  waiting for transfers between devices  15.8 us (15%)
  Pallas kernels  5.98 us (6%)
  other arithmetic  2.32 us (2%)
    ppermute x9, starting transfers between devices, walk_get(): return lax.ppermute(value, 'walk', walk_perm(dz, flip))  40.1 us
    all_to_all x1, starting transfers between devices, shards(): lax.all_to_all(mine, 'par', 0, 0, axis_index_groups=groups, tiled=True)  9.3 us
    ppermute x4, starting transfers between devices, mixed_get(): return lax.ppermute(value, ('walk', 'par'), mixed_perm(moves))  9.2 us
    ppermute x1, starting transfers between devices, shards(): early = (keep, lax.ppermute(send, 'par', core_swap))  8.69 us
    ppermute x1, starting transfers between devices, shards(): single = lax.ppermute(mine[2 * SLICE:], ('walk', 'par'), single_perm)  7.93 us
    ppermute x1, waiting for transfers between devices, shards(): pair = lax.ppermute(mine[:2 * SLICE], ('walk', 'par'), pair_perm)  6.22 us
    ppermute x9, waiting for transfers between devices, walk_get(): return lax.ppermute(value, 'walk', walk_perm(dz, flip))  4.82 us
    pallas_call x2, Pallas kernels, products(): pl.pallas_call(functools.partial(product_kernel, base, count), out_shape=...  4.46 us
  transfers between devices with their start and end apart: 18, of which 7 were waited for; matrix products, arithmetic and copies ran while one was open for 2% of the time, Pallas kernels for 4%

profile of v10, /device:TPU:21, one launch (start us, length us, event | category | flops | bytes accessed | tf_op | source)
XLA Modules:
  0.0 105.8 jit_solution(13344416698430674697)
XLA Ops:
  0.6 0.0 copy-start
  0.6 14.4 %collective-permute-start = (f32[128,512]{1,0:T(8,128)}, f32[128,512]{1,0:T(8,128)S(1)}, u32[]{:S(2)}, u32[]{:S(2)}) collective-permute-start(f32[128,512]{1,0:T(8,128)} %refs_0_.1), channel_id=1, source_target_pairs={{64,0},{96,32},{128,64},{160,96},{192,128},{224,160},{256,192},{28... | collective-permute-start | bytes 786440 | tf_op jit(solution)/shard_map/ppermute | solution.py:201
  15.1 1.9 %collective-permute-start.1 = (f32[128,512]{1,0:T(8,128)}, f32[128,512]{1,0:T(8,128)S(1)}, u32[]{:S(2)}, u32[]{:S(2)}) collective-permute-start(f32[128,512]{1,0:T(8,128)} %refs_0_.1), channel_id=1, source_target_pairs={{128,0},{160,32},{192,64},{224,96},{256,128},{288,160},{320,192},{... | collective-permute-start | bytes 786440 | tf_op jit(solution)/shard_map/ppermute | solution.py:204
  17.0 2.2 %collective-permute-start.3 = (f32[128,512]{1,0:T(8,128)}, f32[128,512]{1,0:T(8,128)S(1)}, u32[]{:S(2)}, u32[]{:S(2)}) collective-permute-start(f32[128,512]{1,0:T(8,128)} %refs_0_.1), channel_id=1, source_target_pairs={{576,0},{608,32},{640,64},{672,96},{704,128},{736,160},{0,192},{32... | collective-permute-start | bytes 786440 | tf_op jit(solution)/shard_map/ppermute | solution.py:204
  19.2 1.2 %collective-permute-done.refs_1_.refs_0_ = f32[128,512]{1,0:T(8,128)S(1)} collective-permute-done((f32[128,512]{1,0:T(8,128)}, f32[128,512]{1,0:T(8,128)S(1)}, u32[]{:S(2)}, u32[]{:S(2)}) %collective-permute-start) | collective-permute-done | bytes 262176 | tf_op jit(solution)/shard_map/ppermute | solution.py:201
  20.4 2.8 %collective-permute-start.4 = (f32[128,512]{1,0:T(8,128)S(1)}, f32[128,512]{1,0:T(8,128)S(1)}, u32[]{:S(2)}, u32[]{:S(2)}) collective-permute-start(f32[128,512]{1,0:T(8,128)S(1)} %collective-permute-done.refs_1_.refs_0_), channel_id=1, source_target_pairs={{32,0},{0,32},{96,64},{64,96},{160,128},{128,160},{224,192},{192,2... | collective-permute-start | bytes 786440 | tf_op jit(solution)/shard_map/ppermute | solution.py:201
  23.2 2.5 %collective-permute-start.5 = (f32[128,512]{1,0:T(8,128)}, f32[128,512]{1,0:T(8,128)S(1)}, u32[]{:S(2)}, u32[]{:S(2)}) collective-permute-start(f32[128,512]{1,0:T(8,128)} %refs_0_.1), channel_id=1, source_target_pairs={{32,0},{0,32},{96,64},{64,96},{160,128},{128,160},{224,192},{192,2... | collective-permute-start | bytes 786440 | tf_op jit(solution)/shard_map/ppermute | solution.py:201
  25.6 1.1 %multiply_reduce_fusion = f32[512]{0:T(512)S(1)} fusion(f32[128,512]{1,0:T(8,128)} %refs_0_.1, f32[128]{0:T(128)} %param.4), kind=kLoop, calls=%fused_computation | loop fusion | flops 130560 | bytes 264704 | tf_op jit(solution)/shard_map/reduce_sum | solution.py:211
  26.7 2.8 %collective-permute-start.2 = (f32[512]{0:T(512)S(1)}, f32[512]{0:T(512)S(1)}, u32[]{:S(2)}, u32[]{:S(2)}) collective-permute-start(f32[512]{0:T(512)S(1)} %multiply_reduce_fusion), channel_id=1, source_target_pairs={{32,0},{0,32},{96,64},{64,96},{160,128},{128,160},{224,192},{192,2... | collective-permute-start | bytes 6152 | tf_op jit(solution)/shard_map/ppermute | solution.py:201
  29.5 2.0 %collective-permute-done.2 = f32[512]{0:T(512)S(1)} collective-permute-done((f32[512]{0:T(512)S(1)}, f32[512]{0:T(512)S(1)}, u32[]{:S(2)}, u32[]{:S(2)}) %collective-permute-start.2) | collective-permute-done | bytes 2080 | tf_op jit(solution)/shard_map/ppermute | solution.py:201
  31.5 2.8 %collective-permute-done.1.refs_2_.refs_1_ = f32[128,512]{1,0:T(8,128)S(1)} collective-permute-done((f32[128,512]{1,0:T(8,128)}, f32[128,512]{1,0:T(8,128)S(1)}, u32[]{:S(2)}, u32[]{:S(2)}) %collective-permute-start.1) | collective-permute-done | bytes 262176 | tf_op jit(solution)/shard_map/ppermute | solution.py:204
  34.3 2.8 %collective-permute-start.7 = (f32[128,512]{1,0:T(8,128)S(1)}, f32[128,512]{1,0:T(8,128)S(1)}, u32[]{:S(2)}, u32[]{:S(2)}) collective-permute-start(f32[128,512]{1,0:T(8,128)S(1)} %collective-permute-done.1.refs_2_.refs_1_), channel_id=1, source_target_pairs={{64,0},{96,32},{128,64},{160,96},{192,128},{224,160},{256,192},{28... | collective-permute-start | bytes 786440 | tf_op jit(solution)/shard_map/ppermute | solution.py:204
  37.1 0.0 collective-permute-done.3.refs_3_.refs_2_
  37.2 0.0 collective-permute-done.4.refs_5_
  37.2 2.3 %collective-permute-start.8 = (f32[128,512]{1,0:T(8,128)S(1)}, f32[128,512]{1,0:T(8,128)S(1)}, u32[]{:S(2)}, u32[]{:S(2)}) collective-permute-start(f32[128,512]{1,0:T(8,128)S(1)} %collective-permute-done.3.refs_3_.refs_2_), channel_id=1, source_target_pairs={{32,0},{0,32},{96,64},{64,96},{160,128},{128,160},{224,192},{192,2... | collective-permute-start | bytes 786440 | tf_op jit(solution)/shard_map/ppermute | solution.py:204
  39.5 0.7 dynamic-slice_bitcast_fusion.table
  40.2 0.0 collective-permute-done.5.refs_4_
  40.2 0.0 copy-done
  40.2 2.9 %shard_map.50 = (f32[9,128,128]{2,1,0:T(8,128)S(1)}, f32[9,128,128]{2,1,0:T(8,128)S(1)}) custom-call(s32[96]{0:T(128)S(1)} %dynamic-slice_bitcast_fusion.table, f32[128,512]{1,0:T(8,128)S(1)} %copy-done, f32[128,512]{1,0:T(8,128)S(1)} %collective-permute-done.refs_1_.refs_0_, f32[128,512]{1,0:T(8,128)S(1)} %collective-permute-done.1.refs_2_.refs_1_, ...), custom_call_target="tpu_custom_call" | custom-call | flops 268435456 | bytes 1048576 | tf_op jit(solution)/shard_map/pallas_call | solution.py:142
  43.1 8.7 %collective-permute-start.6 = (f32[9,128,128]{2,1,0:T(8,128)S(1)}, f32[9,128,128]{2,1,0:T(8,128)S(1)}, u32[]{:S(2)}, u32[]{:S(2)}) collective-permute-start(f32[9,128,128]{2,1,0:T(8,128)S(1)} %get-tuple-element.16), channel_id=1, source_target_pairs={{0,1},{1,0},{2,3},{3,2},{4,5},{5,4},{6,7},{7,6},{8,9},{9,8},{10,11... | collective-permute-start | bytes 1769480 | tf_op jit(solution)/shard_map/ppermute | solution.py:218
  51.8 0.0 collective-permute-done.7.refs_3_
  51.8 0.0 collective-permute-done.8.refs_4_
  51.8 1.6 %shard_map.51 = (f32[3,128,128]{2,1,0:T(8,128)S(1)}, f32[3,128,128]{2,1,0:T(8,128)S(1)}) custom-call(s32[96]{0:T(128)S(1)} %dynamic-slice_bitcast_fusion.table, f32[128,512]{1,0:T(8,128)S(1)} %collective-permute-done.refs_1_.refs_0_, f32[128,512]{1,0:T(8,128)S(1)} %collective-permute-done.1.refs_2_.refs_1_, ...), custom_call_target="tpu_custom_call" | custom-call | flops 34359738368 | bytes 1048576 | tf_op jit(solution)/shard_map/pallas_call | solution.py:142
  53.4 1.9 %collective-permute-start.9 = (f32[3,128,128]{2,1,0:T(8,128)S(1)}, f32[3,128,128]{2,1,0:T(8,128)S(1)}, u32[]{:S(2)}, u32[]{:S(2)}) collective-permute-start(f32[3,128,128]{2,1,0:T(8,128)S(1)} %get-tuple-element.18), channel_id=1, source_target_pairs={{0,1},{1,0},{2,3},{3,2},{4,5},{5,4},{6,7},{7,6},{8,9},{9,8},{10,11... | collective-permute-start | bytes 589832 | tf_op jit(solution)/shard_map/ppermute | solution.py:220
  55.3 1.4 %collective-permute-done.9.refs_3_ = f32[3,128,128]{2,1,0:T(8,128)S(1)} collective-permute-done((f32[3,128,128]{2,1,0:T(8,128)S(1)}, f32[3,128,128]{2,1,0:T(8,128)S(1)}, u32[]{:S(2)}, u32[]{:S(2)}) %collective-permute-start.9) | collective-permute-done | bytes 196640 | tf_op jit(solution)/shard_map/ppermute | solution.py:220
  56.7 0.0 collective-permute-done.6.refs_1_
  56.7 1.5 %shard_map.52 = f32[48,32,128]{2,1,0:T(8,128)} custom-call(s32[96]{0:T(128)S(1)} %dynamic-slice_bitcast_fusion.table, f32[9,128,128]{2,1,0:T(8,128)S(1)} %get-tuple-element.15.refs_0_, f32[9,128,128]{2,1,0:T(8,128)S(1)} %collective-permute-done.6.refs_1_, f32[3,128,128]{2,1,0:T(8,128)S(1)} %get-tuple-element.17.refs_2_, ...), custom_call_target="tpu_custom_call" | custom-call | tf_op jit(solution)/shard_map/pallas_call | solution.py:165
  58.2 9.3 %all-to-all-start = ((f32[16,96,128]{2,1,0:T(8,128)}), f32[16,96,128]{2,1,0:T(8,128)S(1)}, u32[]{:S(2)}, u32[]{:S(2)}) async-start(f32[16,96,128]{2,1,0:T(8,128)} %bitcast.1), calls=%async_computation | async-start | bytes 1572864 | tf_op jit(solution)/shard_map/all_to_all | solution.py:224
  67.5 2.4 %collective-permute-start.13 = (f32[512]{0:T(512)S(1)}, f32[512]{0:T(512)S(1)}, u32[]{:S(2)}, u32[]{:S(2)}) collective-permute-start(f32[512]{0:T(512)S(1)} %add.38), channel_id=1, source_target_pairs={{256,0},{288,32},{320,64},{352,96},{384,128},{416,160},{448,192},{... | collective-permute-start | bytes 6152 | tf_op jit(solution)/shard_map/ppermute | solution.py:201
  69.9 6.8 %collective-permute-start.12 = (f32[512]{0:T(512)S(1)}, f32[512]{0:T(512)S(1)}, u32[]{:S(2)}, u32[]{:S(2)}) collective-permute-start(f32[512]{0:T(512)S(1)} %add.38), channel_id=1, source_target_pairs={{512,0},{544,32},{576,64},{608,96},{640,128},{672,160},{704,192},{... | collective-permute-start | bytes 6152 | tf_op jit(solution)/shard_map/ppermute | solution.py:201
  76.8 0.0 collective-permute-done.13
  76.8 1.7 %collective-permute-done.12 = f32[512]{0:T(512)S(1)} collective-permute-done((f32[512]{0:T(512)S(1)}, f32[512]{0:T(512)S(1)}, u32[]{:S(2)}, u32[]{:S(2)}) %collective-permute-start.12) | collective-permute-done | bytes 2080 | tf_op jit(solution)/shard_map/ppermute | solution.py:201
  78.5 1.9 %collective-permute-start.16 = (f32[512]{0:T(512)S(1)}, f32[512]{0:T(512)S(1)}, u32[]{:S(2)}, u32[]{:S(2)}) collective-permute-start(f32[512]{0:T(512)S(1)} %select_add_fusion), channel_id=1, source_target_pairs={{704,0},{736,32},{0,64},{32,96},{64,128},{96,160},{128,192},{160,2... | collective-permute-start | bytes 6152 | tf_op jit(solution)/shard_map/ppermute | solution.py:201
  80.4 4.6 %collective-permute-start.15 = (f32[512]{0:T(512)S(1)}, f32[512]{0:T(512)S(1)}, u32[]{:S(2)}, u32[]{:S(2)}) collective-permute-start(f32[512]{0:T(512)S(1)} %select_add_fusion), channel_id=1, source_target_pairs={{64,0},{96,32},{128,64},{160,96},{192,128},{224,160},{256,192},{28... | collective-permute-start | bytes 6152 | tf_op jit(solution)/shard_map/ppermute | solution.py:201
  85.0 1.9 %collective-permute-start.14 = (f32[512]{0:T(512)S(1)}, f32[512]{0:T(512)S(1)}, u32[]{:S(2)}, u32[]{:S(2)}) collective-permute-start(f32[512]{0:T(512)S(1)} %select_add_fusion), channel_id=1, source_target_pairs={{128,0},{160,32},{192,64},{224,96},{256,128},{288,160},{320,192},{... | collective-permute-start | bytes 6152 | tf_op jit(solution)/shard_map/ppermute | solution.py:201
  86.9 0.5 all-to-all-done
  87.5 7.9 %collective-permute-start.10 = (f32[32,128]{1,0:T(8,128)S(1)}, f32[32,128]{1,0:T(8,128)S(1)}, u32[]{:S(2)}, u32[]{:S(2)}) collective-permute-start(f32[32,128]{1,0:T(8,128)S(1)} %slice.8), channel_id=1, source_target_pairs={{8,132},{20,133},{24,120},{26,121},{28,56},{10,57},{0,576},{14,577... | collective-permute-start | bytes 49160 | tf_op jit(solution)/shard_map/ppermute | solution.py:236
  95.4 2.9 %collective-permute-start.11 = (f32[64,128]{1,0:T(8,128)S(1)}, f32[64,128]{1,0:T(8,128)S(1)}, u32[]{:S(2)}, u32[]{:S(2)}) collective-permute-start(f32[64,128]{1,0:T(8,128)S(1)} %slice.9), channel_id=1, source_target_pairs={{6,132},{8,120},{28,56},{0,576},{20,5},{10,6},{30,37},{22,38},{14,... | collective-permute-start | bytes 98312 | tf_op jit(solution)/shard_map/ppermute | solution.py:235
  98.3 0.0 collective-permute-done.16
  98.4 0.0 collective-permute-done.15
  98.4 0.0 collective-permute-done.14
  98.4 0.6 add_add_fusion
  99.0 0.0 collective-permute-done.10
  99.0 6.2 %collective-permute-done.11 = f32[64,128]{1,0:T(8,128)S(1)} collective-permute-done((f32[64,128]{1,0:T(8,128)S(1)}, f32[64,128]{1,0:T(8,128)S(1)}, u32[]{:S(2)}, u32[]{:S(2)}) %collective-permute-start.11) | collective-permute-done | bytes 32800 | tf_op jit(solution)/shard_map/ppermute | solution.py:235
  105.2 0.6 fusion
  (5 shorter events, 0.1 us)
Async XLA Ops:
  0.6 39.6 %copy-start = (f32[128,512]{1,0:T(8,128)S(1)}, f32[128,512]{1,0:T(8,128)}, u32[]{:S(2)}) copy-start(f32[128,512]{1,0:T(8,128)} %refs_0_.1) | copy-start | bytes 786436
  0.6 19.7 %collective-permute-start = (f32[128,512]{1,0:T(8,128)}, f32[128,512]{1,0:T(8,128)S(1)}, u32[]{:S(2)}, u32[]{:S(2)}) collective-permute-start(f32[128,512]{1,0:T(8,128)} %refs_0_.1), channel_id=1, source_target_pairs={{64,0},{96,32},{128,64},{160,96},{192,128},{224,160},{256,192},{28... | collective-permute-start | bytes 786440 | tf_op jit(solution)/shard_map/ppermute | solution.py:201
  15.1 19.2 %collective-permute-start.1 = (f32[128,512]{1,0:T(8,128)}, f32[128,512]{1,0:T(8,128)S(1)}, u32[]{:S(2)}, u32[]{:S(2)}) collective-permute-start(f32[128,512]{1,0:T(8,128)} %refs_0_.1), channel_id=1, source_target_pairs={{128,0},{160,32},{192,64},{224,96},{256,128},{288,160},{320,192},{... | collective-permute-start | bytes 786440 | tf_op jit(solution)/shard_map/ppermute | solution.py:204
  17.0 20.1 %collective-permute-start.3 = (f32[128,512]{1,0:T(8,128)}, f32[128,512]{1,0:T(8,128)S(1)}, u32[]{:S(2)}, u32[]{:S(2)}) collective-permute-start(f32[128,512]{1,0:T(8,128)} %refs_0_.1), channel_id=1, source_target_pairs={{576,0},{608,32},{640,64},{672,96},{704,128},{736,160},{0,192},{32... | collective-permute-start | bytes 786440 | tf_op jit(solution)/shard_map/ppermute | solution.py:204
  20.4 16.8 %collective-permute-start.4 = (f32[128,512]{1,0:T(8,128)S(1)}, f32[128,512]{1,0:T(8,128)S(1)}, u32[]{:S(2)}, u32[]{:S(2)}) collective-permute-start(f32[128,512]{1,0:T(8,128)S(1)} %collective-permute-done.refs_1_.refs_0_), channel_id=1, source_target_pairs={{32,0},{0,32},{96,64},{64,96},{160,128},{128,160},{224,192},{192,2... | collective-permute-start | bytes 786440 | tf_op jit(solution)/shard_map/ppermute | solution.py:201
  23.2 17.0 %collective-permute-start.5 = (f32[128,512]{1,0:T(8,128)}, f32[128,512]{1,0:T(8,128)S(1)}, u32[]{:S(2)}, u32[]{:S(2)}) collective-permute-start(f32[128,512]{1,0:T(8,128)} %refs_0_.1), channel_id=1, source_target_pairs={{32,0},{0,32},{96,64},{64,96},{160,128},{128,160},{224,192},{192,2... | collective-permute-start | bytes 786440 | tf_op jit(solution)/shard_map/ppermute | solution.py:201
  26.7 4.8 %collective-permute-start.2 = (f32[512]{0:T(512)S(1)}, f32[512]{0:T(512)S(1)}, u32[]{:S(2)}, u32[]{:S(2)}) collective-permute-start(f32[512]{0:T(512)S(1)} %multiply_reduce_fusion), channel_id=1, source_target_pairs={{32,0},{0,32},{96,64},{64,96},{160,128},{128,160},{224,192},{192,2... | collective-permute-start | bytes 6152 | tf_op jit(solution)/shard_map/ppermute | solution.py:201
  34.3 17.4 %collective-permute-start.7 = (f32[128,512]{1,0:T(8,128)S(1)}, f32[128,512]{1,0:T(8,128)S(1)}, u32[]{:S(2)}, u32[]{:S(2)}) collective-permute-start(f32[128,512]{1,0:T(8,128)S(1)} %collective-permute-done.1.refs_2_.refs_1_), channel_id=1, source_target_pairs={{64,0},{96,32},{128,64},{160,96},{192,128},{224,160},{256,192},{28... | collective-permute-start | bytes 786440 | tf_op jit(solution)/shard_map/ppermute | solution.py:204
  37.2 14.6 %collective-permute-start.8 = (f32[128,512]{1,0:T(8,128)S(1)}, f32[128,512]{1,0:T(8,128)S(1)}, u32[]{:S(2)}, u32[]{:S(2)}) collective-permute-start(f32[128,512]{1,0:T(8,128)S(1)} %collective-permute-done.3.refs_3_.refs_2_), channel_id=1, source_target_pairs={{32,0},{0,32},{96,64},{64,96},{160,128},{128,160},{224,192},{192,2... | collective-permute-start | bytes 786440 | tf_op jit(solution)/shard_map/ppermute | solution.py:204
  43.1 13.7 %collective-permute-start.6 = (f32[9,128,128]{2,1,0:T(8,128)S(1)}, f32[9,128,128]{2,1,0:T(8,128)S(1)}, u32[]{:S(2)}, u32[]{:S(2)}) collective-permute-start(f32[9,128,128]{2,1,0:T(8,128)S(1)} %get-tuple-element.16), channel_id=1, source_target_pairs={{0,1},{1,0},{2,3},{3,2},{4,5},{5,4},{6,7},{7,6},{8,9},{9,8},{10,11... | collective-permute-start | bytes 1769480 | tf_op jit(solution)/shard_map/ppermute | solution.py:218
  53.4 3.3 %collective-permute-start.9 = (f32[3,128,128]{2,1,0:T(8,128)S(1)}, f32[3,128,128]{2,1,0:T(8,128)S(1)}, u32[]{:S(2)}, u32[]{:S(2)}) collective-permute-start(f32[3,128,128]{2,1,0:T(8,128)S(1)} %get-tuple-element.18), channel_id=1, source_target_pairs={{0,1},{1,0},{2,3},{3,2},{4,5},{5,4},{6,7},{7,6},{8,9},{9,8},{10,11... | collective-permute-start | bytes 589832 | tf_op jit(solution)/shard_map/ppermute | solution.py:220
  58.2 29.2 %all-to-all-start = ((f32[16,96,128]{2,1,0:T(8,128)}), f32[16,96,128]{2,1,0:T(8,128)S(1)}, u32[]{:S(2)}, u32[]{:S(2)}) async-start(f32[16,96,128]{2,1,0:T(8,128)} %bitcast.1), calls=%async_computation | async-start | bytes 1572864 | tf_op jit(solution)/shard_map/all_to_all | solution.py:224
  67.5 9.2 %collective-permute-start.13 = (f32[512]{0:T(512)S(1)}, f32[512]{0:T(512)S(1)}, u32[]{:S(2)}, u32[]{:S(2)}) collective-permute-start(f32[512]{0:T(512)S(1)} %add.38), channel_id=1, source_target_pairs={{256,0},{288,32},{320,64},{352,96},{384,128},{416,160},{448,192},{... | collective-permute-start | bytes 6152 | tf_op jit(solution)/shard_map/ppermute | solution.py:201
  69.9 8.5 %collective-permute-start.12 = (f32[512]{0:T(512)S(1)}, f32[512]{0:T(512)S(1)}, u32[]{:S(2)}, u32[]{:S(2)}) collective-permute-start(f32[512]{0:T(512)S(1)} %add.38), channel_id=1, source_target_pairs={{512,0},{544,32},{576,64},{608,96},{640,128},{672,160},{704,192},{... | collective-permute-start | bytes 6152 | tf_op jit(solution)/shard_map/ppermute | solution.py:201
  78.5 19.9 %collective-permute-start.16 = (f32[512]{0:T(512)S(1)}, f32[512]{0:T(512)S(1)}, u32[]{:S(2)}, u32[]{:S(2)}) collective-permute-start(f32[512]{0:T(512)S(1)} %select_add_fusion), channel_id=1, source_target_pairs={{704,0},{736,32},{0,64},{32,96},{64,128},{96,160},{128,192},{160,2... | collective-permute-start | bytes 6152 | tf_op jit(solution)/shard_map/ppermute | solution.py:201
  80.4 18.0 %collective-permute-start.15 = (f32[512]{0:T(512)S(1)}, f32[512]{0:T(512)S(1)}, u32[]{:S(2)}, u32[]{:S(2)}) collective-permute-start(f32[512]{0:T(512)S(1)} %select_add_fusion), channel_id=1, source_target_pairs={{64,0},{96,32},{128,64},{160,96},{192,128},{224,160},{256,192},{28... | collective-permute-start | bytes 6152 | tf_op jit(solution)/shard_map/ppermute | solution.py:201
  85.0 13.4 %collective-permute-start.14 = (f32[512]{0:T(512)S(1)}, f32[512]{0:T(512)S(1)}, u32[]{:S(2)}, u32[]{:S(2)}) collective-permute-start(f32[512]{0:T(512)S(1)} %select_add_fusion), channel_id=1, source_target_pairs={{128,0},{160,32},{192,64},{224,96},{256,128},{288,160},{320,192},{... | collective-permute-start | bytes 6152 | tf_op jit(solution)/shard_map/ppermute | solution.py:201
  87.5 11.5 %collective-permute-start.10 = (f32[32,128]{1,0:T(8,128)S(1)}, f32[32,128]{1,0:T(8,128)S(1)}, u32[]{:S(2)}, u32[]{:S(2)}) collective-permute-start(f32[32,128]{1,0:T(8,128)S(1)} %slice.8), channel_id=1, source_target_pairs={{8,132},{20,133},{24,120},{26,121},{28,56},{10,57},{0,576},{14,577... | collective-permute-start | bytes 49160 | tf_op jit(solution)/shard_map/ppermute | solution.py:236
  95.4 9.8 %collective-permute-start.11 = (f32[64,128]{1,0:T(8,128)S(1)}, f32[64,128]{1,0:T(8,128)S(1)}, u32[]{:S(2)}, u32[]{:S(2)}) collective-permute-start(f32[64,128]{1,0:T(8,128)S(1)} %slice.9), channel_id=1, source_target_pairs={{6,132},{8,120},{28,56},{0,576},{20,5},{10,6},{30,37},{22,38},{14,... | collective-permute-start | bytes 98312 | tf_op jit(solution)/shard_map/ppermute | solution.py:235

commit v11 on v10

--- a/solution.py
+++ b/solution.py
@@ -209,7 +209,7 @@
         pair0 = walk_get(jacobian, 0, 1)
         pair1 = walk_get(up1, 0, 1)
         term = jnp.sum(coeffs[:, None] * jacobian, axis=0)
-        far_a, term = tie((far_a, term + walk_get(term, 0, 1)))
+        far_a, pair0, term, table = tie((far_a, pair0, term + walk_get(term, 0, 1), table))
         far_b, pair1 = tie((far_b, pair1))
         late_a = mixed_get(far_a, (1, 0), (0, 1))
         late_b = mixed_get(far_b, (0, 1), (1, 0))

time: 107 us -> 105 us (0.981)
  starting transfers between devices: 80.1 us -> 78.9 us
    ppermute x1, starting transfers between devices: 8.69 us -> 3.55 us  [shards(): early = (keep, lax.ppermute(send, 'par', core_swap))]
    ppermute x4, waiting for transfers between devices: 2.84 us -> 6.9 us  [mixed_get(): return lax.ppermute(value, ('walk', 'par'), mixed_perm(moves))]
    ppermute x1, starting transfers between devices: 2.93 us -> 5.67 us  [shards(): pair = lax.ppermute(mine[:2 * SLICE], ('walk', 'par'), pair_perm)]
    ppermute x1, waiting for transfers between devices: 6.22 us -> 3.48 us  [shards(): pair = lax.ppermute(mine[:2 * SLICE], ('walk', 'par'), pair_perm)]
    ppermute x9, waiting for transfers between devices: 4.82 us -> 3.75 us  [walk_get(): return lax.ppermute(value, 'walk', walk_perm(dz, flip))]
  transfers between devices with their start and end apart: 18 -> 18, of which waited for: 7 -> 5; matrix products, arithmetic and copies ran while one was open for 2% -> 2% of each run, Pallas kernels for 4% -> 4%
where the time goes in v11:
time: 105 us; the launch traced here: 104 us
  starting transfers between devices  78.9 us (75%)
  waiting for transfers between devices  15.2 us (14%)
  Pallas kernels  5.98 us (6%)
  other arithmetic  2.32 us (2%)
    ppermute x9, starting transfers between devices, walk_get(): return lax.ppermute(value, 'walk', walk_perm(dz, flip))  41.2 us
    all_to_all x1, starting transfers between devices, shards(): lax.all_to_all(mine, 'par', 0, 0, axis_index_groups=groups, tiled=True)  9.3 us
    ppermute x4, starting transfers between devices, mixed_get(): return lax.ppermute(value, ('walk', 'par'), mixed_perm(moves))  8.46 us
    ppermute x1, starting transfers between devices, shards(): single = lax.ppermute(mine[2 * SLICE:], ('walk', 'par'), single_perm)  8.14 us
    ppermute x4, waiting for transfers between devices, mixed_get(): return lax.ppermute(value, ('walk', 'par'), mixed_perm(moves))  6.9 us
    ppermute x1, starting transfers between devices, shards(): pair = lax.ppermute(mine[:2 * SLICE], ('walk', 'par'), pair_perm)  5.67 us
    pallas_call x2, Pallas kernels, products(): pl.pallas_call(functools.partial(product_kernel, base, count), out_shape=...  4.46 us
    ppermute x9, waiting for transfers between devices, walk_get(): return lax.ppermute(value, 'walk', walk_perm(dz, flip))  3.75 us
  transfers between devices with their start and end apart: 18, of which 5 were waited for; matrix products, arithmetic and copies ran while one was open for 2% of the time, Pallas kernels for 4%

profile of v11, /device:TPU:21, one launch (start us, length us, event | category | flops | bytes accessed | tf_op | source)
XLA Modules:
  0.0 104.0 jit_solution(10385830582753188334)
XLA Ops:
  0.6 0.0 copy-start
  0.6 14.4 %collective-permute-start.3 = (f32[128,512]{1,0:T(8,128)}, f32[128,512]{1,0:T(8,128)S(1)}, u32[]{:S(2)}, u32[]{:S(2)}) collective-permute-start(f32[128,512]{1,0:T(8,128)} %refs_0_.1), channel_id=1, source_target_pairs={{64,0},{96,32},{128,64},{160,96},{192,128},{224,160},{256,192},{28... | collective-permute-start | bytes 786440 | tf_op jit(solution)/shard_map/ppermute | solution.py:201
  15.1 2.8 %collective-permute-start.1 = (f32[128,512]{1,0:T(8,128)}, f32[128,512]{1,0:T(8,128)S(1)}, u32[]{:S(2)}, u32[]{:S(2)}) collective-permute-start(f32[128,512]{1,0:T(8,128)} %refs_0_.1), channel_id=1, source_target_pairs={{32,0},{0,32},{96,64},{64,96},{160,128},{128,160},{224,192},{192,2... | collective-permute-start | bytes 786440 | tf_op jit(solution)/shard_map/ppermute | solution.py:201
  17.9 1.9 %collective-permute-start = (f32[128,512]{1,0:T(8,128)}, f32[128,512]{1,0:T(8,128)S(1)}, u32[]{:S(2)}, u32[]{:S(2)}) collective-permute-start(f32[128,512]{1,0:T(8,128)} %refs_0_.1), channel_id=1, source_target_pairs={{128,0},{160,32},{192,64},{224,96},{256,128},{288,160},{320,192},{... | collective-permute-start | bytes 786440 | tf_op jit(solution)/shard_map/ppermute | solution.py:204
  19.8 2.2 %collective-permute-start.4 = (f32[128,512]{1,0:T(8,128)}, f32[128,512]{1,0:T(8,128)S(1)}, u32[]{:S(2)}, u32[]{:S(2)}) collective-permute-start(f32[128,512]{1,0:T(8,128)} %refs_0_.1), channel_id=1, source_target_pairs={{576,0},{608,32},{640,64},{672,96},{704,128},{736,160},{0,192},{32... | collective-permute-start | bytes 786440 | tf_op jit(solution)/shard_map/ppermute | solution.py:204
  22.0 0.0 collective-permute-done.3.refs_1_.refs_0_
  22.0 2.5 %collective-permute-start.5 = (f32[128,512]{1,0:T(8,128)S(1)}, f32[128,512]{1,0:T(8,128)S(1)}, u32[]{:S(2)}, u32[]{:S(2)}) collective-permute-start(f32[128,512]{1,0:T(8,128)S(1)} %collective-permute-done.3.refs_1_.refs_0_), channel_id=1, source_target_pairs={{32,0},{0,32},{96,64},{64,96},{160,128},{128,160},{224,192},{192,2... | collective-permute-start | bytes 786440 | tf_op jit(solution)/shard_map/ppermute | solution.py:201
  24.5 1.1 %multiply_reduce_fusion = f32[512]{0:T(512)S(1)} fusion(f32[128,512]{1,0:T(8,128)} %refs_0_.1, f32[128]{0:T(128)} %param.4), kind=kLoop, calls=%fused_computation | loop fusion | flops 130560 | bytes 264704 | tf_op jit(solution)/shard_map/reduce_sum | solution.py:211
  25.5 2.8 %collective-permute-start.2 = (f32[512]{0:T(512)S(1)}, f32[512]{0:T(512)S(1)}, u32[]{:S(2)}, u32[]{:S(2)}) collective-permute-start(f32[512]{0:T(512)S(1)} %multiply_reduce_fusion), channel_id=1, source_target_pairs={{32,0},{0,32},{96,64},{64,96},{160,128},{128,160},{224,192},{192,2... | collective-permute-start | bytes 6152 | tf_op jit(solution)/shard_map/ppermute | solution.py:201
  28.4 0.7 dynamic-slice_bitcast_fusion.table
  29.1 1.1 %collective-permute-done.2 = f32[512]{0:T(512)S(1)} collective-permute-done((f32[512]{0:T(512)S(1)}, f32[512]{0:T(512)S(1)}, u32[]{:S(2)}, u32[]{:S(2)}) %collective-permute-start.2) | collective-permute-done | bytes 2080 | tf_op jit(solution)/shard_map/ppermute | solution.py:201
  30.3 0.0 collective-permute-done.1.refs_4_
  30.3 6.9 %collective-permute-done.refs_2_.refs_1_ = f32[128,512]{1,0:T(8,128)S(1)} collective-permute-done((f32[128,512]{1,0:T(8,128)}, f32[128,512]{1,0:T(8,128)S(1)}, u32[]{:S(2)}, u32[]{:S(2)}) %collective-permute-start) | collective-permute-done | bytes 262176 | tf_op jit(solution)/shard_map/ppermute | solution.py:204
  37.2 2.4 %collective-permute-start.7 = (f32[128,512]{1,0:T(8,128)S(1)}, f32[128,512]{1,0:T(8,128)S(1)}, u32[]{:S(2)}, u32[]{:S(2)}) collective-permute-start(f32[128,512]{1,0:T(8,128)S(1)} %collective-permute-done.refs_2_.refs_1_), channel_id=1, source_target_pairs={{64,0},{96,32},{128,64},{160,96},{192,128},{224,160},{256,192},{28... | collective-permute-start | bytes 786440 | tf_op jit(solution)/shard_map/ppermute | solution.py:204
  39.6 0.0 collective-permute-done.4.refs_3_.refs_2_
  39.6 0.0 collective-permute-done.5.refs_5_
  39.6 1.9 %collective-permute-start.8 = (f32[128,512]{1,0:T(8,128)S(1)}, f32[128,512]{1,0:T(8,128)S(1)}, u32[]{:S(2)}, u32[]{:S(2)}) collective-permute-start(f32[128,512]{1,0:T(8,128)S(1)} %collective-permute-done.4.refs_3_.refs_2_), channel_id=1, source_target_pairs={{32,0},{0,32},{96,64},{64,96},{160,128},{128,160},{224,192},{192,2... | collective-permute-start | bytes 786440 | tf_op jit(solution)/shard_map/ppermute | solution.py:204
  41.6 0.0 copy-done
  41.6 2.9 %shard_map.50 = (f32[9,128,128]{2,1,0:T(8,128)S(1)}, f32[9,128,128]{2,1,0:T(8,128)S(1)}) custom-call(s32[96]{0:T(128)S(1)} %dynamic-slice_bitcast_fusion.table, f32[128,512]{1,0:T(8,128)S(1)} %copy-done, f32[128,512]{1,0:T(8,128)S(1)} %collective-permute-done.3.refs_1_.refs_0_, f32[128,512]{1,0:T(8,128)S(1)} %collective-permute-done.refs_2_.refs_1_, ...), custom_call_target="tpu_custom_call" | custom-call | flops 268435456 | bytes 1048576 | tf_op jit(solution)/shard_map/pallas_call | solution.py:142
  44.4 3.6 %collective-permute-start.6 = (f32[9,128,128]{2,1,0:T(8,128)S(1)}, f32[9,128,128]{2,1,0:T(8,128)S(1)}, u32[]{:S(2)}, u32[]{:S(2)}) collective-permute-start(f32[9,128,128]{2,1,0:T(8,128)S(1)} %get-tuple-element.20), channel_id=1, source_target_pairs={{0,1},{1,0},{2,3},{3,2},{4,5},{5,4},{6,7},{7,6},{8,9},{9,8},{10,11... | collective-permute-start | bytes 1769480 | tf_op jit(solution)/shard_map/ppermute | solution.py:218
  48.0 0.0 collective-permute-done.7.refs_3_
  48.0 0.0 collective-permute-done.8.refs_4_
  48.0 1.6 %shard_map.51 = (f32[3,128,128]{2,1,0:T(8,128)S(1)}, f32[3,128,128]{2,1,0:T(8,128)S(1)}) custom-call(s32[96]{0:T(128)S(1)} %dynamic-slice_bitcast_fusion.table, f32[128,512]{1,0:T(8,128)S(1)} %collective-permute-done.3.refs_1_.refs_0_, f32[128,512]{1,0:T(8,128)S(1)} %collective-permute-done.refs_2_.refs_1_, ...), custom_call_target="tpu_custom_call" | custom-call | flops 34359738368 | bytes 1048576 | tf_op jit(solution)/shard_map/pallas_call | solution.py:142
  49.6 2.6 %collective-permute-start.9 = (f32[3,128,128]{2,1,0:T(8,128)S(1)}, f32[3,128,128]{2,1,0:T(8,128)S(1)}, u32[]{:S(2)}, u32[]{:S(2)}) collective-permute-start(f32[3,128,128]{2,1,0:T(8,128)S(1)} %get-tuple-element.22), channel_id=1, source_target_pairs={{0,1},{1,0},{2,3},{3,2},{4,5},{5,4},{6,7},{7,6},{8,9},{9,8},{10,11... | collective-permute-start | bytes 589832 | tf_op jit(solution)/shard_map/ppermute | solution.py:220
  52.2 1.0 %collective-permute-done.9.refs_3_ = f32[3,128,128]{2,1,0:T(8,128)S(1)} collective-permute-done((f32[3,128,128]{2,1,0:T(8,128)S(1)}, f32[3,128,128]{2,1,0:T(8,128)S(1)}, u32[]{:S(2)}, u32[]{:S(2)}) %collective-permute-start.9) | collective-permute-done | bytes 196640 | tf_op jit(solution)/shard_map/ppermute | solution.py:220
  53.3 0.0 collective-permute-done.6.refs_1_
  53.3 1.5 %shard_map.52 = f32[48,32,128]{2,1,0:T(8,128)} custom-call(s32[96]{0:T(128)S(1)} %dynamic-slice_bitcast_fusion.table, f32[9,128,128]{2,1,0:T(8,128)S(1)} %get-tuple-element.19.refs_0_, f32[9,128,128]{2,1,0:T(8,128)S(1)} %collective-permute-done.6.refs_1_, f32[3,128,128]{2,1,0:T(8,128)S(1)} %get-tuple-element.21.refs_2_, ...), custom_call_target="tpu_custom_call" | custom-call | tf_op jit(solution)/shard_map/pallas_call | solution.py:165
  54.8 9.3 %all-to-all-start = ((f32[16,96,128]{2,1,0:T(8,128)}), f32[16,96,128]{2,1,0:T(8,128)S(1)}, u32[]{:S(2)}, u32[]{:S(2)}) async-start(f32[16,96,128]{2,1,0:T(8,128)} %bitcast.1), calls=%async_computation | async-start | bytes 1572864 | tf_op jit(solution)/shard_map/all_to_all | solution.py:224
  64.1 3.3 %collective-permute-start.13 = (f32[512]{0:T(512)S(1)}, f32[512]{0:T(512)S(1)}, u32[]{:S(2)}, u32[]{:S(2)}) collective-permute-start(f32[512]{0:T(512)S(1)} %add.35), channel_id=1, source_target_pairs={{256,0},{288,32},{320,64},{352,96},{384,128},{416,160},{448,192},{... | collective-permute-start | bytes 6152 | tf_op jit(solution)/shard_map/ppermute | solution.py:201
  67.4 5.9 %collective-permute-start.12 = (f32[512]{0:T(512)S(1)}, f32[512]{0:T(512)S(1)}, u32[]{:S(2)}, u32[]{:S(2)}) collective-permute-start(f32[512]{0:T(512)S(1)} %add.35), channel_id=1, source_target_pairs={{512,0},{544,32},{576,64},{608,96},{640,128},{672,160},{704,192},{... | collective-permute-start | bytes 6152 | tf_op jit(solution)/shard_map/ppermute | solution.py:201
  73.3 0.0 collective-permute-done.13
  73.3 2.6 %collective-permute-done.12 = f32[512]{0:T(512)S(1)} collective-permute-done((f32[512]{0:T(512)S(1)}, f32[512]{0:T(512)S(1)}, u32[]{:S(2)}, u32[]{:S(2)}) %collective-permute-start.12) | collective-permute-done | bytes 2080 | tf_op jit(solution)/shard_map/ppermute | solution.py:201
  75.9 3.2 %collective-permute-start.16 = (f32[512]{0:T(512)S(1)}, f32[512]{0:T(512)S(1)}, u32[]{:S(2)}, u32[]{:S(2)}) collective-permute-start(f32[512]{0:T(512)S(1)} %select_add_fusion), channel_id=1, source_target_pairs={{704,0},{736,32},{0,64},{32,96},{64,128},{96,160},{128,192},{160,2... | collective-permute-start | bytes 6152 | tf_op jit(solution)/shard_map/ppermute | solution.py:201
  79.1 3.3 %collective-permute-start.15 = (f32[512]{0:T(512)S(1)}, f32[512]{0:T(512)S(1)}, u32[]{:S(2)}, u32[]{:S(2)}) collective-permute-start(f32[512]{0:T(512)S(1)} %select_add_fusion), channel_id=1, source_target_pairs={{64,0},{96,32},{128,64},{160,96},{192,128},{224,160},{256,192},{28... | collective-permute-start | bytes 6152 | tf_op jit(solution)/shard_map/ppermute | solution.py:201
  82.4 3.0 %collective-permute-start.14 = (f32[512]{0:T(512)S(1)}, f32[512]{0:T(512)S(1)}, u32[]{:S(2)}, u32[]{:S(2)}) collective-permute-start(f32[512]{0:T(512)S(1)} %select_add_fusion), channel_id=1, source_target_pairs={{128,0},{160,32},{192,64},{224,96},{256,128},{288,160},{320,192},{... | collective-permute-start | bytes 6152 | tf_op jit(solution)/shard_map/ppermute | solution.py:201
  85.4 0.0 all-to-all-done
  85.5 8.1 %collective-permute-start.10 = (f32[32,128]{1,0:T(8,128)S(1)}, f32[32,128]{1,0:T(8,128)S(1)}, u32[]{:S(2)}, u32[]{:S(2)}) collective-permute-start(f32[32,128]{1,0:T(8,128)S(1)} %slice.8), channel_id=1, source_target_pairs={{8,132},{20,133},{24,120},{26,121},{28,56},{10,57},{0,576},{14,577... | collective-permute-start | bytes 49160 | tf_op jit(solution)/shard_map/ppermute | solution.py:236
  93.6 5.7 %collective-permute-start.11 = (f32[64,128]{1,0:T(8,128)S(1)}, f32[64,128]{1,0:T(8,128)S(1)}, u32[]{:S(2)}, u32[]{:S(2)}) collective-permute-start(f32[64,128]{1,0:T(8,128)S(1)} %slice.9), channel_id=1, source_target_pairs={{6,132},{8,120},{28,56},{0,576},{20,5},{10,6},{30,37},{22,38},{14,... | collective-permute-start | bytes 98312 | tf_op jit(solution)/shard_map/ppermute | solution.py:235
  99.3 0.0 collective-permute-done.16
  99.3 0.0 collective-permute-done.15
  99.3 0.0 collective-permute-done.14
  99.3 0.6 add_add_fusion
  99.9 0.0 collective-permute-done.10
  99.9 3.5 %collective-permute-done.11 = f32[64,128]{1,0:T(8,128)S(1)} collective-permute-done((f32[64,128]{1,0:T(8,128)S(1)}, f32[64,128]{1,0:T(8,128)S(1)}, u32[]{:S(2)}, u32[]{:S(2)}) %collective-permute-start.11) | collective-permute-done | bytes 32800 | tf_op jit(solution)/shard_map/ppermute | solution.py:235
  103.4 0.6 fusion
  (5 shorter events, 0.1 us)
Async XLA Ops:
  0.6 40.9 %copy-start = (f32[128,512]{1,0:T(8,128)S(1)}, f32[128,512]{1,0:T(8,128)}, u32[]{:S(2)}) copy-start(f32[128,512]{1,0:T(8,128)} %refs_0_.1) | copy-start | bytes 786436
  0.6 21.4 %collective-permute-start.3 = (f32[128,512]{1,0:T(8,128)}, f32[128,512]{1,0:T(8,128)S(1)}, u32[]{:S(2)}, u32[]{:S(2)}) collective-permute-start(f32[128,512]{1,0:T(8,128)} %refs_0_.1), channel_id=1, source_target_pairs={{64,0},{96,32},{128,64},{160,96},{192,128},{224,160},{256,192},{28... | collective-permute-start | bytes 786440 | tf_op jit(solution)/shard_map/ppermute | solution.py:201
  15.1 15.2 %collective-permute-start.1 = (f32[128,512]{1,0:T(8,128)}, f32[128,512]{1,0:T(8,128)S(1)}, u32[]{:S(2)}, u32[]{:S(2)}) collective-permute-start(f32[128,512]{1,0:T(8,128)} %refs_0_.1), channel_id=1, source_target_pairs={{32,0},{0,32},{96,64},{64,96},{160,128},{128,160},{224,192},{192,2... | collective-permute-start | bytes 786440 | tf_op jit(solution)/shard_map/ppermute | solution.py:201
  17.9 19.2 %collective-permute-start = (f32[128,512]{1,0:T(8,128)}, f32[128,512]{1,0:T(8,128)S(1)}, u32[]{:S(2)}, u32[]{:S(2)}) collective-permute-start(f32[128,512]{1,0:T(8,128)} %refs_0_.1), channel_id=1, source_target_pairs={{128,0},{160,32},{192,64},{224,96},{256,128},{288,160},{320,192},{... | collective-permute-start | bytes 786440 | tf_op jit(solution)/shard_map/ppermute | solution.py:204
  19.8 19.8 %collective-permute-start.4 = (f32[128,512]{1,0:T(8,128)}, f32[128,512]{1,0:T(8,128)S(1)}, u32[]{:S(2)}, u32[]{:S(2)}) collective-permute-start(f32[128,512]{1,0:T(8,128)} %refs_0_.1), channel_id=1, source_target_pairs={{576,0},{608,32},{640,64},{672,96},{704,128},{736,160},{0,192},{32... | collective-permute-start | bytes 786440 | tf_op jit(solution)/shard_map/ppermute | solution.py:204
  22.0 17.6 %collective-permute-start.5 = (f32[128,512]{1,0:T(8,128)S(1)}, f32[128,512]{1,0:T(8,128)S(1)}, u32[]{:S(2)}, u32[]{:S(2)}) collective-permute-start(f32[128,512]{1,0:T(8,128)S(1)} %collective-permute-done.3.refs_1_.refs_0_), channel_id=1, source_target_pairs={{32,0},{0,32},{96,64},{64,96},{160,128},{128,160},{224,192},{192,2... | collective-permute-start | bytes 786440 | tf_op jit(solution)/shard_map/ppermute | solution.py:201
  25.5 4.7 %collective-permute-start.2 = (f32[512]{0:T(512)S(1)}, f32[512]{0:T(512)S(1)}, u32[]{:S(2)}, u32[]{:S(2)}) collective-permute-start(f32[512]{0:T(512)S(1)} %multiply_reduce_fusion), channel_id=1, source_target_pairs={{32,0},{0,32},{96,64},{64,96},{160,128},{128,160},{224,192},{192,2... | collective-permute-start | bytes 6152 | tf_op jit(solution)/shard_map/ppermute | solution.py:201
  37.2 10.9 %collective-permute-start.7 = (f32[128,512]{1,0:T(8,128)S(1)}, f32[128,512]{1,0:T(8,128)S(1)}, u32[]{:S(2)}, u32[]{:S(2)}) collective-permute-start(f32[128,512]{1,0:T(8,128)S(1)} %collective-permute-done.refs_2_.refs_1_), channel_id=1, source_target_pairs={{64,0},{96,32},{128,64},{160,96},{192,128},{224,160},{256,192},{28... | collective-permute-start | bytes 786440 | tf_op jit(solution)/shard_map/ppermute | solution.py:204
  39.6 8.4 %collective-permute-start.8 = (f32[128,512]{1,0:T(8,128)S(1)}, f32[128,512]{1,0:T(8,128)S(1)}, u32[]{:S(2)}, u32[]{:S(2)}) collective-permute-start(f32[128,512]{1,0:T(8,128)S(1)} %collective-permute-done.4.refs_3_.refs_2_), channel_id=1, source_target_pairs={{32,0},{0,32},{96,64},{64,96},{160,128},{128,160},{224,192},{192,2... | collective-permute-start | bytes 786440 | tf_op jit(solution)/shard_map/ppermute | solution.py:204
  44.4 8.8 %collective-permute-start.6 = (f32[9,128,128]{2,1,0:T(8,128)S(1)}, f32[9,128,128]{2,1,0:T(8,128)S(1)}, u32[]{:S(2)}, u32[]{:S(2)}) collective-permute-start(f32[9,128,128]{2,1,0:T(8,128)S(1)} %get-tuple-element.20), channel_id=1, source_target_pairs={{0,1},{1,0},{2,3},{3,2},{4,5},{5,4},{6,7},{7,6},{8,9},{9,8},{10,11... | collective-permute-start | bytes 1769480 | tf_op jit(solution)/shard_map/ppermute | solution.py:218
  49.6 3.7 %collective-permute-start.9 = (f32[3,128,128]{2,1,0:T(8,128)S(1)}, f32[3,128,128]{2,1,0:T(8,128)S(1)}, u32[]{:S(2)}, u32[]{:S(2)}) collective-permute-start(f32[3,128,128]{2,1,0:T(8,128)S(1)} %get-tuple-element.22), channel_id=1, source_target_pairs={{0,1},{1,0},{2,3},{3,2},{4,5},{5,4},{6,7},{7,6},{8,9},{9,8},{10,11... | collective-permute-start | bytes 589832 | tf_op jit(solution)/shard_map/ppermute | solution.py:220
  54.8 30.6 %all-to-all-start = ((f32[16,96,128]{2,1,0:T(8,128)}), f32[16,96,128]{2,1,0:T(8,128)S(1)}, u32[]{:S(2)}, u32[]{:S(2)}) async-start(f32[16,96,128]{2,1,0:T(8,128)} %bitcast.1), calls=%async_computation | async-start | bytes 1572864 | tf_op jit(solution)/shard_map/all_to_all | solution.py:224
  64.1 9.2 %collective-permute-start.13 = (f32[512]{0:T(512)S(1)}, f32[512]{0:T(512)S(1)}, u32[]{:S(2)}, u32[]{:S(2)}) collective-permute-start(f32[512]{0:T(512)S(1)} %add.35), channel_id=1, source_target_pairs={{256,0},{288,32},{320,64},{352,96},{384,128},{416,160},{448,192},{... | collective-permute-start | bytes 6152 | tf_op jit(solution)/shard_map/ppermute | solution.py:201
  67.4 8.5 %collective-permute-start.12 = (f32[512]{0:T(512)S(1)}, f32[512]{0:T(512)S(1)}, u32[]{:S(2)}, u32[]{:S(2)}) collective-permute-start(f32[512]{0:T(512)S(1)} %add.35), channel_id=1, source_target_pairs={{512,0},{544,32},{576,64},{608,96},{640,128},{672,160},{704,192},{... | collective-permute-start | bytes 6152 | tf_op jit(solution)/shard_map/ppermute | solution.py:201
  75.9 23.4 %collective-permute-start.16 = (f32[512]{0:T(512)S(1)}, f32[512]{0:T(512)S(1)}, u32[]{:S(2)}, u32[]{:S(2)}) collective-permute-start(f32[512]{0:T(512)S(1)} %select_add_fusion), channel_id=1, source_target_pairs={{704,0},{736,32},{0,64},{32,96},{64,128},{96,160},{128,192},{160,2... | collective-permute-start | bytes 6152 | tf_op jit(solution)/shard_map/ppermute | solution.py:201
  79.1 20.2 %collective-permute-start.15 = (f32[512]{0:T(512)S(1)}, f32[512]{0:T(512)S(1)}, u32[]{:S(2)}, u32[]{:S(2)}) collective-permute-start(f32[512]{0:T(512)S(1)} %select_add_fusion), channel_id=1, source_target_pairs={{64,0},{96,32},{128,64},{160,96},{192,128},{224,160},{256,192},{28... | collective-permute-start | bytes 6152 | tf_op jit(solution)/shard_map/ppermute | solution.py:201
  82.4 16.9 %collective-permute-start.14 = (f32[512]{0:T(512)S(1)}, f32[512]{0:T(512)S(1)}, u32[]{:S(2)}, u32[]{:S(2)}) collective-permute-start(f32[512]{0:T(512)S(1)} %select_add_fusion), channel_id=1, source_target_pairs={{128,0},{160,32},{192,64},{224,96},{256,128},{288,160},{320,192},{... | collective-permute-start | bytes 6152 | tf_op jit(solution)/shard_map/ppermute | solution.py:201
  85.5 14.4 %collective-permute-start.10 = (f32[32,128]{1,0:T(8,128)S(1)}, f32[32,128]{1,0:T(8,128)S(1)}, u32[]{:S(2)}, u32[]{:S(2)}) collective-permute-start(f32[32,128]{1,0:T(8,128)S(1)} %slice.8), channel_id=1, source_target_pairs={{8,132},{20,133},{24,120},{26,121},{28,56},{10,57},{0,576},{14,577... | collective-permute-start | bytes 49160 | tf_op jit(solution)/shard_map/ppermute | solution.py:236
  93.6 9.8 %collective-permute-start.11 = (f32[64,128]{1,0:T(8,128)S(1)}, f32[64,128]{1,0:T(8,128)S(1)}, u32[]{:S(2)}, u32[]{:S(2)}) collective-permute-start(f32[64,128]{1,0:T(8,128)S(1)} %slice.9), channel_id=1, source_target_pairs={{6,132},{8,120},{28,56},{0,576},{20,5},{10,6},{30,37},{22,38},{14,... | collective-permute-start | bytes 98312 | tf_op jit(solution)/shard_map/ppermute | solution.py:235

commit v12 on v11

--- a/solution.py
+++ b/solution.py
@@ -229,11 +229,12 @@
         second = jnp.where(place == 0, after, jnp.where(place == 1, term, before))
         third = jnp.where(place == 0, before, jnp.where(place == 1, after, term))
         term = (first + second) + third
-        update = (term + walk_get(term, 2)) + (walk_get(term, 1) + walk_get(term, -1))
-
-        mine = jnp.sum(mine, axis=0)
+        term = term + walk_get(term, 2)
+
+        mine, term = tie((jnp.sum(mine, axis=0), term))
         pair = lax.ppermute(mine[:2 * SLICE], ("walk", "par"), pair_perm)
         single = lax.ppermute(mine[2 * SLICE:], ("walk", "par"), single_perm)
+        update = term + walk_get(term, 1)
         gram = jnp.where(
             par % 4 == 1,
             jnp.concatenate((single, pair), axis=0),

time: 105 us -> 107 us (1.019)
  the two profiles are of different devices: /device:TPU:21 before, /device:TPU:56 now
where the time goes in v12:
time: 107 us
  starting transfers between devices  81.7 us (76%)
  waiting for transfers between devices  15.1 us (14%)
  Pallas kernels  5.98 us (6%)
  other arithmetic  2.32 us (2%)
    ppermute x8, starting transfers between devices, walk_get(): return lax.ppermute(value, 'walk', walk_perm(dz, flip))  39.8 us
    ppermute x4, starting transfers between devices, mixed_get(): return lax.ppermute(value, ('walk', 'par'), mixed_perm(moves))  14.6 us
    ppermute x1, starting transfers between devices, shards(): single = lax.ppermute(mine[2 * SLICE:], ('walk', 'par'), single_perm)  12.6 us
    ppermute x8, waiting for transfers between devices, walk_get(): return lax.ppermute(value, 'walk', walk_perm(dz, flip))  11.3 us
    all_to_all x1, starting transfers between devices, shards(): lax.all_to_all(mine, 'par', 0, 0, axis_index_groups=groups, tiled=True)  9.05 us
    pallas_call x2, Pallas kernels, products(): pl.pallas_call(functools.partial(product_kernel, base, count), out_shape=...  4.46 us
  transfers between devices with their start and end apart: 17, of which 7 were waited for; matrix products, arithmetic and copies ran while one was open for 2% of the time, Pallas kernels for 4%

profile of v12, /device:TPU:56, one launch (start us, length us, event | category | flops | bytes accessed | tf_op | source)
XLA Modules:
  0.0 106.8 jit_solution(4051721314072748676)
XLA Ops:
  0.6 0.0 copy-start
  0.6 14.7 %collective-permute-start.3 = (f32[128,512]{1,0:T(8,128)}, f32[128,512]{1,0:T(8,128)S(1)}, u32[]{:S(2)}, u32[]{:S(2)}) collective-permute-start(f32[128,512]{1,0:T(8,128)} %refs_0_.1), channel_id=1, source_target_pairs={{64,0},{96,32},{128,64},{160,96},{192,128},{224,160},{256,192},{28... | collective-permute-start | bytes 786440 | tf_op jit(solution)/shard_map/ppermute | solution.py:201
  15.4 3.4 %collective-permute-start.1 = (f32[128,512]{1,0:T(8,128)}, f32[128,512]{1,0:T(8,128)S(1)}, u32[]{:S(2)}, u32[]{:S(2)}) collective-permute-start(f32[128,512]{1,0:T(8,128)} %refs_0_.1), channel_id=1, source_target_pairs={{32,0},{0,32},{96,64},{64,96},{160,128},{128,160},{224,192},{192,2... | collective-permute-start | bytes 786440 | tf_op jit(solution)/shard_map/ppermute | solution.py:201
  18.8 2.5 %collective-permute-start = (f32[128,512]{1,0:T(8,128)}, f32[128,512]{1,0:T(8,128)S(1)}, u32[]{:S(2)}, u32[]{:S(2)}) collective-permute-start(f32[128,512]{1,0:T(8,128)} %refs_0_.1), channel_id=1, source_target_pairs={{128,0},{160,32},{192,64},{224,96},{256,128},{288,160},{320,192},{... | collective-permute-start | bytes 786440 | tf_op jit(solution)/shard_map/ppermute | solution.py:204
  21.2 1.9 %collective-permute-start.4 = (f32[128,512]{1,0:T(8,128)}, f32[128,512]{1,0:T(8,128)S(1)}, u32[]{:S(2)}, u32[]{:S(2)}) collective-permute-start(f32[128,512]{1,0:T(8,128)} %refs_0_.1), channel_id=1, source_target_pairs={{576,0},{608,32},{640,64},{672,96},{704,128},{736,160},{0,192},{32... | collective-permute-start | bytes 786440 | tf_op jit(solution)/shard_map/ppermute | solution.py:204
  23.2 0.0 collective-permute-done.3.refs_1_.refs_0_
  23.2 2.4 %collective-permute-start.5 = (f32[128,512]{1,0:T(8,128)S(1)}, f32[128,512]{1,0:T(8,128)S(1)}, u32[]{:S(2)}, u32[]{:S(2)}) collective-permute-start(f32[128,512]{1,0:T(8,128)S(1)} %collective-permute-done.3.refs_1_.refs_0_), channel_id=1, source_target_pairs={{32,0},{0,32},{96,64},{64,96},{160,128},{128,160},{224,192},{192,2... | collective-permute-start | bytes 786440 | tf_op jit(solution)/shard_map/ppermute | solution.py:201
  25.6 1.1 multiply_reduce_fusion
  26.7 3.4 %collective-permute-start.2 = (f32[512]{0:T(512)S(1)}, f32[512]{0:T(512)S(1)}, u32[]{:S(2)}, u32[]{:S(2)}) collective-permute-start(f32[512]{0:T(512)S(1)} %multiply_reduce_fusion), channel_id=1, source_target_pairs={{32,0},{0,32},{96,64},{64,96},{160,128},{128,160},{224,192},{192,2... | collective-permute-start | bytes 6152 | tf_op jit(solution)/shard_map/ppermute | solution.py:201
  30.1 0.7 dynamic-slice_bitcast_fusion.table
  30.8 1.5 %collective-permute-done.2 = f32[512]{0:T(512)S(1)} collective-permute-done((f32[512]{0:T(512)S(1)}, f32[512]{0:T(512)S(1)}, u32[]{:S(2)}, u32[]{:S(2)}) %collective-permute-start.2) | collective-permute-done | bytes 2080 | tf_op jit(solution)/shard_map/ppermute | solution.py:201
  32.3 0.0 collective-permute-done.1.refs_4_
  32.3 0.0 collective-permute-done.refs_2_.refs_1_
  32.3 7.7 %collective-permute-start.7 = (f32[128,512]{1,0:T(8,128)S(1)}, f32[128,512]{1,0:T(8,128)S(1)}, u32[]{:S(2)}, u32[]{:S(2)}) collective-permute-start(f32[128,512]{1,0:T(8,128)S(1)} %collective-permute-done.refs_2_.refs_1_), channel_id=1, source_target_pairs={{64,0},{96,32},{128,64},{160,96},{192,128},{224,160},{256,192},{28... | collective-permute-start | bytes 786440 | tf_op jit(solution)/shard_map/ppermute | solution.py:204
  40.0 0.0 collective-permute-done.4.refs_3_.refs_2_
  40.1 0.0 collective-permute-done.5.refs_5_
  40.1 2.5 %collective-permute-start.8 = (f32[128,512]{1,0:T(8,128)S(1)}, f32[128,512]{1,0:T(8,128)S(1)}, u32[]{:S(2)}, u32[]{:S(2)}) collective-permute-start(f32[128,512]{1,0:T(8,128)S(1)} %collective-permute-done.4.refs_3_.refs_2_), channel_id=1, source_target_pairs={{32,0},{0,32},{96,64},{64,96},{160,128},{128,160},{224,192},{192,2... | collective-permute-start | bytes 786440 | tf_op jit(solution)/shard_map/ppermute | solution.py:204
  42.5 0.0 copy-done
  42.6 2.9 %shard_map.50 = (f32[9,128,128]{2,1,0:T(8,128)S(1)}, f32[9,128,128]{2,1,0:T(8,128)S(1)}) custom-call(s32[96]{0:T(128)S(1)} %dynamic-slice_bitcast_fusion.table, f32[128,512]{1,0:T(8,128)S(1)} %copy-done, f32[128,512]{1,0:T(8,128)S(1)} %collective-permute-done.3.refs_1_.refs_0_, f32[128,512]{1,0:T(8,128)S(1)} %collective-permute-done.refs_2_.refs_1_, ...), custom_call_target="tpu_custom_call" | custom-call | flops 268435456 | bytes 1048576 | tf_op jit(solution)/shard_map/pallas_call | solution.py:142
  45.4 1.9 %collective-permute-start.6 = (f32[9,128,128]{2,1,0:T(8,128)S(1)}, f32[9,128,128]{2,1,0:T(8,128)S(1)}, u32[]{:S(2)}, u32[]{:S(2)}) collective-permute-start(f32[9,128,128]{2,1,0:T(8,128)S(1)} %get-tuple-element.22), channel_id=1, source_target_pairs={{0,1},{1,0},{2,3},{3,2},{4,5},{5,4},{6,7},{7,6},{8,9},{9,8},{10,11... | collective-permute-start | bytes 1769480 | tf_op jit(solution)/shard_map/ppermute | solution.py:218
  47.4 0.0 collective-permute-done.7.refs_3_
  47.4 1.0 collective-permute-done.8.refs_4_
  48.3 1.6 %shard_map.51 = (f32[3,128,128]{2,1,0:T(8,128)S(1)}, f32[3,128,128]{2,1,0:T(8,128)S(1)}) custom-call(s32[96]{0:T(128)S(1)} %dynamic-slice_bitcast_fusion.table, f32[128,512]{1,0:T(8,128)S(1)} %collective-permute-done.3.refs_1_.refs_0_, f32[128,512]{1,0:T(8,128)S(1)} %collective-permute-done.refs_2_.refs_1_, ...), custom_call_target="tpu_custom_call" | custom-call | flops 34359738368 | bytes 1048576 | tf_op jit(solution)/shard_map/pallas_call | solution.py:142
  49.9 1.9 %collective-permute-start.9 = (f32[3,128,128]{2,1,0:T(8,128)S(1)}, f32[3,128,128]{2,1,0:T(8,128)S(1)}, u32[]{:S(2)}, u32[]{:S(2)}) collective-permute-start(f32[3,128,128]{2,1,0:T(8,128)S(1)} %get-tuple-element.24), channel_id=1, source_target_pairs={{0,1},{1,0},{2,3},{3,2},{4,5},{5,4},{6,7},{7,6},{8,9},{9,8},{10,11... | collective-permute-start | bytes 589832 | tf_op jit(solution)/shard_map/ppermute | solution.py:220
  51.9 1.4 %collective-permute-done.9.refs_3_ = f32[3,128,128]{2,1,0:T(8,128)S(1)} collective-permute-done((f32[3,128,128]{2,1,0:T(8,128)S(1)}, f32[3,128,128]{2,1,0:T(8,128)S(1)}, u32[]{:S(2)}, u32[]{:S(2)}) %collective-permute-start.9) | collective-permute-done | bytes 196640 | tf_op jit(solution)/shard_map/ppermute | solution.py:220
  53.3 0.0 collective-permute-done.6.refs_1_
  53.3 1.5 %shard_map.52 = f32[48,32,128]{2,1,0:T(8,128)} custom-call(s32[96]{0:T(128)S(1)} %dynamic-slice_bitcast_fusion.table, f32[9,128,128]{2,1,0:T(8,128)S(1)} %get-tuple-element.21.refs_0_, f32[9,128,128]{2,1,0:T(8,128)S(1)} %collective-permute-done.6.refs_1_, f32[3,128,128]{2,1,0:T(8,128)S(1)} %get-tuple-element.23.refs_2_, ...), custom_call_target="tpu_custom_call" | custom-call | tf_op jit(solution)/shard_map/pallas_call | solution.py:165
  54.8 9.1 %all-to-all-start = ((f32[16,96,128]{2,1,0:T(8,128)}), f32[16,96,128]{2,1,0:T(8,128)S(1)}, u32[]{:S(2)}, u32[]{:S(2)}) async-start(f32[16,96,128]{2,1,0:T(8,128)} %bitcast.1), calls=%async_computation | async-start | bytes 1572864 | tf_op jit(solution)/shard_map/all_to_all | solution.py:224
  63.9 3.6 %collective-permute-start.11 = (f32[512]{0:T(512)S(1)}, f32[512]{0:T(512)S(1)}, u32[]{:S(2)}, u32[]{:S(2)}) collective-permute-start(f32[512]{0:T(512)S(1)} %add.32), channel_id=1, source_target_pairs={{256,0},{288,32},{320,64},{352,96},{384,128},{416,160},{448,192},{... | collective-permute-start | bytes 6152 | tf_op jit(solution)/shard_map/ppermute | solution.py:201
  67.4 6.2 %collective-permute-start.10 = (f32[512]{0:T(512)S(1)}, f32[512]{0:T(512)S(1)}, u32[]{:S(2)}, u32[]{:S(2)}) collective-permute-start(f32[512]{0:T(512)S(1)} %add.32), channel_id=1, source_target_pairs={{512,0},{544,32},{576,64},{608,96},{640,128},{672,160},{704,192},{... | collective-permute-start | bytes 6152 | tf_op jit(solution)/shard_map/ppermute | solution.py:201
  73.6 0.0 collective-permute-done.11
  73.7 3.2 %collective-permute-done.10 = f32[512]{0:T(512)S(1)} collective-permute-done((f32[512]{0:T(512)S(1)}, f32[512]{0:T(512)S(1)}, u32[]{:S(2)}, u32[]{:S(2)}) %collective-permute-start.10) | collective-permute-done | bytes 2080 | tf_op jit(solution)/shard_map/ppermute | solution.py:201
  76.8 4.2 %collective-permute-start.12 = (f32[512]{0:T(512)S(1)}, f32[512]{0:T(512)S(1)}, u32[]{:S(2)}, u32[]{:S(2)}) collective-permute-start(f32[512]{0:T(512)S(1)} %select_add_fusion), channel_id=1, source_target_pairs={{128,0},{160,32},{192,64},{224,96},{256,128},{288,160},{320,192},{... | collective-permute-start | bytes 6152 | tf_op jit(solution)/shard_map/ppermute | solution.py:201
  81.0 3.1 %collective-permute-done.12 = f32[512]{0:T(512)S(1)} collective-permute-done((f32[512]{0:T(512)S(1)}, f32[512]{0:T(512)S(1)}, u32[]{:S(2)}, u32[]{:S(2)}) %collective-permute-start.12) | collective-permute-done | bytes 2080 | tf_op jit(solution)/shard_map/ppermute | solution.py:201
  84.0 1.5 %all-to-all-done = f32[16,96,128]{2,1,0:T(8,128)S(1)} async-done(((f32[16,96,128]{2,1,0:T(8,128)}), f32[16,96,128]{2,1,0:T(8,128)S(1)}, u32[]{:S(2)}, u32[]{:S(2)}) %all-to-all-start) | async-done | bytes 786464 | tf_op jit(solution)/shard_map/all_to_all | solution.py:224
  85.6 1.9 %collective-permute-start.14 = (f32[64,128]{1,0:T(8,128)S(1)}, f32[64,128]{1,0:T(8,128)S(1)}, u32[]{:S(2)}, u32[]{:S(2)}) collective-permute-start(f32[64,128]{1,0:T(8,128)S(1)} %slice.7), channel_id=1, source_target_pairs={{6,132},{8,120},{28,56},{0,576},{20,5},{10,6},{30,37},{22,38},{14,... | collective-permute-start | bytes 98312 | tf_op jit(solution)/shard_map/ppermute | solution.py:235
  87.5 12.6 %collective-permute-start.13 = (f32[32,128]{1,0:T(8,128)S(1)}, f32[32,128]{1,0:T(8,128)S(1)}, u32[]{:S(2)}, u32[]{:S(2)}) collective-permute-start(f32[32,128]{1,0:T(8,128)S(1)} %slice.6), channel_id=1, source_target_pairs={{8,132},{20,133},{24,120},{26,121},{28,56},{10,57},{0,576},{14,577... | collective-permute-start | bytes 49160 | tf_op jit(solution)/shard_map/ppermute | solution.py:236
  100.1 1.9 %collective-permute-start.15 = (f32[512]{0:T(512)S(1)}, f32[512]{0:T(512)S(1)}, u32[]{:S(2)}, u32[]{:S(2)}) collective-permute-start(f32[512]{0:T(512)S(1)} %add.38), channel_id=1, source_target_pairs={{64,0},{96,32},{128,64},{160,96},{192,128},{224,160},{256,192},{28... | collective-permute-start | bytes 6152 | tf_op jit(solution)/shard_map/ppermute | solution.py:201
  102.0 3.5 %collective-permute-done.15 = f32[512]{0:T(512)S(1)} collective-permute-done((f32[512]{0:T(512)S(1)}, f32[512]{0:T(512)S(1)}, u32[]{:S(2)}, u32[]{:S(2)}) %collective-permute-start.15) | collective-permute-done | bytes 2080 | tf_op jit(solution)/shard_map/ppermute | solution.py:201
  105.6 0.6 add.39
  106.1 0.0 collective-permute-done.13
  106.1 0.0 collective-permute-done.14
  106.2 0.6 fusion
  (6 shorter events, 0.1 us)
Async XLA Ops:
  0.6 41.9 %copy-start = (f32[128,512]{1,0:T(8,128)S(1)}, f32[128,512]{1,0:T(8,128)}, u32[]{:S(2)}) copy-start(f32[128,512]{1,0:T(8,128)} %refs_0_.1) | copy-start | bytes 786436
  0.6 22.5 %collective-permute-start.3 = (f32[128,512]{1,0:T(8,128)}, f32[128,512]{1,0:T(8,128)S(1)}, u32[]{:S(2)}, u32[]{:S(2)}) collective-permute-start(f32[128,512]{1,0:T(8,128)} %refs_0_.1), channel_id=1, source_target_pairs={{64,0},{96,32},{128,64},{160,96},{192,128},{224,160},{256,192},{28... | collective-permute-start | bytes 786440 | tf_op jit(solution)/shard_map/ppermute | solution.py:201
  15.4 17.0 %collective-permute-start.1 = (f32[128,512]{1,0:T(8,128)}, f32[128,512]{1,0:T(8,128)S(1)}, u32[]{:S(2)}, u32[]{:S(2)}) collective-permute-start(f32[128,512]{1,0:T(8,128)} %refs_0_.1), channel_id=1, source_target_pairs={{32,0},{0,32},{96,64},{64,96},{160,128},{128,160},{224,192},{192,2... | collective-permute-start | bytes 786440 | tf_op jit(solution)/shard_map/ppermute | solution.py:201
  18.8 13.6 %collective-permute-start = (f32[128,512]{1,0:T(8,128)}, f32[128,512]{1,0:T(8,128)S(1)}, u32[]{:S(2)}, u32[]{:S(2)}) collective-permute-start(f32[128,512]{1,0:T(8,128)} %refs_0_.1), channel_id=1, source_target_pairs={{128,0},{160,32},{192,64},{224,96},{256,128},{288,160},{320,192},{... | collective-permute-start | bytes 786440 | tf_op jit(solution)/shard_map/ppermute | solution.py:204
  21.2 18.8 %collective-permute-start.4 = (f32[128,512]{1,0:T(8,128)}, f32[128,512]{1,0:T(8,128)S(1)}, u32[]{:S(2)}, u32[]{:S(2)}) collective-permute-start(f32[128,512]{1,0:T(8,128)} %refs_0_.1), channel_id=1, source_target_pairs={{576,0},{608,32},{640,64},{672,96},{704,128},{736,160},{0,192},{32... | collective-permute-start | bytes 786440 | tf_op jit(solution)/shard_map/ppermute | solution.py:204
  23.2 16.9 %collective-permute-start.5 = (f32[128,512]{1,0:T(8,128)S(1)}, f32[128,512]{1,0:T(8,128)S(1)}, u32[]{:S(2)}, u32[]{:S(2)}) collective-permute-start(f32[128,512]{1,0:T(8,128)S(1)} %collective-permute-done.3.refs_1_.refs_0_), channel_id=1, source_target_pairs={{32,0},{0,32},{96,64},{64,96},{160,128},{128,160},{224,192},{192,2... | collective-permute-start | bytes 786440 | tf_op jit(solution)/shard_map/ppermute | solution.py:201
  26.7 5.6 %collective-permute-start.2 = (f32[512]{0:T(512)S(1)}, f32[512]{0:T(512)S(1)}, u32[]{:S(2)}, u32[]{:S(2)}) collective-permute-start(f32[512]{0:T(512)S(1)} %multiply_reduce_fusion), channel_id=1, source_target_pairs={{32,0},{0,32},{96,64},{64,96},{160,128},{128,160},{224,192},{192,2... | collective-permute-start | bytes 6152 | tf_op jit(solution)/shard_map/ppermute | solution.py:201
  32.3 15.0 %collective-permute-start.7 = (f32[128,512]{1,0:T(8,128)S(1)}, f32[128,512]{1,0:T(8,128)S(1)}, u32[]{:S(2)}, u32[]{:S(2)}) collective-permute-start(f32[128,512]{1,0:T(8,128)S(1)} %collective-permute-done.refs_2_.refs_1_), channel_id=1, source_target_pairs={{64,0},{96,32},{128,64},{160,96},{192,128},{224,160},{256,192},{28... | collective-permute-start | bytes 786440 | tf_op jit(solution)/shard_map/ppermute | solution.py:204
  40.1 8.3 %collective-permute-start.8 = (f32[128,512]{1,0:T(8,128)S(1)}, f32[128,512]{1,0:T(8,128)S(1)}, u32[]{:S(2)}, u32[]{:S(2)}) collective-permute-start(f32[128,512]{1,0:T(8,128)S(1)} %collective-permute-done.4.refs_3_.refs_2_), channel_id=1, source_target_pairs={{32,0},{0,32},{96,64},{64,96},{160,128},{128,160},{224,192},{192,2... | collective-permute-start | bytes 786440 | tf_op jit(solution)/shard_map/ppermute | solution.py:204
  45.4 7.8 %collective-permute-start.6 = (f32[9,128,128]{2,1,0:T(8,128)S(1)}, f32[9,128,128]{2,1,0:T(8,128)S(1)}, u32[]{:S(2)}, u32[]{:S(2)}) collective-permute-start(f32[9,128,128]{2,1,0:T(8,128)S(1)} %get-tuple-element.22), channel_id=1, source_target_pairs={{0,1},{1,0},{2,3},{3,2},{4,5},{5,4},{6,7},{7,6},{8,9},{9,8},{10,11... | collective-permute-start | bytes 1769480 | tf_op jit(solution)/shard_map/ppermute | solution.py:218
  49.9 3.3 %collective-permute-start.9 = (f32[3,128,128]{2,1,0:T(8,128)S(1)}, f32[3,128,128]{2,1,0:T(8,128)S(1)}, u32[]{:S(2)}, u32[]{:S(2)}) collective-permute-start(f32[3,128,128]{2,1,0:T(8,128)S(1)} %get-tuple-element.24), channel_id=1, source_target_pairs={{0,1},{1,0},{2,3},{3,2},{4,5},{5,4},{6,7},{7,6},{8,9},{9,8},{10,11... | collective-permute-start | bytes 589832 | tf_op jit(solution)/shard_map/ppermute | solution.py:220
  54.8 30.7 %all-to-all-start = ((f32[16,96,128]{2,1,0:T(8,128)}), f32[16,96,128]{2,1,0:T(8,128)S(1)}, u32[]{:S(2)}, u32[]{:S(2)}) async-start(f32[16,96,128]{2,1,0:T(8,128)} %bitcast.1), calls=%async_computation | async-start | bytes 1572864 | tf_op jit(solution)/shard_map/all_to_all | solution.py:224
  63.9 9.8 %collective-permute-start.11 = (f32[512]{0:T(512)S(1)}, f32[512]{0:T(512)S(1)}, u32[]{:S(2)}, u32[]{:S(2)}) collective-permute-start(f32[512]{0:T(512)S(1)} %add.32), channel_id=1, source_target_pairs={{256,0},{288,32},{320,64},{352,96},{384,128},{416,160},{448,192},{... | collective-permute-start | bytes 6152 | tf_op jit(solution)/shard_map/ppermute | solution.py:201
  67.4 9.4 %collective-permute-start.10 = (f32[512]{0:T(512)S(1)}, f32[512]{0:T(512)S(1)}, u32[]{:S(2)}, u32[]{:S(2)}) collective-permute-start(f32[512]{0:T(512)S(1)} %add.32), channel_id=1, source_target_pairs={{512,0},{544,32},{576,64},{608,96},{640,128},{672,160},{704,192},{... | collective-permute-start | bytes 6152 | tf_op jit(solution)/shard_map/ppermute | solution.py:201
  76.8 7.2 %collective-permute-start.12 = (f32[512]{0:T(512)S(1)}, f32[512]{0:T(512)S(1)}, u32[]{:S(2)}, u32[]{:S(2)}) collective-permute-start(f32[512]{0:T(512)S(1)} %select_add_fusion), channel_id=1, source_target_pairs={{128,0},{160,32},{192,64},{224,96},{256,128},{288,160},{320,192},{... | collective-permute-start | bytes 6152 | tf_op jit(solution)/shard_map/ppermute | solution.py:201
  85.6 20.6 %collective-permute-start.14 = (f32[64,128]{1,0:T(8,128)S(1)}, f32[64,128]{1,0:T(8,128)S(1)}, u32[]{:S(2)}, u32[]{:S(2)}) collective-permute-start(f32[64,128]{1,0:T(8,128)S(1)} %slice.7), channel_id=1, source_target_pairs={{6,132},{8,120},{28,56},{0,576},{20,5},{10,6},{30,37},{22,38},{14,... | collective-permute-start | bytes 98312 | tf_op jit(solution)/shard_map/ppermute | solution.py:235
  87.5 18.6 %collective-permute-start.13 = (f32[32,128]{1,0:T(8,128)S(1)}, f32[32,128]{1,0:T(8,128)S(1)}, u32[]{:S(2)}, u32[]{:S(2)}) collective-permute-start(f32[32,128]{1,0:T(8,128)S(1)} %slice.6), channel_id=1, source_target_pairs={{8,132},{20,133},{24,120},{26,121},{28,56},{10,57},{0,576},{14,577... | collective-permute-start | bytes 49160 | tf_op jit(solution)/shard_map/ppermute | solution.py:236
  100.1 5.5 %collective-permute-start.15 = (f32[512]{0:T(512)S(1)}, f32[512]{0:T(512)S(1)}, u32[]{:S(2)}, u32[]{:S(2)}) collective-permute-start(f32[512]{0:T(512)S(1)} %add.38), channel_id=1, source_target_pairs={{64,0},{96,32},{128,64},{160,96},{192,128},{224,160},{256,192},{28... | collective-permute-start | bytes 6152 | tf_op jit(solution)/shard_map/ppermute | solution.py:201

commit v13 on v11

--- a/solution.py
+++ b/solution.py
@@ -110,14 +110,20 @@
     return np.concatenate(tables, axis=1), pairs[0], pairs[2]
 
 
-def product_kernel(base, count, table, *refs):
-    *blocks, keep, send, parts = refs
+def product_kernel(base, count, ready, shared, table, *refs):
+    done, blocks, (keep, send) = refs[:ready], refs[ready:-3 - bool(shared)], refs[-3 - bool(shared):][:2]
+    parts = refs[-1]
     depth = blocks[0].shape[1]
+    if ready:
+        parts[:done[0].shape[0]] = done[0][...]
+    first = done[0].shape[0] if ready else 0
     for b, ref in enumerate(blocks):
         value = ref[...]
         high = value.astype(jnp.bfloat16)
-        parts[b, :, :depth] = high
-        parts[b, :, depth:] = (value - high.astype(jnp.float32)).astype(jnp.bfloat16)
+        parts[first + b, :, :depth] = high
+        parts[first + b, :, depth:] = (value - high.astype(jnp.float32)).astype(jnp.bfloat16)
+    if shared:
+        refs[-2][...] = parts[shared[0]:shared[1]]
     dims = (((1,), (1,)), ((), ()))
 
     def dot(left, right):
@@ -136,18 +142,21 @@
 SMEM = pl.BlockSpec(memory_space=pltpu.SMEM)
 
 
-def products(table, base, count, blocks, cost):
+def products(table, base, count, blocks, cost, ready=(), shared=()):
     rows, depth = blocks[0].shape
-    out = jax.ShapeDtypeStruct((count, rows, rows), jnp.float32)
+    out = [jax.ShapeDtypeStruct((count, rows, rows), jnp.float32)] * 2
+    if shared:
+        out.append(jax.ShapeDtypeStruct((shared[1] - shared[0], rows, 2 * depth), jnp.bfloat16))
+    total = len(blocks) + sum(r.shape[0] for r in ready)
     return pl.pallas_call(
-        functools.partial(product_kernel, base, count),
-        out_shape=(out, out),
-        in_specs=[SMEM] + [VMEM] * len(blocks),
-        out_specs=(VMEM, VMEM),
-        scratch_shapes=[pltpu.VMEM((len(blocks), rows, 2 * depth), jnp.bfloat16)],
+        functools.partial(product_kernel, base, count, len(ready), shared),
+        out_shape=out,
+        in_specs=[SMEM] + [VMEM] * (len(ready) + len(blocks)),
+        out_specs=[VMEM] * len(out),
+        scratch_shapes=[pltpu.VMEM((total, rows, 2 * depth), jnp.bfloat16)],
         compiler_params=pltpu.CompilerParams(vmem_limit_bytes=32 * 2**20),
         cost_estimate=pl.CostEstimate(flops=cost, bytes_accessed=2**20, transcendentals=0),
-    )(table, *blocks)
+    )(table, *ready, *blocks)
 
 
 def join_kernel(table, *refs):
@@ -214,9 +223,11 @@
         late_a = mixed_get(far_a, (1, 0), (0, 1))
         late_b = mixed_get(far_b, (0, 1), (1, 0))
 
-        keep, send = products(table, 0, NEARLY, (jacobian, up1, far_a, far_b, pair0, pair1), 2**28)
+        keep, send, split = products(
+            table, 0, NEARLY, (jacobian, up1, far_a, far_b, pair0, pair1), 2**28, shared=(1, 4)
+        )
         early = (keep, lax.ppermute(send, "par", core_swap))
-        keep, send = products(table, 4 * NEARLY, NLATE, (up1, far_a, far_b, late_a, late_b), 2**35)
+        keep, send = products(table, 4 * NEARLY, NLATE, (late_a, late_b), 2**35, ready=(split,))
         late = (keep, lax.ppermute(send, "par", core_swap))
 
         mine = join(table, *early, *late).reshape(NQ, 3 * SLICE, -1)

time: 105 us -> 104 us (level)
  the two profiles are of different devices: /device:TPU:21 before, /device:TPU:19 now
where the time goes in v13:
time: 104 us; the launch traced here: 103 us
  starting transfers between devices  82.6 us (79%)
  waiting for transfers between devices  10.9 us (10%)
  Pallas kernels  5.91 us (6%)
  other arithmetic  2.32 us (2%)
    ppermute x9, starting transfers between devices, walk_get(): return lax.ppermute(value, 'walk', walk_perm(dz, flip))  42.1 us
    ppermute x4, starting transfers between devices, mixed_get(): return lax.ppermute(value, ('walk', 'par'), mixed_perm(moves))  11.2 us
    all_to_all x1, starting transfers between devices, shards(): lax.all_to_all(mine, 'par', 0, 0, axis_index_groups=groups, tiled=True)  8.45 us
    ppermute x1, starting transfers between devices, shards(): pair = lax.ppermute(mine[:2 * SLICE], ('walk', 'par'), pair_perm)  8.4 us
    ppermute x1, starting transfers between devices, shards(): early = (keep, lax.ppermute(send, 'par', core_swap))  5.76 us
    ppermute x1, waiting for transfers between devices, shards(): single = lax.ppermute(mine[2 * SLICE:], ('walk', 'par'), single_perm)  5.34 us
    ppermute x9, waiting for transfers between devices, walk_get(): return lax.ppermute(value, 'walk', walk_perm(dz, flip))  4.48 us
    pallas_call x2, Pallas kernels, products(): pl.pallas_call(functools.partial(product_kernel, base, count, len(ready),...  4.38 us
  transfers between devices with their start and end apart: 18, of which 4 were waited for; matrix products, arithmetic and copies ran while one was open for 2% of the time, Pallas kernels for 4%

profile of v13, /device:TPU:19, one launch (start us, length us, event | category | flops | bytes accessed | tf_op | source)
XLA Modules:
  0.0 103.4 jit_solution(2363729104883124882)
XLA Ops:
  0.6 0.0 copy-start
  0.6 14.4 %collective-permute-start.3 = (f32[128,512]{1,0:T(8,128)}, f32[128,512]{1,0:T(8,128)S(1)}, u32[]{:S(2)}, u32[]{:S(2)}) collective-permute-start(f32[128,512]{1,0:T(8,128)} %refs_0_.1), channel_id=1, source_target_pairs={{64,0},{96,32},{128,64},{160,96},{192,128},{224,160},{256,192},{28... | collective-permute-start | bytes 786440 | tf_op jit(solution)/shard_map/ppermute | solution.py:210
  15.1 1.9 %collective-permute-start = (f32[128,512]{1,0:T(8,128)}, f32[128,512]{1,0:T(8,128)S(1)}, u32[]{:S(2)}, u32[]{:S(2)}) collective-permute-start(f32[128,512]{1,0:T(8,128)} %refs_0_.1), channel_id=1, source_target_pairs={{128,0},{160,32},{192,64},{224,96},{256,128},{288,160},{320,192},{... | collective-permute-start | bytes 786440 | tf_op jit(solution)/shard_map/ppermute | solution.py:213
  17.0 2.2 %collective-permute-start.1 = (f32[128,512]{1,0:T(8,128)}, f32[128,512]{1,0:T(8,128)S(1)}, u32[]{:S(2)}, u32[]{:S(2)}) collective-permute-start(f32[128,512]{1,0:T(8,128)} %refs_0_.1), channel_id=1, source_target_pairs={{32,0},{0,32},{96,64},{64,96},{160,128},{128,160},{224,192},{192,2... | collective-permute-start | bytes 786440 | tf_op jit(solution)/shard_map/ppermute | solution.py:210
  19.2 2.2 %collective-permute-start.4 = (f32[128,512]{1,0:T(8,128)}, f32[128,512]{1,0:T(8,128)S(1)}, u32[]{:S(2)}, u32[]{:S(2)}) collective-permute-start(f32[128,512]{1,0:T(8,128)} %refs_0_.1), channel_id=1, source_target_pairs={{576,0},{608,32},{640,64},{672,96},{704,128},{736,160},{0,192},{32... | collective-permute-start | bytes 786440 | tf_op jit(solution)/shard_map/ppermute | solution.py:213
  21.4 0.0 collective-permute-done.3.refs_1_
  21.4 3.1 %collective-permute-start.5 = (f32[128,512]{1,0:T(8,128)S(1)}, f32[128,512]{1,0:T(8,128)S(1)}, u32[]{:S(2)}, u32[]{:S(2)}) collective-permute-start(f32[128,512]{1,0:T(8,128)S(1)} %collective-permute-done.3.refs_1_), channel_id=1, source_target_pairs={{32,0},{0,32},{96,64},{64,96},{160,128},{128,160},{224,192},{192,2... | collective-permute-start | bytes 786440 | tf_op jit(solution)/shard_map/ppermute | solution.py:210
  24.5 1.1 %multiply_reduce_fusion = f32[512]{0:T(512)S(1)} fusion(f32[128,512]{1,0:T(8,128)} %refs_0_.1, f32[128]{0:T(128)} %param.4), kind=kLoop, calls=%fused_computation | loop fusion | flops 130560 | bytes 264704 | tf_op jit(solution)/shard_map/reduce_sum | solution.py:220
  25.5 2.2 %collective-permute-start.2 = (f32[512]{0:T(512)S(1)}, f32[512]{0:T(512)S(1)}, u32[]{:S(2)}, u32[]{:S(2)}) collective-permute-start(f32[512]{0:T(512)S(1)} %multiply_reduce_fusion), channel_id=1, source_target_pairs={{32,0},{0,32},{96,64},{64,96},{160,128},{128,160},{224,192},{192,2... | collective-permute-start | bytes 6152 | tf_op jit(solution)/shard_map/ppermute | solution.py:210
  27.7 0.7 dynamic-slice_bitcast_fusion.table
  28.4 3.3 %collective-permute-done.2 = f32[512]{0:T(512)S(1)} collective-permute-done((f32[512]{0:T(512)S(1)}, f32[512]{0:T(512)S(1)}, u32[]{:S(2)}, u32[]{:S(2)}) %collective-permute-start.2) | collective-permute-done | bytes 2080 | tf_op jit(solution)/shard_map/ppermute | solution.py:210
  31.7 0.0 collective-permute-done.refs_2_
  31.7 0.0 collective-permute-done.1.refs_4_
  31.7 2.0 %collective-permute-start.7 = (f32[128,512]{1,0:T(8,128)S(1)}, f32[128,512]{1,0:T(8,128)S(1)}, u32[]{:S(2)}, u32[]{:S(2)}) collective-permute-start(f32[128,512]{1,0:T(8,128)S(1)} %collective-permute-done.refs_2_), channel_id=1, source_target_pairs={{64,0},{96,32},{128,64},{160,96},{192,128},{224,160},{256,192},{28... | collective-permute-start | bytes 786440 | tf_op jit(solution)/shard_map/ppermute | solution.py:213
  33.8 0.0 collective-permute-done.4.refs_3_
  33.8 0.0 collective-permute-done.5.refs_5_
  33.8 5.1 %collective-permute-start.8 = (f32[128,512]{1,0:T(8,128)S(1)}, f32[128,512]{1,0:T(8,128)S(1)}, u32[]{:S(2)}, u32[]{:S(2)}) collective-permute-start(f32[128,512]{1,0:T(8,128)S(1)} %collective-permute-done.4.refs_3_), channel_id=1, source_target_pairs={{32,0},{0,32},{96,64},{64,96},{160,128},{128,160},{224,192},{192,2... | collective-permute-start | bytes 786440 | tf_op jit(solution)/shard_map/ppermute | solution.py:213
  38.9 0.0 copy-done
  38.9 2.9 %shard_map.50 = (f32[9,128,128]{2,1,0:T(8,128)S(1)}, f32[9,128,128]{2,1,0:T(8,128)S(1)}, bf16[3,128,1024]{2,1,0:T(8,128)(2,1)S(1)}) custom-call(s32[96]{0:T(128)S(1)} %dynamic-slice_bitcast_fusion.table, f32[128,512]{1,0:T(8,128)S(1)} %copy-done, f32[128,512]{1,0:T(8,128)S(1)} %collective-permute-done.3.refs_1_, ...), custom_call_target="tpu_custom_call" | custom-call | flops 268435456 | bytes 1048576 | tf_op jit(solution)/shard_map/pallas_call | solution.py:151
  41.8 5.8 %collective-permute-start.6 = (f32[9,128,128]{2,1,0:T(8,128)S(1)}, f32[9,128,128]{2,1,0:T(8,128)S(1)}, u32[]{:S(2)}, u32[]{:S(2)}) collective-permute-start(f32[9,128,128]{2,1,0:T(8,128)S(1)} %get-tuple-element.21), channel_id=1, source_target_pairs={{0,1},{1,0},{2,3},{3,2},{4,5},{5,4},{6,7},{7,6},{8,9},{9,8},{10,11... | collective-permute-start | bytes 1769480 | tf_op jit(solution)/shard_map/ppermute | solution.py:229
  47.6 0.0 collective-permute-done.7.refs_1_
  47.6 0.0 collective-permute-done.8.refs_2_
  47.6 1.5 %shard_map.51 = (f32[3,128,128]{2,1,0:T(8,128)S(1)}, f32[3,128,128]{2,1,0:T(8,128)S(1)}) custom-call(s32[96]{0:T(128)S(1)} %dynamic-slice_bitcast_fusion.table, bf16[3,128,1024]{2,1,0:T(8,128)(2,1)S(1)} %get-tuple-element.22.refs_0_, f32[128,512]{1,0:T(8,128)S(1)} %collective-permute-done.7.refs_1_, f32[128,512]{1,0:T(8,128)S(1)} %collective-permute-done.8.refs_2_), custom_call_target="tpu_custom_call" | custom-call | flops 34359738368 | bytes 1048576 | tf_op jit(solution)/shard_map/pallas_call | solution.py:151
  49.1 2.4 %collective-permute-start.9 = (f32[3,128,128]{2,1,0:T(8,128)S(1)}, f32[3,128,128]{2,1,0:T(8,128)S(1)}, u32[]{:S(2)}, u32[]{:S(2)}) collective-permute-start(f32[3,128,128]{2,1,0:T(8,128)S(1)} %get-tuple-element.24), channel_id=1, source_target_pairs={{0,1},{1,0},{2,3},{3,2},{4,5},{5,4},{6,7},{7,6},{8,9},{9,8},{10,11... | collective-permute-start | bytes 589832 | tf_op jit(solution)/shard_map/ppermute | solution.py:231
  51.5 1.0 %collective-permute-done.9.refs_3_ = f32[3,128,128]{2,1,0:T(8,128)S(1)} collective-permute-done((f32[3,128,128]{2,1,0:T(8,128)S(1)}, f32[3,128,128]{2,1,0:T(8,128)S(1)}, u32[]{:S(2)}, u32[]{:S(2)}) %collective-permute-start.9) | collective-permute-done | bytes 196640 | tf_op jit(solution)/shard_map/ppermute | solution.py:231
  52.5 0.0 collective-permute-done.6.refs_1_
  52.5 1.5 %shard_map.52 = f32[48,32,128]{2,1,0:T(8,128)} custom-call(s32[96]{0:T(128)S(1)} %dynamic-slice_bitcast_fusion.table, f32[9,128,128]{2,1,0:T(8,128)S(1)} %get-tuple-element.20.refs_0_, f32[9,128,128]{2,1,0:T(8,128)S(1)} %collective-permute-done.6.refs_1_, f32[3,128,128]{2,1,0:T(8,128)S(1)} %get-tuple-element.23.refs_2_, ...), custom_call_target="tpu_custom_call" | custom-call | tf_op jit(solution)/shard_map/pallas_call | solution.py:174
  54.0 8.5 %all-to-all-start = ((f32[16,96,128]{2,1,0:T(8,128)}), f32[16,96,128]{2,1,0:T(8,128)S(1)}, u32[]{:S(2)}, u32[]{:S(2)}) async-start(f32[16,96,128]{2,1,0:T(8,128)} %bitcast.1), calls=%async_computation | async-start | bytes 1572864 | tf_op jit(solution)/shard_map/all_to_all | solution.py:235
  62.5 1.9 %collective-permute-start.12 = (f32[512]{0:T(512)S(1)}, f32[512]{0:T(512)S(1)}, u32[]{:S(2)}, u32[]{:S(2)}) collective-permute-start(f32[512]{0:T(512)S(1)} %add.35), channel_id=1, source_target_pairs={{512,0},{544,32},{576,64},{608,96},{640,128},{672,160},{704,192},{... | collective-permute-start | bytes 6152 | tf_op jit(solution)/shard_map/ppermute | solution.py:210
  64.4 7.3 %collective-permute-start.13 = (f32[512]{0:T(512)S(1)}, f32[512]{0:T(512)S(1)}, u32[]{:S(2)}, u32[]{:S(2)}) collective-permute-start(f32[512]{0:T(512)S(1)} %add.35), channel_id=1, source_target_pairs={{256,0},{288,32},{320,64},{352,96},{384,128},{416,160},{448,192},{... | collective-permute-start | bytes 6152 | tf_op jit(solution)/shard_map/ppermute | solution.py:210
  71.7 0.0 collective-permute-done.12
  71.7 1.2 %collective-permute-done.13 = f32[512]{0:T(512)S(1)} collective-permute-done((f32[512]{0:T(512)S(1)}, f32[512]{0:T(512)S(1)}, u32[]{:S(2)}, u32[]{:S(2)}) %collective-permute-start.13) | collective-permute-done | bytes 2080 | tf_op jit(solution)/shard_map/ppermute | solution.py:210
  73.0 5.8 %collective-permute-start.14 = (f32[512]{0:T(512)S(1)}, f32[512]{0:T(512)S(1)}, u32[]{:S(2)}, u32[]{:S(2)}) collective-permute-start(f32[512]{0:T(512)S(1)} %select_add_fusion), channel_id=1, source_target_pairs={{128,0},{160,32},{192,64},{224,96},{256,128},{288,160},{320,192},{... | collective-permute-start | bytes 6152 | tf_op jit(solution)/shard_map/ppermute | solution.py:210
  78.7 1.9 %collective-permute-start.15 = (f32[512]{0:T(512)S(1)}, f32[512]{0:T(512)S(1)}, u32[]{:S(2)}, u32[]{:S(2)}) collective-permute-start(f32[512]{0:T(512)S(1)} %select_add_fusion), channel_id=1, source_target_pairs={{64,0},{96,32},{128,64},{160,96},{192,128},{224,160},{256,192},{28... | collective-permute-start | bytes 6152 | tf_op jit(solution)/shard_map/ppermute | solution.py:210
  80.7 3.4 %collective-permute-start.16 = (f32[512]{0:T(512)S(1)}, f32[512]{0:T(512)S(1)}, u32[]{:S(2)}, u32[]{:S(2)}) collective-permute-start(f32[512]{0:T(512)S(1)} %select_add_fusion), channel_id=1, source_target_pairs={{704,0},{736,32},{0,64},{32,96},{64,128},{96,160},{128,192},{160,2... | collective-permute-start | bytes 6152 | tf_op jit(solution)/shard_map/ppermute | solution.py:210
  84.1 0.0 all-to-all-done
  84.1 8.4 %collective-permute-start.11 = (f32[64,128]{1,0:T(8,128)S(1)}, f32[64,128]{1,0:T(8,128)S(1)}, u32[]{:S(2)}, u32[]{:S(2)}) collective-permute-start(f32[64,128]{1,0:T(8,128)S(1)} %slice.9), channel_id=1, source_target_pairs={{6,132},{8,120},{28,56},{0,576},{20,5},{10,6},{30,37},{22,38},{14,... | collective-permute-start | bytes 98312 | tf_op jit(solution)/shard_map/ppermute | solution.py:246
  92.5 4.2 %collective-permute-start.10 = (f32[32,128]{1,0:T(8,128)S(1)}, f32[32,128]{1,0:T(8,128)S(1)}, u32[]{:S(2)}, u32[]{:S(2)}) collective-permute-start(f32[32,128]{1,0:T(8,128)S(1)} %slice.8), channel_id=1, source_target_pairs={{8,132},{20,133},{24,120},{26,121},{28,56},{10,57},{0,576},{14,577... | collective-permute-start | bytes 49160 | tf_op jit(solution)/shard_map/ppermute | solution.py:247
  96.8 0.0 collective-permute-done.14
  96.8 0.0 collective-permute-done.15
  96.8 0.0 collective-permute-done.16
  96.8 0.6 add_add_fusion
  97.4 5.3 %collective-permute-done.10 = f32[32,128]{1,0:T(8,128)S(1)} collective-permute-done((f32[32,128]{1,0:T(8,128)S(1)}, f32[32,128]{1,0:T(8,128)S(1)}, u32[]{:S(2)}, u32[]{:S(2)}) %collective-permute-start.10) | collective-permute-done | bytes 16416 | tf_op jit(solution)/shard_map/ppermute | solution.py:247
  102.7 0.0 collective-permute-done.11
  102.7 0.6 fusion
  (5 shorter events, 0.1 us)
Async XLA Ops:
  0.6 38.2 %copy-start = (f32[128,512]{1,0:T(8,128)S(1)}, f32[128,512]{1,0:T(8,128)}, u32[]{:S(2)}) copy-start(f32[128,512]{1,0:T(8,128)} %refs_0_.1) | copy-start | bytes 786436
  0.6 20.7 %collective-permute-start.3 = (f32[128,512]{1,0:T(8,128)}, f32[128,512]{1,0:T(8,128)S(1)}, u32[]{:S(2)}, u32[]{:S(2)}) collective-permute-start(f32[128,512]{1,0:T(8,128)} %refs_0_.1), channel_id=1, source_target_pairs={{64,0},{96,32},{128,64},{160,96},{192,128},{224,160},{256,192},{28... | collective-permute-start | bytes 786440 | tf_op jit(solution)/shard_map/ppermute | solution.py:210
  15.1 16.6 %collective-permute-start = (f32[128,512]{1,0:T(8,128)}, f32[128,512]{1,0:T(8,128)S(1)}, u32[]{:S(2)}, u32[]{:S(2)}) collective-permute-start(f32[128,512]{1,0:T(8,128)} %refs_0_.1), channel_id=1, source_target_pairs={{128,0},{160,32},{192,64},{224,96},{256,128},{288,160},{320,192},{... | collective-permute-start | bytes 786440 | tf_op jit(solution)/shard_map/ppermute | solution.py:213
  17.0 14.7 %collective-permute-start.1 = (f32[128,512]{1,0:T(8,128)}, f32[128,512]{1,0:T(8,128)S(1)}, u32[]{:S(2)}, u32[]{:S(2)}) collective-permute-start(f32[128,512]{1,0:T(8,128)} %refs_0_.1), channel_id=1, source_target_pairs={{32,0},{0,32},{96,64},{64,96},{160,128},{128,160},{224,192},{192,2... | collective-permute-start | bytes 786440 | tf_op jit(solution)/shard_map/ppermute | solution.py:210
  19.2 14.6 %collective-permute-start.4 = (f32[128,512]{1,0:T(8,128)}, f32[128,512]{1,0:T(8,128)S(1)}, u32[]{:S(2)}, u32[]{:S(2)}) collective-permute-start(f32[128,512]{1,0:T(8,128)} %refs_0_.1), channel_id=1, source_target_pairs={{576,0},{608,32},{640,64},{672,96},{704,128},{736,160},{0,192},{32... | collective-permute-start | bytes 786440 | tf_op jit(solution)/shard_map/ppermute | solution.py:213
  21.4 12.4 %collective-permute-start.5 = (f32[128,512]{1,0:T(8,128)S(1)}, f32[128,512]{1,0:T(8,128)S(1)}, u32[]{:S(2)}, u32[]{:S(2)}) collective-permute-start(f32[128,512]{1,0:T(8,128)S(1)} %collective-permute-done.3.refs_1_), channel_id=1, source_target_pairs={{32,0},{0,32},{96,64},{64,96},{160,128},{128,160},{224,192},{192,2... | collective-permute-start | bytes 786440 | tf_op jit(solution)/shard_map/ppermute | solution.py:210
  25.5 6.2 %collective-permute-start.2 = (f32[512]{0:T(512)S(1)}, f32[512]{0:T(512)S(1)}, u32[]{:S(2)}, u32[]{:S(2)}) collective-permute-start(f32[512]{0:T(512)S(1)} %multiply_reduce_fusion), channel_id=1, source_target_pairs={{32,0},{0,32},{96,64},{64,96},{160,128},{128,160},{224,192},{192,2... | collective-permute-start | bytes 6152 | tf_op jit(solution)/shard_map/ppermute | solution.py:210
  31.7 15.9 %collective-permute-start.7 = (f32[128,512]{1,0:T(8,128)S(1)}, f32[128,512]{1,0:T(8,128)S(1)}, u32[]{:S(2)}, u32[]{:S(2)}) collective-permute-start(f32[128,512]{1,0:T(8,128)S(1)} %collective-permute-done.refs_2_), channel_id=1, source_target_pairs={{64,0},{96,32},{128,64},{160,96},{192,128},{224,160},{256,192},{28... | collective-permute-start | bytes 786440 | tf_op jit(solution)/shard_map/ppermute | solution.py:213
  33.8 13.8 %collective-permute-start.8 = (f32[128,512]{1,0:T(8,128)S(1)}, f32[128,512]{1,0:T(8,128)S(1)}, u32[]{:S(2)}, u32[]{:S(2)}) collective-permute-start(f32[128,512]{1,0:T(8,128)S(1)} %collective-permute-done.4.refs_3_), channel_id=1, source_target_pairs={{32,0},{0,32},{96,64},{64,96},{160,128},{128,160},{224,192},{192,2... | collective-permute-start | bytes 786440 | tf_op jit(solution)/shard_map/ppermute | solution.py:213
  41.8 10.7 %collective-permute-start.6 = (f32[9,128,128]{2,1,0:T(8,128)S(1)}, f32[9,128,128]{2,1,0:T(8,128)S(1)}, u32[]{:S(2)}, u32[]{:S(2)}) collective-permute-start(f32[9,128,128]{2,1,0:T(8,128)S(1)} %get-tuple-element.21), channel_id=1, source_target_pairs={{0,1},{1,0},{2,3},{3,2},{4,5},{5,4},{6,7},{7,6},{8,9},{9,8},{10,11... | collective-permute-start | bytes 1769480 | tf_op jit(solution)/shard_map/ppermute | solution.py:229
  49.1 3.4 %collective-permute-start.9 = (f32[3,128,128]{2,1,0:T(8,128)S(1)}, f32[3,128,128]{2,1,0:T(8,128)S(1)}, u32[]{:S(2)}, u32[]{:S(2)}) collective-permute-start(f32[3,128,128]{2,1,0:T(8,128)S(1)} %get-tuple-element.24), channel_id=1, source_target_pairs={{0,1},{1,0},{2,3},{3,2},{4,5},{5,4},{6,7},{7,6},{8,9},{9,8},{10,11... | collective-permute-start | bytes 589832 | tf_op jit(solution)/shard_map/ppermute | solution.py:231
  54.0 30.0 %all-to-all-start = ((f32[16,96,128]{2,1,0:T(8,128)}), f32[16,96,128]{2,1,0:T(8,128)S(1)}, u32[]{:S(2)}, u32[]{:S(2)}) async-start(f32[16,96,128]{2,1,0:T(8,128)} %bitcast.1), calls=%async_computation | async-start | bytes 1572864 | tf_op jit(solution)/shard_map/all_to_all | solution.py:235
  62.5 9.2 %collective-permute-start.12 = (f32[512]{0:T(512)S(1)}, f32[512]{0:T(512)S(1)}, u32[]{:S(2)}, u32[]{:S(2)}) collective-permute-start(f32[512]{0:T(512)S(1)} %add.35), channel_id=1, source_target_pairs={{512,0},{544,32},{576,64},{608,96},{640,128},{672,160},{704,192},{... | collective-permute-start | bytes 6152 | tf_op jit(solution)/shard_map/ppermute | solution.py:210
  64.4 8.5 %collective-permute-start.13 = (f32[512]{0:T(512)S(1)}, f32[512]{0:T(512)S(1)}, u32[]{:S(2)}, u32[]{:S(2)}) collective-permute-start(f32[512]{0:T(512)S(1)} %add.35), channel_id=1, source_target_pairs={{256,0},{288,32},{320,64},{352,96},{384,128},{416,160},{448,192},{... | collective-permute-start | bytes 6152 | tf_op jit(solution)/shard_map/ppermute | solution.py:210
  73.0 23.8 %collective-permute-start.14 = (f32[512]{0:T(512)S(1)}, f32[512]{0:T(512)S(1)}, u32[]{:S(2)}, u32[]{:S(2)}) collective-permute-start(f32[512]{0:T(512)S(1)} %select_add_fusion), channel_id=1, source_target_pairs={{128,0},{160,32},{192,64},{224,96},{256,128},{288,160},{320,192},{... | collective-permute-start | bytes 6152 | tf_op jit(solution)/shard_map/ppermute | solution.py:210
  78.7 18.0 %collective-permute-start.15 = (f32[512]{0:T(512)S(1)}, f32[512]{0:T(512)S(1)}, u32[]{:S(2)}, u32[]{:S(2)}) collective-permute-start(f32[512]{0:T(512)S(1)} %select_add_fusion), channel_id=1, source_target_pairs={{64,0},{96,32},{128,64},{160,96},{192,128},{224,160},{256,192},{28... | collective-permute-start | bytes 6152 | tf_op jit(solution)/shard_map/ppermute | solution.py:210
  80.7 16.1 %collective-permute-start.16 = (f32[512]{0:T(512)S(1)}, f32[512]{0:T(512)S(1)}, u32[]{:S(2)}, u32[]{:S(2)}) collective-permute-start(f32[512]{0:T(512)S(1)} %select_add_fusion), channel_id=1, source_target_pairs={{704,0},{736,32},{0,64},{32,96},{64,128},{96,160},{128,192},{160,2... | collective-permute-start | bytes 6152 | tf_op jit(solution)/shard_map/ppermute | solution.py:210
  84.1 18.6 %collective-permute-start.11 = (f32[64,128]{1,0:T(8,128)S(1)}, f32[64,128]{1,0:T(8,128)S(1)}, u32[]{:S(2)}, u32[]{:S(2)}) collective-permute-start(f32[64,128]{1,0:T(8,128)S(1)} %slice.9), channel_id=1, source_target_pairs={{6,132},{8,120},{28,56},{0,576},{20,5},{10,6},{30,37},{22,38},{14,... | collective-permute-start | bytes 98312 | tf_op jit(solution)/shard_map/ppermute | solution.py:246
  92.5 10.2 %collective-permute-start.10 = (f32[32,128]{1,0:T(8,128)S(1)}, f32[32,128]{1,0:T(8,128)S(1)}, u32[]{:S(2)}, u32[]{:S(2)}) collective-permute-start(f32[32,128]{1,0:T(8,128)S(1)} %slice.8), channel_id=1, source_target_pairs={{8,132},{20,133},{24,120},{26,121},{28,56},{10,57},{0,576},{14,577... | collective-permute-start | bytes 49160 | tf_op jit(solution)/shard_map/ppermute | solution.py:247

commit v14 on v13

--- a/solution.py
+++ b/solution.py
@@ -218,8 +218,7 @@
         pair0 = walk_get(jacobian, 0, 1)
         pair1 = walk_get(up1, 0, 1)
         term = jnp.sum(coeffs[:, None] * jacobian, axis=0)
-        far_a, pair0, term, table = tie((far_a, pair0, term + walk_get(term, 0, 1), table))
-        far_b, pair1 = tie((far_b, pair1))
+        far_a, term, table = tie((far_a, term + walk_get(term, 0, 1), table))
         late_a = mixed_get(far_a, (1, 0), (0, 1))
         late_b = mixed_get(far_b, (0, 1), (1, 0))
 

time: 104 us -> 104 us (level)
  starting transfers between devices: 82.6 us -> 76.5 us
  waiting for transfers between devices: 10.9 us -> 16.4 us
    ppermute x4, waiting for transfers between devices: 0.01 us -> 5.87 us  [mixed_get(): return lax.ppermute(value, ('walk', 'par'), mixed_perm(moves))]
    ppermute x4, starting transfers between devices: 11.2 us -> 8.16 us  [mixed_get(): return lax.ppermute(value, ('walk', 'par'), mixed_perm(moves))]
    ppermute x1, starting transfers between devices: 5.76 us -> 4.41 us  [shards(): early = (keep, lax.ppermute(send, 'par', core_swap))]
where the time goes in v14:
time: 104 us; the launch traced here: 103 us
  starting transfers between devices  76.5 us (74%)
  waiting for transfers between devices  16.4 us (16%)
  Pallas kernels  5.9 us (6%)
  other arithmetic  2.33 us (2%)
    ppermute x9, starting transfers between devices, walk_get(): return lax.ppermute(value, 'walk', walk_perm(dz, flip))  41.4 us
    all_to_all x1, starting transfers between devices, shards(): lax.all_to_all(mine, 'par', 0, 0, axis_index_groups=groups, tiled=True)  8.45 us
    ppermute x4, starting transfers between devices, mixed_get(): return lax.ppermute(value, ('walk', 'par'), mixed_perm(moves))  8.16 us
    ppermute x1, starting transfers between devices, shards(): pair = lax.ppermute(mine[:2 * SLICE], ('walk', 'par'), pair_perm)  7.91 us
    ppermute x4, waiting for transfers between devices, mixed_get(): return lax.ppermute(value, ('walk', 'par'), mixed_perm(moves))  5.87 us
    ppermute x1, waiting for transfers between devices, shards(): single = lax.ppermute(mine[2 * SLICE:], ('walk', 'par'), single_perm)  5.3 us
    ppermute x1, starting transfers between devices, shards(): early = (keep, lax.ppermute(send, 'par', core_swap))  4.41 us
    pallas_call x2, Pallas kernels, products(): pl.pallas_call(functools.partial(product_kernel, base, count, len(ready),...  4.38 us
  transfers between devices with their start and end apart: 18, of which 4 were waited for; matrix products, arithmetic and copies ran while one was open for 2% of the time, Pallas kernels for 4%

profile of v14, /device:TPU:19, one launch (start us, length us, event | category | flops | bytes accessed | tf_op | source)
XLA Modules:
  0.0 102.8 jit_solution(10368709073006131472)
XLA Ops:
  0.6 0.0 copy-start
  0.6 14.4 %collective-permute-start.2 = (f32[128,512]{1,0:T(8,128)}, f32[128,512]{1,0:T(8,128)S(1)}, u32[]{:S(2)}, u32[]{:S(2)}) collective-permute-start(f32[128,512]{1,0:T(8,128)} %refs_0_.1), channel_id=1, source_target_pairs={{64,0},{96,32},{128,64},{160,96},{192,128},{224,160},{256,192},{28... | collective-permute-start | bytes 786440 | tf_op jit(solution)/shard_map/ppermute | solution.py:210
  15.1 1.9 %collective-permute-start = (f32[128,512]{1,0:T(8,128)}, f32[128,512]{1,0:T(8,128)S(1)}, u32[]{:S(2)}, u32[]{:S(2)}) collective-permute-start(f32[128,512]{1,0:T(8,128)} %refs_0_.1), channel_id=1, source_target_pairs={{128,0},{160,32},{192,64},{224,96},{256,128},{288,160},{320,192},{... | collective-permute-start | bytes 786440 | tf_op jit(solution)/shard_map/ppermute | solution.py:213
  17.0 2.2 %collective-permute-start.3 = (f32[128,512]{1,0:T(8,128)}, f32[128,512]{1,0:T(8,128)S(1)}, u32[]{:S(2)}, u32[]{:S(2)}) collective-permute-start(f32[128,512]{1,0:T(8,128)} %refs_0_.1), channel_id=1, source_target_pairs={{576,0},{608,32},{640,64},{672,96},{704,128},{736,160},{0,192},{32... | collective-permute-start | bytes 786440 | tf_op jit(solution)/shard_map/ppermute | solution.py:213
  19.2 2.2 %collective-permute-start.4 = (f32[128,512]{1,0:T(8,128)}, f32[128,512]{1,0:T(8,128)S(1)}, u32[]{:S(2)}, u32[]{:S(2)}) collective-permute-start(f32[128,512]{1,0:T(8,128)} %refs_0_.1), channel_id=1, source_target_pairs={{32,0},{0,32},{96,64},{64,96},{160,128},{128,160},{224,192},{192,2... | collective-permute-start | bytes 786440 | tf_op jit(solution)/shard_map/ppermute | solution.py:210
  21.4 1.1 %multiply_reduce_fusion = f32[512]{0:T(512)S(1)} fusion(f32[128,512]{1,0:T(8,128)} %refs_0_.1, f32[128]{0:T(128)} %param.4), kind=kLoop, calls=%fused_computation | loop fusion | flops 130560 | bytes 264704 | tf_op jit(solution)/shard_map/reduce_sum | solution.py:220
  22.4 3.1 %collective-permute-start.1 = (f32[512]{0:T(512)S(1)}, f32[512]{0:T(512)S(1)}, u32[]{:S(2)}, u32[]{:S(2)}) collective-permute-start(f32[512]{0:T(512)S(1)} %multiply_reduce_fusion), channel_id=1, source_target_pairs={{32,0},{0,32},{96,64},{64,96},{160,128},{128,160},{224,192},{192,2... | collective-permute-start | bytes 6152 | tf_op jit(solution)/shard_map/ppermute | solution.py:210
  25.6 0.0 collective-permute-done.2.refs_1_
  25.6 2.2 %collective-permute-start.5 = (f32[128,512]{1,0:T(8,128)S(1)}, f32[128,512]{1,0:T(8,128)S(1)}, u32[]{:S(2)}, u32[]{:S(2)}) collective-permute-start(f32[128,512]{1,0:T(8,128)S(1)} %collective-permute-done.2.refs_1_), channel_id=1, source_target_pairs={{32,0},{0,32},{96,64},{64,96},{160,128},{128,160},{224,192},{192,2... | collective-permute-start | bytes 786440 | tf_op jit(solution)/shard_map/ppermute | solution.py:210
  27.8 0.7 dynamic-slice_bitcast_fusion.table
  28.4 0.0 collective-permute-done.1
  28.5 5.9 %collective-permute-done.refs_2_ = f32[128,512]{1,0:T(8,128)S(1)} collective-permute-done((f32[128,512]{1,0:T(8,128)}, f32[128,512]{1,0:T(8,128)S(1)}, u32[]{:S(2)}, u32[]{:S(2)}) %collective-permute-start) | collective-permute-done | bytes 262176 | tf_op jit(solution)/shard_map/ppermute | solution.py:213
  34.3 2.2 %collective-permute-start.7 = (f32[128,512]{1,0:T(8,128)S(1)}, f32[128,512]{1,0:T(8,128)S(1)}, u32[]{:S(2)}, u32[]{:S(2)}) collective-permute-start(f32[128,512]{1,0:T(8,128)S(1)} %collective-permute-done.refs_2_), channel_id=1, source_target_pairs={{64,0},{96,32},{128,64},{160,96},{192,128},{224,160},{256,192},{28... | collective-permute-start | bytes 786440 | tf_op jit(solution)/shard_map/ppermute | solution.py:213
  36.5 0.0 collective-permute-done.3.refs_3_
  36.5 1.9 %collective-permute-start.8 = (f32[128,512]{1,0:T(8,128)S(1)}, f32[128,512]{1,0:T(8,128)S(1)}, u32[]{:S(2)}, u32[]{:S(2)}) collective-permute-start(f32[128,512]{1,0:T(8,128)S(1)} %collective-permute-done.3.refs_3_), channel_id=1, source_target_pairs={{32,0},{0,32},{96,64},{64,96},{160,128},{128,160},{224,192},{192,2... | collective-permute-start | bytes 786440 | tf_op jit(solution)/shard_map/ppermute | solution.py:213
  38.4 0.0 collective-permute-done.4.refs_4_
  38.4 0.0 collective-permute-done.5.refs_5_
  38.4 0.0 copy-done
  38.4 2.9 %shard_map.50 = (f32[9,128,128]{2,1,0:T(8,128)S(1)}, f32[9,128,128]{2,1,0:T(8,128)S(1)}, bf16[3,128,1024]{2,1,0:T(8,128)(2,1)S(1)}) custom-call(s32[96]{0:T(128)S(1)} %dynamic-slice_bitcast_fusion.table, f32[128,512]{1,0:T(8,128)S(1)} %copy-done, f32[128,512]{1,0:T(8,128)S(1)} %collective-permute-done.2.refs_1_, ...), custom_call_target="tpu_custom_call" | custom-call | flops 268435456 | bytes 1048576 | tf_op jit(solution)/shard_map/pallas_call | solution.py:151
  41.4 4.4 %collective-permute-start.6 = (f32[9,128,128]{2,1,0:T(8,128)S(1)}, f32[9,128,128]{2,1,0:T(8,128)S(1)}, u32[]{:S(2)}, u32[]{:S(2)}) collective-permute-start(f32[9,128,128]{2,1,0:T(8,128)S(1)} %get-tuple-element.15), channel_id=1, source_target_pairs={{0,1},{1,0},{2,3},{3,2},{4,5},{5,4},{6,7},{7,6},{8,9},{9,8},{10,11... | collective-permute-start | bytes 1769480 | tf_op jit(solution)/shard_map/ppermute | solution.py:228
  45.8 0.0 collective-permute-done.7.refs_1_
  45.8 0.0 collective-permute-done.8.refs_2_
  45.8 1.5 %shard_map.51 = (f32[3,128,128]{2,1,0:T(8,128)S(1)}, f32[3,128,128]{2,1,0:T(8,128)S(1)}) custom-call(s32[96]{0:T(128)S(1)} %dynamic-slice_bitcast_fusion.table, bf16[3,128,1024]{2,1,0:T(8,128)(2,1)S(1)} %get-tuple-element.16.refs_0_, f32[128,512]{1,0:T(8,128)S(1)} %collective-permute-done.7.refs_1_, f32[128,512]{1,0:T(8,128)S(1)} %collective-permute-done.8.refs_2_), custom_call_target="tpu_custom_call" | custom-call | flops 34359738368 | bytes 1048576 | tf_op jit(solution)/shard_map/pallas_call | solution.py:151
  47.3 1.9 %collective-permute-start.9 = (f32[3,128,128]{2,1,0:T(8,128)S(1)}, f32[3,128,128]{2,1,0:T(8,128)S(1)}, u32[]{:S(2)}, u32[]{:S(2)}) collective-permute-start(f32[3,128,128]{2,1,0:T(8,128)S(1)} %get-tuple-element.18), channel_id=1, source_target_pairs={{0,1},{1,0},{2,3},{3,2},{4,5},{5,4},{6,7},{7,6},{8,9},{9,8},{10,11... | collective-permute-start | bytes 589832 | tf_op jit(solution)/shard_map/ppermute | solution.py:230
  49.2 1.4 %collective-permute-done.9.refs_3_ = f32[3,128,128]{2,1,0:T(8,128)S(1)} collective-permute-done((f32[3,128,128]{2,1,0:T(8,128)S(1)}, f32[3,128,128]{2,1,0:T(8,128)S(1)}, u32[]{:S(2)}, u32[]{:S(2)}) %collective-permute-start.9) | collective-permute-done | bytes 196640 | tf_op jit(solution)/shard_map/ppermute | solution.py:230
  50.6 0.0 collective-permute-done.6.refs_1_
  50.6 1.5 %shard_map.52 = f32[48,32,128]{2,1,0:T(8,128)} custom-call(s32[96]{0:T(128)S(1)} %dynamic-slice_bitcast_fusion.table, f32[9,128,128]{2,1,0:T(8,128)S(1)} %get-tuple-element.14.refs_0_, f32[9,128,128]{2,1,0:T(8,128)S(1)} %collective-permute-done.6.refs_1_, f32[3,128,128]{2,1,0:T(8,128)S(1)} %get-tuple-element.17.refs_2_, ...), custom_call_target="tpu_custom_call" | custom-call | tf_op jit(solution)/shard_map/pallas_call | solution.py:174
  52.1 8.5 %all-to-all-start = ((f32[16,96,128]{2,1,0:T(8,128)}), f32[16,96,128]{2,1,0:T(8,128)S(1)}, u32[]{:S(2)}, u32[]{:S(2)}) async-start(f32[16,96,128]{2,1,0:T(8,128)} %bitcast.1), calls=%async_computation | async-start | bytes 1572864 | tf_op jit(solution)/shard_map/all_to_all | solution.py:234
  60.6 4.4 %collective-permute-start.12 = (f32[512]{0:T(512)S(1)}, f32[512]{0:T(512)S(1)}, u32[]{:S(2)}, u32[]{:S(2)}) collective-permute-start(f32[512]{0:T(512)S(1)} %add.35), channel_id=1, source_target_pairs={{512,0},{544,32},{576,64},{608,96},{640,128},{672,160},{704,192},{... | collective-permute-start | bytes 6152 | tf_op jit(solution)/shard_map/ppermute | solution.py:210
  65.1 4.7 %collective-permute-start.13 = (f32[512]{0:T(512)S(1)}, f32[512]{0:T(512)S(1)}, u32[]{:S(2)}, u32[]{:S(2)}) collective-permute-start(f32[512]{0:T(512)S(1)} %add.35), channel_id=1, source_target_pairs={{256,0},{288,32},{320,64},{352,96},{384,128},{416,160},{448,192},{... | collective-permute-start | bytes 6152 | tf_op jit(solution)/shard_map/ppermute | solution.py:210
  69.8 0.0 collective-permute-done.12
  69.8 3.7 %collective-permute-done.13 = f32[512]{0:T(512)S(1)} collective-permute-done((f32[512]{0:T(512)S(1)}, f32[512]{0:T(512)S(1)}, u32[]{:S(2)}, u32[]{:S(2)}) %collective-permute-start.13) | collective-permute-done | bytes 2080 | tf_op jit(solution)/shard_map/ppermute | solution.py:210
  73.6 5.1 %collective-permute-start.14 = (f32[512]{0:T(512)S(1)}, f32[512]{0:T(512)S(1)}, u32[]{:S(2)}, u32[]{:S(2)}) collective-permute-start(f32[512]{0:T(512)S(1)} %select_add_fusion), channel_id=1, source_target_pairs={{128,0},{160,32},{192,64},{224,96},{256,128},{288,160},{320,192},{... | collective-permute-start | bytes 6152 | tf_op jit(solution)/shard_map/ppermute | solution.py:210
  78.7 1.9 %collective-permute-start.15 = (f32[512]{0:T(512)S(1)}, f32[512]{0:T(512)S(1)}, u32[]{:S(2)}, u32[]{:S(2)}) collective-permute-start(f32[512]{0:T(512)S(1)} %select_add_fusion), channel_id=1, source_target_pairs={{64,0},{96,32},{128,64},{160,96},{192,128},{224,160},{256,192},{28... | collective-permute-start | bytes 6152 | tf_op jit(solution)/shard_map/ppermute | solution.py:210
  80.6 3.4 %collective-permute-start.16 = (f32[512]{0:T(512)S(1)}, f32[512]{0:T(512)S(1)}, u32[]{:S(2)}, u32[]{:S(2)}) collective-permute-start(f32[512]{0:T(512)S(1)} %select_add_fusion), channel_id=1, source_target_pairs={{704,0},{736,32},{0,64},{32,96},{64,128},{96,160},{128,192},{160,2... | collective-permute-start | bytes 6152 | tf_op jit(solution)/shard_map/ppermute | solution.py:210
  84.0 0.0 all-to-all-done
  84.1 7.9 %collective-permute-start.11 = (f32[64,128]{1,0:T(8,128)S(1)}, f32[64,128]{1,0:T(8,128)S(1)}, u32[]{:S(2)}, u32[]{:S(2)}) collective-permute-start(f32[64,128]{1,0:T(8,128)S(1)} %slice.9), channel_id=1, source_target_pairs={{6,132},{8,120},{28,56},{0,576},{20,5},{10,6},{30,37},{22,38},{14,... | collective-permute-start | bytes 98312 | tf_op jit(solution)/shard_map/ppermute | solution.py:245
  92.0 4.2 %collective-permute-start.10 = (f32[32,128]{1,0:T(8,128)S(1)}, f32[32,128]{1,0:T(8,128)S(1)}, u32[]{:S(2)}, u32[]{:S(2)}) collective-permute-start(f32[32,128]{1,0:T(8,128)S(1)} %slice.8), channel_id=1, source_target_pairs={{8,132},{20,133},{24,120},{26,121},{28,56},{10,57},{0,576},{14,577... | collective-permute-start | bytes 49160 | tf_op jit(solution)/shard_map/ppermute | solution.py:246
  96.2 0.0 collective-permute-done.14
  96.3 0.0 collective-permute-done.15
  96.3 0.0 collective-permute-done.16
  96.3 0.6 add_add_fusion
  96.9 5.3 %collective-permute-done.10 = f32[32,128]{1,0:T(8,128)S(1)} collective-permute-done((f32[32,128]{1,0:T(8,128)S(1)}, f32[32,128]{1,0:T(8,128)S(1)}, u32[]{:S(2)}, u32[]{:S(2)}) %collective-permute-start.10) | collective-permute-done | bytes 16416 | tf_op jit(solution)/shard_map/ppermute | solution.py:246
  102.2 0.0 collective-permute-done.11
  102.2 0.6 fusion
  (5 shorter events, 0.1 us)
Async XLA Ops:
  0.6 37.8 %copy-start = (f32[128,512]{1,0:T(8,128)S(1)}, f32[128,512]{1,0:T(8,128)}, u32[]{:S(2)}) copy-start(f32[128,512]{1,0:T(8,128)} %refs_0_.1) | copy-start | bytes 786436
  0.6 24.9 %collective-permute-start.2 = (f32[128,512]{1,0:T(8,128)}, f32[128,512]{1,0:T(8,128)S(1)}, u32[]{:S(2)}, u32[]{:S(2)}) collective-permute-start(f32[128,512]{1,0:T(8,128)} %refs_0_.1), channel_id=1, source_target_pairs={{64,0},{96,32},{128,64},{160,96},{192,128},{224,160},{256,192},{28... | collective-permute-start | bytes 786440 | tf_op jit(solution)/shard_map/ppermute | solution.py:210
  15.1 19.2 %collective-permute-start = (f32[128,512]{1,0:T(8,128)}, f32[128,512]{1,0:T(8,128)S(1)}, u32[]{:S(2)}, u32[]{:S(2)}) collective-permute-start(f32[128,512]{1,0:T(8,128)} %refs_0_.1), channel_id=1, source_target_pairs={{128,0},{160,32},{192,64},{224,96},{256,128},{288,160},{320,192},{... | collective-permute-start | bytes 786440 | tf_op jit(solution)/shard_map/ppermute | solution.py:213
  17.0 19.5 %collective-permute-start.3 = (f32[128,512]{1,0:T(8,128)}, f32[128,512]{1,0:T(8,128)S(1)}, u32[]{:S(2)}, u32[]{:S(2)}) collective-permute-start(f32[128,512]{1,0:T(8,128)} %refs_0_.1), channel_id=1, source_target_pairs={{576,0},{608,32},{640,64},{672,96},{704,128},{736,160},{0,192},{32... | collective-permute-start | bytes 786440 | tf_op jit(solution)/shard_map/ppermute | solution.py:213
  19.2 19.2 %collective-permute-start.4 = (f32[128,512]{1,0:T(8,128)}, f32[128,512]{1,0:T(8,128)S(1)}, u32[]{:S(2)}, u32[]{:S(2)}) collective-permute-start(f32[128,512]{1,0:T(8,128)} %refs_0_.1), channel_id=1, source_target_pairs={{32,0},{0,32},{96,64},{64,96},{160,128},{128,160},{224,192},{192,2... | collective-permute-start | bytes 786440 | tf_op jit(solution)/shard_map/ppermute | solution.py:210
  22.4 6.0 %collective-permute-start.1 = (f32[512]{0:T(512)S(1)}, f32[512]{0:T(512)S(1)}, u32[]{:S(2)}, u32[]{:S(2)}) collective-permute-start(f32[512]{0:T(512)S(1)} %multiply_reduce_fusion), channel_id=1, source_target_pairs={{32,0},{0,32},{96,64},{64,96},{160,128},{128,160},{224,192},{192,2... | collective-permute-start | bytes 6152 | tf_op jit(solution)/shard_map/ppermute | solution.py:210
  25.6 12.9 %collective-permute-start.5 = (f32[128,512]{1,0:T(8,128)S(1)}, f32[128,512]{1,0:T(8,128)S(1)}, u32[]{:S(2)}, u32[]{:S(2)}) collective-permute-start(f32[128,512]{1,0:T(8,128)S(1)} %collective-permute-done.2.refs_1_), channel_id=1, source_target_pairs={{32,0},{0,32},{96,64},{64,96},{160,128},{128,160},{224,192},{192,2... | collective-permute-start | bytes 786440 | tf_op jit(solution)/shard_map/ppermute | solution.py:210
  34.3 11.5 %collective-permute-start.7 = (f32[128,512]{1,0:T(8,128)S(1)}, f32[128,512]{1,0:T(8,128)S(1)}, u32[]{:S(2)}, u32[]{:S(2)}) collective-permute-start(f32[128,512]{1,0:T(8,128)S(1)} %collective-permute-done.refs_2_), channel_id=1, source_target_pairs={{64,0},{96,32},{128,64},{160,96},{192,128},{224,160},{256,192},{28... | collective-permute-start | bytes 786440 | tf_op jit(solution)/shard_map/ppermute | solution.py:213
  36.5 9.3 %collective-permute-start.8 = (f32[128,512]{1,0:T(8,128)S(1)}, f32[128,512]{1,0:T(8,128)S(1)}, u32[]{:S(2)}, u32[]{:S(2)}) collective-permute-start(f32[128,512]{1,0:T(8,128)S(1)} %collective-permute-done.3.refs_3_), channel_id=1, source_target_pairs={{32,0},{0,32},{96,64},{64,96},{160,128},{128,160},{224,192},{192,2... | collective-permute-start | bytes 786440 | tf_op jit(solution)/shard_map/ppermute | solution.py:213
  41.4 9.3 %collective-permute-start.6 = (f32[9,128,128]{2,1,0:T(8,128)S(1)}, f32[9,128,128]{2,1,0:T(8,128)S(1)}, u32[]{:S(2)}, u32[]{:S(2)}) collective-permute-start(f32[9,128,128]{2,1,0:T(8,128)S(1)} %get-tuple-element.15), channel_id=1, source_target_pairs={{0,1},{1,0},{2,3},{3,2},{4,5},{5,4},{6,7},{7,6},{8,9},{9,8},{10,11... | collective-permute-start | bytes 1769480 | tf_op jit(solution)/shard_map/ppermute | solution.py:228
  47.3 3.3 %collective-permute-start.9 = (f32[3,128,128]{2,1,0:T(8,128)S(1)}, f32[3,128,128]{2,1,0:T(8,128)S(1)}, u32[]{:S(2)}, u32[]{:S(2)}) collective-permute-start(f32[3,128,128]{2,1,0:T(8,128)S(1)} %get-tuple-element.18), channel_id=1, source_target_pairs={{0,1},{1,0},{2,3},{3,2},{4,5},{5,4},{6,7},{7,6},{8,9},{9,8},{10,11... | collective-permute-start | bytes 589832 | tf_op jit(solution)/shard_map/ppermute | solution.py:230
  52.1 31.9 %all-to-all-start = ((f32[16,96,128]{2,1,0:T(8,128)}), f32[16,96,128]{2,1,0:T(8,128)S(1)}, u32[]{:S(2)}, u32[]{:S(2)}) async-start(f32[16,96,128]{2,1,0:T(8,128)} %bitcast.1), calls=%async_computation | async-start | bytes 1572864 | tf_op jit(solution)/shard_map/all_to_all | solution.py:234
  60.6 9.2 %collective-permute-start.12 = (f32[512]{0:T(512)S(1)}, f32[512]{0:T(512)S(1)}, u32[]{:S(2)}, u32[]{:S(2)}) collective-permute-start(f32[512]{0:T(512)S(1)} %add.35), channel_id=1, source_target_pairs={{512,0},{544,32},{576,64},{608,96},{640,128},{672,160},{704,192},{... | collective-permute-start | bytes 6152 | tf_op jit(solution)/shard_map/ppermute | solution.py:210
  65.1 8.5 %collective-permute-start.13 = (f32[512]{0:T(512)S(1)}, f32[512]{0:T(512)S(1)}, u32[]{:S(2)}, u32[]{:S(2)}) collective-permute-start(f32[512]{0:T(512)S(1)} %add.35), channel_id=1, source_target_pairs={{256,0},{288,32},{320,64},{352,96},{384,128},{416,160},{448,192},{... | collective-permute-start | bytes 6152 | tf_op jit(solution)/shard_map/ppermute | solution.py:210
  73.6 22.7 %collective-permute-start.14 = (f32[512]{0:T(512)S(1)}, f32[512]{0:T(512)S(1)}, u32[]{:S(2)}, u32[]{:S(2)}) collective-permute-start(f32[512]{0:T(512)S(1)} %select_add_fusion), channel_id=1, source_target_pairs={{128,0},{160,32},{192,64},{224,96},{256,128},{288,160},{320,192},{... | collective-permute-start | bytes 6152 | tf_op jit(solution)/shard_map/ppermute | solution.py:210
  78.7 17.6 %collective-permute-start.15 = (f32[512]{0:T(512)S(1)}, f32[512]{0:T(512)S(1)}, u32[]{:S(2)}, u32[]{:S(2)}) collective-permute-start(f32[512]{0:T(512)S(1)} %select_add_fusion), channel_id=1, source_target_pairs={{64,0},{96,32},{128,64},{160,96},{192,128},{224,160},{256,192},{28... | collective-permute-start | bytes 6152 | tf_op jit(solution)/shard_map/ppermute | solution.py:210
  80.6 15.7 %collective-permute-start.16 = (f32[512]{0:T(512)S(1)}, f32[512]{0:T(512)S(1)}, u32[]{:S(2)}, u32[]{:S(2)}) collective-permute-start(f32[512]{0:T(512)S(1)} %select_add_fusion), channel_id=1, source_target_pairs={{704,0},{736,32},{0,64},{32,96},{64,128},{96,160},{128,192},{160,2... | collective-permute-start | bytes 6152 | tf_op jit(solution)/shard_map/ppermute | solution.py:210
  84.1 18.1 %collective-permute-start.11 = (f32[64,128]{1,0:T(8,128)S(1)}, f32[64,128]{1,0:T(8,128)S(1)}, u32[]{:S(2)}, u32[]{:S(2)}) collective-permute-start(f32[64,128]{1,0:T(8,128)S(1)} %slice.9), channel_id=1, source_target_pairs={{6,132},{8,120},{28,56},{0,576},{20,5},{10,6},{30,37},{22,38},{14,... | collective-permute-start | bytes 98312 | tf_op jit(solution)/shard_map/ppermute | solution.py:245
  92.0 10.2 %collective-permute-start.10 = (f32[32,128]{1,0:T(8,128)S(1)}, f32[32,128]{1,0:T(8,128)S(1)}, u32[]{:S(2)}, u32[]{:S(2)}) collective-permute-start(f32[32,128]{1,0:T(8,128)S(1)} %slice.8), channel_id=1, source_target_pairs={{8,132},{20,133},{24,120},{26,121},{28,56},{10,57},{0,576},{14,577... | collective-permute-start | bytes 49160 | tf_op jit(solution)/shard_map/ppermute | solution.py:246

commit v15 on v14

--- a/solution.py
+++ b/solution.py
@@ -218,7 +218,7 @@
         pair0 = walk_get(jacobian, 0, 1)
         pair1 = walk_get(up1, 0, 1)
         term = jnp.sum(coeffs[:, None] * jacobian, axis=0)
-        far_a, term, table = tie((far_a, term + walk_get(term, 0, 1), table))
+        far_b, term, table = tie((far_b, term + walk_get(term, 0, 1), table))
         late_a = mixed_get(far_a, (1, 0), (0, 1))
         late_b = mixed_get(far_b, (0, 1), (1, 0))
 

time: 104 us -> 106 us (1.019)
  the two profiles are of different devices: /device:TPU:19 before, /device:TPU:71 now
where the time goes in v15:
time: 106 us
  starting transfers between devices  85.6 us (81%)
  waiting for transfers between devices  10.2 us (10%)
  Pallas kernels  5.9 us (6%)
  other arithmetic  2.33 us (2%)
    ppermute x9, starting transfers between devices, walk_get(): return lax.ppermute(value, 'walk', walk_perm(dz, flip))  31.6 us
    ppermute x4, starting transfers between devices, mixed_get(): return lax.ppermute(value, ('walk', 'par'), mixed_perm(moves))  22.9 us
    ppermute x1, starting transfers between devices, shards(): early = (keep, lax.ppermute(send, 'par', core_swap))  9.7 us
    all_to_all x1, starting transfers between devices, shards(): lax.all_to_all(mine, 'par', 0, 0, axis_index_groups=groups, tiled=True)  9.52 us
    ppermute x1, waiting for transfers between devices, shards(): single = lax.ppermute(mine[2 * SLICE:], ('walk', 'par'), single_perm)  7.52 us
    ppermute x1, starting transfers between devices, shards(): pair = lax.ppermute(mine[:2 * SLICE], ('walk', 'par'), pair_perm)  7.44 us
    pallas_call x2, Pallas kernels, products(): pl.pallas_call(functools.partial(product_kernel, base, count, len(ready),...  4.38 us
    ppermute x1, starting transfers between devices, shards(): single = lax.ppermute(mine[2 * SLICE:], ('walk', 'par'), single_perm)  2.5 us
  transfers between devices with their start and end apart: 18, of which 3 were waited for; matrix products, arithmetic and copies ran while one was open for 2% of the time, Pallas kernels for 4%

profile of v15, /device:TPU:71, one launch (start us, length us, event | category | flops | bytes accessed | tf_op | source)
XLA Modules:
  0.0 105.7 jit_solution(7377316204413442228)
XLA Ops:
  0.6 0.0 copy-start
  0.6 2.1 %collective-permute-start.2 = (f32[128,512]{1,0:T(8,128)}, f32[128,512]{1,0:T(8,128)S(1)}, u32[]{:S(2)}, u32[]{:S(2)}) collective-permute-start(f32[128,512]{1,0:T(8,128)} %refs_0_.1), channel_id=1, source_target_pairs={{64,0},{96,32},{128,64},{160,96},{192,128},{224,160},{256,192},{28... | collective-permute-start | bytes 786440 | tf_op jit(solution)/shard_map/ppermute | solution.py:210
  2.7 13.7 %collective-permute-start = (f32[128,512]{1,0:T(8,128)}, f32[128,512]{1,0:T(8,128)S(1)}, u32[]{:S(2)}, u32[]{:S(2)}) collective-permute-start(f32[128,512]{1,0:T(8,128)} %refs_0_.1), channel_id=1, source_target_pairs={{576,0},{608,32},{640,64},{672,96},{704,128},{736,160},{0,192},{32... | collective-permute-start | bytes 786440 | tf_op jit(solution)/shard_map/ppermute | solution.py:213
  16.4 1.9 %collective-permute-start.3 = (f32[128,512]{1,0:T(8,128)}, f32[128,512]{1,0:T(8,128)S(1)}, u32[]{:S(2)}, u32[]{:S(2)}) collective-permute-start(f32[128,512]{1,0:T(8,128)} %refs_0_.1), channel_id=1, source_target_pairs={{128,0},{160,32},{192,64},{224,96},{256,128},{288,160},{320,192},{... | collective-permute-start | bytes 786440 | tf_op jit(solution)/shard_map/ppermute | solution.py:213
  18.3 2.5 %collective-permute-start.4 = (f32[128,512]{1,0:T(8,128)}, f32[128,512]{1,0:T(8,128)S(1)}, u32[]{:S(2)}, u32[]{:S(2)}) collective-permute-start(f32[128,512]{1,0:T(8,128)} %refs_0_.1), channel_id=1, source_target_pairs={{32,0},{0,32},{96,64},{64,96},{160,128},{128,160},{224,192},{192,2... | collective-permute-start | bytes 786440 | tf_op jit(solution)/shard_map/ppermute | solution.py:210
  20.8 1.1 %multiply_reduce_fusion = f32[512]{0:T(512)S(1)} fusion(f32[128,512]{1,0:T(8,128)} %refs_0_.1, f32[128]{0:T(128)} %param.4), kind=kLoop, calls=%fused_computation | loop fusion | flops 130560 | bytes 264704 | tf_op jit(solution)/shard_map/reduce_sum | solution.py:220
  21.8 2.8 %collective-permute-start.1 = (f32[512]{0:T(512)S(1)}, f32[512]{0:T(512)S(1)}, u32[]{:S(2)}, u32[]{:S(2)}) collective-permute-start(f32[512]{0:T(512)S(1)} %multiply_reduce_fusion), channel_id=1, source_target_pairs={{32,0},{0,32},{96,64},{64,96},{160,128},{128,160},{224,192},{192,2... | collective-permute-start | bytes 6152 | tf_op jit(solution)/shard_map/ppermute | solution.py:210
  24.7 0.0 collective-permute-done.2.refs_1_
  24.7 2.5 %collective-permute-start.5 = (f32[128,512]{1,0:T(8,128)S(1)}, f32[128,512]{1,0:T(8,128)S(1)}, u32[]{:S(2)}, u32[]{:S(2)}) collective-permute-start(f32[128,512]{1,0:T(8,128)S(1)} %collective-permute-done.2.refs_1_), channel_id=1, source_target_pairs={{32,0},{0,32},{96,64},{64,96},{160,128},{128,160},{224,192},{192,2... | collective-permute-start | bytes 786440 | tf_op jit(solution)/shard_map/ppermute | solution.py:210
  27.1 0.7 dynamic-slice_bitcast_fusion.table
  27.8 0.0 collective-permute-done.1
  27.9 0.0 collective-permute-done.refs_3_
  27.9 4.9 %collective-permute-start.8 = (f32[128,512]{1,0:T(8,128)S(1)}, f32[128,512]{1,0:T(8,128)S(1)}, u32[]{:S(2)}, u32[]{:S(2)}) collective-permute-start(f32[128,512]{1,0:T(8,128)S(1)} %collective-permute-done.refs_3_), channel_id=1, source_target_pairs={{32,0},{0,32},{96,64},{64,96},{160,128},{128,160},{224,192},{192,2... | collective-permute-start | bytes 786440 | tf_op jit(solution)/shard_map/ppermute | solution.py:213
  32.7 0.0 collective-permute-done.3.refs_2_
  32.7 2.5 %collective-permute-start.7 = (f32[128,512]{1,0:T(8,128)S(1)}, f32[128,512]{1,0:T(8,128)S(1)}, u32[]{:S(2)}, u32[]{:S(2)}) collective-permute-start(f32[128,512]{1,0:T(8,128)S(1)} %collective-permute-done.3.refs_2_), channel_id=1, source_target_pairs={{64,0},{96,32},{128,64},{160,96},{192,128},{224,160},{256,192},{28... | collective-permute-start | bytes 786440 | tf_op jit(solution)/shard_map/ppermute | solution.py:213
  35.2 0.0 collective-permute-done.4.refs_4_
  35.2 0.0 collective-permute-done.5.refs_5_
  35.2 0.0 copy-done
  35.2 2.9 %shard_map.50 = (f32[9,128,128]{2,1,0:T(8,128)S(1)}, f32[9,128,128]{2,1,0:T(8,128)S(1)}, bf16[3,128,1024]{2,1,0:T(8,128)(2,1)S(1)}) custom-call(s32[96]{0:T(128)S(1)} %dynamic-slice_bitcast_fusion.table, f32[128,512]{1,0:T(8,128)S(1)} %copy-done, f32[128,512]{1,0:T(8,128)S(1)} %collective-permute-done.2.refs_1_, ...), custom_call_target="tpu_custom_call" | custom-call | flops 268435456 | bytes 1048576 | tf_op jit(solution)/shard_map/pallas_call | solution.py:151
  38.1 9.7 %collective-permute-start.6 = (f32[9,128,128]{2,1,0:T(8,128)S(1)}, f32[9,128,128]{2,1,0:T(8,128)S(1)}, u32[]{:S(2)}, u32[]{:S(2)}) collective-permute-start(f32[9,128,128]{2,1,0:T(8,128)S(1)} %get-tuple-element.15), channel_id=1, source_target_pairs={{0,1},{1,0},{2,3},{3,2},{4,5},{5,4},{6,7},{7,6},{8,9},{9,8},{10,11... | collective-permute-start | bytes 1769480 | tf_op jit(solution)/shard_map/ppermute | solution.py:228
  47.9 0.0 collective-permute-done.8.refs_2_
  47.9 0.0 collective-permute-done.7.refs_1_
  47.9 1.5 %shard_map.51 = (f32[3,128,128]{2,1,0:T(8,128)S(1)}, f32[3,128,128]{2,1,0:T(8,128)S(1)}) custom-call(s32[96]{0:T(128)S(1)} %dynamic-slice_bitcast_fusion.table, bf16[3,128,1024]{2,1,0:T(8,128)(2,1)S(1)} %get-tuple-element.16.refs_0_, f32[128,512]{1,0:T(8,128)S(1)} %collective-permute-done.7.refs_1_, f32[128,512]{1,0:T(8,128)S(1)} %collective-permute-done.8.refs_2_), custom_call_target="tpu_custom_call" | custom-call | flops 34359738368 | bytes 1048576 | tf_op jit(solution)/shard_map/pallas_call | solution.py:151
  49.4 1.9 %collective-permute-start.9 = (f32[3,128,128]{2,1,0:T(8,128)S(1)}, f32[3,128,128]{2,1,0:T(8,128)S(1)}, u32[]{:S(2)}, u32[]{:S(2)}) collective-permute-start(f32[3,128,128]{2,1,0:T(8,128)S(1)} %get-tuple-element.18), channel_id=1, source_target_pairs={{0,1},{1,0},{2,3},{3,2},{4,5},{5,4},{6,7},{7,6},{8,9},{9,8},{10,11... | collective-permute-start | bytes 589832 | tf_op jit(solution)/shard_map/ppermute | solution.py:230
  51.3 1.4 %collective-permute-done.9.refs_3_ = f32[3,128,128]{2,1,0:T(8,128)S(1)} collective-permute-done((f32[3,128,128]{2,1,0:T(8,128)S(1)}, f32[3,128,128]{2,1,0:T(8,128)S(1)}, u32[]{:S(2)}, u32[]{:S(2)}) %collective-permute-start.9) | collective-permute-done | bytes 196640 | tf_op jit(solution)/shard_map/ppermute | solution.py:230
  52.7 0.0 collective-permute-done.6.refs_1_
  52.7 1.5 %shard_map.52 = f32[48,32,128]{2,1,0:T(8,128)} custom-call(s32[96]{0:T(128)S(1)} %dynamic-slice_bitcast_fusion.table, f32[9,128,128]{2,1,0:T(8,128)S(1)} %get-tuple-element.14.refs_0_, f32[9,128,128]{2,1,0:T(8,128)S(1)} %collective-permute-done.6.refs_1_, f32[3,128,128]{2,1,0:T(8,128)S(1)} %get-tuple-element.17.refs_2_, ...), custom_call_target="tpu_custom_call" | custom-call | tf_op jit(solution)/shard_map/pallas_call | solution.py:174
  54.2 9.5 %all-to-all-start = ((f32[16,96,128]{2,1,0:T(8,128)}), f32[16,96,128]{2,1,0:T(8,128)S(1)}, u32[]{:S(2)}, u32[]{:S(2)}) async-start(f32[16,96,128]{2,1,0:T(8,128)} %bitcast.1), calls=%async_computation | async-start | bytes 1572864 | tf_op jit(solution)/shard_map/all_to_all | solution.py:234
  63.7 1.9 %collective-permute-start.12 = (f32[512]{0:T(512)S(1)}, f32[512]{0:T(512)S(1)}, u32[]{:S(2)}, u32[]{:S(2)}) collective-permute-start(f32[512]{0:T(512)S(1)} %add.35), channel_id=1, source_target_pairs={{512,0},{544,32},{576,64},{608,96},{640,128},{672,160},{704,192},{... | collective-permute-start | bytes 6152 | tf_op jit(solution)/shard_map/ppermute | solution.py:210
  65.7 7.3 %collective-permute-start.13 = (f32[512]{0:T(512)S(1)}, f32[512]{0:T(512)S(1)}, u32[]{:S(2)}, u32[]{:S(2)}) collective-permute-start(f32[512]{0:T(512)S(1)} %add.35), channel_id=1, source_target_pairs={{256,0},{288,32},{320,64},{352,96},{384,128},{416,160},{448,192},{... | collective-permute-start | bytes 6152 | tf_op jit(solution)/shard_map/ppermute | solution.py:210
  73.0 0.0 collective-permute-done.12
  73.0 1.2 %collective-permute-done.13 = f32[512]{0:T(512)S(1)} collective-permute-done((f32[512]{0:T(512)S(1)}, f32[512]{0:T(512)S(1)}, u32[]{:S(2)}, u32[]{:S(2)}) %collective-permute-start.13) | collective-permute-done | bytes 2080 | tf_op jit(solution)/shard_map/ppermute | solution.py:210
  74.2 7.4 %collective-permute-start.14 = (f32[512]{0:T(512)S(1)}, f32[512]{0:T(512)S(1)}, u32[]{:S(2)}, u32[]{:S(2)}) collective-permute-start(f32[512]{0:T(512)S(1)} %select_add_fusion), channel_id=1, source_target_pairs={{128,0},{160,32},{192,64},{224,96},{256,128},{288,160},{320,192},{... | collective-permute-start | bytes 6152 | tf_op jit(solution)/shard_map/ppermute | solution.py:210
  81.6 1.9 %collective-permute-start.15 = (f32[512]{0:T(512)S(1)}, f32[512]{0:T(512)S(1)}, u32[]{:S(2)}, u32[]{:S(2)}) collective-permute-start(f32[512]{0:T(512)S(1)} %select_add_fusion), channel_id=1, source_target_pairs={{64,0},{96,32},{128,64},{160,96},{192,128},{224,160},{256,192},{28... | collective-permute-start | bytes 6152 | tf_op jit(solution)/shard_map/ppermute | solution.py:210
  83.5 3.4 %collective-permute-start.16 = (f32[512]{0:T(512)S(1)}, f32[512]{0:T(512)S(1)}, u32[]{:S(2)}, u32[]{:S(2)}) collective-permute-start(f32[512]{0:T(512)S(1)} %select_add_fusion), channel_id=1, source_target_pairs={{704,0},{736,32},{0,64},{32,96},{64,128},{96,160},{128,192},{160,2... | collective-permute-start | bytes 6152 | tf_op jit(solution)/shard_map/ppermute | solution.py:210
  86.9 0.0 all-to-all-done
  87.0 7.4 %collective-permute-start.11 = (f32[64,128]{1,0:T(8,128)S(1)}, f32[64,128]{1,0:T(8,128)S(1)}, u32[]{:S(2)}, u32[]{:S(2)}) collective-permute-start(f32[64,128]{1,0:T(8,128)S(1)} %slice.9), channel_id=1, source_target_pairs={{6,132},{8,120},{28,56},{0,576},{20,5},{10,6},{30,37},{22,38},{14,... | collective-permute-start | bytes 98312 | tf_op jit(solution)/shard_map/ppermute | solution.py:245
  94.4 2.5 %collective-permute-start.10 = (f32[32,128]{1,0:T(8,128)S(1)}, f32[32,128]{1,0:T(8,128)S(1)}, u32[]{:S(2)}, u32[]{:S(2)}) collective-permute-start(f32[32,128]{1,0:T(8,128)S(1)} %slice.8), channel_id=1, source_target_pairs={{8,132},{20,133},{24,120},{26,121},{28,56},{10,57},{0,576},{14,577... | collective-permute-start | bytes 49160 | tf_op jit(solution)/shard_map/ppermute | solution.py:246
  96.9 0.0 collective-permute-done.14
  96.9 0.0 collective-permute-done.15
  96.9 0.0 collective-permute-done.16
  96.9 0.6 add_add_fusion
  97.5 7.5 %collective-permute-done.10 = f32[32,128]{1,0:T(8,128)S(1)} collective-permute-done((f32[32,128]{1,0:T(8,128)S(1)}, f32[32,128]{1,0:T(8,128)S(1)}, u32[]{:S(2)}, u32[]{:S(2)}) %collective-permute-start.10) | collective-permute-done | bytes 16416 | tf_op jit(solution)/shard_map/ppermute | solution.py:246
  105.0 0.0 collective-permute-done.11
  105.1 0.6 fusion
  (5 shorter events, 0.1 us)
Async XLA Ops:
  0.6 34.6 %copy-start = (f32[128,512]{1,0:T(8,128)S(1)}, f32[128,512]{1,0:T(8,128)}, u32[]{:S(2)}) copy-start(f32[128,512]{1,0:T(8,128)} %refs_0_.1) | copy-start | bytes 786436
  0.6 24.0 %collective-permute-start.2 = (f32[128,512]{1,0:T(8,128)}, f32[128,512]{1,0:T(8,128)S(1)}, u32[]{:S(2)}, u32[]{:S(2)}) collective-permute-start(f32[128,512]{1,0:T(8,128)} %refs_0_.1), channel_id=1, source_target_pairs={{64,0},{96,32},{128,64},{160,96},{192,128},{224,160},{256,192},{28... | collective-permute-start | bytes 786440 | tf_op jit(solution)/shard_map/ppermute | solution.py:210
  2.7 25.2 %collective-permute-start = (f32[128,512]{1,0:T(8,128)}, f32[128,512]{1,0:T(8,128)S(1)}, u32[]{:S(2)}, u32[]{:S(2)}) collective-permute-start(f32[128,512]{1,0:T(8,128)} %refs_0_.1), channel_id=1, source_target_pairs={{576,0},{608,32},{640,64},{672,96},{704,128},{736,160},{0,192},{32... | collective-permute-start | bytes 786440 | tf_op jit(solution)/shard_map/ppermute | solution.py:213
  16.4 16.4 %collective-permute-start.3 = (f32[128,512]{1,0:T(8,128)}, f32[128,512]{1,0:T(8,128)S(1)}, u32[]{:S(2)}, u32[]{:S(2)}) collective-permute-start(f32[128,512]{1,0:T(8,128)} %refs_0_.1), channel_id=1, source_target_pairs={{128,0},{160,32},{192,64},{224,96},{256,128},{288,160},{320,192},{... | collective-permute-start | bytes 786440 | tf_op jit(solution)/shard_map/ppermute | solution.py:213
  18.3 16.9 %collective-permute-start.4 = (f32[128,512]{1,0:T(8,128)}, f32[128,512]{1,0:T(8,128)S(1)}, u32[]{:S(2)}, u32[]{:S(2)}) collective-permute-start(f32[128,512]{1,0:T(8,128)} %refs_0_.1), channel_id=1, source_target_pairs={{32,0},{0,32},{96,64},{64,96},{160,128},{128,160},{224,192},{192,2... | collective-permute-start | bytes 786440 | tf_op jit(solution)/shard_map/ppermute | solution.py:210
  21.8 6.0 %collective-permute-start.1 = (f32[512]{0:T(512)S(1)}, f32[512]{0:T(512)S(1)}, u32[]{:S(2)}, u32[]{:S(2)}) collective-permute-start(f32[512]{0:T(512)S(1)} %multiply_reduce_fusion), channel_id=1, source_target_pairs={{32,0},{0,32},{96,64},{64,96},{160,128},{128,160},{224,192},{192,2... | collective-permute-start | bytes 6152 | tf_op jit(solution)/shard_map/ppermute | solution.py:210
  24.7 10.5 %collective-permute-start.5 = (f32[128,512]{1,0:T(8,128)S(1)}, f32[128,512]{1,0:T(8,128)S(1)}, u32[]{:S(2)}, u32[]{:S(2)}) collective-permute-start(f32[128,512]{1,0:T(8,128)S(1)} %collective-permute-done.2.refs_1_), channel_id=1, source_target_pairs={{32,0},{0,32},{96,64},{64,96},{160,128},{128,160},{224,192},{192,2... | collective-permute-start | bytes 786440 | tf_op jit(solution)/shard_map/ppermute | solution.py:210
  27.9 20.0 %collective-permute-start.8 = (f32[128,512]{1,0:T(8,128)S(1)}, f32[128,512]{1,0:T(8,128)S(1)}, u32[]{:S(2)}, u32[]{:S(2)}) collective-permute-start(f32[128,512]{1,0:T(8,128)S(1)} %collective-permute-done.refs_3_), channel_id=1, source_target_pairs={{32,0},{0,32},{96,64},{64,96},{160,128},{128,160},{224,192},{192,2... | collective-permute-start | bytes 786440 | tf_op jit(solution)/shard_map/ppermute | solution.py:213
  32.7 15.1 %collective-permute-start.7 = (f32[128,512]{1,0:T(8,128)S(1)}, f32[128,512]{1,0:T(8,128)S(1)}, u32[]{:S(2)}, u32[]{:S(2)}) collective-permute-start(f32[128,512]{1,0:T(8,128)S(1)} %collective-permute-done.3.refs_2_), channel_id=1, source_target_pairs={{64,0},{96,32},{128,64},{160,96},{192,128},{224,160},{256,192},{28... | collective-permute-start | bytes 786440 | tf_op jit(solution)/shard_map/ppermute | solution.py:213
  38.1 14.5 %collective-permute-start.6 = (f32[9,128,128]{2,1,0:T(8,128)S(1)}, f32[9,128,128]{2,1,0:T(8,128)S(1)}, u32[]{:S(2)}, u32[]{:S(2)}) collective-permute-start(f32[9,128,128]{2,1,0:T(8,128)S(1)} %get-tuple-element.15), channel_id=1, source_target_pairs={{0,1},{1,0},{2,3},{3,2},{4,5},{5,4},{6,7},{7,6},{8,9},{9,8},{10,11... | collective-permute-start | bytes 1769480 | tf_op jit(solution)/shard_map/ppermute | solution.py:228
  49.4 3.3 %collective-permute-start.9 = (f32[3,128,128]{2,1,0:T(8,128)S(1)}, f32[3,128,128]{2,1,0:T(8,128)S(1)}, u32[]{:S(2)}, u32[]{:S(2)}) collective-permute-start(f32[3,128,128]{2,1,0:T(8,128)S(1)} %get-tuple-element.18), channel_id=1, source_target_pairs={{0,1},{1,0},{2,3},{3,2},{4,5},{5,4},{6,7},{7,6},{8,9},{9,8},{10,11... | collective-permute-start | bytes 589832 | tf_op jit(solution)/shard_map/ppermute | solution.py:230
  54.2 32.7 %all-to-all-start = ((f32[16,96,128]{2,1,0:T(8,128)}), f32[16,96,128]{2,1,0:T(8,128)S(1)}, u32[]{:S(2)}, u32[]{:S(2)}) async-start(f32[16,96,128]{2,1,0:T(8,128)} %bitcast.1), calls=%async_computation | async-start | bytes 1572864 | tf_op jit(solution)/shard_map/all_to_all | solution.py:234
  63.7 9.2 %collective-permute-start.12 = (f32[512]{0:T(512)S(1)}, f32[512]{0:T(512)S(1)}, u32[]{:S(2)}, u32[]{:S(2)}) collective-permute-start(f32[512]{0:T(512)S(1)} %add.35), channel_id=1, source_target_pairs={{512,0},{544,32},{576,64},{608,96},{640,128},{672,160},{704,192},{... | collective-permute-start | bytes 6152 | tf_op jit(solution)/shard_map/ppermute | solution.py:210
  65.7 8.5 %collective-permute-start.13 = (f32[512]{0:T(512)S(1)}, f32[512]{0:T(512)S(1)}, u32[]{:S(2)}, u32[]{:S(2)}) collective-permute-start(f32[512]{0:T(512)S(1)} %add.35), channel_id=1, source_target_pairs={{256,0},{288,32},{320,64},{352,96},{384,128},{416,160},{448,192},{... | collective-permute-start | bytes 6152 | tf_op jit(solution)/shard_map/ppermute | solution.py:210
  74.2 22.7 %collective-permute-start.14 = (f32[512]{0:T(512)S(1)}, f32[512]{0:T(512)S(1)}, u32[]{:S(2)}, u32[]{:S(2)}) collective-permute-start(f32[512]{0:T(512)S(1)} %select_add_fusion), channel_id=1, source_target_pairs={{128,0},{160,32},{192,64},{224,96},{256,128},{288,160},{320,192},{... | collective-permute-start | bytes 6152 | tf_op jit(solution)/shard_map/ppermute | solution.py:210
  81.6 15.4 %collective-permute-start.15 = (f32[512]{0:T(512)S(1)}, f32[512]{0:T(512)S(1)}, u32[]{:S(2)}, u32[]{:S(2)}) collective-permute-start(f32[512]{0:T(512)S(1)} %select_add_fusion), channel_id=1, source_target_pairs={{64,0},{96,32},{128,64},{160,96},{192,128},{224,160},{256,192},{28... | collective-permute-start | bytes 6152 | tf_op jit(solution)/shard_map/ppermute | solution.py:210
  83.5 13.5 %collective-permute-start.16 = (f32[512]{0:T(512)S(1)}, f32[512]{0:T(512)S(1)}, u32[]{:S(2)}, u32[]{:S(2)}) collective-permute-start(f32[512]{0:T(512)S(1)} %select_add_fusion), channel_id=1, source_target_pairs={{704,0},{736,32},{0,64},{32,96},{64,128},{96,160},{128,192},{160,2... | collective-permute-start | bytes 6152 | tf_op jit(solution)/shard_map/ppermute | solution.py:210
  87.0 18.1 %collective-permute-start.11 = (f32[64,128]{1,0:T(8,128)S(1)}, f32[64,128]{1,0:T(8,128)S(1)}, u32[]{:S(2)}, u32[]{:S(2)}) collective-permute-start(f32[64,128]{1,0:T(8,128)S(1)} %slice.9), channel_id=1, source_target_pairs={{6,132},{8,120},{28,56},{0,576},{20,5},{10,6},{30,37},{22,38},{14,... | collective-permute-start | bytes 98312 | tf_op jit(solution)/shard_map/ppermute | solution.py:245
  94.4 10.6 %collective-permute-start.10 = (f32[32,128]{1,0:T(8,128)S(1)}, f32[32,128]{1,0:T(8,128)S(1)}, u32[]{:S(2)}, u32[]{:S(2)}) collective-permute-start(f32[32,128]{1,0:T(8,128)S(1)} %slice.8), channel_id=1, source_target_pairs={{8,132},{20,133},{24,120},{26,121},{28,56},{10,57},{0,576},{14,577... | collective-permute-start | bytes 49160 | tf_op jit(solution)/shard_map/ppermute | solution.py:246
